TPU v7x, 32 devices: a whole 2x2x4 slice. The times are simulated.
32 devices in a mesh: seq: 8 (over z, x), bin: 4 (over y, core).
Axes of the slice: x: 2, y: 2, z: 4, core: 2. Of those that a mesh axis runs over, the one named last changes fastest.
Arguments:
- tokens: bfloat16 [4, 48, 24, 768], P('bin', 'seq'), may hold values from -8 to 8
- timestep: int32 [1], replicated, may hold values from 0 to 999
- mod_weight: bfloat16 [256, 3072], replicated, may hold values from -0.375 to 0.375
- col_qkv: bfloat16 [768, 2304], replicated, may hold values from -0.41650635 to 0.41650635
- col_out: bfloat16 [768, 768], replicated, may hold values from -0.21875 to 0.21875
- bin_qkv: bfloat16 [768, 2304], replicated, may hold values from -0.41650635 to 0.41650635
- bin_out: bfloat16 [768, 768], replicated, may hold values from -0.21875 to 0.21875
Outputs:
- result: bfloat16 [4, 48, 24, 768], P('bin', 'seq')
All inputs are finite; a program needn't handle non-finite values.
Results may differ from a plain program's by a relative error of at most 0.012.
Values may be sent and summed in bfloat16 or wider, within the bound.
No kernel may reach another device: no remote copies, remote signals or barrier semaphores. Data moves between devices by JAX's collectives and lax.ppermute only.
A program may use at most 128 MiB of HBM per device.

v0:
```python
import math

import jax
import jax.numpy as jnp
from jax import lax
from jax.sharding import PartitionSpec as P

D = 768
HEADS = 12
HD = 64
FREQ = 256


def modulation(timestep, mod_weight):
    half = FREQ // 2
    freqs = jnp.exp(-math.log(10000.0) * jnp.arange(half, dtype=jnp.float32) / half)
    angle = timestep.astype(jnp.float32)[0] * freqs
    emb = jax.nn.silu(jnp.concatenate([jnp.cos(angle), jnp.sin(angle)])).astype(jnp.bfloat16)
    return jnp.dot(emb[None, :], mod_weight, preferred_element_type=jnp.float32)[0]


def layer_norm(values, shift, scale):
    xf = values.astype(jnp.float32)
    mean = jnp.mean(xf, axis=-1, keepdims=True)
    var = jnp.mean((xf - mean) ** 2, axis=-1, keepdims=True)
    return ((xf - mean) * lax.rsqrt(var + 1e-06) * (1.0 + scale) + shift).astype(jnp.bfloat16)


def across_bins(query, key, value):
    scores = jnp.sum(
        query.astype(jnp.float32)[:, None] * key.astype(jnp.float32)[None], axis=-1
    ) * HD ** (-0.5)
    weights = jax.nn.softmax(scores, axis=1).astype(jnp.bfloat16)
    context = jnp.sum(
        weights.astype(jnp.float32)[..., None] * value.astype(jnp.float32)[None], axis=1
    )
    return context.astype(jnp.bfloat16)


def per_device(tokens, timestep, mod_weight, col_qkv, col_out, bin_qkv, bin_out):
    mod = modulation(timestep, mod_weight)
    shift1, scale1, shift2, scale2 = (mod[:D], mod[D : 2 * D], mod[2 * D : 3 * D], mod[3 * D :])
    rows_here = tokens.shape[1]
    width_all = tokens.shape[2]
    owners = lax.axis_size("seq")
    cols_each = width_all // owners
    normed1 = layer_norm(tokens, shift1, scale1)
    grouped = normed1.reshape(1, rows_here, owners, cols_each, D)
    query_weight = col_qkv[:, :D].reshape(D, HEADS, HD)
    key_weight = col_qkv[:, D : 2 * D].reshape(D, HEADS, HD)
    value_weight = col_qkv[:, 2 * D :].reshape(D, HEADS, HD)
    out_weight = col_out.reshape(HEADS, HD, D)
    piece = lax.all_to_all(grouped, "seq", split_axis=2, concat_axis=1, tiled=True)
    height = piece.shape[1]
    count = piece.shape[3]
    local = piece[0, :, 0]
    query = jnp.einsum(
        "iwc,chd->whid", local, query_weight, preferred_element_type=jnp.float32
    ).astype(jnp.bfloat16)
    key = jnp.einsum("iwc,chd->whid", local, key_weight, preferred_element_type=jnp.float32).astype(
        jnp.bfloat16
    )
    value = jnp.einsum(
        "iwc,chd->whid", local, value_weight, preferred_element_type=jnp.float32
    ).astype(jnp.bfloat16)
    scores = jnp.einsum("whid,whjd->whij", query, key, preferred_element_type=jnp.float32) * HD ** (
        -0.5
    )
    weights = jax.nn.softmax(scores, axis=-1).astype(jnp.bfloat16)
    context = jnp.einsum(
        "whij,whjd->whid", weights, value, preferred_element_type=jnp.float32
    ).astype(jnp.bfloat16)
    out = jnp.einsum(
        "whid,hde->iwe", context, out_weight, preferred_element_type=jnp.float32
    ).astype(jnp.bfloat16)
    attended = out.reshape(1, height, 1, count, D)
    back = lax.all_to_all(attended, "seq", split_axis=1, concat_axis=2, tiled=True)
    back = back.reshape(1, rows_here, width_all, D)
    hidden = (tokens.astype(jnp.float32) + back.astype(jnp.float32)).astype(jnp.bfloat16)
    normed2 = layer_norm(hidden, shift2, scale2)
    flat = normed2.reshape(-1, D)
    positions = flat.shape[0]
    every = lax.all_gather(normed2, "bin", axis=0, tiled=True)
    nbins = every.shape[0]
    every_flat = every.reshape(-1, D)
    query = jnp.dot(flat, bin_qkv[:, :D], preferred_element_type=jnp.float32).astype(jnp.bfloat16)
    keys_all = jnp.dot(
        every_flat, bin_qkv[:, D : 2 * D], preferred_element_type=jnp.float32
    ).astype(jnp.bfloat16)
    values_all = jnp.dot(
        every_flat, bin_qkv[:, 2 * D :], preferred_element_type=jnp.float32
    ).astype(jnp.bfloat16)
    context = across_bins(
        query.reshape(1, positions, HEADS, HD),
        keys_all.reshape(nbins, positions, HEADS, HD),
        values_all.reshape(nbins, positions, HEADS, HD),
    )
    projected = jnp.dot(context.reshape(-1, D), bin_out, preferred_element_type=jnp.float32)
    projected = projected.reshape(1, rows_here, width_all, D)
    return (hidden.astype(jnp.float32) + projected).astype(jnp.bfloat16)


def solution(mesh):
    placed = (P("bin", "seq", None, None), P(), P(), P(), P(), P(), P())
    return jax.shard_map(
        per_device,
        mesh=mesh,
        in_specs=placed,
        out_specs=P("bin", "seq", None, None),
        check_vma=False,
    )
```

profile of v0, /device:TPU:0, one launch (start us, length us, event | category | flops | bytes accessed | tf_op | source)
XLA Modules:
  0.0 85.4 jit_solution(10393501054150509935)
XLA Ops:
  0.9 0.6 copy-done
  1.4 0.3 fusion.60
  2.4 0.8 copy.19
  3.2 7.3 %all-to-all-start = ((bf16[1,6,8,3,768]{4,3,1,0,2:T(4,128)(2,1)}), bf16[1,6,8,3,768]{4,3,1,0,2:T(4,128)(2,1)S(1)}, u32[]{:S(2)}, u32[]{:S(2)}) async-start(bf16[1,6,8,3,768]{4,3,1,0,2:T(4,128)(2,1)} %copy.19), calls=%async_computation | async-start | bytes 589824 | tf_op jit(solution)/shard_map/all_to_all | solution.py:53
  10.5 3.6 %fusion.56 = (bf16[768,768]{1,0:T(8,128)(2,1)}, bf16[768,768]{1,0:T(8,128)(2,1)}, bf16[768,768]{1,0:T(8,128)(2,1)S(1)}) fusion(bf16[768,2304]{1,0:T(8,128)(2,1)} %param.10), kind=kLoop, calls=%fused_computation.77 | loop fusion | bytes 7077888 | tf_op jit(solution)/shard_map/slice | solution.py:49
  14.1 2.4 %copy.39 = bf16[768,768]{0,1:T(8,128)(2,1)} copy(bf16[768,768]{1,0:T(8,128)(2,1)} %get-tuple-element.8) | data formatting | bytes 2359296
  16.5 2.4 %copy.38 = bf16[768,768]{0,1:T(8,128)(2,1)} copy(bf16[768,768]{1,0:T(8,128)(2,1)} %get-tuple-element.7) | data formatting | bytes 2359296
  18.8 1.4 %copy.40 = bf16[768,768]{0,1:T(8,128)(2,1)} copy(bf16[768,768]{1,0:T(8,128)(2,1)S(1)} %get-tuple-element.9) | data formatting | bytes 2359296
  20.3 2.9 %fusion.10 = bf16[3,12,48,64]{3,2,1,0:T(8,128)(2,1)} fusion(bf16[768,12,64,1]{0,2,1,3:T(8,128)(2,1)} %bitcast.81, bf16[48,3,768,1]{2,1,0,3:T(4,128)(2,1)S(1)} %bitcast.85), kind=kOutput, calls=%fused_computation.19 | convolution fusion | flops 169979904 | bytes 1622016 | tf_op jit(solution)/shard_map/iwc,chd->whid/dot_general | solution.py:60
  23.1 1.5 %fusion.11 = bf16[3,12,48,64]{3,2,1,0:T(8,128)(2,1)} fusion(bf16[768,12,64,1]{0,2,1,3:T(8,128)(2,1)S(1)} %bitcast.82, bf16[48,3,768,1]{2,1,0,3:T(4,128)(2,1)S(1)} %bitcast.86), kind=kOutput, calls=%fused_computation.20 | convolution fusion | flops 169979904 | bytes 1622016 | tf_op jit(solution)/shard_map/iwc,chd->whid/dot_general | solution.py:63
  24.7 3.0 %fusion.57 = (f32[3,12,48]{2,1,0:T(8,128)S(1)}, f32[3,12,48,48]{2,3,1,0:T(8,128)}) fusion(bf16[3,12,48,64]{3,2,1,0:T(8,128)(2,1)} %fusion.10, bf16[768,12,64,1]{0,2,1,3:T(8,128)(2,1)S(1)} %bitcast.80, bf16[48,3,768,1]{2,1,0,3:T(4,128)(2,1)S(1)} %bitcast.87), kind=kOutput, calls=%fused_computation.78 | convolution fusion | flops 180845616 | bytes 1960704 | tf_op jit(solution)/shard_map/sub | solution.py:69
  27.7 2.3 %fusion.20 = bf16[1,48,1,3,768]{4,1,3,2,0:T(8,128)(2,1)S(1)} fusion(bf16[12,64,768,1]{2,1,0,3:T(8,128)(2,1)} %bitcast.89, bf16[3,12,48,64]{3,2,1,0:T(8,128)(2,1)} %fusion.11, f32[3,12,48,48]{2,3,1,0:T(8,128)} %get-tuple-element.15, f32[3,12,48]{2,1,0:T(8,128)S(1)} %get-tuple-element.14), kind=kOutput, calls=%fused_computation.31 | convolution fusion | flops 180873216 | bytes 1960704 | tf_op jit(solution)/shard_map/whid,hde->iwe/dot_general | solution.py:73
  30.2 15.6 %all_to_all.24 = bf16[1,48,1,3,768]{4,3,2,0,1:T(4,128)(2,1)S(1)} all-to-all(bf16[1,48,1,3,768]{4,3,2,0,1:T(4,128)(2,1)S(1)} %copy.25), channel_id=1, replica_groups=mesh['seq'=8,'bin'=4] {'seq'}, dimensions={1} | all-to-all | bytes 442368 | tf_op jit(solution)/shard_map/all_to_all | solution.py:77
  45.8 0.5 reshape.219
  46.3 0.5 copy.26
  47.2 0.4 copy-done.2
  47.8 0.7 copy-done.4
  48.5 9.3 %all_gather.3 = bf16[4,6,24,768]{3,2,1,0:T(8,128)(2,1)S(1)} all-gather(bf16[1,6,24,768]{3,2,1,0:T(8,128)(2,1)S(1)} %fusion.33), channel_id=1, replica_groups=mesh['seq'=8,'bin'=4] {'bin'}, dimensions={0}, use_global_device_ids=true | all-gather | bytes 1105920 | tf_op jit(solution)/shard_map/all_gather | solution.py:83
  57.8 2.1 %fusion.5 = f32[576,768]{1,0:T(8,128)} fusion(bf16[576,768]{1,0:T(8,128)(2,1)S(1)} %bitcast.83, bf16[768,2304]{1,0:T(8,128)(2,1)S(1)} %copy-done.7), kind=kOutput, calls=%fused_computation.9 | convolution fusion | flops 680361984 | bytes 3833856 | tf_op jit(solution)/shard_map/dot_general | solution.py:87
  59.9 2.1 %fusion.4 = f32[576,768]{1,0:T(8,128)} fusion(bf16[576,768]{1,0:T(8,128)(2,1)S(1)} %bitcast.84, bf16[768,2304]{1,0:T(8,128)(2,1)S(1)} %copy-done.7), kind=kOutput, calls=%fused_computation.7 | convolution fusion | flops 680361984 | bytes 3833856 | tf_op jit(solution)/shard_map/dot_general | solution.py:90
  62.0 1.9 %copy.29 = f32[576,768]{0,1:T(8,128)S(1)} copy(f32[576,768]{1,0:T(8,128)} %fusion.5) | data formatting | bytes 3538944 | tf_op jit(solution)/shard_map/convert_element_type | solution.py:31
  63.8 3.5 %reshape.217 = f32[1,4,144,12,64]{2,1,4,3,0:T(4,128)} reshape(f32[576,768]{0,1:T(8,128)S(1)} %copy.29) | data formatting | bytes 3538944 | tf_op jit(solution)/shard_map/convert_element_type | solution.py:31
  67.3 1.7 %fusion.15 = f32[144,768]{1,0:T(8,128)S(1)} fusion(bf16[144,768]{1,0:T(8,128)(2,1)} %bitcast.77, bf16[768,2304]{1,0:T(8,128)(2,1)} %param.12), kind=kOutput, calls=%fused_computation.26 | convolution fusion | flops 170090496 | bytes 1843200 | tf_op jit(solution)/shard_map/dot_general | solution.py:86
  69.0 0.3 copy.28
  69.3 2.7 %multiply_reduce_fusion.1 = f32[4,144,12]{1,0,2:T(4,128)S(1)} fusion(f32[1,4,144,12,64]{2,1,4,3,0:T(4,128)} %reshape.217, f32[144,12,64]{0,2,1:T(8,128)S(1)} %bitcast.76), kind=kLoop, calls=%fused_computation.4 | loop fusion | flops 877824 | bytes 2239488 | tf_op jit(solution)/shard_map/reduce_sum | solution.py:30
  72.0 0.7 fusion.25
  72.7 1.9 %copy.30 = f32[576,768]{0,1:T(8,128)S(1)} copy(f32[576,768]{1,0:T(8,128)} %fusion.4) | data formatting | bytes 3538944 | tf_op jit(solution)/shard_map/convert_element_type | solution.py:35
  74.6 3.5 %reshape.218 = f32[1,4,144,12,64]{2,1,4,3,0:T(4,128)} reshape(f32[576,768]{0,1:T(8,128)S(1)} %copy.30) | data formatting | bytes 3538944 | tf_op jit(solution)/shard_map/convert_element_type | solution.py:35
  78.0 4.1 %multiply_reduce_fusion = bf16[144,12,64]{0,2,1:T(8,128)(2,1)S(1)} fusion(f32[1,4,144,12,64]{2,1,4,3,0:T(4,128)} %reshape.218, f32[4,144,12]{1,0,2:T(4,128)} %fusion.25), kind=kLoop, calls=%fused_computation.3 | loop fusion | flops 774144 | bytes 2018304 | tf_op jit(solution)/shard_map/reduce_sum | solution.py:34
  82.2 0.5 copy.31
  82.7 0.3 convert_element_type.188
  83.1 2.3 %fusion.13 = bf16[1,6,24,768]{3,2,1,0:T(8,128)(2,1)} fusion(bf16[6,24,768]{2,1,0:T(8,128)(2,1)S(1)} %convert_element_type.188, bf16[768,768]{1,0:T(8,128)(2,1)} %param.13, bf16[1,6,24,768]{3,2,1,0:T(8,128)(2,1)S(1)} %copy-done.3), kind=kOutput, calls=%fused_computation.23 | convolution fusion | flops 170201088 | bytes 1843200 | tf_op jit(solution)/shard_map/dot_general | solution.py:98
  (30 shorter events, 1.4 us)
Async XLA Ops:
  0.0 1.4 %copy-start = (bf16[256,3072]{1,0:T(8,128)(2,1)S(1)}, bf16[256,3072]{1,0:T(8,128)(2,1)}, u32[]{:S(2)}) copy-start(bf16[256,3072]{1,0:T(8,128)(2,1)} %param.9) | copy-start | bytes 4718596
  0.0 1.7 %copy-start.1 = (bf16[1,6,24,768]{3,2,1,0:T(8,128)(2,1)S(1)}, bf16[1,6,24,768]{3,2,1,0:T(8,128)(2,1)}, u32[]{:S(2)}) copy-start(bf16[1,6,24,768]{3,2,1,0:T(8,128)(2,1)} %param.7) | copy-start | bytes 663556
  3.2 17.1 %all-to-all-start = ((bf16[1,6,8,3,768]{4,3,1,0,2:T(4,128)(2,1)}), bf16[1,6,8,3,768]{4,3,1,0,2:T(4,128)(2,1)S(1)}, u32[]{:S(2)}, u32[]{:S(2)}) async-start(bf16[1,6,8,3,768]{4,3,1,0,2:T(4,128)(2,1)} %copy.19), calls=%async_computation | async-start | bytes 589824 | tf_op jit(solution)/shard_map/all_to_all | solution.py:53
  20.3 2.9 %copy-start.6 = (bf16[768,768]{0,1:T(8,128)(2,1)S(1)}, bf16[768,768]{0,1:T(8,128)(2,1)}, u32[]{:S(2)}) copy-start(bf16[768,768]{0,1:T(8,128)(2,1)} %copy.40) | copy-start | bytes 3538948
  23.1 1.5 %copy-start.5 = (bf16[768,768]{0,1:T(8,128)(2,1)S(1)}, bf16[768,768]{0,1:T(8,128)(2,1)}, u32[]{:S(2)}) copy-start(bf16[768,768]{0,1:T(8,128)(2,1)} %copy.38) | copy-start | bytes 3538948
  46.3 11.5 %copy-start.7 = (bf16[768,2304]{1,0:T(8,128)(2,1)S(1)}, bf16[768,2304]{1,0:T(8,128)(2,1)}, u32[]{:S(2)}) copy-start(bf16[768,2304]{1,0:T(8,128)(2,1)} %param.12) | copy-start | bytes 10616836
  46.9 0.7 copy-start.2
  47.8 0.7 copy-start.4
  82.2 0.9 %copy-start.3 = (bf16[1,6,24,768]{3,2,1,0:T(8,128)(2,1)S(1)}, bf16[1,6,24,768]{3,2,1,0:T(8,128)(2,1)}, u32[]{:S(2)}) copy-start(bf16[1,6,24,768]{3,2,1,0:T(8,128)(2,1)} %copy-done.2) | copy-start | bytes 663556
where the time goes:
time: 86 us; the launch traced here: 85.4 us
  local copies, waits for them, and re-layouts  25.4 us (30%)
  blocking collectives  24.9 us (29%)
  matrix products  18.2 us (21%)
  other arithmetic  8.61 us (10%)
  starting transfers between devices  7.25 us (8%)
  between operations  1.01 us (1%)
    all_to_all x1, blocking collectives, per_device(): lax.all_to_all(attended, 'seq', split_axis=1, concat_axis=2, tiled=True)  15.6 us
    all_gather x1, blocking collectives, per_device(): every = lax.all_gather(normed2, 'bin', axis=0, tiled=True)  9.35 us
    unnamed x19, local copies, waits for them, and re-layouts  7.97 us
    all_to_all x1, starting transfers between devices, per_device(): lax.all_to_all(grouped, 'seq', split_axis=2, concat_axis=1, tiled=True)  7.25 us
    convert_element_type x2, local copies, waits for them, and re-layouts, across_bins(): key.astype(jnp.float32)[None]  5.32 us
    convert_element_type x2, local copies, waits for them, and re-layouts, across_bins(): value.astype(jnp.float32)[None]  5.32 us
    reduce_sum x1, other arithmetic, across_bins(): jnp.sum(weights.astype(jnp.float32)[..., None] * value.astype(jnp.float32...  4.14 us
    slice x1, local copies, waits for them, and re-layouts, per_device(): query_weight = col_qkv[:, :D].reshape(D, HEADS, HD)  3.62 us
  transfers between devices with their start and end apart: 1, of which 0 were waited for; matrix products, arithmetic and copies ran while one was open for 11% of the time, Pallas kernels for 0%

commit v1 on v0

--- a/solution.py
+++ b/solution.py
@@ -1,14 +1,20 @@
+import functools
 import math
 
 import jax
 import jax.numpy as jnp
 from jax import lax
+from jax.experimental import pallas as pl
+from jax.experimental.pallas import tpu as pltpu
 from jax.sharding import PartitionSpec as P
 
 D = 768
 HEADS = 12
 HD = 64
 FREQ = 256
+PAIR = 2 * HD
+BF = jnp.bfloat16
+F32 = jnp.float32
 
 
 def modulation(timestep, mod_weight):
@@ -17,6 +23,224 @@
     angle = timestep.astype(jnp.float32)[0] * freqs
     emb = jax.nn.silu(jnp.concatenate([jnp.cos(angle), jnp.sin(angle)])).astype(jnp.bfloat16)
     return jnp.dot(emb[None, :], mod_weight, preferred_element_type=jnp.float32)[0]
+
+
+def norm_rows(xf, mod_ref, which):
+    shift = mod_ref[2 * which : 2 * which + 1, :]
+    scale = mod_ref[2 * which + 1 : 2 * which + 2, :]
+    mean = jnp.mean(xf, axis=-1, keepdims=True)
+    cent = xf - mean
+    var = jnp.mean(cent * cent, axis=-1, keepdims=True)
+    return (cent * lax.rsqrt(var + 1e-06) * (1.0 + scale) + shift).astype(BF)
+
+
+def stacked(refs):
+    return jnp.concatenate([r[...].astype(F32) for r in refs], axis=0)
+
+
+def project(normed, w_ref, which, out_ref, factor=None):
+    y = jnp.dot(normed, w_ref[:, which * D : (which + 1) * D], preferred_element_type=F32)
+    if factor is not None:
+        y = y * factor
+    out_ref[...] = y.astype(BF)
+
+
+def divided(values, by, top):
+    total = jnp.zeros_like(values)
+    for step in range(by, top, by):
+        total = total + (values >= step).astype(jnp.int32)
+    return total
+
+
+def message_rows(shape, row_dim, token_dim, rows, cols, width, owner):
+    r = lax.broadcasted_iota(jnp.int32, shape, row_dim)
+    t = lax.broadcasted_iota(jnp.int32, shape, token_dim)
+    i = divided(r, cols, shape[row_dim])
+    source = i * width + owner * cols + (r - i * cols)
+    hit = (r < rows * cols) & (t == source)
+    return jnp.where(hit, 1.0, 0.0).astype(BF)
+
+
+def pack_kernel(dims, z_ref, tok_ref, *out_refs):
+    rows, cols, width = dims
+    x = tok_ref[...]
+    for m, out in enumerate(out_refs):
+        shape = (out.shape[0], x.shape[0])
+        pick = message_rows(shape, 0, 1, rows, cols, width, z_ref[0] ^ m)
+        out[...] = jnp.dot(pick, x, preferred_element_type=F32).astype(BF)
+
+
+def unpack_kernel(dims, groups, z_ref, *refs):
+    rows, cols, width = dims
+    out = refs[groups]
+    total = None
+    for m in range(groups):
+        shape = (out.shape[0], refs[m].shape[0])
+        put = message_rows(shape, 1, 0, rows, cols, width, z_ref[0] ^ m)
+        part = jnp.dot(put, refs[m][...], preferred_element_type=F32)
+        total = part if total is None else total + part
+    out[...] = total.astype(BF)
+
+
+def col_own_kernel(groups, *refs):
+    own, (mod_ref, w_ref, q_ref, k_ref, v_ref) = refs[:groups], refs[groups:]
+    normed = norm_rows(stacked(own), mod_ref, 0)
+    project(normed, w_ref, 0, q_ref, HD**-0.5)
+    project(normed, w_ref, 1, k_ref)
+    project(normed, w_ref, 2, v_ref)
+
+
+def col_attend_kernel(groups, dims, *refs):
+    rows, cols, _ = dims
+    own, other = refs[:groups], refs[groups : 2 * groups]
+    mod_ref, w_ref, wo_ref, q_ref, k_ref, v_ref, h_ref, k2_ref, v2_ref, c_ref = refs[2 * groups :]
+    normed = norm_rows(stacked(other), mod_ref, 0)
+    project(normed, w_ref, 1, k2_ref)
+    project(normed, w_ref, 2, v2_ref)
+    n = q_ref.shape[0]
+    pad = own[0].shape[0]
+
+    def column(shape, dim):
+        r = lax.broadcasted_iota(jnp.int32, shape, dim)
+        r = r - pad * divided(r, pad, shape[dim])
+        return r, r - cols * divided(r, cols, pad)
+
+    shape = (n, 2 * n)
+    _, q_col = column(shape, 0)
+    k_row, k_col = column(shape, 1)
+    bias = jnp.where((q_col == k_col) & (k_row < rows * cols), 0.0, -1e30).astype(F32)
+    bias = jnp.concatenate([bias, bias], axis=0)
+    low = lax.broadcasted_iota(jnp.int32, (n, PAIR), 1) < HD
+    for j in range(HEADS // 2):
+        lanes = slice(j * PAIR, (j + 1) * PAIR)
+        q = q_ref[:, lanes]
+        zero = jnp.zeros_like(q)
+        q = jnp.concatenate([jnp.where(low, q, zero), jnp.where(low, zero, q)], axis=0)
+        k = jnp.concatenate([k_ref[:, lanes], k2_ref[:, lanes]], axis=0)
+        v = jnp.concatenate([v_ref[:, lanes], v2_ref[:, lanes]], axis=0)
+        s = lax.dot_general(q, k, (((1,), (1,)), ((), ())), preferred_element_type=F32) + bias
+        e = jnp.exp(s - jnp.max(s, axis=-1, keepdims=True))
+        total = jnp.sum(e, axis=-1, keepdims=True)
+        c = jnp.dot(e.astype(BF), v, preferred_element_type=F32) / total
+        c_ref[:, lanes] = jnp.where(low, c[:n], c[n:]).astype(BF)
+    a = jnp.dot(c_ref[...], wo_ref[...], preferred_element_type=F32).astype(BF)
+    h_ref[...] = (stacked(own) + a.astype(F32)).astype(BF)
+
+
+def bin_own_kernel(h_ref, hc_ref, mod_ref, w_ref, q_ref, k_ref, v_ref, kc_ref, vc_ref):
+    normed = norm_rows(h_ref[...].astype(F32), mod_ref, 1)
+    project(normed, w_ref, 0, q_ref, HD**-0.5)
+    project(normed, w_ref, 1, k_ref)
+    project(normed, w_ref, 2, v_ref)
+    normed = norm_rows(hc_ref[...].astype(F32), mod_ref, 1)
+    project(normed, w_ref, 1, kc_ref)
+    project(normed, w_ref, 2, vc_ref)
+
+
+def bin_kv_kernel(h_ref, mod_ref, w_ref, k_ref, v_ref):
+    normed = norm_rows(h_ref[...].astype(F32), mod_ref, 1)
+    project(normed, w_ref, 1, k_ref)
+    project(normed, w_ref, 2, v_ref)
+
+
+def bin_attend_kernel(groups, hd_ref, mod_ref, w_ref, wo_ref, h_ref, q_ref, *refs):
+    keys, values = refs[0:6:2], refs[1:6:2]
+    outs, (kd_ref, vd_ref) = refs[6 : 6 + groups], refs[6 + groups :]
+    bin_kv_kernel(hd_ref, mod_ref, w_ref, kd_ref, vd_ref)
+    lane = lax.broadcasted_iota(jnp.int32, (D, 128), 0)
+    head = lax.broadcasted_iota(jnp.int32, (D, 128), 1)
+    gather = ((lane >= head * HD) & (lane < (head + 1) * HD)).astype(F32).astype(BF)
+    lane = lax.broadcasted_iota(jnp.int32, (128, D), 1)
+    head = lax.broadcasted_iota(jnp.int32, (128, D), 0)
+    spread = ((lane >= head * HD) & (lane < (head + 1) * HD)).astype(F32).astype(BF)
+    q = q_ref[...].astype(F32)
+    scores = [
+        jnp.dot((q * k[...].astype(F32)).astype(BF), gather, preferred_element_type=F32)
+        for k in (*keys, kd_ref)
+    ]
+    top = functools.reduce(jnp.maximum, scores)
+    exps = [jnp.exp(s - top) for s in scores]
+    scale = 1.0 / functools.reduce(jnp.add, exps)
+    c = None
+    for e, v in zip(exps, (*values, vd_ref)):
+        p = jnp.dot((e * scale).astype(BF), spread, preferred_element_type=F32)
+        part = p * v[...].astype(F32)
+        c = part if c is None else c + part
+    out = jnp.dot(c.astype(BF), wo_ref[...], preferred_element_type=F32)
+    out = h_ref[...].astype(F32) + out
+    pad = outs[0].shape[0]
+    for m, o in enumerate(outs):
+        o[...] = out[m * pad : (m + 1) * pad].astype(BF)
+
+
+def call(kernel, outs, scratch, *args, flops=0):
+    def space(a):
+        return pl.BlockSpec(memory_space=pltpu.SMEM if a.dtype == jnp.int32 else pltpu.VMEM)
+
+    moved = sum(a.size * a.dtype.itemsize for a in args)
+    return pl.pallas_call(
+        kernel,
+        out_shape=[jax.ShapeDtypeStruct(o, BF) for o in outs],
+        in_specs=[space(a) for a in args],
+        out_specs=[pl.BlockSpec(memory_space=pltpu.VMEM)] * len(outs),
+        scratch_shapes=[pltpu.VMEM(s, BF) for s in scratch],
+        compiler_params=pltpu.CompilerParams(vmem_limit_bytes=24 * 1024 * 1024),
+        cost_estimate=pl.CostEstimate(flops=flops, bytes_accessed=moved, transcendentals=0),
+    )(*args)
+
+
+def column_path(tokens, timestep, mod_weight, col_qkv, col_out, bin_qkv, bin_out):
+    rows, width = tokens.shape[1], tokens.shape[2]
+    owners = lax.axis_size("seq")
+    groups = owners // 2
+    cols = width // groups
+    dims = (rows, cols, width)
+    pad = -(-rows * cols // 8) * 8
+    n = groups * pad
+
+    def over_group(x, m):
+        return lax.ppermute(x, "seq", [(i, i ^ (2 * m)) for i in range(owners)])
+
+    def over_pair(x):
+        return lax.ppermute(x, "seq", [(i, i ^ 1) for i in range(owners)])
+
+    def over_bin(x, m):
+        return lax.ppermute(x, "bin", [(i, i ^ m) for i in range(4)])
+
+    z = (lax.axis_index("seq") // 2).astype(jnp.int32).reshape(1)
+    flat = tokens.reshape(rows * width, D)
+    sent = call(functools.partial(pack_kernel, dims), [(pad, D)] * groups, [], z, flat)
+    own = [sent[0]] + [over_group(sent[m], m) for m in range(1, groups)]
+    other = [over_pair(x) for x in own]
+    mod = modulation(timestep, mod_weight).reshape(4, D)
+
+    full = (n, D)
+    q, k, v = call(
+        functools.partial(col_own_kernel, groups), [full] * 3, [], *own, mod, col_qkv,
+        flops=6 * n * D * D,
+    )
+    (h,) = call(
+        functools.partial(col_attend_kernel, groups, dims), [full], [full] * 3,
+        *own, *other, mod, col_qkv, col_out, q, k, v,
+        flops=8 * n * D * D,
+    )
+    hy = over_bin(h, 2)
+    hc = over_bin(h, 1)
+    hd = over_bin(hy, 1)
+    q, k, v, kc, vc = call(
+        bin_own_kernel, [full] * 5, [], h, hc, mod, bin_qkv, flops=10 * n * D * D
+    )
+    ky, vy = call(bin_kv_kernel, [full] * 2, [], hy, mod, bin_qkv, flops=4 * n * D * D)
+    done = call(
+        functools.partial(bin_attend_kernel, groups), [(pad, D)] * groups, [full] * 2,
+        hd, mod, bin_qkv, bin_out, h, q, k, v, kc, vc, ky, vy,
+        flops=8 * n * D * D,
+    )
+    back = [done[0]] + [over_group(done[m], m) for m in range(1, groups)]
+    (out,) = call(
+        functools.partial(unpack_kernel, dims, groups), [(rows * width, D)], [], z, *back
+    )
+    return out.reshape(tokens.shape)
 
 
 def layer_norm(values, shift, scale):
@@ -37,7 +261,7 @@
     return context.astype(jnp.bfloat16)
 
 
-def per_device(tokens, timestep, mod_weight, col_qkv, col_out, bin_qkv, bin_out):
+def general_path(tokens, timestep, mod_weight, col_qkv, col_out, bin_qkv, bin_out):
     mod = modulation(timestep, mod_weight)
     shift1, scale1, shift2, scale2 = (mod[:D], mod[D : 2 * D], mod[2 * D : 3 * D], mod[3 * D :])
     rows_here = tokens.shape[1]
@@ -100,6 +324,14 @@
     return (hidden.astype(jnp.float32) + projected).astype(jnp.bfloat16)
 
 
+def per_device(tokens, *rest):
+    owners, width = lax.axis_size("seq"), tokens.shape[2]
+    small = owners in (4, 8) and width % (owners // 2) == 0 and lax.axis_size("bin") == 4
+    if small and tokens.shape[1] * width <= 256:
+        return column_path(tokens, *rest)
+    return general_path(tokens, *rest)
+
+
 def solution(mesh):
     placed = (P("bin", "seq", None, None), P(), P(), P(), P(), P(), P())
     return jax.shard_map(

time: 86 us -> 42.7 us (0.50)
  blocking collectives: 24.9 us -> 0 us
  local copies, waits for them, and re-layouts: 25.4 us -> 3.26 us
  matrix products: 18.2 us -> 1.72 us
  waiting for transfers between devices: 0.01 us -> 10.7 us
  starting transfers between devices: 7.25 us -> 16.8 us
  Pallas kernels: 0 us -> 9.1 us
  other arithmetic: 8.61 us -> 0.06 us
    ppermute x0 -> x13, starting transfers between devices: none -> 16.8 us  [the longest x6 10.1 us: over_group(): return lax.ppermute(x, 'seq', [(i, i ^ 2 * m) for i in range(owners)])]
    all_to_all x1 -> x0, blocking collectives: 15.6 us -> none  [per_device(): lax.all_to_all(attended, 'seq', split_axis=1, concat_axis=2, tiled=True)]
    dot_general x7 -> x0, matrix products: 14.9 us -> none  [the longest x1 2.87 us: per_device(): jnp.einsum('iwc,chd->whid', local, key_weight, preferred_element_type=jnp...]
    convert_element_type x9 -> x0, local copies, waits for them, and re-layouts: 12.7 us -> none  [the longest x2 5.32 us: across_bins(): key.astype(jnp.float32)[None]]
    ppermute x0 -> x13, waiting for transfers between devices: none -> 10.7 us  [the longest x6 6 us: over_group(): return lax.ppermute(x, 'seq', [(i, i ^ 2 * m) for i in range(owners)])]
    all_gather x1 -> x0, blocking collectives: 9.35 us -> none  [per_device(): every = lax.all_gather(normed2, 'bin', axis=0, tiled=True)]
    pallas_call x0 -> x7, Pallas kernels: none -> 9.1 us  [call(): pl.pallas_call(kernel, out_shape=[jax.ShapeDtypeStruct(o, BF) for o in ou...]
    reduce_sum x6 -> x0, other arithmetic: 7.47 us -> none  [the longest x1 4.14 us: across_bins(): jnp.sum(weights.astype(jnp.float32)[..., None] * value.astype(jnp.float32...]
  transfers between devices with their start and end apart: 1 -> 13, of which waited for: 0 -> 6; matrix products, arithmetic and copies ran while one was open for 11% -> 4% of each run, Pallas kernels for 0% -> 7%
where the time goes in v1:
time: 42.7 us; the launch traced here: 42.4 us
  starting transfers between devices  16.8 us (39%)
  waiting for transfers between devices  10.7 us (25%)
  Pallas kernels  9.1 us (21%)
  local copies, waits for them, and re-layouts  3.26 us (8%)
  matrix products  1.72 us (4%)
  between operations  0.81 us (2%)
    ppermute x6, starting transfers between devices, over_group(): return lax.ppermute(x, 'seq', [(i, i ^ 2 * m) for i in range(owners)])  10.1 us
    pallas_call x7, Pallas kernels, call(): pl.pallas_call(kernel, out_shape=[jax.ShapeDtypeStruct(o, BF) for o in ou...  9.1 us
    ppermute x6, waiting for transfers between devices, over_group(): return lax.ppermute(x, 'seq', [(i, i ^ 2 * m) for i in range(owners)])  6 us
    ppermute x4, starting transfers between devices, over_pair(): return lax.ppermute(x, 'seq', [(i, i ^ 1) for i in range(owners)])  5.07 us
    ppermute x3, waiting for transfers between devices, over_bin(): return lax.ppermute(x, 'bin', [(i, i ^ m) for i in range(4)])  4.68 us
    unnamed x10, local copies, waits for them, and re-layouts  3.25 us
    dot_general x1, matrix products, modulation(): jnp.dot(emb[None, :], mod_weight, preferred_element_type=jnp.float32)[0]  1.72 us
    ppermute x3, starting transfers between devices, over_bin(): return lax.ppermute(x, 'bin', [(i, i ^ m) for i in range(4)])  1.59 us
  transfers between devices with their start and end apart: 13, of which 6 were waited for; matrix products, arithmetic and copies ran while one was open for 4% of the time, Pallas kernels for 7%

profile of v1, /device:TPU:0, one launch (start us, length us, event | category | flops | bytes accessed | tf_op | source)
XLA Modules:
  0.0 42.4 jit_solution(2107019610398285328)
XLA Ops:
  0.0 0.9 %copy-done.4 = bf16[1,6,24,768]{3,2,1,0:T(8,128)(2,1)S(1)} copy-done((bf16[1,6,24,768]{3,2,1,0:T(8,128)(2,1)S(1)}, bf16[1,6,24,768]{3,2,1,0:T(8,128)(2,1)}, u32[]{:S(2)}) %copy-start.4) | copy-done | bytes 221208
  0.9 0.3 shard_map.73
  1.2 3.1 %collective-permute-start = (bf16[40,768]{1,0:T(8,128)(2,1)S(1)}, bf16[40,768]{1,0:T(8,128)(2,1)S(1)}, u32[]{:S(2)}, u32[]{:S(2)}) collective-permute-start(bf16[40,768]{1,0:T(8,128)(2,1)S(1)} %get-tuple-element.24), channel_id=1, source_target_pairs={{0,8},{4,12},{8,0},{12,4},{16,24},{20,28},{24,16},{28,20},{1,9},{5... | collective-permute-start | bytes 184328 | tf_op jit(solution)/shard_map/ppermute | solution.py:202
  4.3 2.6 %collective-permute-start.1 = (bf16[40,768]{1,0:T(8,128)(2,1)S(1)}, bf16[40,768]{1,0:T(8,128)(2,1)S(1)}, u32[]{:S(2)}, u32[]{:S(2)}) collective-permute-start(bf16[40,768]{1,0:T(8,128)(2,1)S(1)} %get-tuple-element.25), channel_id=1, source_target_pairs={{0,16},{4,20},{8,24},{12,28},{16,0},{20,4},{24,8},{28,12},{1,17},{... | collective-permute-start | bytes 184328 | tf_op jit(solution)/shard_map/ppermute | solution.py:202
  6.9 1.7 %collective-permute-start.3 = (bf16[40,768]{1,0:T(8,128)(2,1)S(1)}, bf16[40,768]{1,0:T(8,128)(2,1)S(1)}, u32[]{:S(2)}, u32[]{:S(2)}) collective-permute-start(bf16[40,768]{1,0:T(8,128)(2,1)S(1)} %get-tuple-element.23.refs_0_), channel_id=1, source_target_pairs={{0,4},{4,0},{8,12},{12,8},{16,20},{20,16},{24,28},{28,24},{1,5},{5... | collective-permute-start | bytes 184328 | tf_op jit(solution)/shard_map/ppermute | solution.py:205
  9.3 0.0 collective-permute-done.refs_1_
  9.3 0.4 collective-permute-start.4
  9.7 0.9 %collective-permute-done.1.refs_2_ = bf16[40,768]{1,0:T(8,128)(2,1)S(1)} collective-permute-done((bf16[40,768]{1,0:T(8,128)(2,1)S(1)}, bf16[40,768]{1,0:T(8,128)(2,1)S(1)}, u32[]{:S(2)}, u32[]{:S(2)}) %collective-permute-start.1) | collective-permute-done | bytes 61472 | tf_op jit(solution)/shard_map/ppermute | solution.py:202
  10.6 1.5 %collective-permute-start.5 = (bf16[40,768]{1,0:T(8,128)(2,1)S(1)}, bf16[40,768]{1,0:T(8,128)(2,1)S(1)}, u32[]{:S(2)}, u32[]{:S(2)}) collective-permute-start(bf16[40,768]{1,0:T(8,128)(2,1)S(1)} %collective-permute-done.1.refs_2_), channel_id=1, source_target_pairs={{0,4},{4,0},{8,12},{12,8},{16,20},{20,16},{24,28},{28,24},{1,5},{5... | collective-permute-start | bytes 184328 | tf_op jit(solution)/shard_map/ppermute | solution.py:205
  12.1 0.8 %collective-permute-done.2.refs_3_ = bf16[40,768]{1,0:T(8,128)(2,1)S(1)} collective-permute-done((bf16[40,768]{1,0:T(8,128)(2,1)S(1)}, bf16[40,768]{1,0:T(8,128)(2,1)S(1)}, u32[]{:S(2)}, u32[]{:S(2)}) %collective-permute-start.2) | collective-permute-done | bytes 61472 | tf_op jit(solution)/shard_map/ppermute | solution.py:202
  12.9 1.5 %collective-permute-start.6 = (bf16[40,768]{1,0:T(8,128)(2,1)S(1)}, bf16[40,768]{1,0:T(8,128)(2,1)S(1)}, u32[]{:S(2)}, u32[]{:S(2)}) collective-permute-start(bf16[40,768]{1,0:T(8,128)(2,1)S(1)} %collective-permute-done.2.refs_3_), channel_id=1, source_target_pairs={{0,4},{4,0},{8,12},{12,8},{16,20},{20,16},{24,28},{28,24},{1,5},{5... | collective-permute-start | bytes 184328 | tf_op jit(solution)/shard_map/ppermute | solution.py:205
  14.4 1.7 %fusion = f32[1,4,768]{2,0,1:T(1,128)S(1)} fusion(bf16[256,1,1]{0,1,2:T(2,128)(2,1)S(1)} %reshape.19, bf16[32,4,8,768]{3,2,1,0:T(8,128)(2,1)} %bitcast.19), kind=kOutput, calls=%fused_computation | convolution fusion | flops 1572864 | bytes 1585664 | tf_op jit(solution)/shard_map/dot_general | solution.py:25
  16.1 2.0 %copy-done.1 = bf16[768,2304]{1,0:T(8,128)(2,1)S(1)} copy-done((bf16[768,2304]{1,0:T(8,128)(2,1)S(1)}, bf16[768,2304]{1,0:T(8,128)(2,1)}, u32[]{:S(2)}) %copy-start.1) | copy-done | bytes 3538968
  18.1 0.9 %shard_map.74 = (bf16[160,768]{1,0:T(8,128)(2,1)S(1)}, bf16[160,768]{1,0:T(8,128)(2,1)S(1)}, bf16[160,768]{1,0:T(8,128)(2,1)S(1)}) custom-call(bf16[40,768]{1,0:T(8,128)(2,1)S(1)} %get-tuple-element.23.refs_0_, bf16[40,768]{1,0:T(8,128)(2,1)S(1)} %collective-permute-done.refs_1_, bf16[40,768]{1,0:T(8,128)(2,1)S(1)} %collective-permute-done.1.refs_2_, ...), custom_call_target="tpu_custom_call" | custom-call | flops 566231040 | bytes 3796992 | tf_op jit(solution)/shard_map/pallas_call | solution.py:181
  19.1 0.0 collective-permute-done.3.refs_4_
  19.1 0.0 collective-permute-done.6.refs_7_
  19.1 0.3 copy-done.2
  19.4 2.9 %shard_map.75.h_ref = bf16[160,768]{1,0:T(8,128)(2,1)S(1)} custom-call(bf16[40,768]{1,0:T(8,128)(2,1)S(1)} %get-tuple-element.23.refs_0_, bf16[40,768]{1,0:T(8,128)(2,1)S(1)} %collective-permute-done.refs_1_, bf16[40,768]{1,0:T(8,128)(2,1)S(1)} %collective-permute-done.1.refs_2_, bf16[40,768]{1,0:T(8,128)(2,1)S(1)} %collective-permute-done.2.refs_3_, ...), custom_call_target="tpu_custom_call" | custom-call | flops 754974720 | bytes 5959680 | tf_op jit(solution)/shard_map/pallas_call | solution.py:181
  22.3 1.6 %collective-permute-start.7 = (bf16[160,768]{1,0:T(8,128)(2,1)S(1)}, bf16[160,768]{1,0:T(8,128)(2,1)S(1)}, u32[]{:S(2)}, u32[]{:S(2)}) collective-permute-start(bf16[160,768]{1,0:T(8,128)(2,1)S(1)} %shard_map.75.h_ref), channel_id=1, source_target_pairs={{0,2},{1,3},{2,0},{3,1},{4,6},{5,7},{6,4},{7,5},{8,10},{9,11},{10,... | collective-permute-start | bytes 737288 | tf_op jit(solution)/shard_map/ppermute | solution.py:208
  23.9 4.7 %collective-permute-done.7.h_ref = bf16[160,768]{1,0:T(8,128)(2,1)S(1)} collective-permute-done((bf16[160,768]{1,0:T(8,128)(2,1)S(1)}, bf16[160,768]{1,0:T(8,128)(2,1)S(1)}, u32[]{:S(2)}, u32[]{:S(2)}) %collective-permute-start.7) | collective-permute-done | bytes 245792 | tf_op jit(solution)/shard_map/ppermute | solution.py:208
  28.6 0.0 collective-permute-start.8
  28.6 0.7 %shard_map.77 = (bf16[160,768]{1,0:T(8,128)(2,1)S(1)}, bf16[160,768]{1,0:T(8,128)(2,1)S(1)}) custom-call(bf16[160,768]{1,0:T(8,128)(2,1)S(1)} %collective-permute-done.7.h_ref, f32[4,768]{1,0:T(4,128)S(1)} %bitcast.15, bf16[768,2304]{1,0:T(8,128)(2,1)S(1)} %copy-done), custom_call_target="tpu_custom_call" | custom-call | flops 377487360 | bytes 3796992 | tf_op jit(solution)/shard_map/pallas_call | solution.py:181
  29.3 0.0 copy-start.3
  29.3 1.3 %shard_map.76 = (bf16[160,768]{1,0:T(8,128)(2,1)S(1)}, bf16[160,768]{1,0:T(8,128)(2,1)S(1)}, bf16[160,768]{1,0:T(8,128)(2,1)S(1)}, bf16[160,768]{1,0:T(8,128)(2,1)S(1)}, bf16[160,768]{1,0:T(8,128)(2,1)S(1)}) custom-call(bf16[160,768]{1,0:T(8,128)(2,1)S(1)} %shard_map.75.h_ref, bf16[160,768]{1,0:T(8,128)(2,1)S(1)} %collective-permute-done.9.hc_ref, ...), custom_call_target="tpu_custom_call" | custom-call | flops 943718400 | bytes 4042752 | tf_op jit(solution)/shard_map/pallas_call | solution.py:181
  30.7 1.9 %shard_map.78 = (bf16[40,768]{1,0:T(8,128)(2,1)S(1)}, bf16[40,768]{1,0:T(8,128)(2,1)S(1)}, bf16[40,768]{1,0:T(8,128)(2,1)S(1)}, bf16[40,768]{1,0:T(8,128)(2,1)S(1)}) custom-call(bf16[160,768]{1,0:T(8,128)(2,1)S(1)} %collective-permute-done.8.hd_ref, f32[4,768]{1,0:T(4,128)S(1)} %bitcast.17, bf16[768,2304]{1,0:T(8,128)(2,1)S(1)} %copy-done, ...), custom_call_target="tpu_custom_call" | custom-call | flops 754974720 | bytes 6942720 | tf_op jit(solution)/shard_map/pallas_call | solution.py:181
  32.6 0.1 collective-permute-start.10
  32.7 2.6 %collective-permute-start.11 = (bf16[40,768]{1,0:T(8,128)(2,1)S(1)}, bf16[40,768]{1,0:T(8,128)(2,1)S(1)}, u32[]{:S(2)}, u32[]{:S(2)}) collective-permute-start(bf16[40,768]{1,0:T(8,128)(2,1)S(1)} %get-tuple-element.39), channel_id=1, source_target_pairs={{0,16},{4,20},{8,24},{12,28},{16,0},{20,4},{24,8},{28,12},{1,17},{... | collective-permute-start | bytes 184328 | tf_op jit(solution)/shard_map/ppermute | solution.py:202
  35.3 1.8 %collective-permute-start.12 = (bf16[40,768]{1,0:T(8,128)(2,1)S(1)}, bf16[40,768]{1,0:T(8,128)(2,1)S(1)}, u32[]{:S(2)}, u32[]{:S(2)}) collective-permute-start(bf16[40,768]{1,0:T(8,128)(2,1)S(1)} %get-tuple-element.40), channel_id=1, source_target_pairs={{0,24},{4,28},{8,16},{12,20},{16,8},{20,12},{24,0},{28,4},{1,25},{... | collective-permute-start | bytes 184328 | tf_op jit(solution)/shard_map/ppermute | solution.py:202
  37.1 1.3 %collective-permute-done.10.refs_1_ = bf16[40,768]{1,0:T(8,128)(2,1)S(1)} collective-permute-done((bf16[40,768]{1,0:T(8,128)(2,1)S(1)}, bf16[40,768]{1,0:T(8,128)(2,1)S(1)}, u32[]{:S(2)}, u32[]{:S(2)}) %collective-permute-start.10) | collective-permute-done | bytes 61472 | tf_op jit(solution)/shard_map/ppermute | solution.py:202
  38.3 1.1 %collective-permute-done.11.refs_2_ = bf16[40,768]{1,0:T(8,128)(2,1)S(1)} collective-permute-done((bf16[40,768]{1,0:T(8,128)(2,1)S(1)}, bf16[40,768]{1,0:T(8,128)(2,1)S(1)}, u32[]{:S(2)}, u32[]{:S(2)}) %collective-permute-start.11) | collective-permute-done | bytes 61472 | tf_op jit(solution)/shard_map/ppermute | solution.py:202
  39.5 1.9 %collective-permute-done.12.refs_3_ = bf16[40,768]{1,0:T(8,128)(2,1)S(1)} collective-permute-done((bf16[40,768]{1,0:T(8,128)(2,1)S(1)}, bf16[40,768]{1,0:T(8,128)(2,1)S(1)}, u32[]{:S(2)}, u32[]{:S(2)}) %collective-permute-start.12) | collective-permute-done | bytes 61472 | tf_op jit(solution)/shard_map/ppermute | solution.py:202
  41.4 1.1 %shard_map.79 = bf16[144,768]{1,0:T(8,128)(2,1)} custom-call(s32[1]{0:T(128)} %bitcast.z_ref, bf16[40,768]{1,0:T(8,128)(2,1)S(1)} %get-tuple-element.37.refs_0_, bf16[40,768]{1,0:T(8,128)(2,1)S(1)} %collective-permute-done.10.refs_1_, bf16[40,768]{1,0:T(8,128)(2,1)S(1)} %collective-permute-done.11.refs_2_, bf16[40,768]{1,0:T(8,128)(2,1)S(1)} %collective-permute-done.12.refs_3_), custom_call_target="tpu_custom_call" | custom-call | bytes 245764 | tf_op jit(solution)/shard_map/pallas_call | solution.py:181
  (16 shorter events, 0.1 us)
Async XLA Ops:
  0.0 0.9 %copy-start.4 = (bf16[1,6,24,768]{3,2,1,0:T(8,128)(2,1)S(1)}, bf16[1,6,24,768]{3,2,1,0:T(8,128)(2,1)}, u32[]{:S(2)}) copy-start(bf16[1,6,24,768]{3,2,1,0:T(8,128)(2,1)} %param.7) | copy-start | bytes 663556
  1.2 8.1 %collective-permute-start = (bf16[40,768]{1,0:T(8,128)(2,1)S(1)}, bf16[40,768]{1,0:T(8,128)(2,1)S(1)}, u32[]{:S(2)}, u32[]{:S(2)}) collective-permute-start(bf16[40,768]{1,0:T(8,128)(2,1)S(1)} %get-tuple-element.24), channel_id=1, source_target_pairs={{0,8},{4,12},{8,0},{12,4},{16,24},{20,28},{24,16},{28,20},{1,9},{5... | collective-permute-start | bytes 184328 | tf_op jit(solution)/shard_map/ppermute | solution.py:202
  4.3 6.3 %collective-permute-start.1 = (bf16[40,768]{1,0:T(8,128)(2,1)S(1)}, bf16[40,768]{1,0:T(8,128)(2,1)S(1)}, u32[]{:S(2)}, u32[]{:S(2)}) collective-permute-start(bf16[40,768]{1,0:T(8,128)(2,1)S(1)} %get-tuple-element.25), channel_id=1, source_target_pairs={{0,16},{4,20},{8,24},{12,28},{16,0},{20,4},{24,8},{28,12},{1,17},{... | collective-permute-start | bytes 184328 | tf_op jit(solution)/shard_map/ppermute | solution.py:202
  6.9 6.0 %collective-permute-start.2 = (bf16[40,768]{1,0:T(8,128)(2,1)S(1)}, bf16[40,768]{1,0:T(8,128)(2,1)S(1)}, u32[]{:S(2)}, u32[]{:S(2)}) collective-permute-start(bf16[40,768]{1,0:T(8,128)(2,1)S(1)} %get-tuple-element.26), channel_id=1, source_target_pairs={{0,24},{4,28},{8,16},{12,20},{16,8},{20,12},{24,0},{28,4},{1,25},{... | collective-permute-start | bytes 184328 | tf_op jit(solution)/shard_map/ppermute | solution.py:202
  6.9 12.2 %collective-permute-start.3 = (bf16[40,768]{1,0:T(8,128)(2,1)S(1)}, bf16[40,768]{1,0:T(8,128)(2,1)S(1)}, u32[]{:S(2)}, u32[]{:S(2)}) collective-permute-start(bf16[40,768]{1,0:T(8,128)(2,1)S(1)} %get-tuple-element.23.refs_0_), channel_id=1, source_target_pairs={{0,4},{4,0},{8,12},{12,8},{16,20},{20,16},{24,28},{28,24},{1,5},{5... | collective-permute-start | bytes 184328 | tf_op jit(solution)/shard_map/ppermute | solution.py:205
  9.3 9.7 %collective-permute-start.4 = (bf16[40,768]{1,0:T(8,128)(2,1)S(1)}, bf16[40,768]{1,0:T(8,128)(2,1)S(1)}, u32[]{:S(2)}, u32[]{:S(2)}) collective-permute-start(bf16[40,768]{1,0:T(8,128)(2,1)S(1)} %collective-permute-done.refs_1_), channel_id=1, source_target_pairs={{0,4},{4,0},{8,12},{12,8},{16,20},{20,16},{24,28},{28,24},{1,5},{5... | collective-permute-start | bytes 184328 | tf_op jit(solution)/shard_map/ppermute | solution.py:205
  10.6 8.4 %collective-permute-start.5 = (bf16[40,768]{1,0:T(8,128)(2,1)S(1)}, bf16[40,768]{1,0:T(8,128)(2,1)S(1)}, u32[]{:S(2)}, u32[]{:S(2)}) collective-permute-start(bf16[40,768]{1,0:T(8,128)(2,1)S(1)} %collective-permute-done.1.refs_2_), channel_id=1, source_target_pairs={{0,4},{4,0},{8,12},{12,8},{16,20},{20,16},{24,28},{28,24},{1,5},{5... | collective-permute-start | bytes 184328 | tf_op jit(solution)/shard_map/ppermute | solution.py:205
  12.9 6.2 %collective-permute-start.6 = (bf16[40,768]{1,0:T(8,128)(2,1)S(1)}, bf16[40,768]{1,0:T(8,128)(2,1)S(1)}, u32[]{:S(2)}, u32[]{:S(2)}) collective-permute-start(bf16[40,768]{1,0:T(8,128)(2,1)S(1)} %collective-permute-done.2.refs_3_), channel_id=1, source_target_pairs={{0,4},{4,0},{8,12},{12,8},{16,20},{20,16},{24,28},{28,24},{1,5},{5... | collective-permute-start | bytes 184328 | tf_op jit(solution)/shard_map/ppermute | solution.py:205
  16.1 2.0 %copy-start.1 = (bf16[768,2304]{1,0:T(8,128)(2,1)S(1)}, bf16[768,2304]{1,0:T(8,128)(2,1)}, u32[]{:S(2)}) copy-start(bf16[768,2304]{1,0:T(8,128)(2,1)} %refs_9_.1) | copy-start | bytes 10616836
  18.1 1.3 %copy-start.2 = (bf16[768,768]{1,0:T(8,128)(2,1)S(1)}, bf16[768,768]{1,0:T(8,128)(2,1)}, u32[]{:S(2)}) copy-start(bf16[768,768]{1,0:T(8,128)(2,1)} %refs_10_.1) | copy-start | bytes 3538948
  19.4 9.2 %copy-start = (bf16[768,2304]{1,0:T(8,128)(2,1)S(1)}, bf16[768,2304]{1,0:T(8,128)(2,1)}, u32[]{:S(2)}) copy-start(bf16[768,2304]{1,0:T(8,128)(2,1)} %w_ref.5) | copy-start | bytes 10616836
  22.3 6.3 %collective-permute-start.7 = (bf16[160,768]{1,0:T(8,128)(2,1)S(1)}, bf16[160,768]{1,0:T(8,128)(2,1)S(1)}, u32[]{:S(2)}, u32[]{:S(2)}) collective-permute-start(bf16[160,768]{1,0:T(8,128)(2,1)S(1)} %shard_map.75.h_ref), channel_id=1, source_target_pairs={{0,2},{1,3},{2,0},{3,1},{4,6},{5,7},{6,4},{7,5},{8,10},{9,11},{10,... | collective-permute-start | bytes 737288 | tf_op jit(solution)/shard_map/ppermute | solution.py:208
  23.9 5.4 %collective-permute-start.9 = (bf16[160,768]{1,0:T(8,128)(2,1)S(1)}, bf16[160,768]{1,0:T(8,128)(2,1)S(1)}, u32[]{:S(2)}, u32[]{:S(2)}) collective-permute-start(bf16[160,768]{1,0:T(8,128)(2,1)S(1)} %shard_map.75.h_ref), channel_id=1, source_target_pairs={{0,1},{1,0},{2,3},{3,2},{4,5},{5,4},{6,7},{7,6},{8,9},{9,8},{10,11... | collective-permute-start | bytes 737288 | tf_op jit(solution)/shard_map/ppermute | solution.py:208
  28.6 2.1 %collective-permute-start.8 = (bf16[160,768]{1,0:T(8,128)(2,1)S(1)}, bf16[160,768]{1,0:T(8,128)(2,1)S(1)}, u32[]{:S(2)}, u32[]{:S(2)}) collective-permute-start(bf16[160,768]{1,0:T(8,128)(2,1)S(1)} %collective-permute-done.7.h_ref), channel_id=1, source_target_pairs={{0,1},{1,0},{2,3},{3,2},{4,5},{5,4},{6,7},{7,6},{8,9},{9,8},{10,11... | collective-permute-start | bytes 737288 | tf_op jit(solution)/shard_map/ppermute | solution.py:208
  29.3 1.4 %copy-start.3 = (bf16[768,768]{1,0:T(8,128)(2,1)S(1)}, bf16[768,768]{1,0:T(8,128)(2,1)}, u32[]{:S(2)}) copy-start(bf16[768,768]{1,0:T(8,128)(2,1)} %wo_ref.1) | copy-start | bytes 3538948
  32.6 5.7 %collective-permute-start.10 = (bf16[40,768]{1,0:T(8,128)(2,1)S(1)}, bf16[40,768]{1,0:T(8,128)(2,1)S(1)}, u32[]{:S(2)}, u32[]{:S(2)}) collective-permute-start(bf16[40,768]{1,0:T(8,128)(2,1)S(1)} %get-tuple-element.38), channel_id=1, source_target_pairs={{0,8},{4,12},{8,0},{12,4},{16,24},{20,28},{24,16},{28,20},{1,9},{5... | collective-permute-start | bytes 184328 | tf_op jit(solution)/shard_map/ppermute | solution.py:202
  32.7 6.8 %collective-permute-start.11 = (bf16[40,768]{1,0:T(8,128)(2,1)S(1)}, bf16[40,768]{1,0:T(8,128)(2,1)S(1)}, u32[]{:S(2)}, u32[]{:S(2)}) collective-permute-start(bf16[40,768]{1,0:T(8,128)(2,1)S(1)} %get-tuple-element.39), channel_id=1, source_target_pairs={{0,16},{4,20},{8,24},{12,28},{16,0},{20,4},{24,8},{28,12},{1,17},{... | collective-permute-start | bytes 184328 | tf_op jit(solution)/shard_map/ppermute | solution.py:202
  35.3 6.1 %collective-permute-start.12 = (bf16[40,768]{1,0:T(8,128)(2,1)S(1)}, bf16[40,768]{1,0:T(8,128)(2,1)S(1)}, u32[]{:S(2)}, u32[]{:S(2)}) collective-permute-start(bf16[40,768]{1,0:T(8,128)(2,1)S(1)} %get-tuple-element.40), channel_id=1, source_target_pairs={{0,24},{4,28},{8,16},{12,20},{16,8},{20,12},{24,0},{28,4},{1,25},{... | collective-permute-start | bytes 184328 | tf_op jit(solution)/shard_map/ppermute | solution.py:202

commit v2 on v1

--- a/solution.py
+++ b/solution.py
@@ -127,40 +127,45 @@
     h_ref[...] = (stacked(own) + a.astype(F32)).astype(BF)
 
 
-def bin_own_kernel(h_ref, hc_ref, mod_ref, w_ref, q_ref, k_ref, v_ref, kc_ref, vc_ref):
+def head_lanes(shape, lane_dim):
+    lane = lax.broadcasted_iota(jnp.int32, shape, lane_dim)
+    head = lax.broadcasted_iota(jnp.int32, shape, 1 - lane_dim)
+    return ((lane >= head * HD) & (lane < (head + 1) * HD)).astype(F32).astype(BF)
+
+
+def key_scores(query, normed, w_ref, s_ref):
+    k = jnp.dot(normed, w_ref[:, D : 2 * D], preferred_element_type=F32).astype(BF).astype(F32)
+    s_ref[...] = jnp.dot(
+        (query * k).astype(BF), head_lanes((D, 128), 0), preferred_element_type=F32
+    )
+
+
+def bin_own_kernel(h_ref, hc_ref, mod_ref, w_ref, q_ref, v_ref, s_ref, vc_ref, sc_ref):
     normed = norm_rows(h_ref[...].astype(F32), mod_ref, 1)
     project(normed, w_ref, 0, q_ref, HD**-0.5)
-    project(normed, w_ref, 1, k_ref)
+    query = q_ref[...].astype(F32)
+    key_scores(query, normed, w_ref, s_ref)
     project(normed, w_ref, 2, v_ref)
     normed = norm_rows(hc_ref[...].astype(F32), mod_ref, 1)
-    project(normed, w_ref, 1, kc_ref)
+    key_scores(query, normed, w_ref, sc_ref)
     project(normed, w_ref, 2, vc_ref)
 
 
-def bin_kv_kernel(h_ref, mod_ref, w_ref, k_ref, v_ref):
+def bin_kv_kernel(h_ref, q_ref, mod_ref, w_ref, v_ref, s_ref):
     normed = norm_rows(h_ref[...].astype(F32), mod_ref, 1)
-    project(normed, w_ref, 1, k_ref)
+    key_scores(q_ref[...].astype(F32), normed, w_ref, s_ref)
     project(normed, w_ref, 2, v_ref)
 
 
-def bin_attend_kernel(groups, hd_ref, mod_ref, w_ref, wo_ref, h_ref, q_ref, *refs):
-    keys, values = refs[0:6:2], refs[1:6:2]
-    outs, (kd_ref, vd_ref) = refs[6 : 6 + groups], refs[6 + groups :]
-    bin_kv_kernel(hd_ref, mod_ref, w_ref, kd_ref, vd_ref)
-    lane = lax.broadcasted_iota(jnp.int32, (D, 128), 0)
-    head = lax.broadcasted_iota(jnp.int32, (D, 128), 1)
-    gather = ((lane >= head * HD) & (lane < (head + 1) * HD)).astype(F32).astype(BF)
-    lane = lax.broadcasted_iota(jnp.int32, (128, D), 1)
-    head = lax.broadcasted_iota(jnp.int32, (128, D), 0)
-    spread = ((lane >= head * HD) & (lane < (head + 1) * HD)).astype(F32).astype(BF)
-    q = q_ref[...].astype(F32)
-    scores = [
-        jnp.dot((q * k[...].astype(F32)).astype(BF), gather, preferred_element_type=F32)
-        for k in (*keys, kd_ref)
-    ]
+def bin_attend_kernel(groups, hd_ref, q_ref, mod_ref, w_ref, wo_ref, h_ref, *refs):
+    values, scores = refs[0:6:2], refs[1:6:2]
+    outs, (vd_ref, sd_ref) = refs[6 : 6 + groups], refs[6 + groups :]
+    bin_kv_kernel(hd_ref, q_ref, mod_ref, w_ref, vd_ref, sd_ref)
+    scores = [s[...] for s in (*scores, sd_ref)]
     top = functools.reduce(jnp.maximum, scores)
     exps = [jnp.exp(s - top) for s in scores]
     scale = 1.0 / functools.reduce(jnp.add, exps)
+    spread = head_lanes((128, D), 1)
     c = None
     for e, v in zip(exps, (*values, vd_ref)):
         p = jnp.dot((e * scale).astype(BF), spread, preferred_element_type=F32)
@@ -173,19 +178,19 @@
         o[...] = out[m * pad : (m + 1) * pad].astype(BF)
 
 
-def call(kernel, outs, scratch, *args, flops=0):
+def call(kernel, outs, scratch, *args, cost=10**9):
     def space(a):
         return pl.BlockSpec(memory_space=pltpu.SMEM if a.dtype == jnp.int32 else pltpu.VMEM)
 
     moved = sum(a.size * a.dtype.itemsize for a in args)
     return pl.pallas_call(
         kernel,
-        out_shape=[jax.ShapeDtypeStruct(o, BF) for o in outs],
+        out_shape=[jax.ShapeDtypeStruct(*o) for o in outs],
         in_specs=[space(a) for a in args],
         out_specs=[pl.BlockSpec(memory_space=pltpu.VMEM)] * len(outs),
-        scratch_shapes=[pltpu.VMEM(s, BF) for s in scratch],
+        scratch_shapes=[pltpu.VMEM(*s) for s in scratch],
         compiler_params=pltpu.CompilerParams(vmem_limit_bytes=24 * 1024 * 1024),
-        cost_estimate=pl.CostEstimate(flops=flops, bytes_accessed=moved, transcendentals=0),
+        cost_estimate=pl.CostEstimate(flops=cost, bytes_accessed=moved, transcendentals=0),
     )(*args)
 
 
@@ -207,38 +212,37 @@
     def over_bin(x, m):
         return lax.ppermute(x, "bin", [(i, i ^ m) for i in range(4)])
 
+    message, full, lanes = ((pad, D), BF), ((n, D), BF), ((n, 128), F32)
     z = (lax.axis_index("seq") // 2).astype(jnp.int32).reshape(1)
     flat = tokens.reshape(rows * width, D)
-    sent = call(functools.partial(pack_kernel, dims), [(pad, D)] * groups, [], z, flat)
+    sent = call(
+        functools.partial(pack_kernel, dims), [message] * groups, [], z, flat, cost=10**10
+    )
+    mod = modulation(timestep, mod_weight).reshape(4, D)
     own = [sent[0]] + [over_group(sent[m], m) for m in range(1, groups)]
+    own[1], mod = lax.optimization_barrier((own[1], mod))
     other = [over_pair(x) for x in own]
-    mod = modulation(timestep, mod_weight).reshape(4, D)
-
-    full = (n, D)
-    q, k, v = call(
-        functools.partial(col_own_kernel, groups), [full] * 3, [], *own, mod, col_qkv,
-        flops=6 * n * D * D,
-    )
+
+    q, k, v = call(functools.partial(col_own_kernel, groups), [full] * 3, [], *own, mod, col_qkv)
     (h,) = call(
         functools.partial(col_attend_kernel, groups, dims), [full], [full] * 3,
         *own, *other, mod, col_qkv, col_out, q, k, v,
-        flops=8 * n * D * D,
     )
     hy = over_bin(h, 2)
     hc = over_bin(h, 1)
+    q, v, s, vc, sc = call(
+        bin_own_kernel, [full, full, lanes, full, lanes], [], h, hc, mod, bin_qkv
+    )
+    hy, q = lax.optimization_barrier((hy, q))
     hd = over_bin(hy, 1)
-    q, k, v, kc, vc = call(
-        bin_own_kernel, [full] * 5, [], h, hc, mod, bin_qkv, flops=10 * n * D * D
-    )
-    ky, vy = call(bin_kv_kernel, [full] * 2, [], hy, mod, bin_qkv, flops=4 * n * D * D)
+    vy, sy = call(bin_kv_kernel, [full, lanes], [], hy, q, mod, bin_qkv)
     done = call(
-        functools.partial(bin_attend_kernel, groups), [(pad, D)] * groups, [full] * 2,
-        hd, mod, bin_qkv, bin_out, h, q, k, v, kc, vc, ky, vy,
-        flops=8 * n * D * D,
+        functools.partial(bin_attend_kernel, groups), [message] * groups, [full, lanes],
+        hd, q, mod, bin_qkv, bin_out, h, v, s, vc, sc, vy, sy,
     )
     back = [done[0]] + [over_group(done[m], m) for m in range(1, groups)]
     (out,) = call(
-        functools.partial(unpack_kernel, dims, groups), [(rows * width, D)], [], z, *back
+        functools.partial(unpack_kernel, dims, groups), [((rows * width, D), BF)], [], z, *back
     )
     return out.reshape(tokens.shape)
 

time: 42.7 us -> 42.6 us (level)
  waiting for transfers between devices: 10.7 us -> 14.1 us
  local copies, waits for them, and re-layouts: 3.26 us -> 0.97 us
  matrix products: 1.72 us -> 0.32 us
    unnamed x10 -> x12, local copies, waits for them, and re-layouts: 3.25 us -> 0.95 us
    ppermute x4, waiting for transfers between devices: 0.01 us -> 1.78 us  [over_pair(): return lax.ppermute(x, 'seq', [(i, i ^ 1) for i in range(owners)])]
    dot_general x1, matrix products: 1.72 us -> 0.32 us  [modulation(): jnp.dot(emb[None, :], mod_weight, preferred_element_type=jnp.float32)[0]]
    ppermute x3, waiting for transfers between devices: 4.68 us -> 5.7 us  [over_bin(): return lax.ppermute(x, 'bin', [(i, i ^ m) for i in range(4)])]
    ppermute x6, waiting for transfers between devices: 6 us -> 6.57 us  [over_group(): return lax.ppermute(x, 'seq', [(i, i ^ 2 * m) for i in range(owners)])]
  transfers between devices with their start and end apart: 13 -> 13, of which waited for: 6 -> 7; matrix products, arithmetic and copies ran while one was open for 4% -> 1% of each run, Pallas kernels for 7% -> 8%
where the time goes in v2:
time: 42.6 us; the launch traced here: 42.4 us
  starting transfers between devices  16.9 us (40%)
  waiting for transfers between devices  14.1 us (33%)
  Pallas kernels  9.38 us (22%)
  local copies, waits for them, and re-layouts  0.97 us (2%)
  between operations  0.78 us (2%)
    ppermute x6, starting transfers between devices, over_group(): return lax.ppermute(x, 'seq', [(i, i ^ 2 * m) for i in range(owners)])  10.1 us
    pallas_call x7, Pallas kernels, call(): pl.pallas_call(kernel, out_shape=[jax.ShapeDtypeStruct(*o) for o in outs]...  9.38 us
    ppermute x6, waiting for transfers between devices, over_group(): return lax.ppermute(x, 'seq', [(i, i ^ 2 * m) for i in range(owners)])  6.57 us
    ppermute x3, waiting for transfers between devices, over_bin(): return lax.ppermute(x, 'bin', [(i, i ^ m) for i in range(4)])  5.7 us
    ppermute x4, starting transfers between devices, over_pair(): return lax.ppermute(x, 'seq', [(i, i ^ 1) for i in range(owners)])  5.07 us
    ppermute x4, waiting for transfers between devices, over_pair(): return lax.ppermute(x, 'seq', [(i, i ^ 1) for i in range(owners)])  1.78 us
    ppermute x3, starting transfers between devices, over_bin(): return lax.ppermute(x, 'bin', [(i, i ^ m) for i in range(4)])  1.67 us
    unnamed x12, local copies, waits for them, and re-layouts  0.95 us
  transfers between devices with their start and end apart: 13, of which 7 were waited for; matrix products, arithmetic and copies ran while one was open for 1% of the time, Pallas kernels for 8%

profile of v2, /device:TPU:0, one launch (start us, length us, event | category | flops | bytes accessed | tf_op | source)
XLA Modules:
  0.0 42.4 jit_solution(13735510728387067146)
XLA Ops:
  0.0 0.9 %copy-done.4 = bf16[1,6,24,768]{3,2,1,0:T(8,128)(2,1)S(1)} copy-done((bf16[1,6,24,768]{3,2,1,0:T(8,128)(2,1)S(1)}, bf16[1,6,24,768]{3,2,1,0:T(8,128)(2,1)}, u32[]{:S(2)}) %copy-start.4) | copy-done | bytes 221208
  0.9 0.3 shard_map.73
  1.2 3.1 %collective-permute-start = (bf16[40,768]{1,0:T(8,128)(2,1)S(1)}, bf16[40,768]{1,0:T(8,128)(2,1)S(1)}, u32[]{:S(2)}, u32[]{:S(2)}) collective-permute-start(bf16[40,768]{1,0:T(8,128)(2,1)S(1)} %get-tuple-element.28), channel_id=1, source_target_pairs={{0,8},{4,12},{8,0},{12,4},{16,24},{20,28},{24,16},{28,20},{1,9},{5... | collective-permute-start | bytes 184328 | tf_op jit(solution)/shard_map/ppermute | solution.py:207
  4.3 2.6 %collective-permute-start.1 = (bf16[40,768]{1,0:T(8,128)(2,1)S(1)}, bf16[40,768]{1,0:T(8,128)(2,1)S(1)}, u32[]{:S(2)}, u32[]{:S(2)}) collective-permute-start(bf16[40,768]{1,0:T(8,128)(2,1)S(1)} %get-tuple-element.30), channel_id=1, source_target_pairs={{0,16},{4,20},{8,24},{12,28},{16,0},{20,4},{24,8},{28,12},{1,17},{... | collective-permute-start | bytes 184328 | tf_op jit(solution)/shard_map/ppermute | solution.py:207
  6.9 0.0 collective-permute-start.2
  6.9 1.7 %collective-permute-start.3 = (bf16[40,768]{1,0:T(8,128)(2,1)S(1)}, bf16[40,768]{1,0:T(8,128)(2,1)S(1)}, u32[]{:S(2)}, u32[]{:S(2)}) collective-permute-start(bf16[40,768]{1,0:T(8,128)(2,1)S(1)} %get-tuple-element.27.refs_0_), channel_id=1, source_target_pairs={{0,4},{4,0},{8,12},{12,8},{16,20},{20,16},{24,28},{28,24},{1,5},{5... | collective-permute-start | bytes 184328 | tf_op jit(solution)/shard_map/ppermute | solution.py:210
  9.4 0.3 fusion
  9.7 0.0 collective-permute-done.refs_1_
  9.7 0.4 collective-permute-start.4
  10.1 0.6 %collective-permute-done.1.refs_2_ = bf16[40,768]{1,0:T(8,128)(2,1)S(1)} collective-permute-done((bf16[40,768]{1,0:T(8,128)(2,1)S(1)}, bf16[40,768]{1,0:T(8,128)(2,1)S(1)}, u32[]{:S(2)}, u32[]{:S(2)}) %collective-permute-start.1) | collective-permute-done | bytes 61472 | tf_op jit(solution)/shard_map/ppermute | solution.py:207
  10.7 1.5 %collective-permute-start.5 = (bf16[40,768]{1,0:T(8,128)(2,1)S(1)}, bf16[40,768]{1,0:T(8,128)(2,1)S(1)}, u32[]{:S(2)}, u32[]{:S(2)}) collective-permute-start(bf16[40,768]{1,0:T(8,128)(2,1)S(1)} %collective-permute-done.1.refs_2_), channel_id=1, source_target_pairs={{0,4},{4,0},{8,12},{12,8},{16,20},{20,16},{24,28},{28,24},{1,5},{5... | collective-permute-start | bytes 184328 | tf_op jit(solution)/shard_map/ppermute | solution.py:210
  12.1 0.8 %collective-permute-done.2.refs_3_ = bf16[40,768]{1,0:T(8,128)(2,1)S(1)} collective-permute-done((bf16[40,768]{1,0:T(8,128)(2,1)S(1)}, bf16[40,768]{1,0:T(8,128)(2,1)S(1)}, u32[]{:S(2)}, u32[]{:S(2)}) %collective-permute-start.2) | collective-permute-done | bytes 61472 | tf_op jit(solution)/shard_map/ppermute | solution.py:207
  12.9 1.5 %collective-permute-start.6 = (bf16[40,768]{1,0:T(8,128)(2,1)S(1)}, bf16[40,768]{1,0:T(8,128)(2,1)S(1)}, u32[]{:S(2)}, u32[]{:S(2)}) collective-permute-start(bf16[40,768]{1,0:T(8,128)(2,1)S(1)} %collective-permute-done.2.refs_3_), channel_id=1, source_target_pairs={{0,4},{4,0},{8,12},{12,8},{16,20},{20,16},{24,28},{28,24},{1,5},{5... | collective-permute-start | bytes 184328 | tf_op jit(solution)/shard_map/ppermute | solution.py:210
  14.4 0.9 %shard_map.74 = (bf16[160,768]{1,0:T(8,128)(2,1)S(1)}, bf16[160,768]{1,0:T(8,128)(2,1)S(1)}, bf16[160,768]{1,0:T(8,128)(2,1)S(1)}) custom-call(bf16[40,768]{1,0:T(8,128)(2,1)S(1)} %get-tuple-element.27.refs_0_, bf16[40,768]{1,0:T(8,128)(2,1)S(1)} %collective-permute-done.refs_1_, bf16[40,768]{1,0:T(8,128)(2,1)S(1)} %collective-permute-done.1.refs_2_, ...), custom_call_target="tpu_custom_call" | custom-call | flops 1000000000 | bytes 3796992 | tf_op jit(solution)/shard_map/pallas_call | solution.py:186
  15.3 0.0 collective-permute-done.3.refs_4_
  15.4 0.0 collective-permute-done.5.refs_6_
  15.4 1.8 %collective-permute-done.6.refs_7_ = bf16[40,768]{1,0:T(8,128)(2,1)S(1)} collective-permute-done((bf16[40,768]{1,0:T(8,128)(2,1)S(1)}, bf16[40,768]{1,0:T(8,128)(2,1)S(1)}, u32[]{:S(2)}, u32[]{:S(2)}) %collective-permute-start.6) | collective-permute-done | bytes 61472 | tf_op jit(solution)/shard_map/ppermute | solution.py:210
  17.1 2.9 %shard_map.75.h_ref = bf16[160,768]{1,0:T(8,128)(2,1)S(1)} custom-call(bf16[40,768]{1,0:T(8,128)(2,1)S(1)} %get-tuple-element.27.refs_0_, bf16[40,768]{1,0:T(8,128)(2,1)S(1)} %collective-permute-done.refs_1_, bf16[40,768]{1,0:T(8,128)(2,1)S(1)} %collective-permute-done.1.refs_2_, bf16[40,768]{1,0:T(8,128)(2,1)S(1)} %collective-permute-done.2.refs_3_, ...), custom_call_target="tpu_custom_call" | custom-call | flops 1000000000 | bytes 5959680 | tf_op jit(solution)/shard_map/pallas_call | solution.py:186
  20.1 0.1 collective-permute-start.8
  20.1 1.6 %collective-permute-start.7 = (bf16[160,768]{1,0:T(8,128)(2,1)S(1)}, bf16[160,768]{1,0:T(8,128)(2,1)S(1)}, u32[]{:S(2)}, u32[]{:S(2)}) collective-permute-start(bf16[160,768]{1,0:T(8,128)(2,1)S(1)} %shard_map.75.h_ref), channel_id=1, source_target_pairs={{0,2},{1,3},{2,0},{3,1},{4,6},{5,7},{6,4},{7,5},{8,10},{9,11},{10,... | collective-permute-start | bytes 737288 | tf_op jit(solution)/shard_map/ppermute | solution.py:213
  21.7 1.7 %shard_map.76 = (bf16[160,768]{1,0:T(8,128)(2,1)S(1)}, bf16[160,768]{1,0:T(8,128)(2,1)S(1)}, f32[160,128]{1,0:T(8,128)S(1)}, bf16[160,768]{1,0:T(8,128)(2,1)S(1)}, f32[160,128]{1,0:T(8,128)S(1)}) custom-call(bf16[160,768]{1,0:T(8,128)(2,1)S(1)} %shard_map.75.h_ref, bf16[160,768]{1,0:T(8,128)(2,1)S(1)} %collective-permute-done.8.hc_ref, ...), custom_call_target="tpu_custom_call" | custom-call | flops 1000000000 | bytes 4042752 | tf_op jit(solution)/shard_map/pallas_call | solution.py:186
  23.4 5.1 %collective-permute-done.7.h_ref = bf16[160,768]{1,0:T(8,128)(2,1)S(1)} collective-permute-done((bf16[160,768]{1,0:T(8,128)(2,1)S(1)}, bf16[160,768]{1,0:T(8,128)(2,1)S(1)}, u32[]{:S(2)}, u32[]{:S(2)}) %collective-permute-start.7) | collective-permute-done | bytes 245792 | tf_op jit(solution)/shard_map/ppermute | solution.py:213
  28.5 0.9 %shard_map.77 = (bf16[160,768]{1,0:T(8,128)(2,1)S(1)}, f32[160,128]{1,0:T(8,128)S(1)}) custom-call(bf16[160,768]{1,0:T(8,128)(2,1)S(1)} %collective-permute-done.7.h_ref, bf16[160,768]{1,0:T(8,128)(2,1)S(1)} %get-tuple-element.38.q_ref, f32[4,768]{1,0:T(4,128)S(1)} %bitcast.16, bf16[768,2304]{1,0:T(8,128)(2,1)S(1)} %copy-done), custom_call_target="tpu_custom_call" | custom-call | flops 1000000000 | bytes 4042752 | tf_op jit(solution)/shard_map/pallas_call | solution.py:186
  29.4 0.6 %collective-permute-done.9.hd_ref = bf16[160,768]{1,0:T(8,128)(2,1)S(1)} collective-permute-done((bf16[160,768]{1,0:T(8,128)(2,1)S(1)}, bf16[160,768]{1,0:T(8,128)(2,1)S(1)}, u32[]{:S(2)}, u32[]{:S(2)}) %collective-permute-start.9) | collective-permute-done | bytes 245792 | tf_op jit(solution)/shard_map/ppermute | solution.py:213
  30.0 1.7 %shard_map.78 = (bf16[40,768]{1,0:T(8,128)(2,1)S(1)}, bf16[40,768]{1,0:T(8,128)(2,1)S(1)}, bf16[40,768]{1,0:T(8,128)(2,1)S(1)}, bf16[40,768]{1,0:T(8,128)(2,1)S(1)}) custom-call(bf16[160,768]{1,0:T(8,128)(2,1)S(1)} %collective-permute-done.9.hd_ref, bf16[160,768]{1,0:T(8,128)(2,1)S(1)} %get-tuple-element.38.q_ref, f32[4,768]{1,0:T(4,128)S(1)} %bitcast.17, ...), custom_call_target="tpu_custom_call" | custom-call | flops 1000000000 | bytes 6451200 | tf_op jit(solution)/shard_map/pallas_call | solution.py:186
  31.7 0.3 collective-permute-start.10
  32.0 3.4 %collective-permute-start.11 = (bf16[40,768]{1,0:T(8,128)(2,1)S(1)}, bf16[40,768]{1,0:T(8,128)(2,1)S(1)}, u32[]{:S(2)}, u32[]{:S(2)}) collective-permute-start(bf16[40,768]{1,0:T(8,128)(2,1)S(1)} %get-tuple-element.47), channel_id=1, source_target_pairs={{0,16},{4,20},{8,24},{12,28},{16,0},{20,4},{24,8},{28,12},{1,17},{... | collective-permute-start | bytes 184328 | tf_op jit(solution)/shard_map/ppermute | solution.py:207
  35.3 0.8 %collective-permute-start.12 = (bf16[40,768]{1,0:T(8,128)(2,1)S(1)}, bf16[40,768]{1,0:T(8,128)(2,1)S(1)}, u32[]{:S(2)}, u32[]{:S(2)}) collective-permute-start(bf16[40,768]{1,0:T(8,128)(2,1)S(1)} %get-tuple-element.48), channel_id=1, source_target_pairs={{0,24},{4,28},{8,16},{12,20},{16,8},{20,12},{24,0},{28,4},{1,25},{... | collective-permute-start | bytes 184328 | tf_op jit(solution)/shard_map/ppermute | solution.py:207
  36.1 0.0 collective-permute-done.10.refs_1_
  36.2 3.0 %collective-permute-done.11.refs_2_ = bf16[40,768]{1,0:T(8,128)(2,1)S(1)} collective-permute-done((bf16[40,768]{1,0:T(8,128)(2,1)S(1)}, bf16[40,768]{1,0:T(8,128)(2,1)S(1)}, u32[]{:S(2)}, u32[]{:S(2)}) %collective-permute-start.11) | collective-permute-done | bytes 61472 | tf_op jit(solution)/shard_map/ppermute | solution.py:207
  39.2 2.2 %collective-permute-done.12.refs_3_ = bf16[40,768]{1,0:T(8,128)(2,1)S(1)} collective-permute-done((bf16[40,768]{1,0:T(8,128)(2,1)S(1)}, bf16[40,768]{1,0:T(8,128)(2,1)S(1)}, u32[]{:S(2)}, u32[]{:S(2)}) %collective-permute-start.12) | collective-permute-done | bytes 61472 | tf_op jit(solution)/shard_map/ppermute | solution.py:207
  41.4 1.1 %shard_map.79 = bf16[144,768]{1,0:T(8,128)(2,1)} custom-call(s32[1]{0:T(128)} %bitcast.z_ref, bf16[40,768]{1,0:T(8,128)(2,1)S(1)} %get-tuple-element.45.refs_0_, bf16[40,768]{1,0:T(8,128)(2,1)S(1)} %collective-permute-done.10.refs_1_, bf16[40,768]{1,0:T(8,128)(2,1)S(1)} %collective-permute-done.11.refs_2_, bf16[40,768]{1,0:T(8,128)(2,1)S(1)} %collective-permute-done.12.refs_3_), custom_call_target="tpu_custom_call" | custom-call | flops 1000000000 | bytes 245764 | tf_op jit(solution)/shard_map/pallas_call | solution.py:186
  (18 shorter events, 0.1 us)
Async XLA Ops:
  0.0 0.9 %copy-start.4 = (bf16[1,6,24,768]{3,2,1,0:T(8,128)(2,1)S(1)}, bf16[1,6,24,768]{3,2,1,0:T(8,128)(2,1)}, u32[]{:S(2)}) copy-start(bf16[1,6,24,768]{3,2,1,0:T(8,128)(2,1)} %param.7) | copy-start | bytes 663556
  0.9 8.4 %copy-start.5 = (bf16[256,3072]{1,0:T(8,128)(2,1)S(1)}, bf16[256,3072]{1,0:T(8,128)(2,1)}, u32[]{:S(2)}) copy-start(bf16[256,3072]{1,0:T(8,128)(2,1)} %param.9) | copy-start | bytes 4718596
  0.9 13.5 %copy-start.1 = (bf16[768,2304]{1,0:T(8,128)(2,1)S(1)}, bf16[768,2304]{1,0:T(8,128)(2,1)}, u32[]{:S(2)}) copy-start(bf16[768,2304]{1,0:T(8,128)(2,1)} %refs_9_.1) | copy-start | bytes 10616836
  1.2 8.5 %collective-permute-start = (bf16[40,768]{1,0:T(8,128)(2,1)S(1)}, bf16[40,768]{1,0:T(8,128)(2,1)S(1)}, u32[]{:S(2)}, u32[]{:S(2)}) collective-permute-start(bf16[40,768]{1,0:T(8,128)(2,1)S(1)} %get-tuple-element.28), channel_id=1, source_target_pairs={{0,8},{4,12},{8,0},{12,4},{16,24},{20,28},{24,16},{28,20},{1,9},{5... | collective-permute-start | bytes 184328 | tf_op jit(solution)/shard_map/ppermute | solution.py:207
  4.3 6.4 %collective-permute-start.1 = (bf16[40,768]{1,0:T(8,128)(2,1)S(1)}, bf16[40,768]{1,0:T(8,128)(2,1)S(1)}, u32[]{:S(2)}, u32[]{:S(2)}) collective-permute-start(bf16[40,768]{1,0:T(8,128)(2,1)S(1)} %get-tuple-element.30), channel_id=1, source_target_pairs={{0,16},{4,20},{8,24},{12,28},{16,0},{20,4},{24,8},{28,12},{1,17},{... | collective-permute-start | bytes 184328 | tf_op jit(solution)/shard_map/ppermute | solution.py:207
  6.9 6.0 %collective-permute-start.2 = (bf16[40,768]{1,0:T(8,128)(2,1)S(1)}, bf16[40,768]{1,0:T(8,128)(2,1)S(1)}, u32[]{:S(2)}, u32[]{:S(2)}) collective-permute-start(bf16[40,768]{1,0:T(8,128)(2,1)S(1)} %get-tuple-element.31), channel_id=1, source_target_pairs={{0,24},{4,28},{8,16},{12,20},{16,8},{20,12},{24,0},{28,4},{1,25},{... | collective-permute-start | bytes 184328 | tf_op jit(solution)/shard_map/ppermute | solution.py:207
  6.9 8.4 %collective-permute-start.3 = (bf16[40,768]{1,0:T(8,128)(2,1)S(1)}, bf16[40,768]{1,0:T(8,128)(2,1)S(1)}, u32[]{:S(2)}, u32[]{:S(2)}) collective-permute-start(bf16[40,768]{1,0:T(8,128)(2,1)S(1)} %get-tuple-element.27.refs_0_), channel_id=1, source_target_pairs={{0,4},{4,0},{8,12},{12,8},{16,20},{20,16},{24,28},{28,24},{1,5},{5... | collective-permute-start | bytes 184328 | tf_op jit(solution)/shard_map/ppermute | solution.py:210
  9.7 7.5 %copy-start.2 = (bf16[768,768]{1,0:T(8,128)(2,1)S(1)}, bf16[768,768]{1,0:T(8,128)(2,1)}, u32[]{:S(2)}) copy-start(bf16[768,768]{1,0:T(8,128)(2,1)} %refs_10_.1) | copy-start | bytes 3538948
  9.7 5.7 %collective-permute-start.4 = (bf16[40,768]{1,0:T(8,128)(2,1)S(1)}, bf16[40,768]{1,0:T(8,128)(2,1)S(1)}, u32[]{:S(2)}, u32[]{:S(2)}) collective-permute-start(bf16[40,768]{1,0:T(8,128)(2,1)S(1)} %collective-permute-done.refs_1_), channel_id=1, source_target_pairs={{0,4},{4,0},{8,12},{12,8},{16,20},{20,16},{24,28},{28,24},{1,5},{5... | collective-permute-start | bytes 184328 | tf_op jit(solution)/shard_map/ppermute | solution.py:210
  10.7 4.7 %collective-permute-start.5 = (bf16[40,768]{1,0:T(8,128)(2,1)S(1)}, bf16[40,768]{1,0:T(8,128)(2,1)S(1)}, u32[]{:S(2)}, u32[]{:S(2)}) collective-permute-start(bf16[40,768]{1,0:T(8,128)(2,1)S(1)} %collective-permute-done.1.refs_2_), channel_id=1, source_target_pairs={{0,4},{4,0},{8,12},{12,8},{16,20},{20,16},{24,28},{28,24},{1,5},{5... | collective-permute-start | bytes 184328 | tf_op jit(solution)/shard_map/ppermute | solution.py:210
  12.9 4.2 %collective-permute-start.6 = (bf16[40,768]{1,0:T(8,128)(2,1)S(1)}, bf16[40,768]{1,0:T(8,128)(2,1)S(1)}, u32[]{:S(2)}, u32[]{:S(2)}) collective-permute-start(bf16[40,768]{1,0:T(8,128)(2,1)S(1)} %collective-permute-done.2.refs_3_), channel_id=1, source_target_pairs={{0,4},{4,0},{8,12},{12,8},{16,20},{20,16},{24,28},{28,24},{1,5},{5... | collective-permute-start | bytes 184328 | tf_op jit(solution)/shard_map/ppermute | solution.py:210
  17.1 4.6 %copy-start = (bf16[768,2304]{1,0:T(8,128)(2,1)S(1)}, bf16[768,2304]{1,0:T(8,128)(2,1)}, u32[]{:S(2)}) copy-start(bf16[768,2304]{1,0:T(8,128)(2,1)} %w_ref.5) | copy-start | bytes 10616836
  20.1 1.7 %collective-permute-start.8 = (bf16[160,768]{1,0:T(8,128)(2,1)S(1)}, bf16[160,768]{1,0:T(8,128)(2,1)S(1)}, u32[]{:S(2)}, u32[]{:S(2)}) collective-permute-start(bf16[160,768]{1,0:T(8,128)(2,1)S(1)} %shard_map.75.h_ref), channel_id=1, source_target_pairs={{0,1},{1,0},{2,3},{3,2},{4,5},{5,4},{6,7},{7,6},{8,9},{9,8},{10,11... | collective-permute-start | bytes 737288 | tf_op jit(solution)/shard_map/ppermute | solution.py:213
  20.1 8.4 %collective-permute-start.7 = (bf16[160,768]{1,0:T(8,128)(2,1)S(1)}, bf16[160,768]{1,0:T(8,128)(2,1)S(1)}, u32[]{:S(2)}, u32[]{:S(2)}) collective-permute-start(bf16[160,768]{1,0:T(8,128)(2,1)S(1)} %shard_map.75.h_ref), channel_id=1, source_target_pairs={{0,2},{1,3},{2,0},{3,1},{4,6},{5,7},{6,4},{7,5},{8,10},{9,11},{10,... | collective-permute-start | bytes 737288 | tf_op jit(solution)/shard_map/ppermute | solution.py:213
  28.5 1.5 %copy-start.3 = (bf16[768,768]{1,0:T(8,128)(2,1)S(1)}, bf16[768,768]{1,0:T(8,128)(2,1)}, u32[]{:S(2)}) copy-start(bf16[768,768]{1,0:T(8,128)(2,1)} %wo_ref.1) | copy-start | bytes 3538948
  28.5 1.5 %collective-permute-start.9 = (bf16[160,768]{1,0:T(8,128)(2,1)S(1)}, bf16[160,768]{1,0:T(8,128)(2,1)S(1)}, u32[]{:S(2)}, u32[]{:S(2)}) collective-permute-start(bf16[160,768]{1,0:T(8,128)(2,1)S(1)} %collective-permute-done.7.h_ref), channel_id=1, source_target_pairs={{0,1},{1,0},{2,3},{3,2},{4,5},{5,4},{6,7},{7,6},{8,9},{9,8},{10,11... | collective-permute-start | bytes 737288 | tf_op jit(solution)/shard_map/ppermute | solution.py:213
  31.7 4.5 %collective-permute-start.10 = (bf16[40,768]{1,0:T(8,128)(2,1)S(1)}, bf16[40,768]{1,0:T(8,128)(2,1)S(1)}, u32[]{:S(2)}, u32[]{:S(2)}) collective-permute-start(bf16[40,768]{1,0:T(8,128)(2,1)S(1)} %get-tuple-element.46), channel_id=1, source_target_pairs={{0,8},{4,12},{8,0},{12,4},{16,24},{20,28},{24,16},{28,20},{1,9},{5... | collective-permute-start | bytes 184328 | tf_op jit(solution)/shard_map/ppermute | solution.py:207
  32.0 7.2 %collective-permute-start.11 = (bf16[40,768]{1,0:T(8,128)(2,1)S(1)}, bf16[40,768]{1,0:T(8,128)(2,1)S(1)}, u32[]{:S(2)}, u32[]{:S(2)}) collective-permute-start(bf16[40,768]{1,0:T(8,128)(2,1)S(1)} %get-tuple-element.47), channel_id=1, source_target_pairs={{0,16},{4,20},{8,24},{12,28},{16,0},{20,4},{24,8},{28,12},{1,17},{... | collective-permute-start | bytes 184328 | tf_op jit(solution)/shard_map/ppermute | solution.py:207
  35.3 6.0 %collective-permute-start.12 = (bf16[40,768]{1,0:T(8,128)(2,1)S(1)}, bf16[40,768]{1,0:T(8,128)(2,1)S(1)}, u32[]{:S(2)}, u32[]{:S(2)}) collective-permute-start(bf16[40,768]{1,0:T(8,128)(2,1)S(1)} %get-tuple-element.48), channel_id=1, source_target_pairs={{0,24},{4,28},{8,16},{12,20},{16,8},{20,12},{24,0},{28,4},{1,25},{... | collective-permute-start | bytes 184328 | tf_op jit(solution)/shard_map/ppermute | solution.py:207

commit v3 on v2

--- a/solution.py
+++ b/solution.py
@@ -82,47 +82,80 @@
     out[...] = total.astype(BF)
 
 
-def col_own_kernel(groups, *refs):
-    own, (mod_ref, w_ref, q_ref, k_ref, v_ref) = refs[:groups], refs[groups:]
-    normed = norm_rows(stacked(own), mod_ref, 0)
-    project(normed, w_ref, 0, q_ref, HD**-0.5)
-    project(normed, w_ref, 1, k_ref)
-    project(normed, w_ref, 2, v_ref)
-
-
-def col_attend_kernel(groups, dims, *refs):
-    rows, cols, _ = dims
-    own, other = refs[:groups], refs[groups : 2 * groups]
-    mod_ref, w_ref, wo_ref, q_ref, k_ref, v_ref, h_ref, k2_ref, v2_ref, c_ref = refs[2 * groups :]
-    normed = norm_rows(stacked(other), mod_ref, 0)
-    project(normed, w_ref, 1, k2_ref)
-    project(normed, w_ref, 2, v2_ref)
-    n = q_ref.shape[0]
-    pad = own[0].shape[0]
-
+def column_bias(n, pad, keys, rows, cols):
     def column(shape, dim):
         r = lax.broadcasted_iota(jnp.int32, shape, dim)
         r = r - pad * divided(r, pad, shape[dim])
         return r, r - cols * divided(r, cols, pad)
 
-    shape = (n, 2 * n)
-    _, q_col = column(shape, 0)
-    k_row, k_col = column(shape, 1)
-    bias = jnp.where((q_col == k_col) & (k_row < rows * cols), 0.0, -1e30).astype(F32)
-    bias = jnp.concatenate([bias, bias], axis=0)
+    _, q_col = column((n, 1), 0)
+    k_row, k_col = column((1, keys), 1)
+    k_col = jnp.where(k_row < rows * cols, k_col, -1)
+    bias = jnp.where(q_col == k_col, 0.0, -1e30).astype(F32)
+    return jnp.concatenate([bias, bias], axis=0)
+
+
+def head_pair(q):
+    low = lax.broadcasted_iota(jnp.int32, q.shape, 1) < HD
+    zero = jnp.zeros_like(q)
+    return jnp.concatenate([jnp.where(low, q, zero), jnp.where(low, zero, q)], axis=0)
+
+
+def unpaired(c):
+    n = c.shape[0] // 2
     low = lax.broadcasted_iota(jnp.int32, (n, PAIR), 1) < HD
+    return jnp.where(low, c[:n], c[n:])
+
+
+def col_early_kernel(groups, dims, *refs):
+    rows, cols, _ = dims
+    count = 2 * groups - 1
+    chunks, (mod_ref, w_ref, q_ref, m_ref, l_ref, acc_ref, k_ref, v_ref) = refs[:count], refs[count:]
+    n, pad = q_ref.shape[0], chunks[0].shape[0]
+    normed = norm_rows(stacked(chunks), mod_ref, 0)
+    project(normed[:n], w_ref, 0, q_ref, HD**-0.5)
+    project(normed, w_ref, 1, k_ref)
+    project(normed, w_ref, 2, v_ref)
+    bias = column_bias(n, pad, count * pad, rows, cols)
     for j in range(HEADS // 2):
         lanes = slice(j * PAIR, (j + 1) * PAIR)
-        q = q_ref[:, lanes]
-        zero = jnp.zeros_like(q)
-        q = jnp.concatenate([jnp.where(low, q, zero), jnp.where(low, zero, q)], axis=0)
-        k = jnp.concatenate([k_ref[:, lanes], k2_ref[:, lanes]], axis=0)
-        v = jnp.concatenate([v_ref[:, lanes], v2_ref[:, lanes]], axis=0)
-        s = lax.dot_general(q, k, (((1,), (1,)), ((), ())), preferred_element_type=F32) + bias
-        e = jnp.exp(s - jnp.max(s, axis=-1, keepdims=True))
-        total = jnp.sum(e, axis=-1, keepdims=True)
-        c = jnp.dot(e.astype(BF), v, preferred_element_type=F32) / total
-        c_ref[:, lanes] = jnp.where(low, c[:n], c[n:]).astype(BF)
+        q = head_pair(q_ref[:, lanes])
+        s = lax.dot_general(
+            q, k_ref[:, lanes], (((1,), (1,)), ((), ())), preferred_element_type=F32
+        ) + bias
+        top = jnp.max(s, axis=-1, keepdims=True)
+        e = jnp.exp(s - top)
+        m_ref[:, j : j + 1] = top
+        l_ref[:, j : j + 1] = jnp.sum(e, axis=-1, keepdims=True)
+        acc_ref[:, lanes] = unpaired(
+            jnp.dot(e.astype(BF), v_ref[:, lanes], preferred_element_type=F32)
+        )
+
+
+def col_late_kernel(groups, dims, *refs):
+    rows, cols, _ = dims
+    own, last = refs[:groups], refs[groups]
+    mod_ref, w_ref, wo_ref, q_ref, m_ref, l_ref, acc_ref, h_ref, k_ref, v_ref, c_ref = refs[groups + 1 :]
+    n, pad = q_ref.shape[0], last.shape[0]
+    normed = norm_rows(last[...].astype(F32), mod_ref, 0)
+    project(normed, w_ref, 1, k_ref)
+    project(normed, w_ref, 2, v_ref)
+    bias = column_bias(n, pad, pad, rows, cols)
+    for j in range(HEADS // 2):
+        lanes = slice(j * PAIR, (j + 1) * PAIR)
+        q = head_pair(q_ref[:, lanes])
+        s = lax.dot_general(
+            q, k_ref[:, lanes], (((1,), (1,)), ((), ())), preferred_element_type=F32
+        ) + bias
+        before = m_ref[:, j : j + 1]
+        top = jnp.maximum(before, jnp.max(s, axis=-1, keepdims=True))
+        e = jnp.exp(s - top)
+        fade = jnp.exp(before - top)
+        total = fade * l_ref[:, j : j + 1] + jnp.sum(e, axis=-1, keepdims=True)
+        weight = 1.0 / total
+        new = jnp.dot(e.astype(BF), v_ref[:, lanes], preferred_element_type=F32) * weight
+        wide = jnp.broadcast_to(fade * weight, new.shape)
+        c_ref[:, lanes] = (acc_ref[:, lanes] * unpaired(wide) + unpaired(new)).astype(BF)
     a = jnp.dot(c_ref[...], wo_ref[...], preferred_element_type=F32).astype(BF)
     h_ref[...] = (stacked(own) + a.astype(F32)).astype(BF)
 
@@ -140,15 +173,11 @@
     )
 
 
-def bin_own_kernel(h_ref, hc_ref, mod_ref, w_ref, q_ref, v_ref, s_ref, vc_ref, sc_ref):
+def bin_own_kernel(h_ref, mod_ref, w_ref, q_ref, v_ref, s_ref):
     normed = norm_rows(h_ref[...].astype(F32), mod_ref, 1)
     project(normed, w_ref, 0, q_ref, HD**-0.5)
-    query = q_ref[...].astype(F32)
-    key_scores(query, normed, w_ref, s_ref)
-    project(normed, w_ref, 2, v_ref)
-    normed = norm_rows(hc_ref[...].astype(F32), mod_ref, 1)
-    key_scores(query, normed, w_ref, sc_ref)
-    project(normed, w_ref, 2, vc_ref)
+    key_scores(q_ref[...].astype(F32), normed, w_ref, s_ref)
+    project(normed, w_ref, 2, v_ref)
 
 
 def bin_kv_kernel(h_ref, q_ref, mod_ref, w_ref, v_ref, s_ref):
@@ -157,19 +186,29 @@
     project(normed, w_ref, 2, v_ref)
 
 
+def bin_two_kernel(a_ref, b_ref, q_ref, mod_ref, w_ref, v_ref, s_ref):
+    normed = norm_rows(stacked((a_ref, b_ref)), mod_ref, 1)
+    q = q_ref[...].astype(F32)
+    key_scores(jnp.concatenate([q, q], axis=0), normed, w_ref, s_ref)
+    project(normed, w_ref, 2, v_ref)
+
+
 def bin_attend_kernel(groups, hd_ref, q_ref, mod_ref, w_ref, wo_ref, h_ref, *refs):
-    values, scores = refs[0:6:2], refs[1:6:2]
-    outs, (vd_ref, sd_ref) = refs[6 : 6 + groups], refs[6 + groups :]
+    n = h_ref.shape[0]
+    (v_ref, s_ref, v2_ref, s2_ref), refs = refs[:4], refs[4:]
+    outs, (vd_ref, sd_ref) = refs[:groups], refs[groups:]
     bin_kv_kernel(hd_ref, q_ref, mod_ref, w_ref, vd_ref, sd_ref)
-    scores = [s[...] for s in (*scores, sd_ref)]
+    halves = (slice(0, n), slice(n, 2 * n))
+    scores = [s_ref[...], *(s2_ref[half, :] for half in halves), sd_ref[...]]
+    values = [v_ref[...], *(v2_ref[half, :] for half in halves), vd_ref[...]]
     top = functools.reduce(jnp.maximum, scores)
     exps = [jnp.exp(s - top) for s in scores]
     scale = 1.0 / functools.reduce(jnp.add, exps)
     spread = head_lanes((128, D), 1)
     c = None
-    for e, v in zip(exps, (*values, vd_ref)):
+    for e, v in zip(exps, values):
         p = jnp.dot((e * scale).astype(BF), spread, preferred_element_type=F32)
-        part = p * v[...].astype(F32)
+        part = p * v.astype(F32)
         c = part if c is None else c + part
     out = jnp.dot(c.astype(BF), wo_ref[...], preferred_element_type=F32)
     out = h_ref[...].astype(F32) + out
@@ -178,11 +217,10 @@
         o[...] = out[m * pad : (m + 1) * pad].astype(BF)
 
 
-def call(kernel, outs, scratch, *args, cost=10**9):
+def call(kernel, outs, scratch, *args, cost=10**6):
     def space(a):
         return pl.BlockSpec(memory_space=pltpu.SMEM if a.dtype == jnp.int32 else pltpu.VMEM)
 
-    moved = sum(a.size * a.dtype.itemsize for a in args)
     return pl.pallas_call(
         kernel,
         out_shape=[jax.ShapeDtypeStruct(*o) for o in outs],
@@ -190,7 +228,7 @@
         out_specs=[pl.BlockSpec(memory_space=pltpu.VMEM)] * len(outs),
         scratch_shapes=[pltpu.VMEM(*s) for s in scratch],
         compiler_params=pltpu.CompilerParams(vmem_limit_bytes=24 * 1024 * 1024),
-        cost_estimate=pl.CostEstimate(flops=cost, bytes_accessed=moved, transcendentals=0),
+        cost_estimate=pl.CostEstimate(flops=cost, bytes_accessed=cost // 1000, transcendentals=0),
     )(*args)
 
 
@@ -223,22 +261,28 @@
     own[1], mod = lax.optimization_barrier((own[1], mod))
     other = [over_pair(x) for x in own]
 
-    q, k, v = call(functools.partial(col_own_kernel, groups), [full] * 3, [], *own, mod, col_qkv)
+    chunks = [*own, *other[:-1]]
+    kv = ((len(chunks) * pad, D), BF)
+    q, m, l, acc = call(
+        functools.partial(col_early_kernel, groups, dims),
+        [full, ((2 * n, 128), F32), ((2 * n, 128), F32), ((n, D), F32)], [kv, kv],
+        *chunks, mod, col_qkv,
+    )
     (h,) = call(
-        functools.partial(col_attend_kernel, groups, dims), [full], [full] * 3,
-        *own, *other, mod, col_qkv, col_out, q, k, v,
+        functools.partial(col_late_kernel, groups, dims), [full], [message, message, full],
+        *own, other[-1], mod, col_qkv, col_out, q, m, l, acc,
     )
     hy = over_bin(h, 2)
     hc = over_bin(h, 1)
-    q, v, s, vc, sc = call(
-        bin_own_kernel, [full, full, lanes, full, lanes], [], h, hc, mod, bin_qkv
-    )
-    hy, q = lax.optimization_barrier((hy, q))
+    q, v, s = call(bin_own_kernel, [full, full, lanes], [], h, mod, bin_qkv)
+    hy, hc, q = lax.optimization_barrier((hy, hc, q))
     hd = over_bin(hy, 1)
-    vy, sy = call(bin_kv_kernel, [full, lanes], [], hy, q, mod, bin_qkv)
+    v2, s2 = call(
+        bin_two_kernel, [((2 * n, D), BF), ((2 * n, 128), F32)], [], hc, hy, q, mod, bin_qkv
+    )
     done = call(
         functools.partial(bin_attend_kernel, groups), [message] * groups, [full, lanes],
-        hd, q, mod, bin_qkv, bin_out, h, v, s, vc, sc, vy, sy,
+        hd, q, mod, bin_qkv, bin_out, h, v, s, v2, s2,
     )
     back = [done[0]] + [over_group(done[m], m) for m in range(1, groups)]
     (out,) = call(

time: 42.6 us -> 43.2 us (1.014)
  Pallas kernels: 9.38 us -> 12.6 us
  waiting for transfers between devices: 14.1 us -> 11.5 us
    pallas_call x7, Pallas kernels: 9.38 us -> 12.6 us  [call(): pl.pallas_call(kernel, out_shape=[jax.ShapeDtypeStruct(*o) for o in outs]...]
    ppermute x3, waiting for transfers between devices: 5.7 us -> 3.65 us  [over_bin(): return lax.ppermute(x, 'bin', [(i, i ^ m) for i in range(4)])]
    ppermute x4, waiting for transfers between devices: 1.78 us -> 0.89 us  [over_pair(): return lax.ppermute(x, 'seq', [(i, i ^ 1) for i in range(owners)])]
  transfers between devices with their start and end apart: 13 -> 13, of which waited for: 7 -> 7; matrix products, arithmetic and copies ran while one was open for 1% -> 1% of each run, Pallas kernels for 8% -> 13%
where the time goes in v3:
time: 43.2 us; the launch traced here: 43.1 us
  starting transfers between devices  16.8 us (39%)
  Pallas kernels  12.6 us (29%)
  waiting for transfers between devices  11.5 us (27%)
  local copies, waits for them, and re-layouts  0.97 us (2%)
  between operations  0.77 us (2%)
    pallas_call x7, Pallas kernels, call(): pl.pallas_call(kernel, out_shape=[jax.ShapeDtypeStruct(*o) for o in outs]...  12.6 us
    ppermute x6, starting transfers between devices, over_group(): return lax.ppermute(x, 'seq', [(i, i ^ 2 * m) for i in range(owners)])  10.1 us
    ppermute x6, waiting for transfers between devices, over_group(): return lax.ppermute(x, 'seq', [(i, i ^ 2 * m) for i in range(owners)])  6.97 us
    ppermute x4, starting transfers between devices, over_pair(): return lax.ppermute(x, 'seq', [(i, i ^ 1) for i in range(owners)])  5.07 us
    ppermute x3, waiting for transfers between devices, over_bin(): return lax.ppermute(x, 'bin', [(i, i ^ m) for i in range(4)])  3.65 us
    ppermute x3, starting transfers between devices, over_bin(): return lax.ppermute(x, 'bin', [(i, i ^ m) for i in range(4)])  1.59 us
    unnamed x12, local copies, waits for them, and re-layouts  0.96 us
    ppermute x4, waiting for transfers between devices, over_pair(): return lax.ppermute(x, 'seq', [(i, i ^ 1) for i in range(owners)])  0.89 us
  transfers between devices with their start and end apart: 13, of which 7 were waited for; matrix products, arithmetic and copies ran while one was open for 1% of the time, Pallas kernels for 13%

profile of v3, /device:TPU:0, one launch (start us, length us, event | category | flops | bytes accessed | tf_op | source)
XLA Modules:
  0.0 43.1 jit_solution(13992171199868631233)
XLA Ops:
  0.0 0.9 %copy-done.4 = bf16[1,6,24,768]{3,2,1,0:T(8,128)(2,1)S(1)} copy-done((bf16[1,6,24,768]{3,2,1,0:T(8,128)(2,1)S(1)}, bf16[1,6,24,768]{3,2,1,0:T(8,128)(2,1)}, u32[]{:S(2)}) %copy-start.4) | copy-done | bytes 221208
  0.9 0.3 shard_map.73
  1.2 3.1 %collective-permute-start = (bf16[40,768]{1,0:T(8,128)(2,1)S(1)}, bf16[40,768]{1,0:T(8,128)(2,1)S(1)}, u32[]{:S(2)}, u32[]{:S(2)}) collective-permute-start(bf16[40,768]{1,0:T(8,128)(2,1)S(1)} %get-tuple-element.28), channel_id=1, source_target_pairs={{0,8},{4,12},{8,0},{12,4},{16,24},{20,28},{24,16},{28,20},{1,9},{5... | collective-permute-start | bytes 184328 | tf_op jit(solution)/shard_map/ppermute | solution.py:245
  4.3 2.6 %collective-permute-start.1 = (bf16[40,768]{1,0:T(8,128)(2,1)S(1)}, bf16[40,768]{1,0:T(8,128)(2,1)S(1)}, u32[]{:S(2)}, u32[]{:S(2)}) collective-permute-start(bf16[40,768]{1,0:T(8,128)(2,1)S(1)} %get-tuple-element.30), channel_id=1, source_target_pairs={{0,16},{4,20},{8,24},{12,28},{16,0},{20,4},{24,8},{28,12},{1,17},{... | collective-permute-start | bytes 184328 | tf_op jit(solution)/shard_map/ppermute | solution.py:245
  6.9 0.0 collective-permute-start.2
  6.9 1.7 %collective-permute-start.4 = (bf16[40,768]{1,0:T(8,128)(2,1)S(1)}, bf16[40,768]{1,0:T(8,128)(2,1)S(1)}, u32[]{:S(2)}, u32[]{:S(2)}) collective-permute-start(bf16[40,768]{1,0:T(8,128)(2,1)S(1)} %get-tuple-element.27.refs_0_), channel_id=1, source_target_pairs={{0,4},{4,0},{8,12},{12,8},{16,20},{20,16},{24,28},{28,24},{1,5},{5... | collective-permute-start | bytes 184328 | tf_op jit(solution)/shard_map/ppermute | solution.py:248
  9.4 0.3 fusion
  9.7 0.4 collective-permute-start.5
  10.1 0.6 %collective-permute-done.1.refs_2_ = bf16[40,768]{1,0:T(8,128)(2,1)S(1)} collective-permute-done((bf16[40,768]{1,0:T(8,128)(2,1)S(1)}, bf16[40,768]{1,0:T(8,128)(2,1)S(1)}, u32[]{:S(2)}, u32[]{:S(2)}) %collective-permute-start.1) | collective-permute-done | bytes 61472 | tf_op jit(solution)/shard_map/ppermute | solution.py:245
  10.7 1.5 %collective-permute-start.6 = (bf16[40,768]{1,0:T(8,128)(2,1)S(1)}, bf16[40,768]{1,0:T(8,128)(2,1)S(1)}, u32[]{:S(2)}, u32[]{:S(2)}) collective-permute-start(bf16[40,768]{1,0:T(8,128)(2,1)S(1)} %collective-permute-done.1.refs_2_), channel_id=1, source_target_pairs={{0,4},{4,0},{8,12},{12,8},{16,20},{20,16},{24,28},{28,24},{1,5},{5... | collective-permute-start | bytes 184328 | tf_op jit(solution)/shard_map/ppermute | solution.py:248
  12.1 0.8 %collective-permute-done.2.refs_3_ = bf16[40,768]{1,0:T(8,128)(2,1)S(1)} collective-permute-done((bf16[40,768]{1,0:T(8,128)(2,1)S(1)}, bf16[40,768]{1,0:T(8,128)(2,1)S(1)}, u32[]{:S(2)}, u32[]{:S(2)}) %collective-permute-start.2) | collective-permute-done | bytes 61472 | tf_op jit(solution)/shard_map/ppermute | solution.py:245
  12.9 1.5 %collective-permute-start.3 = (bf16[40,768]{1,0:T(8,128)(2,1)S(1)}, bf16[40,768]{1,0:T(8,128)(2,1)S(1)}, u32[]{:S(2)}, u32[]{:S(2)}) collective-permute-start(bf16[40,768]{1,0:T(8,128)(2,1)S(1)} %collective-permute-done.2.refs_3_), channel_id=1, source_target_pairs={{0,4},{4,0},{8,12},{12,8},{16,20},{20,16},{24,28},{28,24},{1,5},{5... | collective-permute-start | bytes 184328 | tf_op jit(solution)/shard_map/ppermute | solution.py:248
  14.4 0.0 collective-permute-done.4.refs_4_
  14.4 0.0 collective-permute-done.5.refs_5_
  14.4 0.9 %collective-permute-done.6.refs_6_ = bf16[40,768]{1,0:T(8,128)(2,1)S(1)} collective-permute-done((bf16[40,768]{1,0:T(8,128)(2,1)S(1)}, bf16[40,768]{1,0:T(8,128)(2,1)S(1)}, u32[]{:S(2)}, u32[]{:S(2)}) %collective-permute-start.6) | collective-permute-done | bytes 61472 | tf_op jit(solution)/shard_map/ppermute | solution.py:248
  15.3 3.2 %shard_map.74 = (bf16[160,768]{1,0:T(8,128)(2,1)S(1)}, f32[320,128]{1,0:T(8,128)S(1)}, f32[320,128]{1,0:T(8,128)S(1)}, f32[160,768]{1,0:T(8,128)S(1)}) custom-call(bf16[40,768]{1,0:T(8,128)(2,1)S(1)} %get-tuple-element.27.refs_0_, bf16[40,768]{1,0:T(8,128)(2,1)S(1)} %collective-permute-done.refs_1_, bf16[40,768]{1,0:T(8,128)(2,1)S(1)} %collective-permute-done.1.refs_2_, ...), custom_call_target="tpu_custom_call" | custom-call | flops 1000000 | bytes 1000 | tf_op jit(solution)/shard_map/pallas_call | solution.py:224
  18.5 0.0 collective-permute-done.3.refs_4_
  18.5 0.0 copy-start
  18.5 3.9 %shard_map.75.h_ref = bf16[160,768]{1,0:T(8,128)(2,1)S(1)} custom-call(bf16[40,768]{1,0:T(8,128)(2,1)S(1)} %get-tuple-element.27.refs_0_, bf16[40,768]{1,0:T(8,128)(2,1)S(1)} %collective-permute-done.refs_1_, bf16[40,768]{1,0:T(8,128)(2,1)S(1)} %collective-permute-done.1.refs_2_, bf16[40,768]{1,0:T(8,128)(2,1)S(1)} %collective-permute-done.2.refs_3_, ...), custom_call_target="tpu_custom_call" | custom-call | flops 1000000 | bytes 1000 | tf_op jit(solution)/shard_map/pallas_call | solution.py:224
  22.5 1.6 %collective-permute-start.7 = (bf16[160,768]{1,0:T(8,128)(2,1)S(1)}, bf16[160,768]{1,0:T(8,128)(2,1)S(1)}, u32[]{:S(2)}, u32[]{:S(2)}) collective-permute-start(bf16[160,768]{1,0:T(8,128)(2,1)S(1)} %shard_map.75.h_ref), channel_id=1, source_target_pairs={{0,2},{1,3},{2,0},{3,1},{4,6},{5,7},{6,4},{7,5},{8,10},{9,11},{10,... | collective-permute-start | bytes 737288 | tf_op jit(solution)/shard_map/ppermute | solution.py:251
  24.1 0.0 collective-permute-start.8
  24.1 1.2 %shard_map.76 = (bf16[160,768]{1,0:T(8,128)(2,1)S(1)}, bf16[160,768]{1,0:T(8,128)(2,1)S(1)}, f32[160,128]{1,0:T(8,128)S(1)}) custom-call(bf16[160,768]{1,0:T(8,128)(2,1)S(1)} %shard_map.75.h_ref, f32[4,768]{1,0:T(4,128)S(1)} %bitcast.15, bf16[768,2304]{1,0:T(8,128)(2,1)S(1)} %copy-done), custom_call_target="tpu_custom_call" | custom-call | flops 1000000 | bytes 1000 | tf_op jit(solution)/shard_map/pallas_call | solution.py:224
  25.3 3.5 %collective-permute-done.7.b_ref = bf16[160,768]{1,0:T(8,128)(2,1)S(1)} collective-permute-done((bf16[160,768]{1,0:T(8,128)(2,1)S(1)}, bf16[160,768]{1,0:T(8,128)(2,1)S(1)}, u32[]{:S(2)}, u32[]{:S(2)}) %collective-permute-start.7) | collective-permute-done | bytes 245792 | tf_op jit(solution)/shard_map/ppermute | solution.py:251
  28.8 1.3 %shard_map.77 = (bf16[320,768]{1,0:T(8,128)(2,1)S(1)}, f32[320,128]{1,0:T(8,128)S(1)}) custom-call(bf16[160,768]{1,0:T(8,128)(2,1)S(1)} %collective-permute-done.8.a_ref, bf16[160,768]{1,0:T(8,128)(2,1)S(1)} %collective-permute-done.7.b_ref, bf16[160,768]{1,0:T(8,128)(2,1)S(1)} %get-tuple-element.39.q_ref, f32[4,768]{1,0:T(4,128)S(1)} %bitcast.16, ...), custom_call_target="tpu_custom_call" | custom-call | flops 1000000 | bytes 1000 | tf_op jit(solution)/shard_map/pallas_call | solution.py:224
  30.1 0.2 collective-permute-done.9.hd_ref
  30.3 1.7 %shard_map.78 = (bf16[40,768]{1,0:T(8,128)(2,1)S(1)}, bf16[40,768]{1,0:T(8,128)(2,1)S(1)}, bf16[40,768]{1,0:T(8,128)(2,1)S(1)}, bf16[40,768]{1,0:T(8,128)(2,1)S(1)}) custom-call(bf16[160,768]{1,0:T(8,128)(2,1)S(1)} %collective-permute-done.9.hd_ref, bf16[160,768]{1,0:T(8,128)(2,1)S(1)} %get-tuple-element.39.q_ref, f32[4,768]{1,0:T(4,128)S(1)} %bitcast.17, ...), custom_call_target="tpu_custom_call" | custom-call | flops 1000000 | bytes 1000 | tf_op jit(solution)/shard_map/pallas_call | solution.py:224
  31.9 0.6 %collective-permute-start.10 = (bf16[40,768]{1,0:T(8,128)(2,1)S(1)}, bf16[40,768]{1,0:T(8,128)(2,1)S(1)}, u32[]{:S(2)}, u32[]{:S(2)}) collective-permute-start(bf16[40,768]{1,0:T(8,128)(2,1)S(1)} %get-tuple-element.46), channel_id=1, source_target_pairs={{0,8},{4,12},{8,0},{12,4},{16,24},{20,28},{24,16},{28,20},{1,9},{5... | collective-permute-start | bytes 184328 | tf_op jit(solution)/shard_map/ppermute | solution.py:245
  32.6 3.4 %collective-permute-start.11 = (bf16[40,768]{1,0:T(8,128)(2,1)S(1)}, bf16[40,768]{1,0:T(8,128)(2,1)S(1)}, u32[]{:S(2)}, u32[]{:S(2)}) collective-permute-start(bf16[40,768]{1,0:T(8,128)(2,1)S(1)} %get-tuple-element.47), channel_id=1, source_target_pairs={{0,16},{4,20},{8,24},{12,28},{16,0},{20,4},{24,8},{28,12},{1,17},{... | collective-permute-start | bytes 184328 | tf_op jit(solution)/shard_map/ppermute | solution.py:245
  35.9 0.5 %collective-permute-start.12 = (bf16[40,768]{1,0:T(8,128)(2,1)S(1)}, bf16[40,768]{1,0:T(8,128)(2,1)S(1)}, u32[]{:S(2)}, u32[]{:S(2)}) collective-permute-start(bf16[40,768]{1,0:T(8,128)(2,1)S(1)} %get-tuple-element.48), channel_id=1, source_target_pairs={{0,24},{4,28},{8,16},{12,20},{16,8},{20,12},{24,0},{28,4},{1,25},{... | collective-permute-start | bytes 184328 | tf_op jit(solution)/shard_map/ppermute | solution.py:245
  36.4 3.4 %collective-permute-done.11.refs_2_ = bf16[40,768]{1,0:T(8,128)(2,1)S(1)} collective-permute-done((bf16[40,768]{1,0:T(8,128)(2,1)S(1)}, bf16[40,768]{1,0:T(8,128)(2,1)S(1)}, u32[]{:S(2)}, u32[]{:S(2)}) %collective-permute-start.11) | collective-permute-done | bytes 61472 | tf_op jit(solution)/shard_map/ppermute | solution.py:245
  39.8 2.2 %collective-permute-done.12.refs_3_ = bf16[40,768]{1,0:T(8,128)(2,1)S(1)} collective-permute-done((bf16[40,768]{1,0:T(8,128)(2,1)S(1)}, bf16[40,768]{1,0:T(8,128)(2,1)S(1)}, u32[]{:S(2)}, u32[]{:S(2)}) %collective-permute-start.12) | collective-permute-done | bytes 61472 | tf_op jit(solution)/shard_map/ppermute | solution.py:245
  42.0 1.1 %shard_map.79 = bf16[144,768]{1,0:T(8,128)(2,1)} custom-call(s32[1]{0:T(128)} %bitcast.z_ref, bf16[40,768]{1,0:T(8,128)(2,1)S(1)} %get-tuple-element.45.refs_0_, bf16[40,768]{1,0:T(8,128)(2,1)S(1)} %collective-permute-done.10.refs_1_, bf16[40,768]{1,0:T(8,128)(2,1)S(1)} %collective-permute-done.11.refs_2_, bf16[40,768]{1,0:T(8,128)(2,1)S(1)} %collective-permute-done.12.refs_3_), custom_call_target="tpu_custom_call" | custom-call | flops 1000000 | bytes 1000 | tf_op jit(solution)/shard_map/pallas_call | solution.py:224
  (18 shorter events, 0.1 us)
Async XLA Ops:
  0.0 0.9 %copy-start.4 = (bf16[1,6,24,768]{3,2,1,0:T(8,128)(2,1)S(1)}, bf16[1,6,24,768]{3,2,1,0:T(8,128)(2,1)}, u32[]{:S(2)}) copy-start(bf16[1,6,24,768]{3,2,1,0:T(8,128)(2,1)} %param.7) | copy-start | bytes 663556
  0.9 8.4 %copy-start.5 = (bf16[256,3072]{1,0:T(8,128)(2,1)S(1)}, bf16[256,3072]{1,0:T(8,128)(2,1)}, u32[]{:S(2)}) copy-start(bf16[256,3072]{1,0:T(8,128)(2,1)} %param.9) | copy-start | bytes 4718596
  0.9 14.4 %copy-start.1 = (bf16[768,2304]{1,0:T(8,128)(2,1)S(1)}, bf16[768,2304]{1,0:T(8,128)(2,1)}, u32[]{:S(2)}) copy-start(bf16[768,2304]{1,0:T(8,128)(2,1)} %refs_6_.1) | copy-start | bytes 10616836
  1.2 8.5 %collective-permute-start = (bf16[40,768]{1,0:T(8,128)(2,1)S(1)}, bf16[40,768]{1,0:T(8,128)(2,1)S(1)}, u32[]{:S(2)}, u32[]{:S(2)}) collective-permute-start(bf16[40,768]{1,0:T(8,128)(2,1)S(1)} %get-tuple-element.28), channel_id=1, source_target_pairs={{0,8},{4,12},{8,0},{12,4},{16,24},{20,28},{24,16},{28,20},{1,9},{5... | collective-permute-start | bytes 184328 | tf_op jit(solution)/shard_map/ppermute | solution.py:245
  4.3 6.4 %collective-permute-start.1 = (bf16[40,768]{1,0:T(8,128)(2,1)S(1)}, bf16[40,768]{1,0:T(8,128)(2,1)S(1)}, u32[]{:S(2)}, u32[]{:S(2)}) collective-permute-start(bf16[40,768]{1,0:T(8,128)(2,1)S(1)} %get-tuple-element.30), channel_id=1, source_target_pairs={{0,16},{4,20},{8,24},{12,28},{16,0},{20,4},{24,8},{28,12},{1,17},{... | collective-permute-start | bytes 184328 | tf_op jit(solution)/shard_map/ppermute | solution.py:245
  6.9 6.0 %collective-permute-start.2 = (bf16[40,768]{1,0:T(8,128)(2,1)S(1)}, bf16[40,768]{1,0:T(8,128)(2,1)S(1)}, u32[]{:S(2)}, u32[]{:S(2)}) collective-permute-start(bf16[40,768]{1,0:T(8,128)(2,1)S(1)} %get-tuple-element.31), channel_id=1, source_target_pairs={{0,24},{4,28},{8,16},{12,20},{16,8},{20,12},{24,0},{28,4},{1,25},{... | collective-permute-start | bytes 184328 | tf_op jit(solution)/shard_map/ppermute | solution.py:245
  6.9 7.5 %collective-permute-start.4 = (bf16[40,768]{1,0:T(8,128)(2,1)S(1)}, bf16[40,768]{1,0:T(8,128)(2,1)S(1)}, u32[]{:S(2)}, u32[]{:S(2)}) collective-permute-start(bf16[40,768]{1,0:T(8,128)(2,1)S(1)} %get-tuple-element.27.refs_0_), channel_id=1, source_target_pairs={{0,4},{4,0},{8,12},{12,8},{16,20},{20,16},{24,28},{28,24},{1,5},{5... | collective-permute-start | bytes 184328 | tf_op jit(solution)/shard_map/ppermute | solution.py:248
  9.7 8.8 %copy-start.2 = (bf16[768,768]{1,0:T(8,128)(2,1)S(1)}, bf16[768,768]{1,0:T(8,128)(2,1)}, u32[]{:S(2)}) copy-start(bf16[768,768]{1,0:T(8,128)(2,1)} %refs_7_.1) | copy-start | bytes 3538948
  9.7 4.7 %collective-permute-start.5 = (bf16[40,768]{1,0:T(8,128)(2,1)S(1)}, bf16[40,768]{1,0:T(8,128)(2,1)S(1)}, u32[]{:S(2)}, u32[]{:S(2)}) collective-permute-start(bf16[40,768]{1,0:T(8,128)(2,1)S(1)} %collective-permute-done.refs_1_), channel_id=1, source_target_pairs={{0,4},{4,0},{8,12},{12,8},{16,20},{20,16},{24,28},{28,24},{1,5},{5... | collective-permute-start | bytes 184328 | tf_op jit(solution)/shard_map/ppermute | solution.py:248
  10.7 4.6 %collective-permute-start.6 = (bf16[40,768]{1,0:T(8,128)(2,1)S(1)}, bf16[40,768]{1,0:T(8,128)(2,1)S(1)}, u32[]{:S(2)}, u32[]{:S(2)}) collective-permute-start(bf16[40,768]{1,0:T(8,128)(2,1)S(1)} %collective-permute-done.1.refs_2_), channel_id=1, source_target_pairs={{0,4},{4,0},{8,12},{12,8},{16,20},{20,16},{24,28},{28,24},{1,5},{5... | collective-permute-start | bytes 184328 | tf_op jit(solution)/shard_map/ppermute | solution.py:248
  12.9 5.6 %collective-permute-start.3 = (bf16[40,768]{1,0:T(8,128)(2,1)S(1)}, bf16[40,768]{1,0:T(8,128)(2,1)S(1)}, u32[]{:S(2)}, u32[]{:S(2)}) collective-permute-start(bf16[40,768]{1,0:T(8,128)(2,1)S(1)} %collective-permute-done.2.refs_3_), channel_id=1, source_target_pairs={{0,4},{4,0},{8,12},{12,8},{16,20},{20,16},{24,28},{28,24},{1,5},{5... | collective-permute-start | bytes 184328 | tf_op jit(solution)/shard_map/ppermute | solution.py:248
  18.5 5.5 %copy-start = (bf16[768,2304]{1,0:T(8,128)(2,1)S(1)}, bf16[768,2304]{1,0:T(8,128)(2,1)}, u32[]{:S(2)}) copy-start(bf16[768,2304]{1,0:T(8,128)(2,1)} %w_ref.5) | copy-start | bytes 10616836
  22.5 6.3 %collective-permute-start.7 = (bf16[160,768]{1,0:T(8,128)(2,1)S(1)}, bf16[160,768]{1,0:T(8,128)(2,1)S(1)}, u32[]{:S(2)}, u32[]{:S(2)}) collective-permute-start(bf16[160,768]{1,0:T(8,128)(2,1)S(1)} %shard_map.75.h_ref), channel_id=1, source_target_pairs={{0,2},{1,3},{2,0},{3,1},{4,6},{5,7},{6,4},{7,5},{8,10},{9,11},{10,... | collective-permute-start | bytes 737288 | tf_op jit(solution)/shard_map/ppermute | solution.py:251
  24.1 4.7 %collective-permute-start.8 = (bf16[160,768]{1,0:T(8,128)(2,1)S(1)}, bf16[160,768]{1,0:T(8,128)(2,1)S(1)}, u32[]{:S(2)}, u32[]{:S(2)}) collective-permute-start(bf16[160,768]{1,0:T(8,128)(2,1)S(1)} %shard_map.75.h_ref), channel_id=1, source_target_pairs={{0,1},{1,0},{2,3},{3,2},{4,5},{5,4},{6,7},{7,6},{8,9},{9,8},{10,11... | collective-permute-start | bytes 737288 | tf_op jit(solution)/shard_map/ppermute | solution.py:251
  28.8 1.5 %copy-start.3 = (bf16[768,768]{1,0:T(8,128)(2,1)S(1)}, bf16[768,768]{1,0:T(8,128)(2,1)}, u32[]{:S(2)}) copy-start(bf16[768,768]{1,0:T(8,128)(2,1)} %wo_ref.1) | copy-start | bytes 3538948
  28.8 1.5 %collective-permute-start.9 = (bf16[160,768]{1,0:T(8,128)(2,1)S(1)}, bf16[160,768]{1,0:T(8,128)(2,1)S(1)}, u32[]{:S(2)}, u32[]{:S(2)}) collective-permute-start(bf16[160,768]{1,0:T(8,128)(2,1)S(1)} %collective-permute-done.7.b_ref), channel_id=1, source_target_pairs={{0,1},{1,0},{2,3},{3,2},{4,5},{5,4},{6,7},{7,6},{8,9},{9,8},{10,11... | collective-permute-start | bytes 737288 | tf_op jit(solution)/shard_map/ppermute | solution.py:251
  31.9 4.5 %collective-permute-start.10 = (bf16[40,768]{1,0:T(8,128)(2,1)S(1)}, bf16[40,768]{1,0:T(8,128)(2,1)S(1)}, u32[]{:S(2)}, u32[]{:S(2)}) collective-permute-start(bf16[40,768]{1,0:T(8,128)(2,1)S(1)} %get-tuple-element.46), channel_id=1, source_target_pairs={{0,8},{4,12},{8,0},{12,4},{16,24},{20,28},{24,16},{28,20},{1,9},{5... | collective-permute-start | bytes 184328 | tf_op jit(solution)/shard_map/ppermute | solution.py:245
  32.6 7.3 %collective-permute-start.11 = (bf16[40,768]{1,0:T(8,128)(2,1)S(1)}, bf16[40,768]{1,0:T(8,128)(2,1)S(1)}, u32[]{:S(2)}, u32[]{:S(2)}) collective-permute-start(bf16[40,768]{1,0:T(8,128)(2,1)S(1)} %get-tuple-element.47), channel_id=1, source_target_pairs={{0,16},{4,20},{8,24},{12,28},{16,0},{20,4},{24,8},{28,12},{1,17},{... | collective-permute-start | bytes 184328 | tf_op jit(solution)/shard_map/ppermute | solution.py:245
  35.9 6.1 %collective-permute-start.12 = (bf16[40,768]{1,0:T(8,128)(2,1)S(1)}, bf16[40,768]{1,0:T(8,128)(2,1)S(1)}, u32[]{:S(2)}, u32[]{:S(2)}) collective-permute-start(bf16[40,768]{1,0:T(8,128)(2,1)S(1)} %get-tuple-element.48), channel_id=1, source_target_pairs={{0,24},{4,28},{8,16},{12,20},{16,8},{20,12},{24,0},{28,4},{1,25},{... | collective-permute-start | bytes 184328 | tf_op jit(solution)/shard_map/ppermute | solution.py:245

commit v4 on v3

--- a/solution.py
+++ b/solution.py
@@ -107,55 +107,33 @@
     return jnp.where(low, c[:n], c[n:])
 
 
-def col_early_kernel(groups, dims, *refs):
-    rows, cols, _ = dims
-    count = 2 * groups - 1
-    chunks, (mod_ref, w_ref, q_ref, m_ref, l_ref, acc_ref, k_ref, v_ref) = refs[:count], refs[count:]
-    n, pad = q_ref.shape[0], chunks[0].shape[0]
-    normed = norm_rows(stacked(chunks), mod_ref, 0)
-    project(normed[:n], w_ref, 0, q_ref, HD**-0.5)
+def col_own_kernel(groups, *refs):
+    own, (mod_ref, w_ref, q_ref, k_ref, v_ref) = refs[:groups], refs[groups:]
+    normed = norm_rows(stacked(own), mod_ref, 0)
+    project(normed, w_ref, 0, q_ref, HD**-0.5)
     project(normed, w_ref, 1, k_ref)
     project(normed, w_ref, 2, v_ref)
-    bias = column_bias(n, pad, count * pad, rows, cols)
+
+
+def col_attend_kernel(groups, dims, *refs):
+    rows, cols, _ = dims
+    own, other = refs[:groups], refs[groups : 2 * groups]
+    mod_ref, w_ref, wo_ref, q_ref, k_ref, v_ref, h_ref, k2_ref, v2_ref, c_ref = refs[2 * groups :]
+    n, pad = q_ref.shape[0], own[0].shape[0]
+    normed = norm_rows(stacked(other), mod_ref, 0)
+    project(normed, w_ref, 1, k2_ref)
+    project(normed, w_ref, 2, v2_ref)
+    bias = column_bias(n, pad, 2 * n, rows, cols)
+    ones = jnp.ones((2 * n, PAIR), BF)
     for j in range(HEADS // 2):
         lanes = slice(j * PAIR, (j + 1) * PAIR)
         q = head_pair(q_ref[:, lanes])
-        s = lax.dot_general(
-            q, k_ref[:, lanes], (((1,), (1,)), ((), ())), preferred_element_type=F32
-        ) + bias
-        top = jnp.max(s, axis=-1, keepdims=True)
-        e = jnp.exp(s - top)
-        m_ref[:, j : j + 1] = top
-        l_ref[:, j : j + 1] = jnp.sum(e, axis=-1, keepdims=True)
-        acc_ref[:, lanes] = unpaired(
-            jnp.dot(e.astype(BF), v_ref[:, lanes], preferred_element_type=F32)
-        )
-
-
-def col_late_kernel(groups, dims, *refs):
-    rows, cols, _ = dims
-    own, last = refs[:groups], refs[groups]
-    mod_ref, w_ref, wo_ref, q_ref, m_ref, l_ref, acc_ref, h_ref, k_ref, v_ref, c_ref = refs[groups + 1 :]
-    n, pad = q_ref.shape[0], last.shape[0]
-    normed = norm_rows(last[...].astype(F32), mod_ref, 0)
-    project(normed, w_ref, 1, k_ref)
-    project(normed, w_ref, 2, v_ref)
-    bias = column_bias(n, pad, pad, rows, cols)
-    for j in range(HEADS // 2):
-        lanes = slice(j * PAIR, (j + 1) * PAIR)
-        q = head_pair(q_ref[:, lanes])
-        s = lax.dot_general(
-            q, k_ref[:, lanes], (((1,), (1,)), ((), ())), preferred_element_type=F32
-        ) + bias
-        before = m_ref[:, j : j + 1]
-        top = jnp.maximum(before, jnp.max(s, axis=-1, keepdims=True))
-        e = jnp.exp(s - top)
-        fade = jnp.exp(before - top)
-        total = fade * l_ref[:, j : j + 1] + jnp.sum(e, axis=-1, keepdims=True)
-        weight = 1.0 / total
-        new = jnp.dot(e.astype(BF), v_ref[:, lanes], preferred_element_type=F32) * weight
-        wide = jnp.broadcast_to(fade * weight, new.shape)
-        c_ref[:, lanes] = (acc_ref[:, lanes] * unpaired(wide) + unpaired(new)).astype(BF)
+        k = jnp.concatenate([k_ref[:, lanes], k2_ref[:, lanes]], axis=0)
+        v = jnp.concatenate([v_ref[:, lanes], v2_ref[:, lanes]], axis=0)
+        s = lax.dot_general(q, k, (((1,), (1,)), ((), ())), preferred_element_type=F32) + bias
+        e = jnp.exp(s - jnp.max(s, axis=-1, keepdims=True)).astype(BF)
+        c = jnp.dot(e, jnp.concatenate([v, ones], axis=1), preferred_element_type=F32)
+        c_ref[:, lanes] = (unpaired(c[:, :PAIR]) / unpaired(c[:, PAIR:])).astype(BF)
     a = jnp.dot(c_ref[...], wo_ref[...], preferred_element_type=F32).astype(BF)
     h_ref[...] = (stacked(own) + a.astype(F32)).astype(BF)
 
@@ -261,16 +239,10 @@
     own[1], mod = lax.optimization_barrier((own[1], mod))
     other = [over_pair(x) for x in own]
 
-    chunks = [*own, *other[:-1]]
-    kv = ((len(chunks) * pad, D), BF)
-    q, m, l, acc = call(
-        functools.partial(col_early_kernel, groups, dims),
-        [full, ((2 * n, 128), F32), ((2 * n, 128), F32), ((n, D), F32)], [kv, kv],
-        *chunks, mod, col_qkv,
-    )
+    q, k, v = call(functools.partial(col_own_kernel, groups), [full] * 3, [], *own, mod, col_qkv)
     (h,) = call(
-        functools.partial(col_late_kernel, groups, dims), [full], [message, message, full],
-        *own, other[-1], mod, col_qkv, col_out, q, m, l, acc,
+        functools.partial(col_attend_kernel, groups, dims), [full], [full] * 3,
+        *own, *other, mod, col_qkv, col_out, q, k, v,
     )
     hy = over_bin(h, 2)
     hc = over_bin(h, 1)

time: 43.2 us -> 40.1 us (0.928)
  Pallas kernels: 12.6 us -> 9.01 us
  waiting for transfers between devices: 11.5 us -> 12 us
    pallas_call x7, Pallas kernels: 12.6 us -> 9.01 us  [call(): pl.pallas_call(kernel, out_shape=[jax.ShapeDtypeStruct(*o) for o in outs]...]
    ppermute x4, waiting for transfers between devices: 0.89 us -> 1.78 us  [over_pair(): return lax.ppermute(x, 'seq', [(i, i ^ 1) for i in range(owners)])]
  transfers between devices with their start and end apart: 13 -> 13, of which waited for: 7 -> 7; matrix products, arithmetic and copies ran while one was open for 1% -> 1% of each run, Pallas kernels for 13% -> 9%
where the time goes in v4:
time: 40.1 us; the launch traced here: 40 us
  starting transfers between devices  16.8 us (42%)
  waiting for transfers between devices  12 us (30%)
  Pallas kernels  9.01 us (22%)
  local copies, waits for them, and re-layouts  0.97 us (2%)
  between operations  0.77 us (2%)
    ppermute x6, starting transfers between devices, over_group(): return lax.ppermute(x, 'seq', [(i, i ^ 2 * m) for i in range(owners)])  10.1 us
    pallas_call x7, Pallas kernels, call(): pl.pallas_call(kernel, out_shape=[jax.ShapeDtypeStruct(*o) for o in outs]...  9.01 us
    ppermute x6, waiting for transfers between devices, over_group(): return lax.ppermute(x, 'seq', [(i, i ^ 2 * m) for i in range(owners)])  6.62 us
    ppermute x4, starting transfers between devices, over_pair(): return lax.ppermute(x, 'seq', [(i, i ^ 1) for i in range(owners)])  5.07 us
    ppermute x3, waiting for transfers between devices, over_bin(): return lax.ppermute(x, 'bin', [(i, i ^ m) for i in range(4)])  3.64 us
    ppermute x4, waiting for transfers between devices, over_pair(): return lax.ppermute(x, 'seq', [(i, i ^ 1) for i in range(owners)])  1.78 us
    ppermute x3, starting transfers between devices, over_bin(): return lax.ppermute(x, 'bin', [(i, i ^ m) for i in range(4)])  1.6 us
    unnamed x12, local copies, waits for them, and re-layouts  0.95 us
  transfers between devices with their start and end apart: 13, of which 7 were waited for; matrix products, arithmetic and copies ran while one was open for 1% of the time, Pallas kernels for 9%

profile of v4, /device:TPU:0, one launch (start us, length us, event | category | flops | bytes accessed | tf_op | source)
XLA Modules:
  0.0 40.0 jit_solution(4643479600438016645)
XLA Ops:
  0.0 0.9 %copy-done.4 = bf16[1,6,24,768]{3,2,1,0:T(8,128)(2,1)S(1)} copy-done((bf16[1,6,24,768]{3,2,1,0:T(8,128)(2,1)S(1)}, bf16[1,6,24,768]{3,2,1,0:T(8,128)(2,1)}, u32[]{:S(2)}) %copy-start.4) | copy-done | bytes 221208
  0.9 0.3 shard_map.73
  1.2 3.1 %collective-permute-start = (bf16[40,768]{1,0:T(8,128)(2,1)S(1)}, bf16[40,768]{1,0:T(8,128)(2,1)S(1)}, u32[]{:S(2)}, u32[]{:S(2)}) collective-permute-start(bf16[40,768]{1,0:T(8,128)(2,1)S(1)} %get-tuple-element.27), channel_id=1, source_target_pairs={{0,8},{4,12},{8,0},{12,4},{16,24},{20,28},{24,16},{28,20},{1,9},{5... | collective-permute-start | bytes 184328 | tf_op jit(solution)/shard_map/ppermute | solution.py:223
  4.3 2.6 %collective-permute-start.1 = (bf16[40,768]{1,0:T(8,128)(2,1)S(1)}, bf16[40,768]{1,0:T(8,128)(2,1)S(1)}, u32[]{:S(2)}, u32[]{:S(2)}) collective-permute-start(bf16[40,768]{1,0:T(8,128)(2,1)S(1)} %get-tuple-element.29), channel_id=1, source_target_pairs={{0,16},{4,20},{8,24},{12,28},{16,0},{20,4},{24,8},{28,12},{1,17},{... | collective-permute-start | bytes 184328 | tf_op jit(solution)/shard_map/ppermute | solution.py:223
  6.9 0.0 collective-permute-start.2
  6.9 1.7 %collective-permute-start.3 = (bf16[40,768]{1,0:T(8,128)(2,1)S(1)}, bf16[40,768]{1,0:T(8,128)(2,1)S(1)}, u32[]{:S(2)}, u32[]{:S(2)}) collective-permute-start(bf16[40,768]{1,0:T(8,128)(2,1)S(1)} %get-tuple-element.26.refs_0_), channel_id=1, source_target_pairs={{0,4},{4,0},{8,12},{12,8},{16,20},{20,16},{24,28},{28,24},{1,5},{5... | collective-permute-start | bytes 184328 | tf_op jit(solution)/shard_map/ppermute | solution.py:226
  9.4 0.3 fusion
  9.7 0.0 collective-permute-done.refs_1_
  9.7 0.0 copy-start.2
  9.7 0.4 collective-permute-start.4
  10.1 0.6 %collective-permute-done.1.refs_2_ = bf16[40,768]{1,0:T(8,128)(2,1)S(1)} collective-permute-done((bf16[40,768]{1,0:T(8,128)(2,1)S(1)}, bf16[40,768]{1,0:T(8,128)(2,1)S(1)}, u32[]{:S(2)}, u32[]{:S(2)}) %collective-permute-start.1) | collective-permute-done | bytes 61472 | tf_op jit(solution)/shard_map/ppermute | solution.py:223
  10.7 1.5 %collective-permute-start.5 = (bf16[40,768]{1,0:T(8,128)(2,1)S(1)}, bf16[40,768]{1,0:T(8,128)(2,1)S(1)}, u32[]{:S(2)}, u32[]{:S(2)}) collective-permute-start(bf16[40,768]{1,0:T(8,128)(2,1)S(1)} %collective-permute-done.1.refs_2_), channel_id=1, source_target_pairs={{0,4},{4,0},{8,12},{12,8},{16,20},{20,16},{24,28},{28,24},{1,5},{5... | collective-permute-start | bytes 184328 | tf_op jit(solution)/shard_map/ppermute | solution.py:226
  12.1 0.8 %collective-permute-done.2.refs_3_ = bf16[40,768]{1,0:T(8,128)(2,1)S(1)} collective-permute-done((bf16[40,768]{1,0:T(8,128)(2,1)S(1)}, bf16[40,768]{1,0:T(8,128)(2,1)S(1)}, u32[]{:S(2)}, u32[]{:S(2)}) %collective-permute-start.2) | collective-permute-done | bytes 61472 | tf_op jit(solution)/shard_map/ppermute | solution.py:223
  12.9 1.5 %collective-permute-start.6 = (bf16[40,768]{1,0:T(8,128)(2,1)S(1)}, bf16[40,768]{1,0:T(8,128)(2,1)S(1)}, u32[]{:S(2)}, u32[]{:S(2)}) collective-permute-start(bf16[40,768]{1,0:T(8,128)(2,1)S(1)} %collective-permute-done.2.refs_3_), channel_id=1, source_target_pairs={{0,4},{4,0},{8,12},{12,8},{16,20},{20,16},{24,28},{28,24},{1,5},{5... | collective-permute-start | bytes 184328 | tf_op jit(solution)/shard_map/ppermute | solution.py:226
  14.4 0.9 %shard_map.74 = (bf16[160,768]{1,0:T(8,128)(2,1)S(1)}, bf16[160,768]{1,0:T(8,128)(2,1)S(1)}, bf16[160,768]{1,0:T(8,128)(2,1)S(1)}) custom-call(bf16[40,768]{1,0:T(8,128)(2,1)S(1)} %get-tuple-element.26.refs_0_, bf16[40,768]{1,0:T(8,128)(2,1)S(1)} %collective-permute-done.refs_1_, bf16[40,768]{1,0:T(8,128)(2,1)S(1)} %collective-permute-done.1.refs_2_, ...), custom_call_target="tpu_custom_call" | custom-call | flops 1000000 | bytes 1000 | tf_op jit(solution)/shard_map/pallas_call | solution.py:202
  15.3 0.0 collective-permute-done.3.refs_4_
  15.4 0.0 collective-permute-done.5.refs_6_
  15.4 1.8 %collective-permute-done.6.refs_7_ = bf16[40,768]{1,0:T(8,128)(2,1)S(1)} collective-permute-done((bf16[40,768]{1,0:T(8,128)(2,1)S(1)}, bf16[40,768]{1,0:T(8,128)(2,1)S(1)}, u32[]{:S(2)}, u32[]{:S(2)}) %collective-permute-start.6) | collective-permute-done | bytes 61472 | tf_op jit(solution)/shard_map/ppermute | solution.py:226
  17.1 2.6 %shard_map.75.h_ref = bf16[160,768]{1,0:T(8,128)(2,1)S(1)} custom-call(bf16[40,768]{1,0:T(8,128)(2,1)S(1)} %get-tuple-element.26.refs_0_, bf16[40,768]{1,0:T(8,128)(2,1)S(1)} %collective-permute-done.refs_1_, bf16[40,768]{1,0:T(8,128)(2,1)S(1)} %collective-permute-done.1.refs_2_, bf16[40,768]{1,0:T(8,128)(2,1)S(1)} %collective-permute-done.2.refs_3_, ...), custom_call_target="tpu_custom_call" | custom-call | flops 1000000 | bytes 1000 | tf_op jit(solution)/shard_map/pallas_call | solution.py:202
  19.7 1.6 %collective-permute-start.7 = (bf16[160,768]{1,0:T(8,128)(2,1)S(1)}, bf16[160,768]{1,0:T(8,128)(2,1)S(1)}, u32[]{:S(2)}, u32[]{:S(2)}) collective-permute-start(bf16[160,768]{1,0:T(8,128)(2,1)S(1)} %shard_map.75.h_ref), channel_id=1, source_target_pairs={{0,2},{1,3},{2,0},{3,1},{4,6},{5,7},{6,4},{7,5},{8,10},{9,11},{10,... | collective-permute-start | bytes 737288 | tf_op jit(solution)/shard_map/ppermute | solution.py:229
  21.3 0.0 collective-permute-start.8
  21.3 1.2 %shard_map.76 = (bf16[160,768]{1,0:T(8,128)(2,1)S(1)}, bf16[160,768]{1,0:T(8,128)(2,1)S(1)}, f32[160,128]{1,0:T(8,128)S(1)}) custom-call(bf16[160,768]{1,0:T(8,128)(2,1)S(1)} %shard_map.75.h_ref, f32[4,768]{1,0:T(4,128)S(1)} %bitcast.15, bf16[768,2304]{1,0:T(8,128)(2,1)S(1)} %copy-done), custom_call_target="tpu_custom_call" | custom-call | flops 1000000 | bytes 1000 | tf_op jit(solution)/shard_map/pallas_call | solution.py:202
  22.5 3.5 %collective-permute-done.7.b_ref = bf16[160,768]{1,0:T(8,128)(2,1)S(1)} collective-permute-done((bf16[160,768]{1,0:T(8,128)(2,1)S(1)}, bf16[160,768]{1,0:T(8,128)(2,1)S(1)}, u32[]{:S(2)}, u32[]{:S(2)}) %collective-permute-start.7) | collective-permute-done | bytes 245792 | tf_op jit(solution)/shard_map/ppermute | solution.py:229
  26.0 1.3 %shard_map.77 = (bf16[320,768]{1,0:T(8,128)(2,1)S(1)}, f32[320,128]{1,0:T(8,128)S(1)}) custom-call(bf16[160,768]{1,0:T(8,128)(2,1)S(1)} %collective-permute-done.8.a_ref, bf16[160,768]{1,0:T(8,128)(2,1)S(1)} %collective-permute-done.7.b_ref, bf16[160,768]{1,0:T(8,128)(2,1)S(1)} %get-tuple-element.37.q_ref, f32[4,768]{1,0:T(4,128)S(1)} %bitcast.16, ...), custom_call_target="tpu_custom_call" | custom-call | flops 1000000 | bytes 1000 | tf_op jit(solution)/shard_map/pallas_call | solution.py:202
  27.3 0.2 collective-permute-done.9.hd_ref
  27.5 1.7 %shard_map.78 = (bf16[40,768]{1,0:T(8,128)(2,1)S(1)}, bf16[40,768]{1,0:T(8,128)(2,1)S(1)}, bf16[40,768]{1,0:T(8,128)(2,1)S(1)}, bf16[40,768]{1,0:T(8,128)(2,1)S(1)}) custom-call(bf16[160,768]{1,0:T(8,128)(2,1)S(1)} %collective-permute-done.9.hd_ref, bf16[160,768]{1,0:T(8,128)(2,1)S(1)} %get-tuple-element.37.q_ref, f32[4,768]{1,0:T(4,128)S(1)} %bitcast.17, ...), custom_call_target="tpu_custom_call" | custom-call | flops 1000000 | bytes 1000 | tf_op jit(solution)/shard_map/pallas_call | solution.py:202
  29.2 0.3 collective-permute-start.10
  29.5 3.4 %collective-permute-start.11 = (bf16[40,768]{1,0:T(8,128)(2,1)S(1)}, bf16[40,768]{1,0:T(8,128)(2,1)S(1)}, u32[]{:S(2)}, u32[]{:S(2)}) collective-permute-start(bf16[40,768]{1,0:T(8,128)(2,1)S(1)} %get-tuple-element.45), channel_id=1, source_target_pairs={{0,16},{4,20},{8,24},{12,28},{16,0},{20,4},{24,8},{28,12},{1,17},{... | collective-permute-start | bytes 184328 | tf_op jit(solution)/shard_map/ppermute | solution.py:223
  32.8 0.8 %collective-permute-start.12 = (bf16[40,768]{1,0:T(8,128)(2,1)S(1)}, bf16[40,768]{1,0:T(8,128)(2,1)S(1)}, u32[]{:S(2)}, u32[]{:S(2)}) collective-permute-start(bf16[40,768]{1,0:T(8,128)(2,1)S(1)} %get-tuple-element.46), channel_id=1, source_target_pairs={{0,24},{4,28},{8,16},{12,20},{16,8},{20,12},{24,0},{28,4},{1,25},{... | collective-permute-start | bytes 184328 | tf_op jit(solution)/shard_map/ppermute | solution.py:223
  33.6 3.0 %collective-permute-done.11.refs_2_ = bf16[40,768]{1,0:T(8,128)(2,1)S(1)} collective-permute-done((bf16[40,768]{1,0:T(8,128)(2,1)S(1)}, bf16[40,768]{1,0:T(8,128)(2,1)S(1)}, u32[]{:S(2)}, u32[]{:S(2)}) %collective-permute-start.11) | collective-permute-done | bytes 61472 | tf_op jit(solution)/shard_map/ppermute | solution.py:223
  36.7 2.2 %collective-permute-done.12.refs_3_ = bf16[40,768]{1,0:T(8,128)(2,1)S(1)} collective-permute-done((bf16[40,768]{1,0:T(8,128)(2,1)S(1)}, bf16[40,768]{1,0:T(8,128)(2,1)S(1)}, u32[]{:S(2)}, u32[]{:S(2)}) %collective-permute-start.12) | collective-permute-done | bytes 61472 | tf_op jit(solution)/shard_map/ppermute | solution.py:223
  38.9 1.1 %shard_map.79 = bf16[144,768]{1,0:T(8,128)(2,1)} custom-call(s32[1]{0:T(128)} %bitcast.z_ref, bf16[40,768]{1,0:T(8,128)(2,1)S(1)} %get-tuple-element.43.refs_0_, bf16[40,768]{1,0:T(8,128)(2,1)S(1)} %collective-permute-done.10.refs_1_, bf16[40,768]{1,0:T(8,128)(2,1)S(1)} %collective-permute-done.11.refs_2_, bf16[40,768]{1,0:T(8,128)(2,1)S(1)} %collective-permute-done.12.refs_3_), custom_call_target="tpu_custom_call" | custom-call | flops 1000000 | bytes 1000 | tf_op jit(solution)/shard_map/pallas_call | solution.py:202
  (18 shorter events, 0.1 us)
Async XLA Ops:
  0.0 0.9 %copy-start.4 = (bf16[1,6,24,768]{3,2,1,0:T(8,128)(2,1)S(1)}, bf16[1,6,24,768]{3,2,1,0:T(8,128)(2,1)}, u32[]{:S(2)}) copy-start(bf16[1,6,24,768]{3,2,1,0:T(8,128)(2,1)} %param.7) | copy-start | bytes 663556
  0.9 8.4 %copy-start.5 = (bf16[256,3072]{1,0:T(8,128)(2,1)S(1)}, bf16[256,3072]{1,0:T(8,128)(2,1)}, u32[]{:S(2)}) copy-start(bf16[256,3072]{1,0:T(8,128)(2,1)} %param.9) | copy-start | bytes 4718596
  0.9 13.5 %copy-start.1 = (bf16[768,2304]{1,0:T(8,128)(2,1)S(1)}, bf16[768,2304]{1,0:T(8,128)(2,1)}, u32[]{:S(2)}) copy-start(bf16[768,2304]{1,0:T(8,128)(2,1)} %refs_9_.1) | copy-start | bytes 10616836
  1.2 8.5 %collective-permute-start = (bf16[40,768]{1,0:T(8,128)(2,1)S(1)}, bf16[40,768]{1,0:T(8,128)(2,1)S(1)}, u32[]{:S(2)}, u32[]{:S(2)}) collective-permute-start(bf16[40,768]{1,0:T(8,128)(2,1)S(1)} %get-tuple-element.27), channel_id=1, source_target_pairs={{0,8},{4,12},{8,0},{12,4},{16,24},{20,28},{24,16},{28,20},{1,9},{5... | collective-permute-start | bytes 184328 | tf_op jit(solution)/shard_map/ppermute | solution.py:223
  4.3 6.4 %collective-permute-start.1 = (bf16[40,768]{1,0:T(8,128)(2,1)S(1)}, bf16[40,768]{1,0:T(8,128)(2,1)S(1)}, u32[]{:S(2)}, u32[]{:S(2)}) collective-permute-start(bf16[40,768]{1,0:T(8,128)(2,1)S(1)} %get-tuple-element.29), channel_id=1, source_target_pairs={{0,16},{4,20},{8,24},{12,28},{16,0},{20,4},{24,8},{28,12},{1,17},{... | collective-permute-start | bytes 184328 | tf_op jit(solution)/shard_map/ppermute | solution.py:223
  6.9 6.0 %collective-permute-start.2 = (bf16[40,768]{1,0:T(8,128)(2,1)S(1)}, bf16[40,768]{1,0:T(8,128)(2,1)S(1)}, u32[]{:S(2)}, u32[]{:S(2)}) collective-permute-start(bf16[40,768]{1,0:T(8,128)(2,1)S(1)} %get-tuple-element.30), channel_id=1, source_target_pairs={{0,24},{4,28},{8,16},{12,20},{16,8},{20,12},{24,0},{28,4},{1,25},{... | collective-permute-start | bytes 184328 | tf_op jit(solution)/shard_map/ppermute | solution.py:223
  6.9 8.4 %collective-permute-start.3 = (bf16[40,768]{1,0:T(8,128)(2,1)S(1)}, bf16[40,768]{1,0:T(8,128)(2,1)S(1)}, u32[]{:S(2)}, u32[]{:S(2)}) collective-permute-start(bf16[40,768]{1,0:T(8,128)(2,1)S(1)} %get-tuple-element.26.refs_0_), channel_id=1, source_target_pairs={{0,4},{4,0},{8,12},{12,8},{16,20},{20,16},{24,28},{28,24},{1,5},{5... | collective-permute-start | bytes 184328 | tf_op jit(solution)/shard_map/ppermute | solution.py:226
  9.7 7.5 %copy-start.2 = (bf16[768,768]{1,0:T(8,128)(2,1)S(1)}, bf16[768,768]{1,0:T(8,128)(2,1)}, u32[]{:S(2)}) copy-start(bf16[768,768]{1,0:T(8,128)(2,1)} %refs_10_.1) | copy-start | bytes 3538948
  9.7 5.7 %collective-permute-start.4 = (bf16[40,768]{1,0:T(8,128)(2,1)S(1)}, bf16[40,768]{1,0:T(8,128)(2,1)S(1)}, u32[]{:S(2)}, u32[]{:S(2)}) collective-permute-start(bf16[40,768]{1,0:T(8,128)(2,1)S(1)} %collective-permute-done.refs_1_), channel_id=1, source_target_pairs={{0,4},{4,0},{8,12},{12,8},{16,20},{20,16},{24,28},{28,24},{1,5},{5... | collective-permute-start | bytes 184328 | tf_op jit(solution)/shard_map/ppermute | solution.py:226
  10.7 4.7 %collective-permute-start.5 = (bf16[40,768]{1,0:T(8,128)(2,1)S(1)}, bf16[40,768]{1,0:T(8,128)(2,1)S(1)}, u32[]{:S(2)}, u32[]{:S(2)}) collective-permute-start(bf16[40,768]{1,0:T(8,128)(2,1)S(1)} %collective-permute-done.1.refs_2_), channel_id=1, source_target_pairs={{0,4},{4,0},{8,12},{12,8},{16,20},{20,16},{24,28},{28,24},{1,5},{5... | collective-permute-start | bytes 184328 | tf_op jit(solution)/shard_map/ppermute | solution.py:226
  12.9 4.2 %collective-permute-start.6 = (bf16[40,768]{1,0:T(8,128)(2,1)S(1)}, bf16[40,768]{1,0:T(8,128)(2,1)S(1)}, u32[]{:S(2)}, u32[]{:S(2)}) collective-permute-start(bf16[40,768]{1,0:T(8,128)(2,1)S(1)} %collective-permute-done.2.refs_3_), channel_id=1, source_target_pairs={{0,4},{4,0},{8,12},{12,8},{16,20},{20,16},{24,28},{28,24},{1,5},{5... | collective-permute-start | bytes 184328 | tf_op jit(solution)/shard_map/ppermute | solution.py:226
  17.1 4.2 %copy-start = (bf16[768,2304]{1,0:T(8,128)(2,1)S(1)}, bf16[768,2304]{1,0:T(8,128)(2,1)}, u32[]{:S(2)}) copy-start(bf16[768,2304]{1,0:T(8,128)(2,1)} %w_ref.5) | copy-start | bytes 10616836
  19.7 6.3 %collective-permute-start.7 = (bf16[160,768]{1,0:T(8,128)(2,1)S(1)}, bf16[160,768]{1,0:T(8,128)(2,1)S(1)}, u32[]{:S(2)}, u32[]{:S(2)}) collective-permute-start(bf16[160,768]{1,0:T(8,128)(2,1)S(1)} %shard_map.75.h_ref), channel_id=1, source_target_pairs={{0,2},{1,3},{2,0},{3,1},{4,6},{5,7},{6,4},{7,5},{8,10},{9,11},{10,... | collective-permute-start | bytes 737288 | tf_op jit(solution)/shard_map/ppermute | solution.py:229
  21.3 4.7 %collective-permute-start.8 = (bf16[160,768]{1,0:T(8,128)(2,1)S(1)}, bf16[160,768]{1,0:T(8,128)(2,1)S(1)}, u32[]{:S(2)}, u32[]{:S(2)}) collective-permute-start(bf16[160,768]{1,0:T(8,128)(2,1)S(1)} %shard_map.75.h_ref), channel_id=1, source_target_pairs={{0,1},{1,0},{2,3},{3,2},{4,5},{5,4},{6,7},{7,6},{8,9},{9,8},{10,11... | collective-permute-start | bytes 737288 | tf_op jit(solution)/shard_map/ppermute | solution.py:229
  26.0 1.5 %copy-start.3 = (bf16[768,768]{1,0:T(8,128)(2,1)S(1)}, bf16[768,768]{1,0:T(8,128)(2,1)}, u32[]{:S(2)}) copy-start(bf16[768,768]{1,0:T(8,128)(2,1)} %wo_ref.1) | copy-start | bytes 3538948
  26.0 1.5 %collective-permute-start.9 = (bf16[160,768]{1,0:T(8,128)(2,1)S(1)}, bf16[160,768]{1,0:T(8,128)(2,1)S(1)}, u32[]{:S(2)}, u32[]{:S(2)}) collective-permute-start(bf16[160,768]{1,0:T(8,128)(2,1)S(1)} %collective-permute-done.7.b_ref), channel_id=1, source_target_pairs={{0,1},{1,0},{2,3},{3,2},{4,5},{5,4},{6,7},{7,6},{8,9},{9,8},{10,11... | collective-permute-start | bytes 737288 | tf_op jit(solution)/shard_map/ppermute | solution.py:229
  29.2 4.5 %collective-permute-start.10 = (bf16[40,768]{1,0:T(8,128)(2,1)S(1)}, bf16[40,768]{1,0:T(8,128)(2,1)S(1)}, u32[]{:S(2)}, u32[]{:S(2)}) collective-permute-start(bf16[40,768]{1,0:T(8,128)(2,1)S(1)} %get-tuple-element.44), channel_id=1, source_target_pairs={{0,8},{4,12},{8,0},{12,4},{16,24},{20,28},{24,16},{28,20},{1,9},{5... | collective-permute-start | bytes 184328 | tf_op jit(solution)/shard_map/ppermute | solution.py:223
  29.5 7.2 %collective-permute-start.11 = (bf16[40,768]{1,0:T(8,128)(2,1)S(1)}, bf16[40,768]{1,0:T(8,128)(2,1)S(1)}, u32[]{:S(2)}, u32[]{:S(2)}) collective-permute-start(bf16[40,768]{1,0:T(8,128)(2,1)S(1)} %get-tuple-element.45), channel_id=1, source_target_pairs={{0,16},{4,20},{8,24},{12,28},{16,0},{20,4},{24,8},{28,12},{1,17},{... | collective-permute-start | bytes 184328 | tf_op jit(solution)/shard_map/ppermute | solution.py:223
  32.8 6.1 %collective-permute-start.12 = (bf16[40,768]{1,0:T(8,128)(2,1)S(1)}, bf16[40,768]{1,0:T(8,128)(2,1)S(1)}, u32[]{:S(2)}, u32[]{:S(2)}) collective-permute-start(bf16[40,768]{1,0:T(8,128)(2,1)S(1)} %get-tuple-element.46), channel_id=1, source_target_pairs={{0,24},{4,28},{8,16},{12,20},{16,8},{20,12},{24,0},{28,4},{1,25},{... | collective-permute-start | bytes 184328 | tf_op jit(solution)/shard_map/ppermute | solution.py:223

commit v5 on v4

--- a/solution.py
+++ b/solution.py
@@ -82,17 +82,29 @@
     out[...] = total.astype(BF)
 
 
-def column_bias(n, pad, keys, rows, cols):
-    def column(shape, dim):
-        r = lax.broadcasted_iota(jnp.int32, shape, dim)
-        r = r - pad * divided(r, pad, shape[dim])
-        return r, r - cols * divided(r, cols, pad)
-
-    _, q_col = column((n, 1), 0)
-    k_row, k_col = column((1, keys), 1)
-    k_col = jnp.where(k_row < rows * cols, k_col, -1)
-    bias = jnp.where(q_col == k_col, 0.0, -1e30).astype(F32)
-    return jnp.concatenate([bias, bias], axis=0)
+def grouped_rows(dims, groups, pad, shape, row_dim):
+    rows, cols, _ = dims
+    flat = (shape[0], 1) if row_dim == 0 else (1, shape[1])
+    r = lax.broadcasted_iota(jnp.int32, flat, row_dim)
+    part, here = groups * rows * 2, rows * 2
+    g = divided(r, part, shape[row_dim])
+    r = r - g * part
+    m = divided(r, here, part)
+    r = r - m * here
+    i = divided(r, 2, here)
+    source = m * pad + i * cols + 2 * g + (r - 2 * i)
+    hit = source == lax.broadcasted_iota(jnp.int32, shape, 1 - row_dim)
+    return jnp.where(hit, 1.0, 0.0).astype(BF)
+
+
+def column_marks(n, keys):
+    def odd(count):
+        return lax.broadcasted_iota(jnp.int32, (count, PAIR), 0) & 1
+
+    lane = lax.broadcasted_iota(jnp.int32, (n, PAIR), 1)
+    query = jnp.where(lane == odd(n), 1.0, 0.0).astype(BF)
+    lane = lax.broadcasted_iota(jnp.int32, (keys, PAIR), 1)
+    return query, jnp.where(lane == odd(keys), 0.0, -(2.0**100)).astype(BF)
 
 
 def head_pair(q):
@@ -107,35 +119,50 @@
     return jnp.where(low, c[:n], c[n:])
 
 
-def col_own_kernel(groups, *refs):
-    own, (mod_ref, w_ref, q_ref, k_ref, v_ref) = refs[:groups], refs[groups:]
-    normed = norm_rows(stacked(own), mod_ref, 0)
-    project(normed, w_ref, 0, q_ref, HD**-0.5)
+def regrouped(refs, dims):
+    pad = refs[0].shape[0]
+    n = len(refs) * dims[0] * dims[1]
+    pick = grouped_rows(dims, len(refs), pad, (n, len(refs) * pad), 0)
+    return jnp.dot(pick, stacked(refs).astype(BF), preferred_element_type=F32)
+
+
+def col_own_kernel(groups, dims, *refs):
+    own, (mod_ref, w_ref, t_ref, q_ref, k_ref, v_ref) = refs[:groups], refs[groups:]
+    rows = regrouped(own, dims)
+    t_ref[...] = rows.astype(BF)
+    normed = norm_rows(rows, mod_ref, 0)
+    project(normed, w_ref, 0, q_ref, HD**-0.5 * math.log2(math.e))
     project(normed, w_ref, 1, k_ref)
     project(normed, w_ref, 2, v_ref)
 
 
 def col_attend_kernel(groups, dims, *refs):
-    rows, cols, _ = dims
-    own, other = refs[:groups], refs[groups : 2 * groups]
-    mod_ref, w_ref, wo_ref, q_ref, k_ref, v_ref, h_ref, k2_ref, v2_ref, c_ref = refs[2 * groups :]
-    n, pad = q_ref.shape[0], own[0].shape[0]
-    normed = norm_rows(stacked(other), mod_ref, 0)
+    other = refs[:groups]
+    mod_ref, w_ref, wo_ref, t_ref, q_ref, k_ref, v_ref, h_ref, *refs = refs[groups:]
+    low_ref, high_ref, k2_ref, v2_ref, c_ref = refs
+    normed = norm_rows(regrouped(other, dims), mod_ref, 0)
     project(normed, w_ref, 1, k2_ref)
     project(normed, w_ref, 2, v2_ref)
-    bias = column_bias(n, pad, 2 * n, rows, cols)
-    ones = jnp.ones((2 * n, PAIR), BF)
-    for j in range(HEADS // 2):
-        lanes = slice(j * PAIR, (j + 1) * PAIR)
-        q = head_pair(q_ref[:, lanes])
-        k = jnp.concatenate([k_ref[:, lanes], k2_ref[:, lanes]], axis=0)
-        v = jnp.concatenate([v_ref[:, lanes], v2_ref[:, lanes]], axis=0)
-        s = lax.dot_general(q, k, (((1,), (1,)), ((), ())), preferred_element_type=F32) + bias
-        e = jnp.exp(s - jnp.max(s, axis=-1, keepdims=True)).astype(BF)
-        c = jnp.dot(e, jnp.concatenate([v, ones], axis=1), preferred_element_type=F32)
-        c_ref[:, lanes] = (unpaired(c[:, :PAIR]) / unpaired(c[:, PAIR:])).astype(BF)
+    part = groups * dims[0] * 2
+    q_mark, k_mark = column_marks(2 * part, 2 * part)
+    ones = jnp.ones((2 * part, PAIR), BF)
+    for g in range(dims[1] // 2):
+        here = slice(g * part, (g + 1) * part)
+        for j in range(HEADS // 2):
+            lanes = slice(j * PAIR, (j + 1) * PAIR)
+            q = jnp.concatenate([head_pair(q_ref[here, lanes]), q_mark], axis=1)
+            k = jnp.concatenate([k_ref[here, lanes], k2_ref[here, lanes]], axis=0)
+            v = jnp.concatenate([v_ref[here, lanes], v2_ref[here, lanes]], axis=0)
+            k = jnp.concatenate([k, k_mark], axis=1)
+            s = lax.dot_general(q, k, (((1,), (1,)), ((), ())), preferred_element_type=F32)
+            e = jnp.exp2((s - jnp.max(s, axis=-1, keepdims=True)).astype(BF))
+            c = jnp.dot(e, jnp.concatenate([v, ones], axis=1), preferred_element_type=F32)
+            c_ref[here, lanes] = (unpaired(c[:, :PAIR]) / unpaired(c[:, PAIR:])).astype(BF)
     a = jnp.dot(c_ref[...], wo_ref[...], preferred_element_type=F32).astype(BF)
-    h_ref[...] = (stacked(own) + a.astype(F32)).astype(BF)
+    h = t_ref[...].astype(F32) + a.astype(F32)
+    h_ref[...] = h.astype(BF)
+    low_ref[...] = h[: low_ref.shape[0]].astype(BF)
+    high_ref[...] = h[low_ref.shape[0] :].astype(BF)
 
 
 def head_lanes(shape, lane_dim):
@@ -151,10 +178,12 @@
     )
 
 
-def bin_own_kernel(h_ref, mod_ref, w_ref, q_ref, v_ref, s_ref):
-    normed = norm_rows(h_ref[...].astype(F32), mod_ref, 1)
-    project(normed, w_ref, 0, q_ref, HD**-0.5)
-    key_scores(q_ref[...].astype(F32), normed, w_ref, s_ref)
+def bin_own_kernel(h_ref, low_ref, high_ref, mod_ref, w_ref, q_ref, v_ref, s_ref):
+    n = h_ref.shape[0]
+    normed = norm_rows(stacked((h_ref, low_ref, high_ref)), mod_ref, 1)
+    project(normed[:n], w_ref, 0, q_ref, HD**-0.5)
+    q = q_ref[...].astype(F32)
+    key_scores(jnp.concatenate([q, q], axis=0), normed, w_ref, s_ref)
     project(normed, w_ref, 2, v_ref)
 
 
@@ -164,21 +193,14 @@
     project(normed, w_ref, 2, v_ref)
 
 
-def bin_two_kernel(a_ref, b_ref, q_ref, mod_ref, w_ref, v_ref, s_ref):
-    normed = norm_rows(stacked((a_ref, b_ref)), mod_ref, 1)
-    q = q_ref[...].astype(F32)
-    key_scores(jnp.concatenate([q, q], axis=0), normed, w_ref, s_ref)
-    project(normed, w_ref, 2, v_ref)
-
-
-def bin_attend_kernel(groups, hd_ref, q_ref, mod_ref, w_ref, wo_ref, h_ref, *refs):
+def bin_attend_kernel(groups, dims, hd_ref, q_ref, mod_ref, w_ref, wo_ref, h_ref, *refs):
     n = h_ref.shape[0]
     (v_ref, s_ref, v2_ref, s2_ref), refs = refs[:4], refs[4:]
     outs, (vd_ref, sd_ref) = refs[:groups], refs[groups:]
     bin_kv_kernel(hd_ref, q_ref, mod_ref, w_ref, vd_ref, sd_ref)
     halves = (slice(0, n), slice(n, 2 * n))
-    scores = [s_ref[...], *(s2_ref[half, :] for half in halves), sd_ref[...]]
-    values = [v_ref[...], *(v2_ref[half, :] for half in halves), vd_ref[...]]
+    scores = [*(s_ref[half, :] for half in halves), s2_ref[...], sd_ref[...]]
+    values = [*(v_ref[half, :] for half in halves), v2_ref[...], vd_ref[...]]
     top = functools.reduce(jnp.maximum, scores)
     exps = [jnp.exp(s - top) for s in scores]
     scale = 1.0 / functools.reduce(jnp.add, exps)
@@ -189,8 +211,10 @@
         part = p * v.astype(F32)
         c = part if c is None else c + part
     out = jnp.dot(c.astype(BF), wo_ref[...], preferred_element_type=F32)
-    out = h_ref[...].astype(F32) + out
+    out = (h_ref[...].astype(F32) + out).astype(BF)
     pad = outs[0].shape[0]
+    put = grouped_rows(dims, groups, pad, (groups * pad, n), 1)
+    out = jnp.dot(put, out, preferred_element_type=F32)
     for m, o in enumerate(outs):
         o[...] = out[m * pad : (m + 1) * pad].astype(BF)
 
@@ -217,7 +241,7 @@
     cols = width // groups
     dims = (rows, cols, width)
     pad = -(-rows * cols // 8) * 8
-    n = groups * pad
+    n = rows * width
 
     def over_group(x, m):
         return lax.ppermute(x, "seq", [(i, i ^ (2 * m)) for i in range(owners)])
@@ -239,21 +263,25 @@
     own[1], mod = lax.optimization_barrier((own[1], mod))
     other = [over_pair(x) for x in own]
 
-    q, k, v = call(functools.partial(col_own_kernel, groups), [full] * 3, [], *own, mod, col_qkv)
-    (h,) = call(
-        functools.partial(col_attend_kernel, groups, dims), [full], [full] * 3,
-        *own, *other, mod, col_qkv, col_out, q, k, v,
+    t, q, k, v = call(
+        functools.partial(col_own_kernel, groups, dims), [full] * 4, [], *own, mod, col_qkv
+    )
+    low = -(-n // 32) * 16
+    h, low, high = call(
+        functools.partial(col_attend_kernel, groups, dims),
+        [full, ((low, D), BF), ((n - low, D), BF)], [full] * 3,
+        *other, mod, col_qkv, col_out, t, q, k, v,
     )
     hy = over_bin(h, 2)
-    hc = over_bin(h, 1)
-    q, v, s = call(bin_own_kernel, [full, full, lanes], [], h, mod, bin_qkv)
-    hy, hc, q = lax.optimization_barrier((hy, hc, q))
+    twice = [((2 * n, D), BF), ((2 * n, 128), F32)]
+    q, v, s = call(
+        bin_own_kernel, [full, *twice], [], h, over_bin(low, 1), over_bin(high, 1), mod, bin_qkv
+    )
+    hy, q = lax.optimization_barrier((hy, q))
     hd = over_bin(hy, 1)
-    v2, s2 = call(
-        bin_two_kernel, [((2 * n, D), BF), ((2 * n, 128), F32)], [], hc, hy, q, mod, bin_qkv
-    )
+    v2, s2 = call(bin_kv_kernel, [full, lanes], [], hy, q, mod, bin_qkv)
     done = call(
-        functools.partial(bin_attend_kernel, groups), [message] * groups, [full, lanes],
+        functools.partial(bin_attend_kernel, groups, dims), [message] * groups, [full, lanes],
         hd, q, mod, bin_qkv, bin_out, h, v, s, v2, s2,
     )
     back = [done[0]] + [over_group(done[m], m) for m in range(1, groups)]
@@ -346,8 +374,8 @@
 
 def per_device(tokens, *rest):
     owners, width = lax.axis_size("seq"), tokens.shape[2]
-    small = owners in (4, 8) and width % (owners // 2) == 0 and lax.axis_size("bin") == 4
-    if small and tokens.shape[1] * width <= 256:
+    small = owners in (4, 8) and width % owners == 0 and lax.axis_size("bin") == 4
+    if small and tokens.shape[1] * owners % 16 == 0 and tokens.shape[1] * width <= 256:
         return column_path(tokens, *rest)
     return general_path(tokens, *rest)
 

time: 40.1 us -> 39 us (0.973)
  Pallas kernels: 9.01 us -> 8.1 us
  waiting for transfers between devices: 12 us -> 11.3 us
  starting transfers between devices: 16.8 us -> 17.3 us
    pallas_call x7, Pallas kernels: 9.01 us -> 8.1 us  [call(): pl.pallas_call(kernel, out_shape=[jax.ShapeDtypeStruct(*o) for o in outs]...]
    ppermute x3 -> x4, waiting for transfers between devices: 3.64 us -> 3.1 us  [over_bin(): return lax.ppermute(x, 'bin', [(i, i ^ m) for i in range(4)])]
    ppermute x3 -> x4, starting transfers between devices: 1.6 us -> 2.11 us  [over_bin(): return lax.ppermute(x, 'bin', [(i, i ^ m) for i in range(4)])]
  transfers between devices with their start and end apart: 13 -> 14, of which waited for: 7 -> 8; matrix products, arithmetic and copies ran while one was open for 1% -> 1% of each run, Pallas kernels for 9% -> 8%
where the time goes in v5:
time: 39 us; the launch traced here: 38.9 us
  starting transfers between devices  17.3 us (44%)
  waiting for transfers between devices  11.3 us (29%)
  Pallas kernels  8.1 us (21%)
  local copies, waits for them, and re-layouts  0.97 us (2%)
  between operations  0.77 us (2%)
    ppermute x6, starting transfers between devices, over_group(): return lax.ppermute(x, 'seq', [(i, i ^ 2 * m) for i in range(owners)])  10.1 us
    pallas_call x7, Pallas kernels, call(): pl.pallas_call(kernel, out_shape=[jax.ShapeDtypeStruct(*o) for o in outs]...  8.1 us
    ppermute x6, waiting for transfers between devices, over_group(): return lax.ppermute(x, 'seq', [(i, i ^ 2 * m) for i in range(owners)])  6.58 us
    ppermute x4, starting transfers between devices, over_pair(): return lax.ppermute(x, 'seq', [(i, i ^ 1) for i in range(owners)])  5.07 us
    ppermute x4, waiting for transfers between devices, over_bin(): return lax.ppermute(x, 'bin', [(i, i ^ m) for i in range(4)])  3.1 us
    ppermute x4, starting transfers between devices, over_bin(): return lax.ppermute(x, 'bin', [(i, i ^ m) for i in range(4)])  2.11 us
    ppermute x4, waiting for transfers between devices, over_pair(): return lax.ppermute(x, 'seq', [(i, i ^ 1) for i in range(owners)])  1.64 us
    unnamed x12, local copies, waits for them, and re-layouts  0.95 us
  transfers between devices with their start and end apart: 14, of which 8 were waited for; matrix products, arithmetic and copies ran while one was open for 1% of the time, Pallas kernels for 8%

profile of v5, /device:TPU:0, one launch (start us, length us, event | category | flops | bytes accessed | tf_op | source)
XLA Modules:
  0.0 38.9 jit_solution(2819661369731427645)
XLA Ops:
  0.0 0.9 %copy-done.4 = bf16[1,6,24,768]{3,2,1,0:T(8,128)(2,1)S(1)} copy-done((bf16[1,6,24,768]{3,2,1,0:T(8,128)(2,1)S(1)}, bf16[1,6,24,768]{3,2,1,0:T(8,128)(2,1)}, u32[]{:S(2)}) %copy-start.4) | copy-done | bytes 221208
  0.9 0.3 shard_map.73
  1.2 3.1 %collective-permute-start.1 = (bf16[40,768]{1,0:T(8,128)(2,1)S(1)}, bf16[40,768]{1,0:T(8,128)(2,1)S(1)}, u32[]{:S(2)}, u32[]{:S(2)}) collective-permute-start(bf16[40,768]{1,0:T(8,128)(2,1)S(1)} %get-tuple-element.30), channel_id=1, source_target_pairs={{0,8},{4,12},{8,0},{12,4},{16,24},{20,28},{24,16},{28,20},{1,9},{5... | collective-permute-start | bytes 184328 | tf_op jit(solution)/shard_map/ppermute | solution.py:247
  4.3 2.6 %collective-permute-start.3 = (bf16[40,768]{1,0:T(8,128)(2,1)S(1)}, bf16[40,768]{1,0:T(8,128)(2,1)S(1)}, u32[]{:S(2)}, u32[]{:S(2)}) collective-permute-start(bf16[40,768]{1,0:T(8,128)(2,1)S(1)} %get-tuple-element.32), channel_id=1, source_target_pairs={{0,16},{4,20},{8,24},{12,28},{16,0},{20,4},{24,8},{28,12},{1,17},{... | collective-permute-start | bytes 184328 | tf_op jit(solution)/shard_map/ppermute | solution.py:247
  6.9 1.7 %collective-permute-start = (bf16[40,768]{1,0:T(8,128)(2,1)S(1)}, bf16[40,768]{1,0:T(8,128)(2,1)S(1)}, u32[]{:S(2)}, u32[]{:S(2)}) collective-permute-start(bf16[40,768]{1,0:T(8,128)(2,1)S(1)} %get-tuple-element.29.refs_0_), channel_id=1, source_target_pairs={{0,4},{4,0},{8,12},{12,8},{16,20},{20,16},{24,28},{28,24},{1,5},{5... | collective-permute-start | bytes 184328 | tf_op jit(solution)/shard_map/ppermute | solution.py:250
  9.4 0.3 fusion
  9.7 0.0 collective-permute-done.1.refs_1_
  9.7 0.0 copy-start.2
  9.7 0.4 collective-permute-start.2
  10.1 0.6 %collective-permute-done.3.refs_2_ = bf16[40,768]{1,0:T(8,128)(2,1)S(1)} collective-permute-done((bf16[40,768]{1,0:T(8,128)(2,1)S(1)}, bf16[40,768]{1,0:T(8,128)(2,1)S(1)}, u32[]{:S(2)}, u32[]{:S(2)}) %collective-permute-start.3) | collective-permute-done | bytes 61472 | tf_op jit(solution)/shard_map/ppermute | solution.py:247
  10.7 1.5 %collective-permute-start.4 = (bf16[40,768]{1,0:T(8,128)(2,1)S(1)}, bf16[40,768]{1,0:T(8,128)(2,1)S(1)}, u32[]{:S(2)}, u32[]{:S(2)}) collective-permute-start(bf16[40,768]{1,0:T(8,128)(2,1)S(1)} %collective-permute-done.3.refs_2_), channel_id=1, source_target_pairs={{0,4},{4,0},{8,12},{12,8},{16,20},{20,16},{24,28},{28,24},{1,5},{5... | collective-permute-start | bytes 184328 | tf_op jit(solution)/shard_map/ppermute | solution.py:250
  12.1 0.8 %collective-permute-done.5.refs_3_ = bf16[40,768]{1,0:T(8,128)(2,1)S(1)} collective-permute-done((bf16[40,768]{1,0:T(8,128)(2,1)S(1)}, bf16[40,768]{1,0:T(8,128)(2,1)S(1)}, u32[]{:S(2)}, u32[]{:S(2)}) %collective-permute-start.5) | collective-permute-done | bytes 61472 | tf_op jit(solution)/shard_map/ppermute | solution.py:247
  12.9 1.5 %collective-permute-start.6 = (bf16[40,768]{1,0:T(8,128)(2,1)S(1)}, bf16[40,768]{1,0:T(8,128)(2,1)S(1)}, u32[]{:S(2)}, u32[]{:S(2)}) collective-permute-start(bf16[40,768]{1,0:T(8,128)(2,1)S(1)} %collective-permute-done.5.refs_3_), channel_id=1, source_target_pairs={{0,4},{4,0},{8,12},{12,8},{16,20},{20,16},{24,28},{28,24},{1,5},{5... | collective-permute-start | bytes 184328 | tf_op jit(solution)/shard_map/ppermute | solution.py:250
  14.4 1.1 %shard_map.74 = (bf16[144,768]{1,0:T(8,128)(2,1)S(1)}, bf16[144,768]{1,0:T(8,128)(2,1)S(1)}, bf16[144,768]{1,0:T(8,128)(2,1)S(1)}, bf16[144,768]{1,0:T(8,128)(2,1)S(1)}) custom-call(bf16[40,768]{1,0:T(8,128)(2,1)S(1)} %get-tuple-element.29.refs_0_, bf16[40,768]{1,0:T(8,128)(2,1)S(1)} %collective-permute-done.1.refs_1_, ...), custom_call_target="tpu_custom_call" | custom-call | flops 1000000 | bytes 1000 | tf_op jit(solution)/shard_map/pallas_call | solution.py:226
  15.5 0.0 collective-permute-done.refs_0_
  15.5 0.0 collective-permute-done.2.refs_1_
  15.5 1.6 %collective-permute-done.6.refs_3_ = bf16[40,768]{1,0:T(8,128)(2,1)S(1)} collective-permute-done((bf16[40,768]{1,0:T(8,128)(2,1)S(1)}, bf16[40,768]{1,0:T(8,128)(2,1)S(1)}, u32[]{:S(2)}, u32[]{:S(2)}) %collective-permute-start.6) | collective-permute-done | bytes 61472 | tf_op jit(solution)/shard_map/ppermute | solution.py:250
  17.1 1.8 %shard_map.75 = (bf16[144,768]{1,0:T(8,128)(2,1)S(1)}, bf16[80,768]{1,0:T(8,128)(2,1)S(1)}, bf16[64,768]{1,0:T(8,128)(2,1)S(1)}) custom-call(bf16[40,768]{1,0:T(8,128)(2,1)S(1)} %collective-permute-done.refs_0_, bf16[40,768]{1,0:T(8,128)(2,1)S(1)} %collective-permute-done.2.refs_1_, bf16[40,768]{1,0:T(8,128)(2,1)S(1)} %collective-permute-done.4.refs_2_, ...), custom_call_target="tpu_custom_call" | custom-call | flops 1000000 | bytes 1000 | tf_op jit(solution)/shard_map/pallas_call | solution.py:226
  19.0 1.6 %collective-permute-start.7 = (bf16[144,768]{1,0:T(8,128)(2,1)S(1)}, bf16[144,768]{1,0:T(8,128)(2,1)S(1)}, u32[]{:S(2)}, u32[]{:S(2)}) collective-permute-start(bf16[144,768]{1,0:T(8,128)(2,1)S(1)} %get-tuple-element.39.h_ref), channel_id=1, source_target_pairs={{0,2},{1,3},{2,0},{3,1},{4,6},{5,7},{6,4},{7,5},{8,10},{9,11},{10,... | collective-permute-start | bytes 663560 | tf_op jit(solution)/shard_map/ppermute | solution.py:253
  20.6 0.5 %collective-permute-start.9 = (bf16[64,768]{1,0:T(8,128)(2,1)S(1)}, bf16[64,768]{1,0:T(8,128)(2,1)S(1)}, u32[]{:S(2)}, u32[]{:S(2)}) collective-permute-start(bf16[64,768]{1,0:T(8,128)(2,1)S(1)} %get-tuple-element.41), channel_id=1, source_target_pairs={{0,1},{1,0},{2,3},{3,2},{4,5},{5,4},{6,7},{7,6},{8,9},{9,8},{10,11... | collective-permute-start | bytes 294920 | tf_op jit(solution)/shard_map/ppermute | solution.py:253
  21.1 1.0 %collective-permute-done.9.high_ref = bf16[64,768]{1,0:T(8,128)(2,1)S(1)} collective-permute-done((bf16[64,768]{1,0:T(8,128)(2,1)S(1)}, bf16[64,768]{1,0:T(8,128)(2,1)S(1)}, u32[]{:S(2)}, u32[]{:S(2)}) %collective-permute-start.9) | collective-permute-done | bytes 98336 | tf_op jit(solution)/shard_map/ppermute | solution.py:253
  22.0 1.4 %shard_map.76 = (bf16[144,768]{1,0:T(8,128)(2,1)S(1)}, bf16[288,768]{1,0:T(8,128)(2,1)S(1)}, f32[288,128]{1,0:T(8,128)S(1)}) custom-call(bf16[144,768]{1,0:T(8,128)(2,1)S(1)} %get-tuple-element.39.h_ref, bf16[80,768]{1,0:T(8,128)(2,1)S(1)} %collective-permute-done.8.low_ref, bf16[64,768]{1,0:T(8,128)(2,1)S(1)} %collective-permute-done.9.high_ref, ...), custom_call_target="tpu_custom_call" | custom-call | flops 1000000 | bytes 1000 | tf_op jit(solution)/shard_map/pallas_call | solution.py:226
  23.5 1.5 %collective-permute-done.7.h_ref = bf16[144,768]{1,0:T(8,128)(2,1)S(1)} collective-permute-done((bf16[144,768]{1,0:T(8,128)(2,1)S(1)}, bf16[144,768]{1,0:T(8,128)(2,1)S(1)}, u32[]{:S(2)}, u32[]{:S(2)}) %collective-permute-start.7) | collective-permute-done | bytes 221216 | tf_op jit(solution)/shard_map/ppermute | solution.py:253
  25.0 0.8 %shard_map.77 = (bf16[144,768]{1,0:T(8,128)(2,1)S(1)}, f32[144,128]{1,0:T(8,128)S(1)}) custom-call(bf16[144,768]{1,0:T(8,128)(2,1)S(1)} %collective-permute-done.7.h_ref, bf16[144,768]{1,0:T(8,128)(2,1)S(1)} %get-tuple-element.44.q_ref, f32[4,768]{1,0:T(4,128)S(1)} %bitcast.16, bf16[768,2304]{1,0:T(8,128)(2,1)S(1)} %copy-done), custom_call_target="tpu_custom_call" | custom-call | flops 1000000 | bytes 1000 | tf_op jit(solution)/shard_map/pallas_call | solution.py:226
  25.8 0.7 %collective-permute-done.10.hd_ref = bf16[144,768]{1,0:T(8,128)(2,1)S(1)} collective-permute-done((bf16[144,768]{1,0:T(8,128)(2,1)S(1)}, bf16[144,768]{1,0:T(8,128)(2,1)S(1)}, u32[]{:S(2)}, u32[]{:S(2)}) %collective-permute-start.10) | collective-permute-done | bytes 221216 | tf_op jit(solution)/shard_map/ppermute | solution.py:253
  26.4 1.7 %shard_map.78 = (bf16[40,768]{1,0:T(8,128)(2,1)S(1)}, bf16[40,768]{1,0:T(8,128)(2,1)S(1)}, bf16[40,768]{1,0:T(8,128)(2,1)S(1)}, bf16[40,768]{1,0:T(8,128)(2,1)S(1)}) custom-call(bf16[144,768]{1,0:T(8,128)(2,1)S(1)} %collective-permute-done.10.hd_ref, bf16[144,768]{1,0:T(8,128)(2,1)S(1)} %get-tuple-element.44.q_ref, f32[4,768]{1,0:T(4,128)S(1)} %bitcast.17, ...), custom_call_target="tpu_custom_call" | custom-call | flops 1000000 | bytes 1000 | tf_op jit(solution)/shard_map/pallas_call | solution.py:226
  28.1 0.3 collective-permute-start.11
  28.4 3.4 %collective-permute-start.12 = (bf16[40,768]{1,0:T(8,128)(2,1)S(1)}, bf16[40,768]{1,0:T(8,128)(2,1)S(1)}, u32[]{:S(2)}, u32[]{:S(2)}) collective-permute-start(bf16[40,768]{1,0:T(8,128)(2,1)S(1)} %get-tuple-element.51), channel_id=1, source_target_pairs={{0,16},{4,20},{8,24},{12,28},{16,0},{20,4},{24,8},{28,12},{1,17},{... | collective-permute-start | bytes 184328 | tf_op jit(solution)/shard_map/ppermute | solution.py:247
  31.8 0.8 %collective-permute-start.13 = (bf16[40,768]{1,0:T(8,128)(2,1)S(1)}, bf16[40,768]{1,0:T(8,128)(2,1)S(1)}, u32[]{:S(2)}, u32[]{:S(2)}) collective-permute-start(bf16[40,768]{1,0:T(8,128)(2,1)S(1)} %get-tuple-element.52), channel_id=1, source_target_pairs={{0,24},{4,28},{8,16},{12,20},{16,8},{20,12},{24,0},{28,4},{1,25},{... | collective-permute-start | bytes 184328 | tf_op jit(solution)/shard_map/ppermute | solution.py:247
  32.6 3.0 %collective-permute-done.12.refs_2_ = bf16[40,768]{1,0:T(8,128)(2,1)S(1)} collective-permute-done((bf16[40,768]{1,0:T(8,128)(2,1)S(1)}, bf16[40,768]{1,0:T(8,128)(2,1)S(1)}, u32[]{:S(2)}, u32[]{:S(2)}) %collective-permute-start.12) | collective-permute-done | bytes 61472 | tf_op jit(solution)/shard_map/ppermute | solution.py:247
  35.6 2.2 %collective-permute-done.13.refs_3_ = bf16[40,768]{1,0:T(8,128)(2,1)S(1)} collective-permute-done((bf16[40,768]{1,0:T(8,128)(2,1)S(1)}, bf16[40,768]{1,0:T(8,128)(2,1)S(1)}, u32[]{:S(2)}, u32[]{:S(2)}) %collective-permute-start.13) | collective-permute-done | bytes 61472 | tf_op jit(solution)/shard_map/ppermute | solution.py:247
  37.8 1.1 %shard_map.79 = bf16[144,768]{1,0:T(8,128)(2,1)} custom-call(s32[1]{0:T(128)} %bitcast.z_ref, bf16[40,768]{1,0:T(8,128)(2,1)S(1)} %get-tuple-element.49.refs_0_, bf16[40,768]{1,0:T(8,128)(2,1)S(1)} %collective-permute-done.11.refs_1_, bf16[40,768]{1,0:T(8,128)(2,1)S(1)} %collective-permute-done.12.refs_2_, bf16[40,768]{1,0:T(8,128)(2,1)S(1)} %collective-permute-done.13.refs_3_), custom_call_target="tpu_custom_call" | custom-call | flops 1000000 | bytes 1000 | tf_op jit(solution)/shard_map/pallas_call | solution.py:226
  (20 shorter events, 0.1 us)
Async XLA Ops:
  0.0 0.9 %copy-start.4 = (bf16[1,6,24,768]{3,2,1,0:T(8,128)(2,1)S(1)}, bf16[1,6,24,768]{3,2,1,0:T(8,128)(2,1)}, u32[]{:S(2)}) copy-start(bf16[1,6,24,768]{3,2,1,0:T(8,128)(2,1)} %param.7) | copy-start | bytes 663556
  0.9 8.4 %copy-start.5 = (bf16[256,3072]{1,0:T(8,128)(2,1)S(1)}, bf16[256,3072]{1,0:T(8,128)(2,1)}, u32[]{:S(2)}) copy-start(bf16[256,3072]{1,0:T(8,128)(2,1)} %param.9) | copy-start | bytes 4718596
  0.9 13.5 %copy-start.1 = (bf16[768,2304]{1,0:T(8,128)(2,1)S(1)}, bf16[768,2304]{1,0:T(8,128)(2,1)}, u32[]{:S(2)}) copy-start(bf16[768,2304]{1,0:T(8,128)(2,1)} %refs_5_.3) | copy-start | bytes 10616836
  1.2 8.5 %collective-permute-start.1 = (bf16[40,768]{1,0:T(8,128)(2,1)S(1)}, bf16[40,768]{1,0:T(8,128)(2,1)S(1)}, u32[]{:S(2)}, u32[]{:S(2)}) collective-permute-start(bf16[40,768]{1,0:T(8,128)(2,1)S(1)} %get-tuple-element.30), channel_id=1, source_target_pairs={{0,8},{4,12},{8,0},{12,4},{16,24},{20,28},{24,16},{28,20},{1,9},{5... | collective-permute-start | bytes 184328 | tf_op jit(solution)/shard_map/ppermute | solution.py:247
  4.3 6.4 %collective-permute-start.3 = (bf16[40,768]{1,0:T(8,128)(2,1)S(1)}, bf16[40,768]{1,0:T(8,128)(2,1)S(1)}, u32[]{:S(2)}, u32[]{:S(2)}) collective-permute-start(bf16[40,768]{1,0:T(8,128)(2,1)S(1)} %get-tuple-element.32), channel_id=1, source_target_pairs={{0,16},{4,20},{8,24},{12,28},{16,0},{20,4},{24,8},{28,12},{1,17},{... | collective-permute-start | bytes 184328 | tf_op jit(solution)/shard_map/ppermute | solution.py:247
  6.9 6.0 %collective-permute-start.5 = (bf16[40,768]{1,0:T(8,128)(2,1)S(1)}, bf16[40,768]{1,0:T(8,128)(2,1)S(1)}, u32[]{:S(2)}, u32[]{:S(2)}) collective-permute-start(bf16[40,768]{1,0:T(8,128)(2,1)S(1)} %get-tuple-element.33), channel_id=1, source_target_pairs={{0,24},{4,28},{8,16},{12,20},{16,8},{20,12},{24,0},{28,4},{1,25},{... | collective-permute-start | bytes 184328 | tf_op jit(solution)/shard_map/ppermute | solution.py:247
  6.9 8.6 %collective-permute-start = (bf16[40,768]{1,0:T(8,128)(2,1)S(1)}, bf16[40,768]{1,0:T(8,128)(2,1)S(1)}, u32[]{:S(2)}, u32[]{:S(2)}) collective-permute-start(bf16[40,768]{1,0:T(8,128)(2,1)S(1)} %get-tuple-element.29.refs_0_), channel_id=1, source_target_pairs={{0,4},{4,0},{8,12},{12,8},{16,20},{20,16},{24,28},{28,24},{1,5},{5... | collective-permute-start | bytes 184328 | tf_op jit(solution)/shard_map/ppermute | solution.py:250
  9.7 7.5 %copy-start.2 = (bf16[768,768]{1,0:T(8,128)(2,1)S(1)}, bf16[768,768]{1,0:T(8,128)(2,1)}, u32[]{:S(2)}) copy-start(bf16[768,768]{1,0:T(8,128)(2,1)} %refs_6_.1) | copy-start | bytes 3538948
  9.7 5.8 %collective-permute-start.2 = (bf16[40,768]{1,0:T(8,128)(2,1)S(1)}, bf16[40,768]{1,0:T(8,128)(2,1)S(1)}, u32[]{:S(2)}, u32[]{:S(2)}) collective-permute-start(bf16[40,768]{1,0:T(8,128)(2,1)S(1)} %collective-permute-done.1.refs_1_), channel_id=1, source_target_pairs={{0,4},{4,0},{8,12},{12,8},{16,20},{20,16},{24,28},{28,24},{1,5},{5... | collective-permute-start | bytes 184328 | tf_op jit(solution)/shard_map/ppermute | solution.py:250
  10.7 4.8 %collective-permute-start.4 = (bf16[40,768]{1,0:T(8,128)(2,1)S(1)}, bf16[40,768]{1,0:T(8,128)(2,1)S(1)}, u32[]{:S(2)}, u32[]{:S(2)}) collective-permute-start(bf16[40,768]{1,0:T(8,128)(2,1)S(1)} %collective-permute-done.3.refs_2_), channel_id=1, source_target_pairs={{0,4},{4,0},{8,12},{12,8},{16,20},{20,16},{24,28},{28,24},{1,5},{5... | collective-permute-start | bytes 184328 | tf_op jit(solution)/shard_map/ppermute | solution.py:250
  12.9 4.2 %collective-permute-start.6 = (bf16[40,768]{1,0:T(8,128)(2,1)S(1)}, bf16[40,768]{1,0:T(8,128)(2,1)S(1)}, u32[]{:S(2)}, u32[]{:S(2)}) collective-permute-start(bf16[40,768]{1,0:T(8,128)(2,1)S(1)} %collective-permute-done.5.refs_3_), channel_id=1, source_target_pairs={{0,4},{4,0},{8,12},{12,8},{16,20},{20,16},{24,28},{28,24},{1,5},{5... | collective-permute-start | bytes 184328 | tf_op jit(solution)/shard_map/ppermute | solution.py:250
  17.1 4.9 %copy-start = (bf16[768,2304]{1,0:T(8,128)(2,1)S(1)}, bf16[768,2304]{1,0:T(8,128)(2,1)}, u32[]{:S(2)}) copy-start(bf16[768,2304]{1,0:T(8,128)(2,1)} %w_ref.5) | copy-start | bytes 10616836
  19.0 6.0 %collective-permute-start.7 = (bf16[144,768]{1,0:T(8,128)(2,1)S(1)}, bf16[144,768]{1,0:T(8,128)(2,1)S(1)}, u32[]{:S(2)}, u32[]{:S(2)}) collective-permute-start(bf16[144,768]{1,0:T(8,128)(2,1)S(1)} %get-tuple-element.39.h_ref), channel_id=1, source_target_pairs={{0,2},{1,3},{2,0},{3,1},{4,6},{5,7},{6,4},{7,5},{8,10},{9,11},{10,... | collective-permute-start | bytes 663560 | tf_op jit(solution)/shard_map/ppermute | solution.py:253
  20.6 1.5 %collective-permute-start.8 = (bf16[80,768]{1,0:T(8,128)(2,1)S(1)}, bf16[80,768]{1,0:T(8,128)(2,1)S(1)}, u32[]{:S(2)}, u32[]{:S(2)}) collective-permute-start(bf16[80,768]{1,0:T(8,128)(2,1)S(1)} %get-tuple-element.40), channel_id=1, source_target_pairs={{0,1},{1,0},{2,3},{3,2},{4,5},{5,4},{6,7},{7,6},{8,9},{9,8},{10,11... | collective-permute-start | bytes 368648 | tf_op jit(solution)/shard_map/ppermute | solution.py:253
  20.6 1.5 %collective-permute-start.9 = (bf16[64,768]{1,0:T(8,128)(2,1)S(1)}, bf16[64,768]{1,0:T(8,128)(2,1)S(1)}, u32[]{:S(2)}, u32[]{:S(2)}) collective-permute-start(bf16[64,768]{1,0:T(8,128)(2,1)S(1)} %get-tuple-element.41), channel_id=1, source_target_pairs={{0,1},{1,0},{2,3},{3,2},{4,5},{5,4},{6,7},{7,6},{8,9},{9,8},{10,11... | collective-permute-start | bytes 294920 | tf_op jit(solution)/shard_map/ppermute | solution.py:253
  25.0 1.5 %copy-start.3 = (bf16[768,768]{1,0:T(8,128)(2,1)S(1)}, bf16[768,768]{1,0:T(8,128)(2,1)}, u32[]{:S(2)}) copy-start(bf16[768,768]{1,0:T(8,128)(2,1)} %wo_ref.1) | copy-start | bytes 3538948
  25.0 1.5 %collective-permute-start.10 = (bf16[144,768]{1,0:T(8,128)(2,1)S(1)}, bf16[144,768]{1,0:T(8,128)(2,1)S(1)}, u32[]{:S(2)}, u32[]{:S(2)}) collective-permute-start(bf16[144,768]{1,0:T(8,128)(2,1)S(1)} %collective-permute-done.7.h_ref), channel_id=1, source_target_pairs={{0,1},{1,0},{2,3},{3,2},{4,5},{5,4},{6,7},{7,6},{8,9},{9,8},{10,11... | collective-permute-start | bytes 663560 | tf_op jit(solution)/shard_map/ppermute | solution.py:253
  28.1 4.5 %collective-permute-start.11 = (bf16[40,768]{1,0:T(8,128)(2,1)S(1)}, bf16[40,768]{1,0:T(8,128)(2,1)S(1)}, u32[]{:S(2)}, u32[]{:S(2)}) collective-permute-start(bf16[40,768]{1,0:T(8,128)(2,1)S(1)} %get-tuple-element.50), channel_id=1, source_target_pairs={{0,8},{4,12},{8,0},{12,4},{16,24},{20,28},{24,16},{28,20},{1,9},{5... | collective-permute-start | bytes 184328 | tf_op jit(solution)/shard_map/ppermute | solution.py:247
  28.4 7.2 %collective-permute-start.12 = (bf16[40,768]{1,0:T(8,128)(2,1)S(1)}, bf16[40,768]{1,0:T(8,128)(2,1)S(1)}, u32[]{:S(2)}, u32[]{:S(2)}) collective-permute-start(bf16[40,768]{1,0:T(8,128)(2,1)S(1)} %get-tuple-element.51), channel_id=1, source_target_pairs={{0,16},{4,20},{8,24},{12,28},{16,0},{20,4},{24,8},{28,12},{1,17},{... | collective-permute-start | bytes 184328 | tf_op jit(solution)/shard_map/ppermute | solution.py:247
  31.8 6.0 %collective-permute-start.13 = (bf16[40,768]{1,0:T(8,128)(2,1)S(1)}, bf16[40,768]{1,0:T(8,128)(2,1)S(1)}, u32[]{:S(2)}, u32[]{:S(2)}) collective-permute-start(bf16[40,768]{1,0:T(8,128)(2,1)S(1)} %get-tuple-element.52), channel_id=1, source_target_pairs={{0,24},{4,28},{8,16},{12,20},{16,8},{20,12},{24,0},{28,4},{1,25},{... | collective-permute-start | bytes 184328 | tf_op jit(solution)/shard_map/ppermute | solution.py:247

commit v6 on v5

--- a/solution.py
+++ b/solution.py
@@ -70,16 +70,15 @@
         out[...] = jnp.dot(pick, x, preferred_element_type=F32).astype(BF)
 
 
-def unpack_kernel(dims, groups, z_ref, *refs):
+def token_rows(dims, pad, shape, z):
     rows, cols, width = dims
-    out = refs[groups]
-    total = None
-    for m in range(groups):
-        shape = (out.shape[0], refs[m].shape[0])
-        put = message_rows(shape, 1, 0, rows, cols, width, z_ref[0] ^ m)
-        part = jnp.dot(put, refs[m][...], preferred_element_type=F32)
-        total = part if total is None else total + part
-    out[...] = total.astype(BF)
+    r = lax.broadcasted_iota(jnp.int32, (1, shape[1]), 1)
+    m = divided(r, pad, shape[1])
+    r = r - m * pad
+    i = divided(r, cols, pad)
+    source = i * width + (z ^ m) * cols + (r - i * cols)
+    source = jnp.where(r < rows * cols, source, -1)
+    return jnp.where(source == lax.broadcasted_iota(jnp.int32, shape, 0), 1.0, 0.0).astype(BF)
 
 
 def grouped_rows(dims, groups, pad, shape, row_dim):
@@ -138,8 +137,8 @@
 
 def col_attend_kernel(groups, dims, *refs):
     other = refs[:groups]
-    mod_ref, w_ref, wo_ref, t_ref, q_ref, k_ref, v_ref, h_ref, *refs = refs[groups:]
-    low_ref, high_ref, k2_ref, v2_ref, c_ref = refs
+    mod_ref, w_ref, wo_ref, t_ref, q_ref, k_ref, v_ref, *refs = refs[groups:]
+    *outs, k2_ref, v2_ref, c_ref = refs
     normed = norm_rows(regrouped(other, dims), mod_ref, 0)
     project(normed, w_ref, 1, k2_ref)
     project(normed, w_ref, 2, v2_ref)
@@ -159,10 +158,12 @@
             c = jnp.dot(e, jnp.concatenate([v, ones], axis=1), preferred_element_type=F32)
             c_ref[here, lanes] = (unpaired(c[:, :PAIR]) / unpaired(c[:, PAIR:])).astype(BF)
     a = jnp.dot(c_ref[...], wo_ref[...], preferred_element_type=F32).astype(BF)
-    h = t_ref[...].astype(F32) + a.astype(F32)
-    h_ref[...] = h.astype(BF)
-    low_ref[...] = h[: low_ref.shape[0]].astype(BF)
-    high_ref[...] = h[low_ref.shape[0] :].astype(BF)
+    h = (t_ref[...].astype(F32) + a.astype(F32)).astype(BF)
+    pad = outs[0].shape[0]
+    put = grouped_rows(dims, groups, pad, (groups * pad, h.shape[0]), 1)
+    h = jnp.dot(put, h, preferred_element_type=F32)
+    for m, o in enumerate(outs):
+        o[...] = h[m * pad : (m + 1) * pad].astype(BF)
 
 
 def head_lanes(shape, lane_dim):
@@ -178,29 +179,68 @@
     )
 
 
-def bin_own_kernel(h_ref, low_ref, high_ref, mod_ref, w_ref, q_ref, v_ref, s_ref):
-    n = h_ref.shape[0]
-    normed = norm_rows(stacked((h_ref, low_ref, high_ref)), mod_ref, 1)
-    project(normed[:n], w_ref, 0, q_ref, HD**-0.5)
-    q = q_ref[...].astype(F32)
+def split_rows(rows, parts):
+    start = 0
+    for part in parts:
+        part[...] = rows[start : start + part.shape[0]].astype(BF)
+        start += part.shape[0]
+
+
+def bin_own_kernel(count, *refs):
+    chunks, (mod_ref, w_ref, q_ref, v_ref, s_ref, *parts) = refs[:count], refs[count:]
+    rows = stacked(chunks)
+    split_rows(rows, parts)
+    normed = norm_rows(rows, mod_ref, 1)
+    project(normed, w_ref, 0, q_ref, HD**-0.5)
+    key_scores(q_ref[...].astype(F32), normed, w_ref, s_ref)
+    project(normed, w_ref, 2, v_ref)
+
+
+def bin_early_kernel(count, own_ref, *refs):
+    chunks, (q_ref, mod_ref, w_ref, q2_ref, v_ref, s_ref, *parts) = refs[:count], refs[count:]
+    rows = stacked(chunks)
+    split_rows(rows, parts)
+    rows = jnp.concatenate([rows, own_ref[...].astype(F32)], axis=0)
+    normed = norm_rows(rows, mod_ref, 1)
+    split = q_ref.shape[0]
+    q2 = jnp.dot(normed, w_ref[:, :D], preferred_element_type=F32)[split:] * HD**-0.5
+    q2_ref[...] = q2.astype(BF)
+    query = jnp.concatenate([q_ref[...].astype(F32), q2_ref[...].astype(F32)], axis=0)
+    key_scores(query, normed, w_ref, s_ref)
+    project(normed, w_ref, 2, v_ref)
+
+
+def bin_late_kernel(count, *refs):
+    chunks, (q_ref, q2_ref, mod_ref, w_ref, v_ref, s_ref) = refs[:count], refs[count:]
+    normed = norm_rows(stacked(chunks), mod_ref, 1)
+    q = stacked((q_ref, q2_ref))
     key_scores(jnp.concatenate([q, q], axis=0), normed, w_ref, s_ref)
     project(normed, w_ref, 2, v_ref)
 
 
-def bin_kv_kernel(h_ref, q_ref, mod_ref, w_ref, v_ref, s_ref):
-    normed = norm_rows(h_ref[...].astype(F32), mod_ref, 1)
-    key_scores(q_ref[...].astype(F32), normed, w_ref, s_ref)
-    project(normed, w_ref, 2, v_ref)
-
-
-def bin_attend_kernel(groups, dims, hd_ref, q_ref, mod_ref, w_ref, wo_ref, h_ref, *refs):
-    n = h_ref.shape[0]
-    (v_ref, s_ref, v2_ref, s2_ref), refs = refs[:4], refs[4:]
-    outs, (vd_ref, sd_ref) = refs[:groups], refs[groups:]
-    bin_kv_kernel(hd_ref, q_ref, mod_ref, w_ref, vd_ref, sd_ref)
-    halves = (slice(0, n), slice(n, 2 * n))
-    scores = [*(s_ref[half, :] for half in halves), s2_ref[...], sd_ref[...]]
-    values = [*(v_ref[half, :] for half in halves), v2_ref[...], vd_ref[...]]
+def bin_attend_kernel(groups, dims, z_ref, last_ref, *refs):
+    own, refs = refs[:groups], refs[groups:]
+    q2_ref, mod_ref, w_ref, wo_ref, v1_ref, s1_ref, v2_ref, s2_ref, v3_ref, s3_ref = refs[:-1]
+    out_ref = refs[-1]
+    n, m = s2_ref.shape[0], s1_ref.shape[0]
+    normed = norm_rows(last_ref[...].astype(F32), mod_ref, 1)
+    k = jnp.dot(normed, w_ref[:, D : 2 * D], preferred_element_type=F32).astype(BF).astype(F32)
+    s4 = jnp.dot(
+        (q2_ref[...].astype(F32) * k).astype(BF), head_lanes((D, 128), 0),
+        preferred_element_type=F32,
+    )
+    v4 = jnp.dot(normed, w_ref[:, 2 * D :], preferred_element_type=F32)
+
+    def of_bins(one, two, three, four):
+        return [
+            jnp.concatenate([one, two[m:]], axis=0),
+            three[:n],
+            jnp.concatenate([two[:m], three[n + m :]], axis=0),
+            jnp.concatenate([three[n : n + m], four], axis=0),
+        ]
+
+    scores = of_bins(s1_ref[...], s2_ref[...], s3_ref[...], s4)
+    values = of_bins(*(r[...].astype(F32) for r in (v1_ref, v2_ref, v3_ref)), v4)
     top = functools.reduce(jnp.maximum, scores)
     exps = [jnp.exp(s - top) for s in scores]
     scale = 1.0 / functools.reduce(jnp.add, exps)
@@ -208,15 +248,12 @@
     c = None
     for e, v in zip(exps, values):
         p = jnp.dot((e * scale).astype(BF), spread, preferred_element_type=F32)
-        part = p * v.astype(F32)
+        part = p * v
         c = part if c is None else c + part
     out = jnp.dot(c.astype(BF), wo_ref[...], preferred_element_type=F32)
-    out = (h_ref[...].astype(F32) + out).astype(BF)
-    pad = outs[0].shape[0]
-    put = grouped_rows(dims, groups, pad, (groups * pad, n), 1)
-    out = jnp.dot(put, out, preferred_element_type=F32)
-    for m, o in enumerate(outs):
-        o[...] = out[m * pad : (m + 1) * pad].astype(BF)
+    out = (stacked(own) + out).astype(BF)
+    put = token_rows(dims, own[0].shape[0], (out_ref.shape[0], n), z_ref[0])
+    out_ref[...] = jnp.dot(put, out, preferred_element_type=F32).astype(BF)
 
 
 def call(kernel, outs, scratch, *args, cost=10**6):
@@ -252,7 +289,7 @@
     def over_bin(x, m):
         return lax.ppermute(x, "bin", [(i, i ^ m) for i in range(4)])
 
-    message, full, lanes = ((pad, D), BF), ((n, D), BF), ((n, 128), F32)
+    message, full = ((pad, D), BF), ((n, D), BF)
     z = (lax.axis_index("seq") // 2).astype(jnp.int32).reshape(1)
     flat = tokens.reshape(rows * width, D)
     sent = call(
@@ -266,27 +303,38 @@
     t, q, k, v = call(
         functools.partial(col_own_kernel, groups, dims), [full] * 4, [], *own, mod, col_qkv
     )
-    low = -(-n // 32) * 16
-    h, low, high = call(
-        functools.partial(col_attend_kernel, groups, dims),
-        [full, ((low, D), BF), ((n - low, D), BF)], [full] * 3,
+    sent = call(
+        functools.partial(col_attend_kernel, groups, dims), [message] * groups, [full] * 3,
         *other, mod, col_qkv, col_out, t, q, k, v,
     )
-    hy = over_bin(h, 2)
-    twice = [((2 * n, D), BF), ((2 * n, 128), F32)]
-    q, v, s = call(
-        bin_own_kernel, [full, *twice], [], h, over_bin(low, 1), over_bin(high, 1), mod, bin_qkv
-    )
-    hy, q = lax.optimization_barrier((hy, q))
-    hd = over_bin(hy, 1)
-    v2, s2 = call(bin_kv_kernel, [full, lanes], [], hy, q, mod, bin_qkv)
-    done = call(
-        functools.partial(bin_attend_kernel, groups, dims), [message] * groups, [full, lanes],
-        hd, q, mod, bin_qkv, bin_out, h, v, s, v2, s2,
-    )
-    back = [done[0]] + [over_group(done[m], m) for m in range(1, groups)]
+    h = [sent[0]] + [over_group(sent[m], m) for m in range(1, groups)]
+    hy = [over_bin(x, 2) for x in h]
+
+    def rows_of(count):
+        return [((count, D), BF), ((count, 128), F32)]
+
+    padded, early = groups * pad, (groups - 1) * pad
+    parts = [((padded // 2, D), BF), ((early - padded // 2, D), BF)]
+    q, v1, s1, *h_parts = call(
+        functools.partial(bin_own_kernel, groups - 1),
+        [((early, D), BF), *rows_of(early), *parts], [], *h[:-1], mod, bin_qkv,
+    )
+    hc = [over_bin(x, 1) for x in (*h_parts, h[-1])]
+    q2, v2, s2, *hy_parts = call(
+        functools.partial(bin_early_kernel, groups - 1), [message, *rows_of(padded), *parts], [],
+        h[-1], *hy[:-1], q, mod, bin_qkv,
+    )
+    hd_early = [over_bin(x, 1) for x in hy_parts]
+    last, v2 = lax.optimization_barrier((hy[-1], v2))
+    hd = over_bin(last, 1)
+    others = [*hc, *hd_early, last]
+    v3, s3 = call(
+        functools.partial(bin_late_kernel, len(others)), rows_of(2 * padded), [],
+        *others, q, q2, mod, bin_qkv,
+    )
     (out,) = call(
-        functools.partial(unpack_kernel, dims, groups), [((rows * width, D), BF)], [], z, *back
+        functools.partial(bin_attend_kernel, groups, dims), [full], [],
+        z, hd, *h, q2, mod, bin_qkv, bin_out, v1, s1, v2, s2, v3, s3,
     )
     return out.reshape(tokens.shape)
 

time: 39 us -> 38.1 us (0.977)
  waiting for transfers between devices: 11.3 us -> 5.1 us
  starting transfers between devices: 17.3 us -> 21.5 us
  Pallas kernels: 8.1 us -> 9.25 us
    ppermute x6, waiting for transfers between devices: 6.58 us -> 1.88 us  [over_group(): return lax.ppermute(x, 'seq', [(i, i ^ 2 * m) for i in range(owners)])]
    ppermute x4 -> x10, starting transfers between devices: 2.11 us -> 6.29 us  [over_bin(): return lax.ppermute(x, 'bin', [(i, i ^ m) for i in range(4)])]
    ppermute x4 -> x10, waiting for transfers between devices: 3.1 us -> 1.59 us  [over_bin(): return lax.ppermute(x, 'bin', [(i, i ^ m) for i in range(4)])]
    pallas_call x7, Pallas kernels: 8.1 us -> 9.25 us  [call(): pl.pallas_call(kernel, out_shape=[jax.ShapeDtypeStruct(*o) for o in outs]...]
  transfers between devices with their start and end apart: 14 -> 20, of which waited for: 8 -> 6; matrix products, arithmetic and copies ran while one was open for 1% -> 1% of each run, Pallas kernels for 8% -> 12%
where the time goes in v6:
time: 38.1 us; the launch traced here: 38 us
  starting transfers between devices  21.5 us (56%)
  Pallas kernels  9.25 us (24%)
  waiting for transfers between devices  5.1 us (13%)
  local copies, waits for them, and re-layouts  0.97 us (3%)
  between operations  0.81 us (2%)
    ppermute x6, starting transfers between devices, over_group(): return lax.ppermute(x, 'seq', [(i, i ^ 2 * m) for i in range(owners)])  10.1 us
    pallas_call x7, Pallas kernels, call(): pl.pallas_call(kernel, out_shape=[jax.ShapeDtypeStruct(*o) for o in outs]...  9.25 us
    ppermute x10, starting transfers between devices, over_bin(): return lax.ppermute(x, 'bin', [(i, i ^ m) for i in range(4)])  6.29 us
    ppermute x4, starting transfers between devices, over_pair(): return lax.ppermute(x, 'seq', [(i, i ^ 1) for i in range(owners)])  5.07 us
    ppermute x6, waiting for transfers between devices, over_group(): return lax.ppermute(x, 'seq', [(i, i ^ 2 * m) for i in range(owners)])  1.88 us
    ppermute x4, waiting for transfers between devices, over_pair(): return lax.ppermute(x, 'seq', [(i, i ^ 1) for i in range(owners)])  1.63 us
    ppermute x10, waiting for transfers between devices, over_bin(): return lax.ppermute(x, 'bin', [(i, i ^ m) for i in range(4)])  1.59 us
    unnamed x12, local copies, waits for them, and re-layouts  0.95 us
  transfers between devices with their start and end apart: 20, of which 6 were waited for; matrix products, arithmetic and copies ran while one was open for 1% of the time, Pallas kernels for 12%

profile of v6, /device:TPU:0, one launch (start us, length us, event | category | flops | bytes accessed | tf_op | source)
XLA Modules:
  0.0 38.0 jit_solution(6632384156171744602)
XLA Ops:
  0.0 0.9 %copy-done.4 = bf16[1,6,24,768]{3,2,1,0:T(8,128)(2,1)S(1)} copy-done((bf16[1,6,24,768]{3,2,1,0:T(8,128)(2,1)S(1)}, bf16[1,6,24,768]{3,2,1,0:T(8,128)(2,1)}, u32[]{:S(2)}) %copy-start.4) | copy-done | bytes 221208
  0.9 0.3 shard_map.73
  1.2 3.1 %collective-permute-start.1 = (bf16[40,768]{1,0:T(8,128)(2,1)S(1)}, bf16[40,768]{1,0:T(8,128)(2,1)S(1)}, u32[]{:S(2)}, u32[]{:S(2)}) collective-permute-start(bf16[40,768]{1,0:T(8,128)(2,1)S(1)} %get-tuple-element.34), channel_id=1, source_target_pairs={{0,8},{4,12},{8,0},{12,4},{16,24},{20,28},{24,16},{28,20},{1,9},{5... | collective-permute-start | bytes 184328 | tf_op jit(solution)/shard_map/ppermute | solution.py:284
  4.3 2.6 %collective-permute-start.3 = (bf16[40,768]{1,0:T(8,128)(2,1)S(1)}, bf16[40,768]{1,0:T(8,128)(2,1)S(1)}, u32[]{:S(2)}, u32[]{:S(2)}) collective-permute-start(bf16[40,768]{1,0:T(8,128)(2,1)S(1)} %get-tuple-element.36), channel_id=1, source_target_pairs={{0,16},{4,20},{8,24},{12,28},{16,0},{20,4},{24,8},{28,12},{1,17},{... | collective-permute-start | bytes 184328 | tf_op jit(solution)/shard_map/ppermute | solution.py:284
  6.9 1.7 %collective-permute-start = (bf16[40,768]{1,0:T(8,128)(2,1)S(1)}, bf16[40,768]{1,0:T(8,128)(2,1)S(1)}, u32[]{:S(2)}, u32[]{:S(2)}) collective-permute-start(bf16[40,768]{1,0:T(8,128)(2,1)S(1)} %get-tuple-element.33.refs_0_), channel_id=1, source_target_pairs={{0,4},{4,0},{8,12},{12,8},{16,20},{20,16},{24,28},{28,24},{1,5},{5... | collective-permute-start | bytes 184328 | tf_op jit(solution)/shard_map/ppermute | solution.py:287
  9.4 0.3 fusion
  9.7 0.4 %collective-permute-start.2 = (bf16[40,768]{1,0:T(8,128)(2,1)S(1)}, bf16[40,768]{1,0:T(8,128)(2,1)S(1)}, u32[]{:S(2)}, u32[]{:S(2)}) collective-permute-start(bf16[40,768]{1,0:T(8,128)(2,1)S(1)} %collective-permute-done.1.refs_1_), channel_id=1, source_target_pairs={{0,4},{4,0},{8,12},{12,8},{16,20},{20,16},{24,28},{28,24},{1,5},{5... | collective-permute-start | bytes 184328 | tf_op jit(solution)/shard_map/ppermute | solution.py:287
  10.1 0.6 %collective-permute-done.3.refs_2_ = bf16[40,768]{1,0:T(8,128)(2,1)S(1)} collective-permute-done((bf16[40,768]{1,0:T(8,128)(2,1)S(1)}, bf16[40,768]{1,0:T(8,128)(2,1)S(1)}, u32[]{:S(2)}, u32[]{:S(2)}) %collective-permute-start.3) | collective-permute-done | bytes 61472 | tf_op jit(solution)/shard_map/ppermute | solution.py:284
  10.7 1.5 %collective-permute-start.4 = (bf16[40,768]{1,0:T(8,128)(2,1)S(1)}, bf16[40,768]{1,0:T(8,128)(2,1)S(1)}, u32[]{:S(2)}, u32[]{:S(2)}) collective-permute-start(bf16[40,768]{1,0:T(8,128)(2,1)S(1)} %collective-permute-done.3.refs_2_), channel_id=1, source_target_pairs={{0,4},{4,0},{8,12},{12,8},{16,20},{20,16},{24,28},{28,24},{1,5},{5... | collective-permute-start | bytes 184328 | tf_op jit(solution)/shard_map/ppermute | solution.py:287
  12.1 0.8 %collective-permute-done.5.refs_3_ = bf16[40,768]{1,0:T(8,128)(2,1)S(1)} collective-permute-done((bf16[40,768]{1,0:T(8,128)(2,1)S(1)}, bf16[40,768]{1,0:T(8,128)(2,1)S(1)}, u32[]{:S(2)}, u32[]{:S(2)}) %collective-permute-start.5) | collective-permute-done | bytes 61472 | tf_op jit(solution)/shard_map/ppermute | solution.py:284
  12.9 1.5 %collective-permute-start.6 = (bf16[40,768]{1,0:T(8,128)(2,1)S(1)}, bf16[40,768]{1,0:T(8,128)(2,1)S(1)}, u32[]{:S(2)}, u32[]{:S(2)}) collective-permute-start(bf16[40,768]{1,0:T(8,128)(2,1)S(1)} %collective-permute-done.5.refs_3_), channel_id=1, source_target_pairs={{0,4},{4,0},{8,12},{12,8},{16,20},{20,16},{24,28},{28,24},{1,5},{5... | collective-permute-start | bytes 184328 | tf_op jit(solution)/shard_map/ppermute | solution.py:287
  14.4 1.1 %shard_map.74 = (bf16[144,768]{1,0:T(8,128)(2,1)S(1)}, bf16[144,768]{1,0:T(8,128)(2,1)S(1)}, bf16[144,768]{1,0:T(8,128)(2,1)S(1)}, bf16[144,768]{1,0:T(8,128)(2,1)S(1)}) custom-call(bf16[40,768]{1,0:T(8,128)(2,1)S(1)} %get-tuple-element.33.refs_0_, bf16[40,768]{1,0:T(8,128)(2,1)S(1)} %collective-permute-done.1.refs_1_, ...), custom_call_target="tpu_custom_call" | custom-call | flops 1000000 | bytes 1000 | tf_op jit(solution)/shard_map/pallas_call | solution.py:263
  15.5 1.6 %collective-permute-done.6.refs_3_ = bf16[40,768]{1,0:T(8,128)(2,1)S(1)} collective-permute-done((bf16[40,768]{1,0:T(8,128)(2,1)S(1)}, bf16[40,768]{1,0:T(8,128)(2,1)S(1)}, u32[]{:S(2)}, u32[]{:S(2)}) %collective-permute-start.6) | collective-permute-done | bytes 61472 | tf_op jit(solution)/shard_map/ppermute | solution.py:287
  17.1 2.0 %shard_map.75 = (bf16[40,768]{1,0:T(8,128)(2,1)S(1)}, bf16[40,768]{1,0:T(8,128)(2,1)S(1)}, bf16[40,768]{1,0:T(8,128)(2,1)S(1)}, bf16[40,768]{1,0:T(8,128)(2,1)S(1)}) custom-call(bf16[40,768]{1,0:T(8,128)(2,1)S(1)} %collective-permute-done.refs_0_, bf16[40,768]{1,0:T(8,128)(2,1)S(1)} %collective-permute-done.2.refs_1_, ...), custom_call_target="tpu_custom_call" | custom-call | flops 1000000 | bytes 1000 | tf_op jit(solution)/shard_map/pallas_call | solution.py:263
  19.1 0.3 collective-permute-start.10
  19.4 3.4 %collective-permute-start.12 = (bf16[40,768]{1,0:T(8,128)(2,1)S(1)}, bf16[40,768]{1,0:T(8,128)(2,1)S(1)}, u32[]{:S(2)}, u32[]{:S(2)}) collective-permute-start(bf16[40,768]{1,0:T(8,128)(2,1)S(1)} %get-tuple-element.46), channel_id=1, source_target_pairs={{0,16},{4,20},{8,24},{12,28},{16,0},{20,4},{24,8},{28,12},{1,17},{... | collective-permute-start | bytes 184328 | tf_op jit(solution)/shard_map/ppermute | solution.py:284
  22.8 0.8 %collective-permute-start.7 = (bf16[40,768]{1,0:T(8,128)(2,1)S(1)}, bf16[40,768]{1,0:T(8,128)(2,1)S(1)}, u32[]{:S(2)}, u32[]{:S(2)}) collective-permute-start(bf16[40,768]{1,0:T(8,128)(2,1)S(1)} %get-tuple-element.43), channel_id=1, source_target_pairs={{0,24},{4,28},{8,16},{12,20},{16,8},{20,12},{24,0},{28,4},{1,25},{... | collective-permute-start | bytes 184328 | tf_op jit(solution)/shard_map/ppermute | solution.py:284
  23.6 1.5 %collective-permute-start.9 = (bf16[40,768]{1,0:T(8,128)(2,1)S(1)}, bf16[40,768]{1,0:T(8,128)(2,1)S(1)}, u32[]{:S(2)}, u32[]{:S(2)}) collective-permute-start(bf16[40,768]{1,0:T(8,128)(2,1)S(1)} %get-tuple-element.44.refs_0_), channel_id=1, source_target_pairs={{0,2},{1,3},{2,0},{3,1},{4,6},{5,7},{6,4},{7,5},{8,10},{9,11},{10,... | collective-permute-start | bytes 184328 | tf_op jit(solution)/shard_map/ppermute | solution.py:290
  25.1 0.5 %collective-permute-start.11 = (bf16[40,768]{1,0:T(8,128)(2,1)S(1)}, bf16[40,768]{1,0:T(8,128)(2,1)S(1)}, u32[]{:S(2)}, u32[]{:S(2)}) collective-permute-start(bf16[40,768]{1,0:T(8,128)(2,1)S(1)} %collective-permute-done.10.refs_1_), channel_id=1, source_target_pairs={{0,2},{1,3},{2,0},{3,1},{4,6},{5,7},{6,4},{7,5},{8,10},{9,11},{10,... | collective-permute-start | bytes 184328 | tf_op jit(solution)/shard_map/ppermute | solution.py:290
  25.6 1.5 %collective-permute-start.13 = (bf16[40,768]{1,0:T(8,128)(2,1)S(1)}, bf16[40,768]{1,0:T(8,128)(2,1)S(1)}, u32[]{:S(2)}, u32[]{:S(2)}) collective-permute-start(bf16[40,768]{1,0:T(8,128)(2,1)S(1)} %collective-permute-done.12.refs_2_), channel_id=1, source_target_pairs={{0,2},{1,3},{2,0},{3,1},{4,6},{5,7},{6,4},{7,5},{8,10},{9,11},{10,... | collective-permute-start | bytes 184328 | tf_op jit(solution)/shard_map/ppermute | solution.py:290
  27.1 1.0 %shard_map.76 = (bf16[120,768]{1,0:T(8,128)(2,1)S(1)}, bf16[120,768]{1,0:T(8,128)(2,1)S(1)}, f32[120,128]{1,0:T(8,128)S(1)}, bf16[80,768]{1,0:T(8,128)(2,1)S(1)}, bf16[40,768]{1,0:T(8,128)(2,1)S(1)}) custom-call(bf16[40,768]{1,0:T(8,128)(2,1)S(1)} %get-tuple-element.44.refs_0_, bf16[40,768]{1,0:T(8,128)(2,1)S(1)} %collective-permute-done.10.refs_1_, ...), custom_call_target="tpu_custom_call" | custom-call | flops 1000000 | bytes 1000 | tf_op jit(solution)/shard_map/pallas_call | solution.py:263
  28.2 0.1 collective-permute-start.15
  28.3 0.5 %collective-permute-done.7.own_ref.refs_3_ = bf16[40,768]{1,0:T(8,128)(2,1)S(1)} collective-permute-done((bf16[40,768]{1,0:T(8,128)(2,1)S(1)}, bf16[40,768]{1,0:T(8,128)(2,1)S(1)}, u32[]{:S(2)}, u32[]{:S(2)}) %collective-permute-start.7) | collective-permute-done | bytes 61472 | tf_op jit(solution)/shard_map/ppermute | solution.py:284
  28.8 1.5 %collective-permute-start.8 = (bf16[40,768]{1,0:T(8,128)(2,1)S(1)}, bf16[40,768]{1,0:T(8,128)(2,1)S(1)}, u32[]{:S(2)}, u32[]{:S(2)}) collective-permute-start(bf16[40,768]{1,0:T(8,128)(2,1)S(1)} %collective-permute-done.7.own_ref.refs_3_), channel_id=1, source_target_pairs={{0,2},{1,3},{2,0},{3,1},{4,6},{5,7},{6,4},{7,5},{8,10},{9,11},{10,... | collective-permute-start | bytes 184328 | tf_op jit(solution)/shard_map/ppermute | solution.py:290
  30.3 1.2 %shard_map.77 = (bf16[40,768]{1,0:T(8,128)(2,1)S(1)}, bf16[160,768]{1,0:T(8,128)(2,1)S(1)}, f32[160,128]{1,0:T(8,128)S(1)}, bf16[80,768]{1,0:T(8,128)(2,1)S(1)}, bf16[40,768]{1,0:T(8,128)(2,1)S(1)}) custom-call(bf16[40,768]{1,0:T(8,128)(2,1)S(1)} %collective-permute-done.7.own_ref.refs_3_, bf16[40,768]{1,0:T(8,128)(2,1)S(1)} %collective-permute-done.9.refs_0_, ...), custom_call_target="tpu_custom_call" | custom-call | flops 1000000 | bytes 1000 | tf_op jit(solution)/shard_map/pallas_call | solution.py:263
  31.6 0.5 %collective-permute-start.16 = (bf16[40,768]{1,0:T(8,128)(2,1)S(1)}, bf16[40,768]{1,0:T(8,128)(2,1)S(1)}, u32[]{:S(2)}, u32[]{:S(2)}) collective-permute-start(bf16[40,768]{1,0:T(8,128)(2,1)S(1)} %get-tuple-element.56), channel_id=1, source_target_pairs={{0,1},{1,0},{2,3},{3,2},{4,5},{5,4},{6,7},{7,6},{8,9},{9,8},{10,11... | collective-permute-start | bytes 184328 | tf_op jit(solution)/shard_map/ppermute | solution.py:290
  32.1 0.1 collective-permute-start.17
  32.2 0.8 %collective-permute-done.8.refs_5_ = bf16[40,768]{1,0:T(8,128)(2,1)S(1)} collective-permute-done((bf16[40,768]{1,0:T(8,128)(2,1)S(1)}, bf16[40,768]{1,0:T(8,128)(2,1)S(1)}, u32[]{:S(2)}, u32[]{:S(2)}) %collective-permute-start.8) | collective-permute-done | bytes 61472 | tf_op jit(solution)/shard_map/ppermute | solution.py:290
  33.0 0.5 %collective-permute-start.14 = (bf16[40,768]{1,0:T(8,128)(2,1)S(1)}, bf16[40,768]{1,0:T(8,128)(2,1)S(1)}, u32[]{:S(2)}, u32[]{:S(2)}) collective-permute-start(bf16[40,768]{1,0:T(8,128)(2,1)S(1)} %collective-permute-done.8.refs_5_), channel_id=1, source_target_pairs={{0,1},{1,0},{2,3},{3,2},{4,5},{5,4},{6,7},{7,6},{8,9},{9,8},{10,11... | collective-permute-start | bytes 184328 | tf_op jit(solution)/shard_map/ppermute | solution.py:290
  33.5 0.7 %collective-permute-done.19.refs_4_ = bf16[40,768]{1,0:T(8,128)(2,1)S(1)} collective-permute-done((bf16[40,768]{1,0:T(8,128)(2,1)S(1)}, bf16[40,768]{1,0:T(8,128)(2,1)S(1)}, u32[]{:S(2)}, u32[]{:S(2)}) %collective-permute-start.19) | collective-permute-done | bytes 61472 | tf_op jit(solution)/shard_map/ppermute | solution.py:290
  34.3 1.4 %shard_map.78 = (bf16[320,768]{1,0:T(8,128)(2,1)S(1)}, f32[320,128]{1,0:T(8,128)S(1)}) custom-call(bf16[80,768]{1,0:T(8,128)(2,1)S(1)} %collective-permute-done.15.refs_0_, bf16[40,768]{1,0:T(8,128)(2,1)S(1)} %collective-permute-done.16.refs_1_, bf16[40,768]{1,0:T(8,128)(2,1)S(1)} %collective-permute-done.17.refs_2_, ...), custom_call_target="tpu_custom_call" | custom-call | flops 1000000 | bytes 1000 | tf_op jit(solution)/shard_map/pallas_call | solution.py:263
  35.6 2.4 %shard_map.79 = bf16[144,768]{1,0:T(8,128)(2,1)} custom-call(s32[1]{0:T(128)} %bitcast.z_ref, bf16[40,768]{1,0:T(8,128)(2,1)S(1)} %collective-permute-done.14.last_ref, bf16[40,768]{1,0:T(8,128)(2,1)S(1)} %get-tuple-element.44.refs_0_, bf16[40,768]{1,0:T(8,128)(2,1)S(1)} %collective-permute-done.10.refs_1_, ...), custom_call_target="tpu_custom_call" | custom-call | flops 1000000 | bytes 1000 | tf_op jit(solution)/shard_map/pallas_call | solution.py:263
  (32 shorter events, 0.2 us)
Async XLA Ops:
  0.0 0.9 %copy-start.4 = (bf16[1,6,24,768]{3,2,1,0:T(8,128)(2,1)S(1)}, bf16[1,6,24,768]{3,2,1,0:T(8,128)(2,1)}, u32[]{:S(2)}) copy-start(bf16[1,6,24,768]{3,2,1,0:T(8,128)(2,1)} %param.7) | copy-start | bytes 663556
  0.9 8.4 %copy-start.5 = (bf16[256,3072]{1,0:T(8,128)(2,1)S(1)}, bf16[256,3072]{1,0:T(8,128)(2,1)}, u32[]{:S(2)}) copy-start(bf16[256,3072]{1,0:T(8,128)(2,1)} %param.9) | copy-start | bytes 4718596
  0.9 13.5 %copy-start.1 = (bf16[768,2304]{1,0:T(8,128)(2,1)S(1)}, bf16[768,2304]{1,0:T(8,128)(2,1)}, u32[]{:S(2)}) copy-start(bf16[768,2304]{1,0:T(8,128)(2,1)} %refs_5_.4) | copy-start | bytes 10616836
  1.2 8.5 %collective-permute-start.1 = (bf16[40,768]{1,0:T(8,128)(2,1)S(1)}, bf16[40,768]{1,0:T(8,128)(2,1)S(1)}, u32[]{:S(2)}, u32[]{:S(2)}) collective-permute-start(bf16[40,768]{1,0:T(8,128)(2,1)S(1)} %get-tuple-element.34), channel_id=1, source_target_pairs={{0,8},{4,12},{8,0},{12,4},{16,24},{20,28},{24,16},{28,20},{1,9},{5... | collective-permute-start | bytes 184328 | tf_op jit(solution)/shard_map/ppermute | solution.py:284
  4.3 6.4 %collective-permute-start.3 = (bf16[40,768]{1,0:T(8,128)(2,1)S(1)}, bf16[40,768]{1,0:T(8,128)(2,1)S(1)}, u32[]{:S(2)}, u32[]{:S(2)}) collective-permute-start(bf16[40,768]{1,0:T(8,128)(2,1)S(1)} %get-tuple-element.36), channel_id=1, source_target_pairs={{0,16},{4,20},{8,24},{12,28},{16,0},{20,4},{24,8},{28,12},{1,17},{... | collective-permute-start | bytes 184328 | tf_op jit(solution)/shard_map/ppermute | solution.py:284
  6.9 6.0 %collective-permute-start.5 = (bf16[40,768]{1,0:T(8,128)(2,1)S(1)}, bf16[40,768]{1,0:T(8,128)(2,1)S(1)}, u32[]{:S(2)}, u32[]{:S(2)}) collective-permute-start(bf16[40,768]{1,0:T(8,128)(2,1)S(1)} %get-tuple-element.37), channel_id=1, source_target_pairs={{0,24},{4,28},{8,16},{12,20},{16,8},{20,12},{24,0},{28,4},{1,25},{... | collective-permute-start | bytes 184328 | tf_op jit(solution)/shard_map/ppermute | solution.py:284
  6.9 8.6 %collective-permute-start = (bf16[40,768]{1,0:T(8,128)(2,1)S(1)}, bf16[40,768]{1,0:T(8,128)(2,1)S(1)}, u32[]{:S(2)}, u32[]{:S(2)}) collective-permute-start(bf16[40,768]{1,0:T(8,128)(2,1)S(1)} %get-tuple-element.33.refs_0_), channel_id=1, source_target_pairs={{0,4},{4,0},{8,12},{12,8},{16,20},{20,16},{24,28},{28,24},{1,5},{5... | collective-permute-start | bytes 184328 | tf_op jit(solution)/shard_map/ppermute | solution.py:287
  9.7 7.5 %copy-start.2 = (bf16[768,768]{1,0:T(8,128)(2,1)S(1)}, bf16[768,768]{1,0:T(8,128)(2,1)}, u32[]{:S(2)}) copy-start(bf16[768,768]{1,0:T(8,128)(2,1)} %refs_6_.2) | copy-start | bytes 3538948
  9.7 5.8 %collective-permute-start.2 = (bf16[40,768]{1,0:T(8,128)(2,1)S(1)}, bf16[40,768]{1,0:T(8,128)(2,1)S(1)}, u32[]{:S(2)}, u32[]{:S(2)}) collective-permute-start(bf16[40,768]{1,0:T(8,128)(2,1)S(1)} %collective-permute-done.1.refs_1_), channel_id=1, source_target_pairs={{0,4},{4,0},{8,12},{12,8},{16,20},{20,16},{24,28},{28,24},{1,5},{5... | collective-permute-start | bytes 184328 | tf_op jit(solution)/shard_map/ppermute | solution.py:287
  10.7 4.8 %collective-permute-start.4 = (bf16[40,768]{1,0:T(8,128)(2,1)S(1)}, bf16[40,768]{1,0:T(8,128)(2,1)S(1)}, u32[]{:S(2)}, u32[]{:S(2)}) collective-permute-start(bf16[40,768]{1,0:T(8,128)(2,1)S(1)} %collective-permute-done.3.refs_2_), channel_id=1, source_target_pairs={{0,4},{4,0},{8,12},{12,8},{16,20},{20,16},{24,28},{28,24},{1,5},{5... | collective-permute-start | bytes 184328 | tf_op jit(solution)/shard_map/ppermute | solution.py:287
  12.9 4.2 %collective-permute-start.6 = (bf16[40,768]{1,0:T(8,128)(2,1)S(1)}, bf16[40,768]{1,0:T(8,128)(2,1)S(1)}, u32[]{:S(2)}, u32[]{:S(2)}) collective-permute-start(bf16[40,768]{1,0:T(8,128)(2,1)S(1)} %collective-permute-done.5.refs_3_), channel_id=1, source_target_pairs={{0,4},{4,0},{8,12},{12,8},{16,20},{20,16},{24,28},{28,24},{1,5},{5... | collective-permute-start | bytes 184328 | tf_op jit(solution)/shard_map/ppermute | solution.py:287
  17.1 10.0 %copy-start = (bf16[768,2304]{1,0:T(8,128)(2,1)S(1)}, bf16[768,2304]{1,0:T(8,128)(2,1)}, u32[]{:S(2)}) copy-start(bf16[768,2304]{1,0:T(8,128)(2,1)} %refs_6_.3) | copy-start | bytes 10616836
  19.1 6.0 %collective-permute-start.10 = (bf16[40,768]{1,0:T(8,128)(2,1)S(1)}, bf16[40,768]{1,0:T(8,128)(2,1)S(1)}, u32[]{:S(2)}, u32[]{:S(2)}) collective-permute-start(bf16[40,768]{1,0:T(8,128)(2,1)S(1)} %get-tuple-element.45), channel_id=1, source_target_pairs={{0,8},{4,12},{8,0},{12,4},{16,24},{20,28},{24,16},{28,20},{1,9},{5... | collective-permute-start | bytes 184328 | tf_op jit(solution)/shard_map/ppermute | solution.py:284
  19.4 6.2 %collective-permute-start.12 = (bf16[40,768]{1,0:T(8,128)(2,1)S(1)}, bf16[40,768]{1,0:T(8,128)(2,1)S(1)}, u32[]{:S(2)}, u32[]{:S(2)}) collective-permute-start(bf16[40,768]{1,0:T(8,128)(2,1)S(1)} %get-tuple-element.46), channel_id=1, source_target_pairs={{0,16},{4,20},{8,24},{12,28},{16,0},{20,4},{24,8},{28,12},{1,17},{... | collective-permute-start | bytes 184328 | tf_op jit(solution)/shard_map/ppermute | solution.py:284
  22.8 6.0 %collective-permute-start.7 = (bf16[40,768]{1,0:T(8,128)(2,1)S(1)}, bf16[40,768]{1,0:T(8,128)(2,1)S(1)}, u32[]{:S(2)}, u32[]{:S(2)}) collective-permute-start(bf16[40,768]{1,0:T(8,128)(2,1)S(1)} %get-tuple-element.43), channel_id=1, source_target_pairs={{0,24},{4,28},{8,16},{12,20},{16,8},{20,12},{24,0},{28,4},{1,25},{... | collective-permute-start | bytes 184328 | tf_op jit(solution)/shard_map/ppermute | solution.py:284
  23.6 6.7 %collective-permute-start.9 = (bf16[40,768]{1,0:T(8,128)(2,1)S(1)}, bf16[40,768]{1,0:T(8,128)(2,1)S(1)}, u32[]{:S(2)}, u32[]{:S(2)}) collective-permute-start(bf16[40,768]{1,0:T(8,128)(2,1)S(1)} %get-tuple-element.44.refs_0_), channel_id=1, source_target_pairs={{0,2},{1,3},{2,0},{3,1},{4,6},{5,7},{6,4},{7,5},{8,10},{9,11},{10,... | collective-permute-start | bytes 184328 | tf_op jit(solution)/shard_map/ppermute | solution.py:290
  25.1 5.2 %collective-permute-start.11 = (bf16[40,768]{1,0:T(8,128)(2,1)S(1)}, bf16[40,768]{1,0:T(8,128)(2,1)S(1)}, u32[]{:S(2)}, u32[]{:S(2)}) collective-permute-start(bf16[40,768]{1,0:T(8,128)(2,1)S(1)} %collective-permute-done.10.refs_1_), channel_id=1, source_target_pairs={{0,2},{1,3},{2,0},{3,1},{4,6},{5,7},{6,4},{7,5},{8,10},{9,11},{10,... | collective-permute-start | bytes 184328 | tf_op jit(solution)/shard_map/ppermute | solution.py:290
  25.6 4.7 %collective-permute-start.13 = (bf16[40,768]{1,0:T(8,128)(2,1)S(1)}, bf16[40,768]{1,0:T(8,128)(2,1)S(1)}, u32[]{:S(2)}, u32[]{:S(2)}) collective-permute-start(bf16[40,768]{1,0:T(8,128)(2,1)S(1)} %collective-permute-done.12.refs_2_), channel_id=1, source_target_pairs={{0,2},{1,3},{2,0},{3,1},{4,6},{5,7},{6,4},{7,5},{8,10},{9,11},{10,... | collective-permute-start | bytes 184328 | tf_op jit(solution)/shard_map/ppermute | solution.py:290
  28.2 6.1 %collective-permute-start.15 = (bf16[80,768]{1,0:T(8,128)(2,1)S(1)}, bf16[80,768]{1,0:T(8,128)(2,1)S(1)}, u32[]{:S(2)}, u32[]{:S(2)}) collective-permute-start(bf16[80,768]{1,0:T(8,128)(2,1)S(1)} %get-tuple-element.55), channel_id=1, source_target_pairs={{0,1},{1,0},{2,3},{3,2},{4,5},{5,4},{6,7},{7,6},{8,9},{9,8},{10,11... | collective-permute-start | bytes 368648 | tf_op jit(solution)/shard_map/ppermute | solution.py:290
  28.8 4.2 %collective-permute-start.8 = (bf16[40,768]{1,0:T(8,128)(2,1)S(1)}, bf16[40,768]{1,0:T(8,128)(2,1)S(1)}, u32[]{:S(2)}, u32[]{:S(2)}) collective-permute-start(bf16[40,768]{1,0:T(8,128)(2,1)S(1)} %collective-permute-done.7.own_ref.refs_3_), channel_id=1, source_target_pairs={{0,2},{1,3},{2,0},{3,1},{4,6},{5,7},{6,4},{7,5},{8,10},{9,11},{10,... | collective-permute-start | bytes 184328 | tf_op jit(solution)/shard_map/ppermute | solution.py:290
  31.5 2.7 %collective-permute-start.18 = (bf16[80,768]{1,0:T(8,128)(2,1)S(1)}, bf16[80,768]{1,0:T(8,128)(2,1)S(1)}, u32[]{:S(2)}, u32[]{:S(2)}) collective-permute-start(bf16[80,768]{1,0:T(8,128)(2,1)S(1)} %get-tuple-element.57), channel_id=1, source_target_pairs={{0,1},{1,0},{2,3},{3,2},{4,5},{5,4},{6,7},{7,6},{8,9},{9,8},{10,11... | collective-permute-start | bytes 368648 | tf_op jit(solution)/shard_map/ppermute | solution.py:290
  31.6 1.4 %collective-permute-start.16 = (bf16[40,768]{1,0:T(8,128)(2,1)S(1)}, bf16[40,768]{1,0:T(8,128)(2,1)S(1)}, u32[]{:S(2)}, u32[]{:S(2)}) collective-permute-start(bf16[40,768]{1,0:T(8,128)(2,1)S(1)} %get-tuple-element.56), channel_id=1, source_target_pairs={{0,1},{1,0},{2,3},{3,2},{4,5},{5,4},{6,7},{7,6},{8,9},{9,8},{10,11... | collective-permute-start | bytes 184328 | tf_op jit(solution)/shard_map/ppermute | solution.py:290
  32.1 1.4 %collective-permute-start.17 = (bf16[40,768]{1,0:T(8,128)(2,1)S(1)}, bf16[40,768]{1,0:T(8,128)(2,1)S(1)}, u32[]{:S(2)}, u32[]{:S(2)}) collective-permute-start(bf16[40,768]{1,0:T(8,128)(2,1)S(1)} %collective-permute-done.7.own_ref.refs_3_), channel_id=1, source_target_pairs={{0,1},{1,0},{2,3},{3,2},{4,5},{5,4},{6,7},{7,6},{8,9},{9,8},{10,11... | collective-permute-start | bytes 184328 | tf_op jit(solution)/shard_map/ppermute | solution.py:290
  33.0 1.2 %collective-permute-start.19 = (bf16[40,768]{1,0:T(8,128)(2,1)S(1)}, bf16[40,768]{1,0:T(8,128)(2,1)S(1)}, u32[]{:S(2)}, u32[]{:S(2)}) collective-permute-start(bf16[40,768]{1,0:T(8,128)(2,1)S(1)} %get-tuple-element.58), channel_id=1, source_target_pairs={{0,1},{1,0},{2,3},{3,2},{4,5},{5,4},{6,7},{7,6},{8,9},{9,8},{10,11... | collective-permute-start | bytes 184328 | tf_op jit(solution)/shard_map/ppermute | solution.py:290
  33.0 2.6 %collective-permute-start.14 = (bf16[40,768]{1,0:T(8,128)(2,1)S(1)}, bf16[40,768]{1,0:T(8,128)(2,1)S(1)}, u32[]{:S(2)}, u32[]{:S(2)}) collective-permute-start(bf16[40,768]{1,0:T(8,128)(2,1)S(1)} %collective-permute-done.8.refs_5_), channel_id=1, source_target_pairs={{0,1},{1,0},{2,3},{3,2},{4,5},{5,4},{6,7},{7,6},{8,9},{9,8},{10,11... | collective-permute-start | bytes 184328 | tf_op jit(solution)/shard_map/ppermute | solution.py:290
  34.3 1.4 %copy-start.3 = (bf16[768,768]{1,0:T(8,128)(2,1)S(1)}, bf16[768,768]{1,0:T(8,128)(2,1)}, u32[]{:S(2)}) copy-start(bf16[768,768]{1,0:T(8,128)(2,1)} %refs_7_.1) | copy-start | bytes 3538948

commit v7 on v6

--- a/solution.py
+++ b/solution.py
@@ -317,7 +317,7 @@
     parts = [((padded // 2, D), BF), ((early - padded // 2, D), BF)]
     q, v1, s1, *h_parts = call(
         functools.partial(bin_own_kernel, groups - 1),
-        [((early, D), BF), *rows_of(early), *parts], [], *h[:-1], mod, bin_qkv,
+        [((early, D), BF), *rows_of(early), ((early, D), BF)], [], *h[:-1], mod, bin_qkv,
     )
     hc = [over_bin(x, 1) for x in (*h_parts, h[-1])]
     q2, v2, s2, *hy_parts = call(

time: 38.1 us -> 37.2 us (0.976)
  starting transfers between devices: 21.5 us -> 21 us
  waiting for transfers between devices: 5.1 us -> 4.69 us
    ppermute x10 -> x9, starting transfers between devices: 6.29 us -> 5.79 us  [over_bin(): return lax.ppermute(x, 'bin', [(i, i ^ m) for i in range(4)])]
    ppermute x10 -> x9, waiting for transfers between devices: 1.59 us -> 1.18 us  [over_bin(): return lax.ppermute(x, 'bin', [(i, i ^ m) for i in range(4)])]
  transfers between devices with their start and end apart: 20 -> 19, of which waited for: 6 -> 6; matrix products, arithmetic and copies ran while one was open for 1% -> 1% of each run, Pallas kernels for 12% -> 13%
where the time goes in v7:
time: 37.2 us; the launch traced here: 37.1 us
  starting transfers between devices  21 us (56%)
  Pallas kernels  9.24 us (25%)
  waiting for transfers between devices  4.69 us (13%)
  local copies, waits for them, and re-layouts  0.97 us (3%)
  between operations  0.81 us (2%)
    ppermute x6, starting transfers between devices, over_group(): return lax.ppermute(x, 'seq', [(i, i ^ 2 * m) for i in range(owners)])  10.1 us
    pallas_call x7, Pallas kernels, call(): pl.pallas_call(kernel, out_shape=[jax.ShapeDtypeStruct(*o) for o in outs]...  9.24 us
    ppermute x9, starting transfers between devices, over_bin(): return lax.ppermute(x, 'bin', [(i, i ^ m) for i in range(4)])  5.79 us
    ppermute x4, starting transfers between devices, over_pair(): return lax.ppermute(x, 'seq', [(i, i ^ 1) for i in range(owners)])  5.07 us
    ppermute x6, waiting for transfers between devices, over_group(): return lax.ppermute(x, 'seq', [(i, i ^ 2 * m) for i in range(owners)])  1.88 us
    ppermute x4, waiting for transfers between devices, over_pair(): return lax.ppermute(x, 'seq', [(i, i ^ 1) for i in range(owners)])  1.63 us
    ppermute x9, waiting for transfers between devices, over_bin(): return lax.ppermute(x, 'bin', [(i, i ^ m) for i in range(4)])  1.18 us
    unnamed x12, local copies, waits for them, and re-layouts  0.95 us
  transfers between devices with their start and end apart: 19, of which 6 were waited for; matrix products, arithmetic and copies ran while one was open for 1% of the time, Pallas kernels for 13%

profile of v7, /device:TPU:0, one launch (start us, length us, event | category | flops | bytes accessed | tf_op | source)
XLA Modules:
  0.0 37.1 jit_solution(17204032382430797584)
XLA Ops:
  0.0 0.9 %copy-done.4 = bf16[1,6,24,768]{3,2,1,0:T(8,128)(2,1)S(1)} copy-done((bf16[1,6,24,768]{3,2,1,0:T(8,128)(2,1)S(1)}, bf16[1,6,24,768]{3,2,1,0:T(8,128)(2,1)}, u32[]{:S(2)}) %copy-start.4) | copy-done | bytes 221208
  0.9 0.3 shard_map.73
  1.2 3.1 %collective-permute-start.1 = (bf16[40,768]{1,0:T(8,128)(2,1)S(1)}, bf16[40,768]{1,0:T(8,128)(2,1)S(1)}, u32[]{:S(2)}, u32[]{:S(2)}) collective-permute-start(bf16[40,768]{1,0:T(8,128)(2,1)S(1)} %get-tuple-element.33), channel_id=1, source_target_pairs={{0,8},{4,12},{8,0},{12,4},{16,24},{20,28},{24,16},{28,20},{1,9},{5... | collective-permute-start | bytes 184328 | tf_op jit(solution)/shard_map/ppermute | solution.py:284
  4.3 2.6 %collective-permute-start.3 = (bf16[40,768]{1,0:T(8,128)(2,1)S(1)}, bf16[40,768]{1,0:T(8,128)(2,1)S(1)}, u32[]{:S(2)}, u32[]{:S(2)}) collective-permute-start(bf16[40,768]{1,0:T(8,128)(2,1)S(1)} %get-tuple-element.35), channel_id=1, source_target_pairs={{0,16},{4,20},{8,24},{12,28},{16,0},{20,4},{24,8},{28,12},{1,17},{... | collective-permute-start | bytes 184328 | tf_op jit(solution)/shard_map/ppermute | solution.py:284
  6.9 1.7 %collective-permute-start = (bf16[40,768]{1,0:T(8,128)(2,1)S(1)}, bf16[40,768]{1,0:T(8,128)(2,1)S(1)}, u32[]{:S(2)}, u32[]{:S(2)}) collective-permute-start(bf16[40,768]{1,0:T(8,128)(2,1)S(1)} %get-tuple-element.32.refs_0_), channel_id=1, source_target_pairs={{0,4},{4,0},{8,12},{12,8},{16,20},{20,16},{24,28},{28,24},{1,5},{5... | collective-permute-start | bytes 184328 | tf_op jit(solution)/shard_map/ppermute | solution.py:287
  9.4 0.3 fusion
  9.7 0.4 %collective-permute-start.2 = (bf16[40,768]{1,0:T(8,128)(2,1)S(1)}, bf16[40,768]{1,0:T(8,128)(2,1)S(1)}, u32[]{:S(2)}, u32[]{:S(2)}) collective-permute-start(bf16[40,768]{1,0:T(8,128)(2,1)S(1)} %collective-permute-done.1.refs_1_), channel_id=1, source_target_pairs={{0,4},{4,0},{8,12},{12,8},{16,20},{20,16},{24,28},{28,24},{1,5},{5... | collective-permute-start | bytes 184328 | tf_op jit(solution)/shard_map/ppermute | solution.py:287
  10.1 0.6 %collective-permute-done.3.refs_2_ = bf16[40,768]{1,0:T(8,128)(2,1)S(1)} collective-permute-done((bf16[40,768]{1,0:T(8,128)(2,1)S(1)}, bf16[40,768]{1,0:T(8,128)(2,1)S(1)}, u32[]{:S(2)}, u32[]{:S(2)}) %collective-permute-start.3) | collective-permute-done | bytes 61472 | tf_op jit(solution)/shard_map/ppermute | solution.py:284
  10.7 1.5 %collective-permute-start.4 = (bf16[40,768]{1,0:T(8,128)(2,1)S(1)}, bf16[40,768]{1,0:T(8,128)(2,1)S(1)}, u32[]{:S(2)}, u32[]{:S(2)}) collective-permute-start(bf16[40,768]{1,0:T(8,128)(2,1)S(1)} %collective-permute-done.3.refs_2_), channel_id=1, source_target_pairs={{0,4},{4,0},{8,12},{12,8},{16,20},{20,16},{24,28},{28,24},{1,5},{5... | collective-permute-start | bytes 184328 | tf_op jit(solution)/shard_map/ppermute | solution.py:287
  12.1 0.8 %collective-permute-done.5.refs_3_ = bf16[40,768]{1,0:T(8,128)(2,1)S(1)} collective-permute-done((bf16[40,768]{1,0:T(8,128)(2,1)S(1)}, bf16[40,768]{1,0:T(8,128)(2,1)S(1)}, u32[]{:S(2)}, u32[]{:S(2)}) %collective-permute-start.5) | collective-permute-done | bytes 61472 | tf_op jit(solution)/shard_map/ppermute | solution.py:284
  12.9 1.5 %collective-permute-start.6 = (bf16[40,768]{1,0:T(8,128)(2,1)S(1)}, bf16[40,768]{1,0:T(8,128)(2,1)S(1)}, u32[]{:S(2)}, u32[]{:S(2)}) collective-permute-start(bf16[40,768]{1,0:T(8,128)(2,1)S(1)} %collective-permute-done.5.refs_3_), channel_id=1, source_target_pairs={{0,4},{4,0},{8,12},{12,8},{16,20},{20,16},{24,28},{28,24},{1,5},{5... | collective-permute-start | bytes 184328 | tf_op jit(solution)/shard_map/ppermute | solution.py:287
  14.4 1.1 %shard_map.74 = (bf16[144,768]{1,0:T(8,128)(2,1)S(1)}, bf16[144,768]{1,0:T(8,128)(2,1)S(1)}, bf16[144,768]{1,0:T(8,128)(2,1)S(1)}, bf16[144,768]{1,0:T(8,128)(2,1)S(1)}) custom-call(bf16[40,768]{1,0:T(8,128)(2,1)S(1)} %get-tuple-element.32.refs_0_, bf16[40,768]{1,0:T(8,128)(2,1)S(1)} %collective-permute-done.1.refs_1_, ...), custom_call_target="tpu_custom_call" | custom-call | flops 1000000 | bytes 1000 | tf_op jit(solution)/shard_map/pallas_call | solution.py:263
  15.5 1.6 %collective-permute-done.6.refs_3_ = bf16[40,768]{1,0:T(8,128)(2,1)S(1)} collective-permute-done((bf16[40,768]{1,0:T(8,128)(2,1)S(1)}, bf16[40,768]{1,0:T(8,128)(2,1)S(1)}, u32[]{:S(2)}, u32[]{:S(2)}) %collective-permute-start.6) | collective-permute-done | bytes 61472 | tf_op jit(solution)/shard_map/ppermute | solution.py:287
  17.1 2.0 %shard_map.75 = (bf16[40,768]{1,0:T(8,128)(2,1)S(1)}, bf16[40,768]{1,0:T(8,128)(2,1)S(1)}, bf16[40,768]{1,0:T(8,128)(2,1)S(1)}, bf16[40,768]{1,0:T(8,128)(2,1)S(1)}) custom-call(bf16[40,768]{1,0:T(8,128)(2,1)S(1)} %collective-permute-done.refs_0_, bf16[40,768]{1,0:T(8,128)(2,1)S(1)} %collective-permute-done.2.refs_1_, ...), custom_call_target="tpu_custom_call" | custom-call | flops 1000000 | bytes 1000 | tf_op jit(solution)/shard_map/pallas_call | solution.py:263
  19.1 0.3 collective-permute-start.10
  19.4 3.4 %collective-permute-start.12 = (bf16[40,768]{1,0:T(8,128)(2,1)S(1)}, bf16[40,768]{1,0:T(8,128)(2,1)S(1)}, u32[]{:S(2)}, u32[]{:S(2)}) collective-permute-start(bf16[40,768]{1,0:T(8,128)(2,1)S(1)} %get-tuple-element.45), channel_id=1, source_target_pairs={{0,16},{4,20},{8,24},{12,28},{16,0},{20,4},{24,8},{28,12},{1,17},{... | collective-permute-start | bytes 184328 | tf_op jit(solution)/shard_map/ppermute | solution.py:284
  22.8 0.8 %collective-permute-start.7 = (bf16[40,768]{1,0:T(8,128)(2,1)S(1)}, bf16[40,768]{1,0:T(8,128)(2,1)S(1)}, u32[]{:S(2)}, u32[]{:S(2)}) collective-permute-start(bf16[40,768]{1,0:T(8,128)(2,1)S(1)} %get-tuple-element.42), channel_id=1, source_target_pairs={{0,24},{4,28},{8,16},{12,20},{16,8},{20,12},{24,0},{28,4},{1,25},{... | collective-permute-start | bytes 184328 | tf_op jit(solution)/shard_map/ppermute | solution.py:284
  23.6 1.5 %collective-permute-start.9 = (bf16[40,768]{1,0:T(8,128)(2,1)S(1)}, bf16[40,768]{1,0:T(8,128)(2,1)S(1)}, u32[]{:S(2)}, u32[]{:S(2)}) collective-permute-start(bf16[40,768]{1,0:T(8,128)(2,1)S(1)} %get-tuple-element.43.refs_0_), channel_id=1, source_target_pairs={{0,2},{1,3},{2,0},{3,1},{4,6},{5,7},{6,4},{7,5},{8,10},{9,11},{10,... | collective-permute-start | bytes 184328 | tf_op jit(solution)/shard_map/ppermute | solution.py:290
  25.1 0.5 %collective-permute-start.11 = (bf16[40,768]{1,0:T(8,128)(2,1)S(1)}, bf16[40,768]{1,0:T(8,128)(2,1)S(1)}, u32[]{:S(2)}, u32[]{:S(2)}) collective-permute-start(bf16[40,768]{1,0:T(8,128)(2,1)S(1)} %collective-permute-done.10.refs_1_), channel_id=1, source_target_pairs={{0,2},{1,3},{2,0},{3,1},{4,6},{5,7},{6,4},{7,5},{8,10},{9,11},{10,... | collective-permute-start | bytes 184328 | tf_op jit(solution)/shard_map/ppermute | solution.py:290
  25.6 1.5 %collective-permute-start.13 = (bf16[40,768]{1,0:T(8,128)(2,1)S(1)}, bf16[40,768]{1,0:T(8,128)(2,1)S(1)}, u32[]{:S(2)}, u32[]{:S(2)}) collective-permute-start(bf16[40,768]{1,0:T(8,128)(2,1)S(1)} %collective-permute-done.12.refs_2_), channel_id=1, source_target_pairs={{0,2},{1,3},{2,0},{3,1},{4,6},{5,7},{6,4},{7,5},{8,10},{9,11},{10,... | collective-permute-start | bytes 184328 | tf_op jit(solution)/shard_map/ppermute | solution.py:290
  27.1 1.0 %shard_map.76 = (bf16[120,768]{1,0:T(8,128)(2,1)S(1)}, bf16[120,768]{1,0:T(8,128)(2,1)S(1)}, f32[120,128]{1,0:T(8,128)S(1)}, bf16[120,768]{1,0:T(8,128)(2,1)S(1)}) custom-call(bf16[40,768]{1,0:T(8,128)(2,1)S(1)} %get-tuple-element.43.refs_0_, bf16[40,768]{1,0:T(8,128)(2,1)S(1)} %collective-permute-done.10.refs_1_, ...), custom_call_target="tpu_custom_call" | custom-call | flops 1000000 | bytes 1000 | tf_op jit(solution)/shard_map/pallas_call | solution.py:263
  28.2 0.1 collective-permute-start.15
  28.3 0.5 %collective-permute-done.7.own_ref.refs_3_ = bf16[40,768]{1,0:T(8,128)(2,1)S(1)} collective-permute-done((bf16[40,768]{1,0:T(8,128)(2,1)S(1)}, bf16[40,768]{1,0:T(8,128)(2,1)S(1)}, u32[]{:S(2)}, u32[]{:S(2)}) %collective-permute-start.7) | collective-permute-done | bytes 61472 | tf_op jit(solution)/shard_map/ppermute | solution.py:284
  28.8 1.5 %collective-permute-start.8 = (bf16[40,768]{1,0:T(8,128)(2,1)S(1)}, bf16[40,768]{1,0:T(8,128)(2,1)S(1)}, u32[]{:S(2)}, u32[]{:S(2)}) collective-permute-start(bf16[40,768]{1,0:T(8,128)(2,1)S(1)} %collective-permute-done.7.own_ref.refs_3_), channel_id=1, source_target_pairs={{0,2},{1,3},{2,0},{3,1},{4,6},{5,7},{6,4},{7,5},{8,10},{9,11},{10,... | collective-permute-start | bytes 184328 | tf_op jit(solution)/shard_map/ppermute | solution.py:290
  30.3 1.2 %shard_map.77 = (bf16[40,768]{1,0:T(8,128)(2,1)S(1)}, bf16[160,768]{1,0:T(8,128)(2,1)S(1)}, f32[160,128]{1,0:T(8,128)S(1)}, bf16[80,768]{1,0:T(8,128)(2,1)S(1)}, bf16[40,768]{1,0:T(8,128)(2,1)S(1)}) custom-call(bf16[40,768]{1,0:T(8,128)(2,1)S(1)} %collective-permute-done.7.own_ref.refs_3_, bf16[40,768]{1,0:T(8,128)(2,1)S(1)} %collective-permute-done.9.refs_0_, ...), custom_call_target="tpu_custom_call" | custom-call | flops 1000000 | bytes 1000 | tf_op jit(solution)/shard_map/pallas_call | solution.py:263
  31.5 0.1 collective-permute-start.17
  31.6 0.5 %collective-permute-start.16 = (bf16[40,768]{1,0:T(8,128)(2,1)S(1)}, bf16[40,768]{1,0:T(8,128)(2,1)S(1)}, u32[]{:S(2)}, u32[]{:S(2)}) collective-permute-start(bf16[40,768]{1,0:T(8,128)(2,1)S(1)} %collective-permute-done.7.own_ref.refs_3_), channel_id=1, source_target_pairs={{0,1},{1,0},{2,3},{3,2},{4,5},{5,4},{6,7},{7,6},{8,9},{9,8},{10,11... | collective-permute-start | bytes 184328 | tf_op jit(solution)/shard_map/ppermute | solution.py:290
  32.1 0.1 collective-permute-start.18
  32.2 0.8 %collective-permute-done.8.refs_4_ = bf16[40,768]{1,0:T(8,128)(2,1)S(1)} collective-permute-done((bf16[40,768]{1,0:T(8,128)(2,1)S(1)}, bf16[40,768]{1,0:T(8,128)(2,1)S(1)}, u32[]{:S(2)}, u32[]{:S(2)}) %collective-permute-start.8) | collective-permute-done | bytes 61472 | tf_op jit(solution)/shard_map/ppermute | solution.py:290
  33.0 0.3 collective-permute-done.18.refs_3_
  33.4 1.4 %shard_map.78 = (bf16[320,768]{1,0:T(8,128)(2,1)S(1)}, f32[320,128]{1,0:T(8,128)S(1)}) custom-call(bf16[120,768]{1,0:T(8,128)(2,1)S(1)} %collective-permute-done.15.refs_0_, bf16[40,768]{1,0:T(8,128)(2,1)S(1)} %collective-permute-done.16.refs_1_, bf16[80,768]{1,0:T(8,128)(2,1)S(1)} %collective-permute-done.17.refs_2_, ...), custom_call_target="tpu_custom_call" | custom-call | flops 1000000 | bytes 1000 | tf_op jit(solution)/shard_map/pallas_call | solution.py:263
  34.7 2.3 %shard_map.79 = bf16[144,768]{1,0:T(8,128)(2,1)} custom-call(s32[1]{0:T(128)} %bitcast.z_ref, bf16[40,768]{1,0:T(8,128)(2,1)S(1)} %collective-permute-done.14.last_ref, bf16[40,768]{1,0:T(8,128)(2,1)S(1)} %get-tuple-element.43.refs_0_, bf16[40,768]{1,0:T(8,128)(2,1)S(1)} %collective-permute-done.10.refs_1_, ...), custom_call_target="tpu_custom_call" | custom-call | flops 1000000 | bytes 1000 | tf_op jit(solution)/shard_map/pallas_call | solution.py:263
  (30 shorter events, 0.1 us)
Async XLA Ops:
  0.0 0.9 %copy-start.4 = (bf16[1,6,24,768]{3,2,1,0:T(8,128)(2,1)S(1)}, bf16[1,6,24,768]{3,2,1,0:T(8,128)(2,1)}, u32[]{:S(2)}) copy-start(bf16[1,6,24,768]{3,2,1,0:T(8,128)(2,1)} %param.7) | copy-start | bytes 663556
  0.9 8.4 %copy-start.5 = (bf16[256,3072]{1,0:T(8,128)(2,1)S(1)}, bf16[256,3072]{1,0:T(8,128)(2,1)}, u32[]{:S(2)}) copy-start(bf16[256,3072]{1,0:T(8,128)(2,1)} %param.9) | copy-start | bytes 4718596
  0.9 13.5 %copy-start.1 = (bf16[768,2304]{1,0:T(8,128)(2,1)S(1)}, bf16[768,2304]{1,0:T(8,128)(2,1)}, u32[]{:S(2)}) copy-start(bf16[768,2304]{1,0:T(8,128)(2,1)} %refs_5_.4) | copy-start | bytes 10616836
  1.2 8.5 %collective-permute-start.1 = (bf16[40,768]{1,0:T(8,128)(2,1)S(1)}, bf16[40,768]{1,0:T(8,128)(2,1)S(1)}, u32[]{:S(2)}, u32[]{:S(2)}) collective-permute-start(bf16[40,768]{1,0:T(8,128)(2,1)S(1)} %get-tuple-element.33), channel_id=1, source_target_pairs={{0,8},{4,12},{8,0},{12,4},{16,24},{20,28},{24,16},{28,20},{1,9},{5... | collective-permute-start | bytes 184328 | tf_op jit(solution)/shard_map/ppermute | solution.py:284
  4.3 6.4 %collective-permute-start.3 = (bf16[40,768]{1,0:T(8,128)(2,1)S(1)}, bf16[40,768]{1,0:T(8,128)(2,1)S(1)}, u32[]{:S(2)}, u32[]{:S(2)}) collective-permute-start(bf16[40,768]{1,0:T(8,128)(2,1)S(1)} %get-tuple-element.35), channel_id=1, source_target_pairs={{0,16},{4,20},{8,24},{12,28},{16,0},{20,4},{24,8},{28,12},{1,17},{... | collective-permute-start | bytes 184328 | tf_op jit(solution)/shard_map/ppermute | solution.py:284
  6.9 6.0 %collective-permute-start.5 = (bf16[40,768]{1,0:T(8,128)(2,1)S(1)}, bf16[40,768]{1,0:T(8,128)(2,1)S(1)}, u32[]{:S(2)}, u32[]{:S(2)}) collective-permute-start(bf16[40,768]{1,0:T(8,128)(2,1)S(1)} %get-tuple-element.36), channel_id=1, source_target_pairs={{0,24},{4,28},{8,16},{12,20},{16,8},{20,12},{24,0},{28,4},{1,25},{... | collective-permute-start | bytes 184328 | tf_op jit(solution)/shard_map/ppermute | solution.py:284
  6.9 8.6 %collective-permute-start = (bf16[40,768]{1,0:T(8,128)(2,1)S(1)}, bf16[40,768]{1,0:T(8,128)(2,1)S(1)}, u32[]{:S(2)}, u32[]{:S(2)}) collective-permute-start(bf16[40,768]{1,0:T(8,128)(2,1)S(1)} %get-tuple-element.32.refs_0_), channel_id=1, source_target_pairs={{0,4},{4,0},{8,12},{12,8},{16,20},{20,16},{24,28},{28,24},{1,5},{5... | collective-permute-start | bytes 184328 | tf_op jit(solution)/shard_map/ppermute | solution.py:287
  9.7 7.5 %copy-start.2 = (bf16[768,768]{1,0:T(8,128)(2,1)S(1)}, bf16[768,768]{1,0:T(8,128)(2,1)}, u32[]{:S(2)}) copy-start(bf16[768,768]{1,0:T(8,128)(2,1)} %refs_6_.2) | copy-start | bytes 3538948
  9.7 5.8 %collective-permute-start.2 = (bf16[40,768]{1,0:T(8,128)(2,1)S(1)}, bf16[40,768]{1,0:T(8,128)(2,1)S(1)}, u32[]{:S(2)}, u32[]{:S(2)}) collective-permute-start(bf16[40,768]{1,0:T(8,128)(2,1)S(1)} %collective-permute-done.1.refs_1_), channel_id=1, source_target_pairs={{0,4},{4,0},{8,12},{12,8},{16,20},{20,16},{24,28},{28,24},{1,5},{5... | collective-permute-start | bytes 184328 | tf_op jit(solution)/shard_map/ppermute | solution.py:287
  10.7 4.8 %collective-permute-start.4 = (bf16[40,768]{1,0:T(8,128)(2,1)S(1)}, bf16[40,768]{1,0:T(8,128)(2,1)S(1)}, u32[]{:S(2)}, u32[]{:S(2)}) collective-permute-start(bf16[40,768]{1,0:T(8,128)(2,1)S(1)} %collective-permute-done.3.refs_2_), channel_id=1, source_target_pairs={{0,4},{4,0},{8,12},{12,8},{16,20},{20,16},{24,28},{28,24},{1,5},{5... | collective-permute-start | bytes 184328 | tf_op jit(solution)/shard_map/ppermute | solution.py:287
  12.9 4.2 %collective-permute-start.6 = (bf16[40,768]{1,0:T(8,128)(2,1)S(1)}, bf16[40,768]{1,0:T(8,128)(2,1)S(1)}, u32[]{:S(2)}, u32[]{:S(2)}) collective-permute-start(bf16[40,768]{1,0:T(8,128)(2,1)S(1)} %collective-permute-done.5.refs_3_), channel_id=1, source_target_pairs={{0,4},{4,0},{8,12},{12,8},{16,20},{20,16},{24,28},{28,24},{1,5},{5... | collective-permute-start | bytes 184328 | tf_op jit(solution)/shard_map/ppermute | solution.py:287
  17.1 10.0 %copy-start = (bf16[768,2304]{1,0:T(8,128)(2,1)S(1)}, bf16[768,2304]{1,0:T(8,128)(2,1)}, u32[]{:S(2)}) copy-start(bf16[768,2304]{1,0:T(8,128)(2,1)} %refs_6_.3) | copy-start | bytes 10616836
  19.1 6.0 %collective-permute-start.10 = (bf16[40,768]{1,0:T(8,128)(2,1)S(1)}, bf16[40,768]{1,0:T(8,128)(2,1)S(1)}, u32[]{:S(2)}, u32[]{:S(2)}) collective-permute-start(bf16[40,768]{1,0:T(8,128)(2,1)S(1)} %get-tuple-element.44), channel_id=1, source_target_pairs={{0,8},{4,12},{8,0},{12,4},{16,24},{20,28},{24,16},{28,20},{1,9},{5... | collective-permute-start | bytes 184328 | tf_op jit(solution)/shard_map/ppermute | solution.py:284
  19.4 6.2 %collective-permute-start.12 = (bf16[40,768]{1,0:T(8,128)(2,1)S(1)}, bf16[40,768]{1,0:T(8,128)(2,1)S(1)}, u32[]{:S(2)}, u32[]{:S(2)}) collective-permute-start(bf16[40,768]{1,0:T(8,128)(2,1)S(1)} %get-tuple-element.45), channel_id=1, source_target_pairs={{0,16},{4,20},{8,24},{12,28},{16,0},{20,4},{24,8},{28,12},{1,17},{... | collective-permute-start | bytes 184328 | tf_op jit(solution)/shard_map/ppermute | solution.py:284
  22.8 6.0 %collective-permute-start.7 = (bf16[40,768]{1,0:T(8,128)(2,1)S(1)}, bf16[40,768]{1,0:T(8,128)(2,1)S(1)}, u32[]{:S(2)}, u32[]{:S(2)}) collective-permute-start(bf16[40,768]{1,0:T(8,128)(2,1)S(1)} %get-tuple-element.42), channel_id=1, source_target_pairs={{0,24},{4,28},{8,16},{12,20},{16,8},{20,12},{24,0},{28,4},{1,25},{... | collective-permute-start | bytes 184328 | tf_op jit(solution)/shard_map/ppermute | solution.py:284
  23.6 6.7 %collective-permute-start.9 = (bf16[40,768]{1,0:T(8,128)(2,1)S(1)}, bf16[40,768]{1,0:T(8,128)(2,1)S(1)}, u32[]{:S(2)}, u32[]{:S(2)}) collective-permute-start(bf16[40,768]{1,0:T(8,128)(2,1)S(1)} %get-tuple-element.43.refs_0_), channel_id=1, source_target_pairs={{0,2},{1,3},{2,0},{3,1},{4,6},{5,7},{6,4},{7,5},{8,10},{9,11},{10,... | collective-permute-start | bytes 184328 | tf_op jit(solution)/shard_map/ppermute | solution.py:290
  25.1 5.2 %collective-permute-start.11 = (bf16[40,768]{1,0:T(8,128)(2,1)S(1)}, bf16[40,768]{1,0:T(8,128)(2,1)S(1)}, u32[]{:S(2)}, u32[]{:S(2)}) collective-permute-start(bf16[40,768]{1,0:T(8,128)(2,1)S(1)} %collective-permute-done.10.refs_1_), channel_id=1, source_target_pairs={{0,2},{1,3},{2,0},{3,1},{4,6},{5,7},{6,4},{7,5},{8,10},{9,11},{10,... | collective-permute-start | bytes 184328 | tf_op jit(solution)/shard_map/ppermute | solution.py:290
  25.6 4.7 %collective-permute-start.13 = (bf16[40,768]{1,0:T(8,128)(2,1)S(1)}, bf16[40,768]{1,0:T(8,128)(2,1)S(1)}, u32[]{:S(2)}, u32[]{:S(2)}) collective-permute-start(bf16[40,768]{1,0:T(8,128)(2,1)S(1)} %collective-permute-done.12.refs_2_), channel_id=1, source_target_pairs={{0,2},{1,3},{2,0},{3,1},{4,6},{5,7},{6,4},{7,5},{8,10},{9,11},{10,... | collective-permute-start | bytes 184328 | tf_op jit(solution)/shard_map/ppermute | solution.py:290
  28.2 5.2 %collective-permute-start.15 = (bf16[120,768]{1,0:T(8,128)(2,1)S(1)}, bf16[120,768]{1,0:T(8,128)(2,1)S(1)}, u32[]{:S(2)}, u32[]{:S(2)}) collective-permute-start(bf16[120,768]{1,0:T(8,128)(2,1)S(1)} %get-tuple-element.54), channel_id=1, source_target_pairs={{0,1},{1,0},{2,3},{3,2},{4,5},{5,4},{6,7},{7,6},{8,9},{9,8},{10,11... | collective-permute-start | bytes 552968 | tf_op jit(solution)/shard_map/ppermute | solution.py:290
  28.8 4.2 %collective-permute-start.8 = (bf16[40,768]{1,0:T(8,128)(2,1)S(1)}, bf16[40,768]{1,0:T(8,128)(2,1)S(1)}, u32[]{:S(2)}, u32[]{:S(2)}) collective-permute-start(bf16[40,768]{1,0:T(8,128)(2,1)S(1)} %collective-permute-done.7.own_ref.refs_3_), channel_id=1, source_target_pairs={{0,2},{1,3},{2,0},{3,1},{4,6},{5,7},{6,4},{7,5},{8,10},{9,11},{10,... | collective-permute-start | bytes 184328 | tf_op jit(solution)/shard_map/ppermute | solution.py:290
  31.5 1.8 %collective-permute-start.17 = (bf16[80,768]{1,0:T(8,128)(2,1)S(1)}, bf16[80,768]{1,0:T(8,128)(2,1)S(1)}, u32[]{:S(2)}, u32[]{:S(2)}) collective-permute-start(bf16[80,768]{1,0:T(8,128)(2,1)S(1)} %get-tuple-element.55), channel_id=1, source_target_pairs={{0,1},{1,0},{2,3},{3,2},{4,5},{5,4},{6,7},{7,6},{8,9},{9,8},{10,11... | collective-permute-start | bytes 368648 | tf_op jit(solution)/shard_map/ppermute | solution.py:290
  31.6 1.4 %collective-permute-start.16 = (bf16[40,768]{1,0:T(8,128)(2,1)S(1)}, bf16[40,768]{1,0:T(8,128)(2,1)S(1)}, u32[]{:S(2)}, u32[]{:S(2)}) collective-permute-start(bf16[40,768]{1,0:T(8,128)(2,1)S(1)} %collective-permute-done.7.own_ref.refs_3_), channel_id=1, source_target_pairs={{0,1},{1,0},{2,3},{3,2},{4,5},{5,4},{6,7},{7,6},{8,9},{9,8},{10,11... | collective-permute-start | bytes 184328 | tf_op jit(solution)/shard_map/ppermute | solution.py:290
  32.1 1.2 %collective-permute-start.18 = (bf16[40,768]{1,0:T(8,128)(2,1)S(1)}, bf16[40,768]{1,0:T(8,128)(2,1)S(1)}, u32[]{:S(2)}, u32[]{:S(2)}) collective-permute-start(bf16[40,768]{1,0:T(8,128)(2,1)S(1)} %get-tuple-element.56), channel_id=1, source_target_pairs={{0,1},{1,0},{2,3},{3,2},{4,5},{5,4},{6,7},{7,6},{8,9},{9,8},{10,11... | collective-permute-start | bytes 184328 | tf_op jit(solution)/shard_map/ppermute | solution.py:290
  33.0 1.7 %collective-permute-start.14 = (bf16[40,768]{1,0:T(8,128)(2,1)S(1)}, bf16[40,768]{1,0:T(8,128)(2,1)S(1)}, u32[]{:S(2)}, u32[]{:S(2)}) collective-permute-start(bf16[40,768]{1,0:T(8,128)(2,1)S(1)} %collective-permute-done.8.refs_4_), channel_id=1, source_target_pairs={{0,1},{1,0},{2,3},{3,2},{4,5},{5,4},{6,7},{7,6},{8,9},{9,8},{10,11... | collective-permute-start | bytes 184328 | tf_op jit(solution)/shard_map/ppermute | solution.py:290
  33.3 1.4 %copy-start.3 = (bf16[768,768]{1,0:T(8,128)(2,1)S(1)}, bf16[768,768]{1,0:T(8,128)(2,1)}, u32[]{:S(2)}) copy-start(bf16[768,768]{1,0:T(8,128)(2,1)} %refs_7_.1) | copy-start | bytes 3538948

commit v8 on v7

--- a/solution.py
+++ b/solution.py
@@ -13,6 +13,7 @@
 HD = 64
 FREQ = 256
 PAIR = 2 * HD
+ORDER = (0, 1, 3, 2)
 BF = jnp.bfloat16
 F32 = jnp.float32
 
@@ -52,6 +53,10 @@
     return total
 
 
+def partner(m, groups):
+    return ORDER[m] if groups == len(ORDER) else m
+
+
 def message_rows(shape, row_dim, token_dim, rows, cols, width, owner):
     r = lax.broadcasted_iota(jnp.int32, shape, row_dim)
     t = lax.broadcasted_iota(jnp.int32, shape, token_dim)
@@ -66,7 +71,7 @@
     x = tok_ref[...]
     for m, out in enumerate(out_refs):
         shape = (out.shape[0], x.shape[0])
-        pick = message_rows(shape, 0, 1, rows, cols, width, z_ref[0] ^ m)
+        pick = message_rows(shape, 0, 1, rows, cols, width, z_ref[0] ^ partner(m, len(out_refs)))
         out[...] = jnp.dot(pick, x, preferred_element_type=F32).astype(BF)
 
 
@@ -76,7 +81,9 @@
     m = divided(r, pad, shape[1])
     r = r - m * pad
     i = divided(r, cols, pad)
-    source = i * width + (z ^ m) * cols + (r - i * cols)
+    groups = shape[1] // pad
+    differs = sum(jnp.where(m == k, partner(k, groups), 0) for k in range(groups))
+    source = i * width + (z ^ differs) * cols + (r - i * cols)
     source = jnp.where(r < rows * cols, source, -1)
     return jnp.where(source == lax.broadcasted_iota(jnp.int32, shape, 0), 1.0, 0.0).astype(BF)
 
@@ -281,7 +288,7 @@
     n = rows * width
 
     def over_group(x, m):
-        return lax.ppermute(x, "seq", [(i, i ^ (2 * m)) for i in range(owners)])
+        return lax.ppermute(x, "seq", [(i, i ^ (2 * partner(m, groups))) for i in range(owners)])
 
     def over_pair(x):
         return lax.ppermute(x, "seq", [(i, i ^ 1) for i in range(owners)])

time: 37.2 us -> 37 us (level)
  starting transfers between devices: 21 us -> 20.5 us
    ppermute x6, starting transfers between devices: 10.1 us -> 9.57 us  [over_group(): lax.ppermute(x, 'seq', [(i, i ^ 2 * partner(m, groups)) for i in range(ow...]
    ppermute x9, waiting for transfers between devices: 1.18 us -> 1.61 us  [over_bin(): return lax.ppermute(x, 'bin', [(i, i ^ m) for i in range(4)])]
  transfers between devices with their start and end apart: 19 -> 19, of which waited for: 6 -> 7; matrix products, arithmetic and copies ran while one was open for 1% -> 1% of each run, Pallas kernels for 13% -> 13%
where the time goes in v8:
time: 37 us; the launch traced here: 36.8 us
  starting transfers between devices  20.5 us (55%)
  Pallas kernels  9.24 us (25%)
  waiting for transfers between devices  4.98 us (13%)
  local copies, waits for them, and re-layouts  0.97 us (3%)
  between operations  0.82 us (2%)
    ppermute x6, starting transfers between devices, over_group(): lax.ppermute(x, 'seq', [(i, i ^ 2 * partner(m, groups)) for i in range(ow...  9.57 us
    pallas_call x7, Pallas kernels, call(): pl.pallas_call(kernel, out_shape=[jax.ShapeDtypeStruct(*o) for o in outs]...  9.24 us
    ppermute x9, starting transfers between devices, over_bin(): return lax.ppermute(x, 'bin', [(i, i ^ m) for i in range(4)])  5.82 us
    ppermute x4, starting transfers between devices, over_pair(): return lax.ppermute(x, 'seq', [(i, i ^ 1) for i in range(owners)])  5.08 us
    ppermute x6, waiting for transfers between devices, over_group(): lax.ppermute(x, 'seq', [(i, i ^ 2 * partner(m, groups)) for i in range(ow...  1.75 us
    ppermute x4, waiting for transfers between devices, over_pair(): return lax.ppermute(x, 'seq', [(i, i ^ 1) for i in range(owners)])  1.63 us
    ppermute x9, waiting for transfers between devices, over_bin(): return lax.ppermute(x, 'bin', [(i, i ^ m) for i in range(4)])  1.61 us
    unnamed x12, local copies, waits for them, and re-layouts  0.95 us
  transfers between devices with their start and end apart: 19, of which 7 were waited for; matrix products, arithmetic and copies ran while one was open for 1% of the time, Pallas kernels for 13%

profile of v8, /device:TPU:0, one launch (start us, length us, event | category | flops | bytes accessed | tf_op | source)
XLA Modules:
  0.0 36.8 jit_solution(7555576509338807516)
XLA Ops:
  0.0 0.9 %copy-done.4 = bf16[1,6,24,768]{3,2,1,0:T(8,128)(2,1)S(1)} copy-done((bf16[1,6,24,768]{3,2,1,0:T(8,128)(2,1)S(1)}, bf16[1,6,24,768]{3,2,1,0:T(8,128)(2,1)}, u32[]{:S(2)}) %copy-start.4) | copy-done | bytes 221208
  0.9 0.3 shard_map.73
  1.2 3.1 %collective-permute-start.1 = (bf16[40,768]{1,0:T(8,128)(2,1)S(1)}, bf16[40,768]{1,0:T(8,128)(2,1)S(1)}, u32[]{:S(2)}, u32[]{:S(2)}) collective-permute-start(bf16[40,768]{1,0:T(8,128)(2,1)S(1)} %get-tuple-element.33), channel_id=1, source_target_pairs={{0,8},{4,12},{8,0},{12,4},{16,24},{20,28},{24,16},{28,20},{1,9},{5... | collective-permute-start | bytes 184328 | tf_op jit(solution)/shard_map/ppermute | solution.py:291
  4.3 2.5 %collective-permute-start.3 = (bf16[40,768]{1,0:T(8,128)(2,1)S(1)}, bf16[40,768]{1,0:T(8,128)(2,1)S(1)}, u32[]{:S(2)}, u32[]{:S(2)}) collective-permute-start(bf16[40,768]{1,0:T(8,128)(2,1)S(1)} %get-tuple-element.35), channel_id=1, source_target_pairs={{0,24},{4,28},{8,16},{12,20},{16,8},{20,12},{24,0},{28,4},{1,25},{... | collective-permute-start | bytes 184328 | tf_op jit(solution)/shard_map/ppermute | solution.py:291
  6.8 0.1 collective-permute-start.5
  6.9 1.5 %collective-permute-start = (bf16[40,768]{1,0:T(8,128)(2,1)S(1)}, bf16[40,768]{1,0:T(8,128)(2,1)S(1)}, u32[]{:S(2)}, u32[]{:S(2)}) collective-permute-start(bf16[40,768]{1,0:T(8,128)(2,1)S(1)} %get-tuple-element.32.refs_0_), channel_id=1, source_target_pairs={{0,4},{4,0},{8,12},{12,8},{16,20},{20,16},{24,28},{28,24},{1,5},{5... | collective-permute-start | bytes 184328 | tf_op jit(solution)/shard_map/ppermute | solution.py:294
  9.1 0.3 fusion
  9.5 0.6 %collective-permute-start.2 = (bf16[40,768]{1,0:T(8,128)(2,1)S(1)}, bf16[40,768]{1,0:T(8,128)(2,1)S(1)}, u32[]{:S(2)}, u32[]{:S(2)}) collective-permute-start(bf16[40,768]{1,0:T(8,128)(2,1)S(1)} %collective-permute-done.1.refs_1_), channel_id=1, source_target_pairs={{0,4},{4,0},{8,12},{12,8},{16,20},{20,16},{24,28},{28,24},{1,5},{5... | collective-permute-start | bytes 184328 | tf_op jit(solution)/shard_map/ppermute | solution.py:294
  10.1 1.0 %collective-permute-done.3.refs_2_ = bf16[40,768]{1,0:T(8,128)(2,1)S(1)} collective-permute-done((bf16[40,768]{1,0:T(8,128)(2,1)S(1)}, bf16[40,768]{1,0:T(8,128)(2,1)S(1)}, u32[]{:S(2)}, u32[]{:S(2)}) %collective-permute-start.3) | collective-permute-done | bytes 61472 | tf_op jit(solution)/shard_map/ppermute | solution.py:291
  11.1 1.5 %collective-permute-start.4 = (bf16[40,768]{1,0:T(8,128)(2,1)S(1)}, bf16[40,768]{1,0:T(8,128)(2,1)S(1)}, u32[]{:S(2)}, u32[]{:S(2)}) collective-permute-start(bf16[40,768]{1,0:T(8,128)(2,1)S(1)} %collective-permute-done.3.refs_2_), channel_id=1, source_target_pairs={{0,4},{4,0},{8,12},{12,8},{16,20},{20,16},{24,28},{28,24},{1,5},{5... | collective-permute-start | bytes 184328 | tf_op jit(solution)/shard_map/ppermute | solution.py:294
  12.6 0.3 collective-permute-done.5.refs_3_
  12.9 1.5 %collective-permute-start.6 = (bf16[40,768]{1,0:T(8,128)(2,1)S(1)}, bf16[40,768]{1,0:T(8,128)(2,1)S(1)}, u32[]{:S(2)}, u32[]{:S(2)}) collective-permute-start(bf16[40,768]{1,0:T(8,128)(2,1)S(1)} %collective-permute-done.5.refs_3_), channel_id=1, source_target_pairs={{0,4},{4,0},{8,12},{12,8},{16,20},{20,16},{24,28},{28,24},{1,5},{5... | collective-permute-start | bytes 184328 | tf_op jit(solution)/shard_map/ppermute | solution.py:294
  14.4 1.1 %shard_map.74 = (bf16[144,768]{1,0:T(8,128)(2,1)S(1)}, bf16[144,768]{1,0:T(8,128)(2,1)S(1)}, bf16[144,768]{1,0:T(8,128)(2,1)S(1)}, bf16[144,768]{1,0:T(8,128)(2,1)S(1)}) custom-call(bf16[40,768]{1,0:T(8,128)(2,1)S(1)} %get-tuple-element.32.refs_0_, bf16[40,768]{1,0:T(8,128)(2,1)S(1)} %collective-permute-done.1.refs_1_, ...), custom_call_target="tpu_custom_call" | custom-call | flops 1000000 | bytes 1000 | tf_op jit(solution)/shard_map/pallas_call | solution.py:270
  15.5 1.6 %collective-permute-done.6.refs_3_ = bf16[40,768]{1,0:T(8,128)(2,1)S(1)} collective-permute-done((bf16[40,768]{1,0:T(8,128)(2,1)S(1)}, bf16[40,768]{1,0:T(8,128)(2,1)S(1)}, u32[]{:S(2)}, u32[]{:S(2)}) %collective-permute-start.6) | collective-permute-done | bytes 61472 | tf_op jit(solution)/shard_map/ppermute | solution.py:294
  17.1 2.0 %shard_map.75 = (bf16[40,768]{1,0:T(8,128)(2,1)S(1)}, bf16[40,768]{1,0:T(8,128)(2,1)S(1)}, bf16[40,768]{1,0:T(8,128)(2,1)S(1)}, bf16[40,768]{1,0:T(8,128)(2,1)S(1)}) custom-call(bf16[40,768]{1,0:T(8,128)(2,1)S(1)} %collective-permute-done.refs_0_, bf16[40,768]{1,0:T(8,128)(2,1)S(1)} %collective-permute-done.2.refs_1_, ...), custom_call_target="tpu_custom_call" | custom-call | flops 1000000 | bytes 1000 | tf_op jit(solution)/shard_map/pallas_call | solution.py:270
  19.1 0.5 %collective-permute-start.10 = (bf16[40,768]{1,0:T(8,128)(2,1)S(1)}, bf16[40,768]{1,0:T(8,128)(2,1)S(1)}, u32[]{:S(2)}, u32[]{:S(2)}) collective-permute-start(bf16[40,768]{1,0:T(8,128)(2,1)S(1)} %get-tuple-element.44), channel_id=1, source_target_pairs={{0,8},{4,12},{8,0},{12,4},{16,24},{20,28},{24,16},{28,20},{1,9},{5... | collective-permute-start | bytes 184328 | tf_op jit(solution)/shard_map/ppermute | solution.py:291
  19.6 3.4 %collective-permute-start.12 = (bf16[40,768]{1,0:T(8,128)(2,1)S(1)}, bf16[40,768]{1,0:T(8,128)(2,1)S(1)}, u32[]{:S(2)}, u32[]{:S(2)}) collective-permute-start(bf16[40,768]{1,0:T(8,128)(2,1)S(1)} %get-tuple-element.45), channel_id=1, source_target_pairs={{0,24},{4,28},{8,16},{12,20},{16,8},{20,12},{24,0},{28,4},{1,25},{... | collective-permute-start | bytes 184328 | tf_op jit(solution)/shard_map/ppermute | solution.py:291
  23.0 1.5 %collective-permute-start.9 = (bf16[40,768]{1,0:T(8,128)(2,1)S(1)}, bf16[40,768]{1,0:T(8,128)(2,1)S(1)}, u32[]{:S(2)}, u32[]{:S(2)}) collective-permute-start(bf16[40,768]{1,0:T(8,128)(2,1)S(1)} %get-tuple-element.43.refs_0_), channel_id=1, source_target_pairs={{0,2},{1,3},{2,0},{3,1},{4,6},{5,7},{6,4},{7,5},{8,10},{9,11},{10,... | collective-permute-start | bytes 184328 | tf_op jit(solution)/shard_map/ppermute | solution.py:297
  24.5 0.9 %collective-permute-start.11 = (bf16[40,768]{1,0:T(8,128)(2,1)S(1)}, bf16[40,768]{1,0:T(8,128)(2,1)S(1)}, u32[]{:S(2)}, u32[]{:S(2)}) collective-permute-start(bf16[40,768]{1,0:T(8,128)(2,1)S(1)} %collective-permute-done.10.refs_1_), channel_id=1, source_target_pairs={{0,2},{1,3},{2,0},{3,1},{4,6},{5,7},{6,4},{7,5},{8,10},{9,11},{10,... | collective-permute-start | bytes 184328 | tf_op jit(solution)/shard_map/ppermute | solution.py:297
  25.5 0.4 %collective-permute-done.12.refs_2_ = bf16[40,768]{1,0:T(8,128)(2,1)S(1)} collective-permute-done((bf16[40,768]{1,0:T(8,128)(2,1)S(1)}, bf16[40,768]{1,0:T(8,128)(2,1)S(1)}, u32[]{:S(2)}, u32[]{:S(2)}) %collective-permute-start.12) | collective-permute-done | bytes 61472 | tf_op jit(solution)/shard_map/ppermute | solution.py:291
  25.9 1.5 %collective-permute-start.13 = (bf16[40,768]{1,0:T(8,128)(2,1)S(1)}, bf16[40,768]{1,0:T(8,128)(2,1)S(1)}, u32[]{:S(2)}, u32[]{:S(2)}) collective-permute-start(bf16[40,768]{1,0:T(8,128)(2,1)S(1)} %collective-permute-done.12.refs_2_), channel_id=1, source_target_pairs={{0,2},{1,3},{2,0},{3,1},{4,6},{5,7},{6,4},{7,5},{8,10},{9,11},{10,... | collective-permute-start | bytes 184328 | tf_op jit(solution)/shard_map/ppermute | solution.py:297
  27.4 1.0 %shard_map.76 = (bf16[120,768]{1,0:T(8,128)(2,1)S(1)}, bf16[120,768]{1,0:T(8,128)(2,1)S(1)}, f32[120,128]{1,0:T(8,128)S(1)}, bf16[120,768]{1,0:T(8,128)(2,1)S(1)}) custom-call(bf16[40,768]{1,0:T(8,128)(2,1)S(1)} %get-tuple-element.43.refs_0_, bf16[40,768]{1,0:T(8,128)(2,1)S(1)} %collective-permute-done.10.refs_1_, ...), custom_call_target="tpu_custom_call" | custom-call | flops 1000000 | bytes 1000 | tf_op jit(solution)/shard_map/pallas_call | solution.py:270
  28.5 1.1 %collective-permute-start.8 = (bf16[40,768]{1,0:T(8,128)(2,1)S(1)}, bf16[40,768]{1,0:T(8,128)(2,1)S(1)}, u32[]{:S(2)}, u32[]{:S(2)}) collective-permute-start(bf16[40,768]{1,0:T(8,128)(2,1)S(1)} %collective-permute-done.7.own_ref.refs_3_), channel_id=1, source_target_pairs={{0,2},{1,3},{2,0},{3,1},{4,6},{5,7},{6,4},{7,5},{8,10},{9,11},{10,... | collective-permute-start | bytes 184328 | tf_op jit(solution)/shard_map/ppermute | solution.py:297
  29.7 0.4 %collective-permute-done.13.refs_2_ = bf16[40,768]{1,0:T(8,128)(2,1)S(1)} collective-permute-done((bf16[40,768]{1,0:T(8,128)(2,1)S(1)}, bf16[40,768]{1,0:T(8,128)(2,1)S(1)}, u32[]{:S(2)}, u32[]{:S(2)}) %collective-permute-start.13) | collective-permute-done | bytes 61472 | tf_op jit(solution)/shard_map/ppermute | solution.py:297
  30.1 1.2 %shard_map.77 = (bf16[40,768]{1,0:T(8,128)(2,1)S(1)}, bf16[160,768]{1,0:T(8,128)(2,1)S(1)}, f32[160,128]{1,0:T(8,128)S(1)}, bf16[80,768]{1,0:T(8,128)(2,1)S(1)}, bf16[40,768]{1,0:T(8,128)(2,1)S(1)}) custom-call(bf16[40,768]{1,0:T(8,128)(2,1)S(1)} %collective-permute-done.7.own_ref.refs_3_, bf16[40,768]{1,0:T(8,128)(2,1)S(1)} %collective-permute-done.9.refs_0_, ...), custom_call_target="tpu_custom_call" | custom-call | flops 1000000 | bytes 1000 | tf_op jit(solution)/shard_map/pallas_call | solution.py:270
  31.3 0.1 collective-permute-start.17
  31.4 0.5 %collective-permute-start.16 = (bf16[40,768]{1,0:T(8,128)(2,1)S(1)}, bf16[40,768]{1,0:T(8,128)(2,1)S(1)}, u32[]{:S(2)}, u32[]{:S(2)}) collective-permute-start(bf16[40,768]{1,0:T(8,128)(2,1)S(1)} %collective-permute-done.7.own_ref.refs_3_), channel_id=1, source_target_pairs={{0,1},{1,0},{2,3},{3,2},{4,5},{5,4},{6,7},{7,6},{8,9},{9,8},{10,11... | collective-permute-start | bytes 184328 | tf_op jit(solution)/shard_map/ppermute | solution.py:297
  31.9 0.1 collective-permute-start.18
  31.9 1.0 %collective-permute-done.8.refs_4_ = bf16[40,768]{1,0:T(8,128)(2,1)S(1)} collective-permute-done((bf16[40,768]{1,0:T(8,128)(2,1)S(1)}, bf16[40,768]{1,0:T(8,128)(2,1)S(1)}, u32[]{:S(2)}, u32[]{:S(2)}) %collective-permute-start.8) | collective-permute-done | bytes 61472 | tf_op jit(solution)/shard_map/ppermute | solution.py:297
  32.9 0.2 collective-permute-done.18.refs_3_
  33.1 1.4 %shard_map.78 = (bf16[320,768]{1,0:T(8,128)(2,1)S(1)}, f32[320,128]{1,0:T(8,128)S(1)}) custom-call(bf16[120,768]{1,0:T(8,128)(2,1)S(1)} %collective-permute-done.15.refs_0_, bf16[40,768]{1,0:T(8,128)(2,1)S(1)} %collective-permute-done.16.refs_1_, bf16[80,768]{1,0:T(8,128)(2,1)S(1)} %collective-permute-done.17.refs_2_, ...), custom_call_target="tpu_custom_call" | custom-call | flops 1000000 | bytes 1000 | tf_op jit(solution)/shard_map/pallas_call | solution.py:270
  34.5 2.4 %shard_map.79 = bf16[144,768]{1,0:T(8,128)(2,1)} custom-call(s32[1]{0:T(128)} %bitcast.z_ref, bf16[40,768]{1,0:T(8,128)(2,1)S(1)} %collective-permute-done.14.last_ref, bf16[40,768]{1,0:T(8,128)(2,1)S(1)} %get-tuple-element.43.refs_0_, bf16[40,768]{1,0:T(8,128)(2,1)S(1)} %collective-permute-done.10.refs_1_, ...), custom_call_target="tpu_custom_call" | custom-call | flops 1000000 | bytes 1000 | tf_op jit(solution)/shard_map/pallas_call | solution.py:270
  (30 shorter events, 0.2 us)
Async XLA Ops:
  0.0 0.9 %copy-start.4 = (bf16[1,6,24,768]{3,2,1,0:T(8,128)(2,1)S(1)}, bf16[1,6,24,768]{3,2,1,0:T(8,128)(2,1)}, u32[]{:S(2)}) copy-start(bf16[1,6,24,768]{3,2,1,0:T(8,128)(2,1)} %param.7) | copy-start | bytes 663556
  0.9 8.2 %copy-start.5 = (bf16[256,3072]{1,0:T(8,128)(2,1)S(1)}, bf16[256,3072]{1,0:T(8,128)(2,1)}, u32[]{:S(2)}) copy-start(bf16[256,3072]{1,0:T(8,128)(2,1)} %param.9) | copy-start | bytes 4718596
  0.9 13.5 %copy-start.1 = (bf16[768,2304]{1,0:T(8,128)(2,1)S(1)}, bf16[768,2304]{1,0:T(8,128)(2,1)}, u32[]{:S(2)}) copy-start(bf16[768,2304]{1,0:T(8,128)(2,1)} %refs_5_.4) | copy-start | bytes 10616836
  1.2 8.2 %collective-permute-start.1 = (bf16[40,768]{1,0:T(8,128)(2,1)S(1)}, bf16[40,768]{1,0:T(8,128)(2,1)S(1)}, u32[]{:S(2)}, u32[]{:S(2)}) collective-permute-start(bf16[40,768]{1,0:T(8,128)(2,1)S(1)} %get-tuple-element.33), channel_id=1, source_target_pairs={{0,8},{4,12},{8,0},{12,4},{16,24},{20,28},{24,16},{28,20},{1,9},{5... | collective-permute-start | bytes 184328 | tf_op jit(solution)/shard_map/ppermute | solution.py:291
  4.3 6.8 %collective-permute-start.3 = (bf16[40,768]{1,0:T(8,128)(2,1)S(1)}, bf16[40,768]{1,0:T(8,128)(2,1)S(1)}, u32[]{:S(2)}, u32[]{:S(2)}) collective-permute-start(bf16[40,768]{1,0:T(8,128)(2,1)S(1)} %get-tuple-element.35), channel_id=1, source_target_pairs={{0,24},{4,28},{8,16},{12,20},{16,8},{20,12},{24,0},{28,4},{1,25},{... | collective-permute-start | bytes 184328 | tf_op jit(solution)/shard_map/ppermute | solution.py:291
  6.8 6.1 %collective-permute-start.5 = (bf16[40,768]{1,0:T(8,128)(2,1)S(1)}, bf16[40,768]{1,0:T(8,128)(2,1)S(1)}, u32[]{:S(2)}, u32[]{:S(2)}) collective-permute-start(bf16[40,768]{1,0:T(8,128)(2,1)S(1)} %get-tuple-element.36), channel_id=1, source_target_pairs={{0,16},{4,20},{8,24},{12,28},{16,0},{20,4},{24,8},{28,12},{1,17},{... | collective-permute-start | bytes 184328 | tf_op jit(solution)/shard_map/ppermute | solution.py:291
  6.9 8.6 %collective-permute-start = (bf16[40,768]{1,0:T(8,128)(2,1)S(1)}, bf16[40,768]{1,0:T(8,128)(2,1)S(1)}, u32[]{:S(2)}, u32[]{:S(2)}) collective-permute-start(bf16[40,768]{1,0:T(8,128)(2,1)S(1)} %get-tuple-element.32.refs_0_), channel_id=1, source_target_pairs={{0,4},{4,0},{8,12},{12,8},{16,20},{20,16},{24,28},{28,24},{1,5},{5... | collective-permute-start | bytes 184328 | tf_op jit(solution)/shard_map/ppermute | solution.py:294
  9.5 7.7 %copy-start.2 = (bf16[768,768]{1,0:T(8,128)(2,1)S(1)}, bf16[768,768]{1,0:T(8,128)(2,1)}, u32[]{:S(2)}) copy-start(bf16[768,768]{1,0:T(8,128)(2,1)} %refs_6_.2) | copy-start | bytes 3538948
  9.5 6.0 %collective-permute-start.2 = (bf16[40,768]{1,0:T(8,128)(2,1)S(1)}, bf16[40,768]{1,0:T(8,128)(2,1)S(1)}, u32[]{:S(2)}, u32[]{:S(2)}) collective-permute-start(bf16[40,768]{1,0:T(8,128)(2,1)S(1)} %collective-permute-done.1.refs_1_), channel_id=1, source_target_pairs={{0,4},{4,0},{8,12},{12,8},{16,20},{20,16},{24,28},{28,24},{1,5},{5... | collective-permute-start | bytes 184328 | tf_op jit(solution)/shard_map/ppermute | solution.py:294
  11.1 4.4 %collective-permute-start.4 = (bf16[40,768]{1,0:T(8,128)(2,1)S(1)}, bf16[40,768]{1,0:T(8,128)(2,1)S(1)}, u32[]{:S(2)}, u32[]{:S(2)}) collective-permute-start(bf16[40,768]{1,0:T(8,128)(2,1)S(1)} %collective-permute-done.3.refs_2_), channel_id=1, source_target_pairs={{0,4},{4,0},{8,12},{12,8},{16,20},{20,16},{24,28},{28,24},{1,5},{5... | collective-permute-start | bytes 184328 | tf_op jit(solution)/shard_map/ppermute | solution.py:294
  12.9 4.2 %collective-permute-start.6 = (bf16[40,768]{1,0:T(8,128)(2,1)S(1)}, bf16[40,768]{1,0:T(8,128)(2,1)S(1)}, u32[]{:S(2)}, u32[]{:S(2)}) collective-permute-start(bf16[40,768]{1,0:T(8,128)(2,1)S(1)} %collective-permute-done.5.refs_3_), channel_id=1, source_target_pairs={{0,4},{4,0},{8,12},{12,8},{16,20},{20,16},{24,28},{28,24},{1,5},{5... | collective-permute-start | bytes 184328 | tf_op jit(solution)/shard_map/ppermute | solution.py:294
  17.1 10.2 %copy-start = (bf16[768,2304]{1,0:T(8,128)(2,1)S(1)}, bf16[768,2304]{1,0:T(8,128)(2,1)}, u32[]{:S(2)}) copy-start(bf16[768,2304]{1,0:T(8,128)(2,1)} %refs_6_.3) | copy-start | bytes 10616836
  19.1 5.4 %collective-permute-start.10 = (bf16[40,768]{1,0:T(8,128)(2,1)S(1)}, bf16[40,768]{1,0:T(8,128)(2,1)S(1)}, u32[]{:S(2)}, u32[]{:S(2)}) collective-permute-start(bf16[40,768]{1,0:T(8,128)(2,1)S(1)} %get-tuple-element.44), channel_id=1, source_target_pairs={{0,8},{4,12},{8,0},{12,4},{16,24},{20,28},{24,16},{28,20},{1,9},{5... | collective-permute-start | bytes 184328 | tf_op jit(solution)/shard_map/ppermute | solution.py:291
  19.6 6.2 %collective-permute-start.12 = (bf16[40,768]{1,0:T(8,128)(2,1)S(1)}, bf16[40,768]{1,0:T(8,128)(2,1)S(1)}, u32[]{:S(2)}, u32[]{:S(2)}) collective-permute-start(bf16[40,768]{1,0:T(8,128)(2,1)S(1)} %get-tuple-element.45), channel_id=1, source_target_pairs={{0,24},{4,28},{8,16},{12,20},{16,8},{20,12},{24,0},{28,4},{1,25},{... | collective-permute-start | bytes 184328 | tf_op jit(solution)/shard_map/ppermute | solution.py:291
  23.0 5.5 %collective-permute-start.7 = (bf16[40,768]{1,0:T(8,128)(2,1)S(1)}, bf16[40,768]{1,0:T(8,128)(2,1)S(1)}, u32[]{:S(2)}, u32[]{:S(2)}) collective-permute-start(bf16[40,768]{1,0:T(8,128)(2,1)S(1)} %get-tuple-element.42), channel_id=1, source_target_pairs={{0,16},{4,20},{8,24},{12,28},{16,0},{20,4},{24,8},{28,12},{1,17},{... | collective-permute-start | bytes 184328 | tf_op jit(solution)/shard_map/ppermute | solution.py:291
  23.0 6.6 %collective-permute-start.9 = (bf16[40,768]{1,0:T(8,128)(2,1)S(1)}, bf16[40,768]{1,0:T(8,128)(2,1)S(1)}, u32[]{:S(2)}, u32[]{:S(2)}) collective-permute-start(bf16[40,768]{1,0:T(8,128)(2,1)S(1)} %get-tuple-element.43.refs_0_), channel_id=1, source_target_pairs={{0,2},{1,3},{2,0},{3,1},{4,6},{5,7},{6,4},{7,5},{8,10},{9,11},{10,... | collective-permute-start | bytes 184328 | tf_op jit(solution)/shard_map/ppermute | solution.py:297
  24.5 5.1 %collective-permute-start.11 = (bf16[40,768]{1,0:T(8,128)(2,1)S(1)}, bf16[40,768]{1,0:T(8,128)(2,1)S(1)}, u32[]{:S(2)}, u32[]{:S(2)}) collective-permute-start(bf16[40,768]{1,0:T(8,128)(2,1)S(1)} %collective-permute-done.10.refs_1_), channel_id=1, source_target_pairs={{0,2},{1,3},{2,0},{3,1},{4,6},{5,7},{6,4},{7,5},{8,10},{9,11},{10,... | collective-permute-start | bytes 184328 | tf_op jit(solution)/shard_map/ppermute | solution.py:297
  25.9 4.2 %collective-permute-start.13 = (bf16[40,768]{1,0:T(8,128)(2,1)S(1)}, bf16[40,768]{1,0:T(8,128)(2,1)S(1)}, u32[]{:S(2)}, u32[]{:S(2)}) collective-permute-start(bf16[40,768]{1,0:T(8,128)(2,1)S(1)} %collective-permute-done.12.refs_2_), channel_id=1, source_target_pairs={{0,2},{1,3},{2,0},{3,1},{4,6},{5,7},{6,4},{7,5},{8,10},{9,11},{10,... | collective-permute-start | bytes 184328 | tf_op jit(solution)/shard_map/ppermute | solution.py:297
  28.4 4.7 %collective-permute-start.15 = (bf16[120,768]{1,0:T(8,128)(2,1)S(1)}, bf16[120,768]{1,0:T(8,128)(2,1)S(1)}, u32[]{:S(2)}, u32[]{:S(2)}) collective-permute-start(bf16[120,768]{1,0:T(8,128)(2,1)S(1)} %get-tuple-element.54), channel_id=1, source_target_pairs={{0,1},{1,0},{2,3},{3,2},{4,5},{5,4},{6,7},{7,6},{8,9},{9,8},{10,11... | collective-permute-start | bytes 552968 | tf_op jit(solution)/shard_map/ppermute | solution.py:297
  28.5 4.4 %collective-permute-start.8 = (bf16[40,768]{1,0:T(8,128)(2,1)S(1)}, bf16[40,768]{1,0:T(8,128)(2,1)S(1)}, u32[]{:S(2)}, u32[]{:S(2)}) collective-permute-start(bf16[40,768]{1,0:T(8,128)(2,1)S(1)} %collective-permute-done.7.own_ref.refs_3_), channel_id=1, source_target_pairs={{0,2},{1,3},{2,0},{3,1},{4,6},{5,7},{6,4},{7,5},{8,10},{9,11},{10,... | collective-permute-start | bytes 184328 | tf_op jit(solution)/shard_map/ppermute | solution.py:297
  31.3 1.8 %collective-permute-start.17 = (bf16[80,768]{1,0:T(8,128)(2,1)S(1)}, bf16[80,768]{1,0:T(8,128)(2,1)S(1)}, u32[]{:S(2)}, u32[]{:S(2)}) collective-permute-start(bf16[80,768]{1,0:T(8,128)(2,1)S(1)} %get-tuple-element.55), channel_id=1, source_target_pairs={{0,1},{1,0},{2,3},{3,2},{4,5},{5,4},{6,7},{7,6},{8,9},{9,8},{10,11... | collective-permute-start | bytes 368648 | tf_op jit(solution)/shard_map/ppermute | solution.py:297
  31.4 1.6 %collective-permute-start.16 = (bf16[40,768]{1,0:T(8,128)(2,1)S(1)}, bf16[40,768]{1,0:T(8,128)(2,1)S(1)}, u32[]{:S(2)}, u32[]{:S(2)}) collective-permute-start(bf16[40,768]{1,0:T(8,128)(2,1)S(1)} %collective-permute-done.7.own_ref.refs_3_), channel_id=1, source_target_pairs={{0,1},{1,0},{2,3},{3,2},{4,5},{5,4},{6,7},{7,6},{8,9},{9,8},{10,11... | collective-permute-start | bytes 184328 | tf_op jit(solution)/shard_map/ppermute | solution.py:297
  31.9 1.2 %collective-permute-start.18 = (bf16[40,768]{1,0:T(8,128)(2,1)S(1)}, bf16[40,768]{1,0:T(8,128)(2,1)S(1)}, u32[]{:S(2)}, u32[]{:S(2)}) collective-permute-start(bf16[40,768]{1,0:T(8,128)(2,1)S(1)} %get-tuple-element.56), channel_id=1, source_target_pairs={{0,1},{1,0},{2,3},{3,2},{4,5},{5,4},{6,7},{7,6},{8,9},{9,8},{10,11... | collective-permute-start | bytes 184328 | tf_op jit(solution)/shard_map/ppermute | solution.py:297
  32.9 1.5 %collective-permute-start.14 = (bf16[40,768]{1,0:T(8,128)(2,1)S(1)}, bf16[40,768]{1,0:T(8,128)(2,1)S(1)}, u32[]{:S(2)}, u32[]{:S(2)}) collective-permute-start(bf16[40,768]{1,0:T(8,128)(2,1)S(1)} %collective-permute-done.8.refs_4_), channel_id=1, source_target_pairs={{0,1},{1,0},{2,3},{3,2},{4,5},{5,4},{6,7},{7,6},{8,9},{9,8},{10,11... | collective-permute-start | bytes 184328 | tf_op jit(solution)/shard_map/ppermute | solution.py:297
  33.1 1.4 %copy-start.3 = (bf16[768,768]{1,0:T(8,128)(2,1)S(1)}, bf16[768,768]{1,0:T(8,128)(2,1)}, u32[]{:S(2)}) copy-start(bf16[768,768]{1,0:T(8,128)(2,1)} %refs_7_.1) | copy-start | bytes 3538948

commit v9 on v8

--- a/solution.py
+++ b/solution.py
@@ -13,7 +13,8 @@
 HD = 64
 FREQ = 256
 PAIR = 2 * HD
-ORDER = (0, 1, 3, 2)
+ORDER = (0, 1, 2, 3)
+RETURN = (0, 1, 3, 2)
 BF = jnp.bfloat16
 F32 = jnp.float32
 
@@ -82,7 +83,8 @@
     r = r - m * pad
     i = divided(r, cols, pad)
     groups = shape[1] // pad
-    differs = sum(jnp.where(m == k, partner(k, groups), 0) for k in range(groups))
+    back = RETURN if groups == len(RETURN) else range(groups)
+    differs = sum(jnp.where(m == k, back[k], 0) for k in range(groups))
     source = i * width + (z ^ differs) * cols + (r - i * cols)
     source = jnp.where(r < rows * cols, source, -1)
     return jnp.where(source == lax.broadcasted_iota(jnp.int32, shape, 0), 1.0, 0.0).astype(BF)
@@ -314,7 +316,10 @@
         functools.partial(col_attend_kernel, groups, dims), [message] * groups, [full] * 3,
         *other, mod, col_qkv, col_out, t, q, k, v,
     )
-    h = [sent[0]] + [over_group(sent[m], m) for m in range(1, groups)]
+    back = RETURN if groups == len(RETURN) else range(groups)
+    places = [partner(m, groups) for m in range(groups)]
+    places = [places.index(far) for far in back]
+    h = [sent[0]] + [over_group(sent[m], m) for m in places[1:]]
     hy = [over_bin(x, 2) for x in h]
 
     def rows_of(count):

time: 37 us -> 36.7 us (level)
  no operation moved by 1% of the time
where the time goes in v9:
time: 36.7 us; the launch traced here: 36.5 us
  starting transfers between devices  20.2 us (55%)
  Pallas kernels  9.24 us (25%)
  waiting for transfers between devices  4.9 us (13%)
  local copies, waits for them, and re-layouts  0.97 us (3%)
  between operations  0.82 us (2%)
    ppermute x6, starting transfers between devices, over_group(): lax.ppermute(x, 'seq', [(i, i ^ 2 * partner(m, groups)) for i in range(ow...  9.32 us
    pallas_call x7, Pallas kernels, call(): pl.pallas_call(kernel, out_shape=[jax.ShapeDtypeStruct(*o) for o in outs]...  9.24 us
    ppermute x9, starting transfers between devices, over_bin(): return lax.ppermute(x, 'bin', [(i, i ^ m) for i in range(4)])  5.8 us
    ppermute x4, starting transfers between devices, over_pair(): return lax.ppermute(x, 'seq', [(i, i ^ 1) for i in range(owners)])  5.07 us
    ppermute x6, waiting for transfers between devices, over_group(): lax.ppermute(x, 'seq', [(i, i ^ 2 * partner(m, groups)) for i in range(ow...  1.94 us
    ppermute x4, waiting for transfers between devices, over_pair(): return lax.ppermute(x, 'seq', [(i, i ^ 1) for i in range(owners)])  1.63 us
    ppermute x9, waiting for transfers between devices, over_bin(): return lax.ppermute(x, 'bin', [(i, i ^ m) for i in range(4)])  1.33 us
    unnamed x12, local copies, waits for them, and re-layouts  0.95 us
  transfers between devices with their start and end apart: 19, of which 7 were waited for; matrix products, arithmetic and copies ran while one was open for 1% of the time, Pallas kernels for 13%

profile of v9, /device:TPU:0, one launch (start us, length us, event | category | flops | bytes accessed | tf_op | source)
XLA Modules:
  0.0 36.5 jit_solution(13723317866756867569)
XLA Ops:
  0.0 0.9 %copy-done.4 = bf16[1,6,24,768]{3,2,1,0:T(8,128)(2,1)S(1)} copy-done((bf16[1,6,24,768]{3,2,1,0:T(8,128)(2,1)S(1)}, bf16[1,6,24,768]{3,2,1,0:T(8,128)(2,1)}, u32[]{:S(2)}) %copy-start.4) | copy-done | bytes 221208
  0.9 0.3 shard_map.73
  1.2 3.1 %collective-permute-start.1 = (bf16[40,768]{1,0:T(8,128)(2,1)S(1)}, bf16[40,768]{1,0:T(8,128)(2,1)S(1)}, u32[]{:S(2)}, u32[]{:S(2)}) collective-permute-start(bf16[40,768]{1,0:T(8,128)(2,1)S(1)} %get-tuple-element.33), channel_id=1, source_target_pairs={{0,8},{4,12},{8,0},{12,4},{16,24},{20,28},{24,16},{28,20},{1,9},{5... | collective-permute-start | bytes 184328 | tf_op jit(solution)/shard_map/ppermute | solution.py:293
  4.3 2.6 %collective-permute-start.3 = (bf16[40,768]{1,0:T(8,128)(2,1)S(1)}, bf16[40,768]{1,0:T(8,128)(2,1)S(1)}, u32[]{:S(2)}, u32[]{:S(2)}) collective-permute-start(bf16[40,768]{1,0:T(8,128)(2,1)S(1)} %get-tuple-element.35), channel_id=1, source_target_pairs={{0,16},{4,20},{8,24},{12,28},{16,0},{20,4},{24,8},{28,12},{1,17},{... | collective-permute-start | bytes 184328 | tf_op jit(solution)/shard_map/ppermute | solution.py:293
  6.9 1.7 %collective-permute-start = (bf16[40,768]{1,0:T(8,128)(2,1)S(1)}, bf16[40,768]{1,0:T(8,128)(2,1)S(1)}, u32[]{:S(2)}, u32[]{:S(2)}) collective-permute-start(bf16[40,768]{1,0:T(8,128)(2,1)S(1)} %get-tuple-element.32.refs_0_), channel_id=1, source_target_pairs={{0,4},{4,0},{8,12},{12,8},{16,20},{20,16},{24,28},{28,24},{1,5},{5... | collective-permute-start | bytes 184328 | tf_op jit(solution)/shard_map/ppermute | solution.py:296
  9.4 0.3 fusion
  9.7 0.4 %collective-permute-start.2 = (bf16[40,768]{1,0:T(8,128)(2,1)S(1)}, bf16[40,768]{1,0:T(8,128)(2,1)S(1)}, u32[]{:S(2)}, u32[]{:S(2)}) collective-permute-start(bf16[40,768]{1,0:T(8,128)(2,1)S(1)} %collective-permute-done.1.refs_1_), channel_id=1, source_target_pairs={{0,4},{4,0},{8,12},{12,8},{16,20},{20,16},{24,28},{28,24},{1,5},{5... | collective-permute-start | bytes 184328 | tf_op jit(solution)/shard_map/ppermute | solution.py:296
  10.1 0.6 %collective-permute-done.3.refs_2_ = bf16[40,768]{1,0:T(8,128)(2,1)S(1)} collective-permute-done((bf16[40,768]{1,0:T(8,128)(2,1)S(1)}, bf16[40,768]{1,0:T(8,128)(2,1)S(1)}, u32[]{:S(2)}, u32[]{:S(2)}) %collective-permute-start.3) | collective-permute-done | bytes 61472 | tf_op jit(solution)/shard_map/ppermute | solution.py:293
  10.7 1.5 %collective-permute-start.4 = (bf16[40,768]{1,0:T(8,128)(2,1)S(1)}, bf16[40,768]{1,0:T(8,128)(2,1)S(1)}, u32[]{:S(2)}, u32[]{:S(2)}) collective-permute-start(bf16[40,768]{1,0:T(8,128)(2,1)S(1)} %collective-permute-done.3.refs_2_), channel_id=1, source_target_pairs={{0,4},{4,0},{8,12},{12,8},{16,20},{20,16},{24,28},{28,24},{1,5},{5... | collective-permute-start | bytes 184328 | tf_op jit(solution)/shard_map/ppermute | solution.py:296
  12.1 0.8 %collective-permute-done.5.refs_3_ = bf16[40,768]{1,0:T(8,128)(2,1)S(1)} collective-permute-done((bf16[40,768]{1,0:T(8,128)(2,1)S(1)}, bf16[40,768]{1,0:T(8,128)(2,1)S(1)}, u32[]{:S(2)}, u32[]{:S(2)}) %collective-permute-start.5) | collective-permute-done | bytes 61472 | tf_op jit(solution)/shard_map/ppermute | solution.py:293
  12.9 1.5 %collective-permute-start.6 = (bf16[40,768]{1,0:T(8,128)(2,1)S(1)}, bf16[40,768]{1,0:T(8,128)(2,1)S(1)}, u32[]{:S(2)}, u32[]{:S(2)}) collective-permute-start(bf16[40,768]{1,0:T(8,128)(2,1)S(1)} %collective-permute-done.5.refs_3_), channel_id=1, source_target_pairs={{0,4},{4,0},{8,12},{12,8},{16,20},{20,16},{24,28},{28,24},{1,5},{5... | collective-permute-start | bytes 184328 | tf_op jit(solution)/shard_map/ppermute | solution.py:296
  14.4 1.1 %shard_map.74 = (bf16[144,768]{1,0:T(8,128)(2,1)S(1)}, bf16[144,768]{1,0:T(8,128)(2,1)S(1)}, bf16[144,768]{1,0:T(8,128)(2,1)S(1)}, bf16[144,768]{1,0:T(8,128)(2,1)S(1)}) custom-call(bf16[40,768]{1,0:T(8,128)(2,1)S(1)} %get-tuple-element.32.refs_0_, bf16[40,768]{1,0:T(8,128)(2,1)S(1)} %collective-permute-done.1.refs_1_, ...), custom_call_target="tpu_custom_call" | custom-call | flops 1000000 | bytes 1000 | tf_op jit(solution)/shard_map/pallas_call | solution.py:272
  15.5 1.6 %collective-permute-done.6.refs_3_ = bf16[40,768]{1,0:T(8,128)(2,1)S(1)} collective-permute-done((bf16[40,768]{1,0:T(8,128)(2,1)S(1)}, bf16[40,768]{1,0:T(8,128)(2,1)S(1)}, u32[]{:S(2)}, u32[]{:S(2)}) %collective-permute-start.6) | collective-permute-done | bytes 61472 | tf_op jit(solution)/shard_map/ppermute | solution.py:296
  17.1 2.0 %shard_map.75 = (bf16[40,768]{1,0:T(8,128)(2,1)S(1)}, bf16[40,768]{1,0:T(8,128)(2,1)S(1)}, bf16[40,768]{1,0:T(8,128)(2,1)S(1)}, bf16[40,768]{1,0:T(8,128)(2,1)S(1)}) custom-call(bf16[40,768]{1,0:T(8,128)(2,1)S(1)} %collective-permute-done.refs_0_, bf16[40,768]{1,0:T(8,128)(2,1)S(1)} %collective-permute-done.2.refs_1_, ...), custom_call_target="tpu_custom_call" | custom-call | flops 1000000 | bytes 1000 | tf_op jit(solution)/shard_map/pallas_call | solution.py:272
  19.1 0.3 collective-permute-start.10
  19.4 2.9 %collective-permute-start.12 = (bf16[40,768]{1,0:T(8,128)(2,1)S(1)}, bf16[40,768]{1,0:T(8,128)(2,1)S(1)}, u32[]{:S(2)}, u32[]{:S(2)}) collective-permute-start(bf16[40,768]{1,0:T(8,128)(2,1)S(1)} %get-tuple-element.45), channel_id=1, source_target_pairs={{0,24},{4,28},{8,16},{12,20},{16,8},{20,12},{24,0},{28,4},{1,25},{... | collective-permute-start | bytes 184328 | tf_op jit(solution)/shard_map/ppermute | solution.py:293
  22.3 0.5 %collective-permute-start.7 = (bf16[40,768]{1,0:T(8,128)(2,1)S(1)}, bf16[40,768]{1,0:T(8,128)(2,1)S(1)}, u32[]{:S(2)}, u32[]{:S(2)}) collective-permute-start(bf16[40,768]{1,0:T(8,128)(2,1)S(1)} %get-tuple-element.42), channel_id=1, source_target_pairs={{0,16},{4,20},{8,24},{12,28},{16,0},{20,4},{24,8},{28,12},{1,17},{... | collective-permute-start | bytes 184328 | tf_op jit(solution)/shard_map/ppermute | solution.py:293
  22.8 1.5 %collective-permute-start.9 = (bf16[40,768]{1,0:T(8,128)(2,1)S(1)}, bf16[40,768]{1,0:T(8,128)(2,1)S(1)}, u32[]{:S(2)}, u32[]{:S(2)}) collective-permute-start(bf16[40,768]{1,0:T(8,128)(2,1)S(1)} %get-tuple-element.43.refs_0_), channel_id=1, source_target_pairs={{0,2},{1,3},{2,0},{3,1},{4,6},{5,7},{6,4},{7,5},{8,10},{9,11},{10,... | collective-permute-start | bytes 184328 | tf_op jit(solution)/shard_map/ppermute | solution.py:299
  24.3 0.6 %collective-permute-start.11 = (bf16[40,768]{1,0:T(8,128)(2,1)S(1)}, bf16[40,768]{1,0:T(8,128)(2,1)S(1)}, u32[]{:S(2)}, u32[]{:S(2)}) collective-permute-start(bf16[40,768]{1,0:T(8,128)(2,1)S(1)} %collective-permute-done.10.refs_1_), channel_id=1, source_target_pairs={{0,2},{1,3},{2,0},{3,1},{4,6},{5,7},{6,4},{7,5},{8,10},{9,11},{10,... | collective-permute-start | bytes 184328 | tf_op jit(solution)/shard_map/ppermute | solution.py:299
  24.9 0.6 %collective-permute-done.12.refs_2_ = bf16[40,768]{1,0:T(8,128)(2,1)S(1)} collective-permute-done((bf16[40,768]{1,0:T(8,128)(2,1)S(1)}, bf16[40,768]{1,0:T(8,128)(2,1)S(1)}, u32[]{:S(2)}, u32[]{:S(2)}) %collective-permute-start.12) | collective-permute-done | bytes 61472 | tf_op jit(solution)/shard_map/ppermute | solution.py:293
  25.5 1.5 %collective-permute-start.13 = (bf16[40,768]{1,0:T(8,128)(2,1)S(1)}, bf16[40,768]{1,0:T(8,128)(2,1)S(1)}, u32[]{:S(2)}, u32[]{:S(2)}) collective-permute-start(bf16[40,768]{1,0:T(8,128)(2,1)S(1)} %collective-permute-done.12.refs_2_), channel_id=1, source_target_pairs={{0,2},{1,3},{2,0},{3,1},{4,6},{5,7},{6,4},{7,5},{8,10},{9,11},{10,... | collective-permute-start | bytes 184328 | tf_op jit(solution)/shard_map/ppermute | solution.py:299
  27.0 1.0 %shard_map.76 = (bf16[120,768]{1,0:T(8,128)(2,1)S(1)}, bf16[120,768]{1,0:T(8,128)(2,1)S(1)}, f32[120,128]{1,0:T(8,128)S(1)}, bf16[120,768]{1,0:T(8,128)(2,1)S(1)}) custom-call(bf16[40,768]{1,0:T(8,128)(2,1)S(1)} %get-tuple-element.43.refs_0_, bf16[40,768]{1,0:T(8,128)(2,1)S(1)} %collective-permute-done.10.refs_1_, ...), custom_call_target="tpu_custom_call" | custom-call | flops 1000000 | bytes 1000 | tf_op jit(solution)/shard_map/pallas_call | solution.py:272
  28.1 0.1 collective-permute-start.15
  28.2 1.4 %collective-permute-start.8 = (bf16[40,768]{1,0:T(8,128)(2,1)S(1)}, bf16[40,768]{1,0:T(8,128)(2,1)S(1)}, u32[]{:S(2)}, u32[]{:S(2)}) collective-permute-start(bf16[40,768]{1,0:T(8,128)(2,1)S(1)} %collective-permute-done.7.own_ref.refs_3_), channel_id=1, source_target_pairs={{0,2},{1,3},{2,0},{3,1},{4,6},{5,7},{6,4},{7,5},{8,10},{9,11},{10,... | collective-permute-start | bytes 184328 | tf_op jit(solution)/shard_map/ppermute | solution.py:299
  29.6 0.1 collective-permute-done.13.refs_2_
  29.7 1.2 %shard_map.77 = (bf16[40,768]{1,0:T(8,128)(2,1)S(1)}, bf16[160,768]{1,0:T(8,128)(2,1)S(1)}, f32[160,128]{1,0:T(8,128)S(1)}, bf16[80,768]{1,0:T(8,128)(2,1)S(1)}, bf16[40,768]{1,0:T(8,128)(2,1)S(1)}) custom-call(bf16[40,768]{1,0:T(8,128)(2,1)S(1)} %collective-permute-done.7.own_ref.refs_3_, bf16[40,768]{1,0:T(8,128)(2,1)S(1)} %collective-permute-done.9.refs_0_, ...), custom_call_target="tpu_custom_call" | custom-call | flops 1000000 | bytes 1000 | tf_op jit(solution)/shard_map/pallas_call | solution.py:272
  31.0 0.5 %collective-permute-start.16 = (bf16[40,768]{1,0:T(8,128)(2,1)S(1)}, bf16[40,768]{1,0:T(8,128)(2,1)S(1)}, u32[]{:S(2)}, u32[]{:S(2)}) collective-permute-start(bf16[40,768]{1,0:T(8,128)(2,1)S(1)} %collective-permute-done.7.own_ref.refs_3_), channel_id=1, source_target_pairs={{0,1},{1,0},{2,3},{3,2},{4,5},{5,4},{6,7},{7,6},{8,9},{9,8},{10,11... | collective-permute-start | bytes 184328 | tf_op jit(solution)/shard_map/ppermute | solution.py:299
  31.5 0.1 collective-permute-start.18
  31.6 1.0 %collective-permute-done.8.refs_4_ = bf16[40,768]{1,0:T(8,128)(2,1)S(1)} collective-permute-done((bf16[40,768]{1,0:T(8,128)(2,1)S(1)}, bf16[40,768]{1,0:T(8,128)(2,1)S(1)}, u32[]{:S(2)}, u32[]{:S(2)}) %collective-permute-start.8) | collective-permute-done | bytes 61472 | tf_op jit(solution)/shard_map/ppermute | solution.py:299
  32.6 0.2 collective-permute-done.18.refs_3_
  32.8 1.4 %shard_map.78 = (bf16[320,768]{1,0:T(8,128)(2,1)S(1)}, f32[320,128]{1,0:T(8,128)S(1)}) custom-call(bf16[120,768]{1,0:T(8,128)(2,1)S(1)} %collective-permute-done.15.refs_0_, bf16[40,768]{1,0:T(8,128)(2,1)S(1)} %collective-permute-done.16.refs_1_, bf16[80,768]{1,0:T(8,128)(2,1)S(1)} %collective-permute-done.17.refs_2_, ...), custom_call_target="tpu_custom_call" | custom-call | flops 1000000 | bytes 1000 | tf_op jit(solution)/shard_map/pallas_call | solution.py:272
  34.1 2.4 %shard_map.79 = bf16[144,768]{1,0:T(8,128)(2,1)} custom-call(s32[1]{0:T(128)} %bitcast.z_ref, bf16[40,768]{1,0:T(8,128)(2,1)S(1)} %collective-permute-done.14.last_ref, bf16[40,768]{1,0:T(8,128)(2,1)S(1)} %get-tuple-element.43.refs_0_, bf16[40,768]{1,0:T(8,128)(2,1)S(1)} %collective-permute-done.10.refs_1_, ...), custom_call_target="tpu_custom_call" | custom-call | flops 1000000 | bytes 1000 | tf_op jit(solution)/shard_map/pallas_call | solution.py:272
  (30 shorter events, 0.2 us)
Async XLA Ops:
  0.0 0.9 %copy-start.4 = (bf16[1,6,24,768]{3,2,1,0:T(8,128)(2,1)S(1)}, bf16[1,6,24,768]{3,2,1,0:T(8,128)(2,1)}, u32[]{:S(2)}) copy-start(bf16[1,6,24,768]{3,2,1,0:T(8,128)(2,1)} %param.7) | copy-start | bytes 663556
  0.9 8.4 %copy-start.5 = (bf16[256,3072]{1,0:T(8,128)(2,1)S(1)}, bf16[256,3072]{1,0:T(8,128)(2,1)}, u32[]{:S(2)}) copy-start(bf16[256,3072]{1,0:T(8,128)(2,1)} %param.9) | copy-start | bytes 4718596
  0.9 13.5 %copy-start.1 = (bf16[768,2304]{1,0:T(8,128)(2,1)S(1)}, bf16[768,2304]{1,0:T(8,128)(2,1)}, u32[]{:S(2)}) copy-start(bf16[768,2304]{1,0:T(8,128)(2,1)} %refs_5_.4) | copy-start | bytes 10616836
  1.2 8.5 %collective-permute-start.1 = (bf16[40,768]{1,0:T(8,128)(2,1)S(1)}, bf16[40,768]{1,0:T(8,128)(2,1)S(1)}, u32[]{:S(2)}, u32[]{:S(2)}) collective-permute-start(bf16[40,768]{1,0:T(8,128)(2,1)S(1)} %get-tuple-element.33), channel_id=1, source_target_pairs={{0,8},{4,12},{8,0},{12,4},{16,24},{20,28},{24,16},{28,20},{1,9},{5... | collective-permute-start | bytes 184328 | tf_op jit(solution)/shard_map/ppermute | solution.py:293
  4.3 6.4 %collective-permute-start.3 = (bf16[40,768]{1,0:T(8,128)(2,1)S(1)}, bf16[40,768]{1,0:T(8,128)(2,1)S(1)}, u32[]{:S(2)}, u32[]{:S(2)}) collective-permute-start(bf16[40,768]{1,0:T(8,128)(2,1)S(1)} %get-tuple-element.35), channel_id=1, source_target_pairs={{0,16},{4,20},{8,24},{12,28},{16,0},{20,4},{24,8},{28,12},{1,17},{... | collective-permute-start | bytes 184328 | tf_op jit(solution)/shard_map/ppermute | solution.py:293
  6.9 6.0 %collective-permute-start.5 = (bf16[40,768]{1,0:T(8,128)(2,1)S(1)}, bf16[40,768]{1,0:T(8,128)(2,1)S(1)}, u32[]{:S(2)}, u32[]{:S(2)}) collective-permute-start(bf16[40,768]{1,0:T(8,128)(2,1)S(1)} %get-tuple-element.36), channel_id=1, source_target_pairs={{0,24},{4,28},{8,16},{12,20},{16,8},{20,12},{24,0},{28,4},{1,25},{... | collective-permute-start | bytes 184328 | tf_op jit(solution)/shard_map/ppermute | solution.py:293
  6.9 8.6 %collective-permute-start = (bf16[40,768]{1,0:T(8,128)(2,1)S(1)}, bf16[40,768]{1,0:T(8,128)(2,1)S(1)}, u32[]{:S(2)}, u32[]{:S(2)}) collective-permute-start(bf16[40,768]{1,0:T(8,128)(2,1)S(1)} %get-tuple-element.32.refs_0_), channel_id=1, source_target_pairs={{0,4},{4,0},{8,12},{12,8},{16,20},{20,16},{24,28},{28,24},{1,5},{5... | collective-permute-start | bytes 184328 | tf_op jit(solution)/shard_map/ppermute | solution.py:296
  9.7 7.5 %copy-start.2 = (bf16[768,768]{1,0:T(8,128)(2,1)S(1)}, bf16[768,768]{1,0:T(8,128)(2,1)}, u32[]{:S(2)}) copy-start(bf16[768,768]{1,0:T(8,128)(2,1)} %refs_6_.2) | copy-start | bytes 3538948
  9.7 5.8 %collective-permute-start.2 = (bf16[40,768]{1,0:T(8,128)(2,1)S(1)}, bf16[40,768]{1,0:T(8,128)(2,1)S(1)}, u32[]{:S(2)}, u32[]{:S(2)}) collective-permute-start(bf16[40,768]{1,0:T(8,128)(2,1)S(1)} %collective-permute-done.1.refs_1_), channel_id=1, source_target_pairs={{0,4},{4,0},{8,12},{12,8},{16,20},{20,16},{24,28},{28,24},{1,5},{5... | collective-permute-start | bytes 184328 | tf_op jit(solution)/shard_map/ppermute | solution.py:296
  10.7 4.8 %collective-permute-start.4 = (bf16[40,768]{1,0:T(8,128)(2,1)S(1)}, bf16[40,768]{1,0:T(8,128)(2,1)S(1)}, u32[]{:S(2)}, u32[]{:S(2)}) collective-permute-start(bf16[40,768]{1,0:T(8,128)(2,1)S(1)} %collective-permute-done.3.refs_2_), channel_id=1, source_target_pairs={{0,4},{4,0},{8,12},{12,8},{16,20},{20,16},{24,28},{28,24},{1,5},{5... | collective-permute-start | bytes 184328 | tf_op jit(solution)/shard_map/ppermute | solution.py:296
  12.9 4.2 %collective-permute-start.6 = (bf16[40,768]{1,0:T(8,128)(2,1)S(1)}, bf16[40,768]{1,0:T(8,128)(2,1)S(1)}, u32[]{:S(2)}, u32[]{:S(2)}) collective-permute-start(bf16[40,768]{1,0:T(8,128)(2,1)S(1)} %collective-permute-done.5.refs_3_), channel_id=1, source_target_pairs={{0,4},{4,0},{8,12},{12,8},{16,20},{20,16},{24,28},{28,24},{1,5},{5... | collective-permute-start | bytes 184328 | tf_op jit(solution)/shard_map/ppermute | solution.py:296
  17.1 9.9 %copy-start = (bf16[768,2304]{1,0:T(8,128)(2,1)S(1)}, bf16[768,2304]{1,0:T(8,128)(2,1)}, u32[]{:S(2)}) copy-start(bf16[768,2304]{1,0:T(8,128)(2,1)} %refs_6_.3) | copy-start | bytes 10616836
  19.1 5.2 %collective-permute-start.10 = (bf16[40,768]{1,0:T(8,128)(2,1)S(1)}, bf16[40,768]{1,0:T(8,128)(2,1)S(1)}, u32[]{:S(2)}, u32[]{:S(2)}) collective-permute-start(bf16[40,768]{1,0:T(8,128)(2,1)S(1)} %get-tuple-element.44), channel_id=1, source_target_pairs={{0,8},{4,12},{8,0},{12,4},{16,24},{20,28},{24,16},{28,20},{1,9},{5... | collective-permute-start | bytes 184328 | tf_op jit(solution)/shard_map/ppermute | solution.py:293
  19.4 6.1 %collective-permute-start.12 = (bf16[40,768]{1,0:T(8,128)(2,1)S(1)}, bf16[40,768]{1,0:T(8,128)(2,1)S(1)}, u32[]{:S(2)}, u32[]{:S(2)}) collective-permute-start(bf16[40,768]{1,0:T(8,128)(2,1)S(1)} %get-tuple-element.45), channel_id=1, source_target_pairs={{0,24},{4,28},{8,16},{12,20},{16,8},{20,12},{24,0},{28,4},{1,25},{... | collective-permute-start | bytes 184328 | tf_op jit(solution)/shard_map/ppermute | solution.py:293
  22.3 5.9 %collective-permute-start.7 = (bf16[40,768]{1,0:T(8,128)(2,1)S(1)}, bf16[40,768]{1,0:T(8,128)(2,1)S(1)}, u32[]{:S(2)}, u32[]{:S(2)}) collective-permute-start(bf16[40,768]{1,0:T(8,128)(2,1)S(1)} %get-tuple-element.42), channel_id=1, source_target_pairs={{0,16},{4,20},{8,24},{12,28},{16,0},{20,4},{24,8},{28,12},{1,17},{... | collective-permute-start | bytes 184328 | tf_op jit(solution)/shard_map/ppermute | solution.py:293
  22.8 6.8 %collective-permute-start.9 = (bf16[40,768]{1,0:T(8,128)(2,1)S(1)}, bf16[40,768]{1,0:T(8,128)(2,1)S(1)}, u32[]{:S(2)}, u32[]{:S(2)}) collective-permute-start(bf16[40,768]{1,0:T(8,128)(2,1)S(1)} %get-tuple-element.43.refs_0_), channel_id=1, source_target_pairs={{0,2},{1,3},{2,0},{3,1},{4,6},{5,7},{6,4},{7,5},{8,10},{9,11},{10,... | collective-permute-start | bytes 184328 | tf_op jit(solution)/shard_map/ppermute | solution.py:299
  24.3 5.3 %collective-permute-start.11 = (bf16[40,768]{1,0:T(8,128)(2,1)S(1)}, bf16[40,768]{1,0:T(8,128)(2,1)S(1)}, u32[]{:S(2)}, u32[]{:S(2)}) collective-permute-start(bf16[40,768]{1,0:T(8,128)(2,1)S(1)} %collective-permute-done.10.refs_1_), channel_id=1, source_target_pairs={{0,2},{1,3},{2,0},{3,1},{4,6},{5,7},{6,4},{7,5},{8,10},{9,11},{10,... | collective-permute-start | bytes 184328 | tf_op jit(solution)/shard_map/ppermute | solution.py:299
  25.5 4.2 %collective-permute-start.13 = (bf16[40,768]{1,0:T(8,128)(2,1)S(1)}, bf16[40,768]{1,0:T(8,128)(2,1)S(1)}, u32[]{:S(2)}, u32[]{:S(2)}) collective-permute-start(bf16[40,768]{1,0:T(8,128)(2,1)S(1)} %collective-permute-done.12.refs_2_), channel_id=1, source_target_pairs={{0,2},{1,3},{2,0},{3,1},{4,6},{5,7},{6,4},{7,5},{8,10},{9,11},{10,... | collective-permute-start | bytes 184328 | tf_op jit(solution)/shard_map/ppermute | solution.py:299
  28.1 4.7 %collective-permute-start.15 = (bf16[120,768]{1,0:T(8,128)(2,1)S(1)}, bf16[120,768]{1,0:T(8,128)(2,1)S(1)}, u32[]{:S(2)}, u32[]{:S(2)}) collective-permute-start(bf16[120,768]{1,0:T(8,128)(2,1)S(1)} %get-tuple-element.54), channel_id=1, source_target_pairs={{0,1},{1,0},{2,3},{3,2},{4,5},{5,4},{6,7},{7,6},{8,9},{9,8},{10,11... | collective-permute-start | bytes 552968 | tf_op jit(solution)/shard_map/ppermute | solution.py:299
  28.2 4.4 %collective-permute-start.8 = (bf16[40,768]{1,0:T(8,128)(2,1)S(1)}, bf16[40,768]{1,0:T(8,128)(2,1)S(1)}, u32[]{:S(2)}, u32[]{:S(2)}) collective-permute-start(bf16[40,768]{1,0:T(8,128)(2,1)S(1)} %collective-permute-done.7.own_ref.refs_3_), channel_id=1, source_target_pairs={{0,2},{1,3},{2,0},{3,1},{4,6},{5,7},{6,4},{7,5},{8,10},{9,11},{10,... | collective-permute-start | bytes 184328 | tf_op jit(solution)/shard_map/ppermute | solution.py:299
  30.9 1.8 %collective-permute-start.17 = (bf16[80,768]{1,0:T(8,128)(2,1)S(1)}, bf16[80,768]{1,0:T(8,128)(2,1)S(1)}, u32[]{:S(2)}, u32[]{:S(2)}) collective-permute-start(bf16[80,768]{1,0:T(8,128)(2,1)S(1)} %get-tuple-element.55), channel_id=1, source_target_pairs={{0,1},{1,0},{2,3},{3,2},{4,5},{5,4},{6,7},{7,6},{8,9},{9,8},{10,11... | collective-permute-start | bytes 368648 | tf_op jit(solution)/shard_map/ppermute | solution.py:299
  31.0 1.6 %collective-permute-start.16 = (bf16[40,768]{1,0:T(8,128)(2,1)S(1)}, bf16[40,768]{1,0:T(8,128)(2,1)S(1)}, u32[]{:S(2)}, u32[]{:S(2)}) collective-permute-start(bf16[40,768]{1,0:T(8,128)(2,1)S(1)} %collective-permute-done.7.own_ref.refs_3_), channel_id=1, source_target_pairs={{0,1},{1,0},{2,3},{3,2},{4,5},{5,4},{6,7},{7,6},{8,9},{9,8},{10,11... | collective-permute-start | bytes 184328 | tf_op jit(solution)/shard_map/ppermute | solution.py:299
  31.5 1.2 %collective-permute-start.18 = (bf16[40,768]{1,0:T(8,128)(2,1)S(1)}, bf16[40,768]{1,0:T(8,128)(2,1)S(1)}, u32[]{:S(2)}, u32[]{:S(2)}) collective-permute-start(bf16[40,768]{1,0:T(8,128)(2,1)S(1)} %get-tuple-element.56), channel_id=1, source_target_pairs={{0,1},{1,0},{2,3},{3,2},{4,5},{5,4},{6,7},{7,6},{8,9},{9,8},{10,11... | collective-permute-start | bytes 184328 | tf_op jit(solution)/shard_map/ppermute | solution.py:299
  32.6 1.5 %collective-permute-start.14 = (bf16[40,768]{1,0:T(8,128)(2,1)S(1)}, bf16[40,768]{1,0:T(8,128)(2,1)S(1)}, u32[]{:S(2)}, u32[]{:S(2)}) collective-permute-start(bf16[40,768]{1,0:T(8,128)(2,1)S(1)} %collective-permute-done.8.refs_4_), channel_id=1, source_target_pairs={{0,1},{1,0},{2,3},{3,2},{4,5},{5,4},{6,7},{7,6},{8,9},{9,8},{10,11... | collective-permute-start | bytes 184328 | tf_op jit(solution)/shard_map/ppermute | solution.py:299
  32.8 1.4 %copy-start.3 = (bf16[768,768]{1,0:T(8,128)(2,1)S(1)}, bf16[768,768]{1,0:T(8,128)(2,1)}, u32[]{:S(2)}) copy-start(bf16[768,768]{1,0:T(8,128)(2,1)} %refs_7_.1) | copy-start | bytes 3538948

commit v10 on v9

--- a/solution.py
+++ b/solution.py
@@ -197,9 +197,8 @@
 
 def bin_own_kernel(count, *refs):
     chunks, (mod_ref, w_ref, q_ref, v_ref, s_ref, *parts) = refs[:count], refs[count:]
-    rows = stacked(chunks)
-    split_rows(rows, parts)
-    normed = norm_rows(rows, mod_ref, 1)
+    normed = norm_rows(stacked(chunks), mod_ref, 1)
+    split_rows(normed.astype(F32), parts)
     project(normed, w_ref, 0, q_ref, HD**-0.5)
     key_scores(q_ref[...].astype(F32), normed, w_ref, s_ref)
     project(normed, w_ref, 2, v_ref)
@@ -207,11 +206,9 @@
 
 def bin_early_kernel(count, own_ref, *refs):
     chunks, (q_ref, mod_ref, w_ref, q2_ref, v_ref, s_ref, *parts) = refs[:count], refs[count:]
-    rows = stacked(chunks)
-    split_rows(rows, parts)
-    rows = jnp.concatenate([rows, own_ref[...].astype(F32)], axis=0)
-    normed = norm_rows(rows, mod_ref, 1)
     split = q_ref.shape[0]
+    normed = norm_rows(stacked((*chunks, own_ref)), mod_ref, 1)
+    split_rows(normed.astype(F32)[:split], parts)
     q2 = jnp.dot(normed, w_ref[:, :D], preferred_element_type=F32)[split:] * HD**-0.5
     q2_ref[...] = q2.astype(BF)
     query = jnp.concatenate([q_ref[...].astype(F32), q2_ref[...].astype(F32)], axis=0)
@@ -221,7 +218,11 @@
 
 def bin_late_kernel(count, *refs):
     chunks, (q_ref, q2_ref, mod_ref, w_ref, v_ref, s_ref) = refs[:count], refs[count:]
-    normed = norm_rows(stacked(chunks), mod_ref, 1)
+    core_ref, core_last_ref, *far, last_ref = chunks
+    fresh = norm_rows(stacked((core_last_ref, last_ref)), mod_ref, 1).astype(F32)
+    pad = last_ref.shape[0]
+    pieces = [core_ref[...].astype(F32), fresh[:pad], stacked(far), fresh[pad:]]
+    normed = jnp.concatenate(pieces, axis=0).astype(BF)
     q = stacked((q_ref, q2_ref))
     key_scores(jnp.concatenate([q, q], axis=0), normed, w_ref, s_ref)
     project(normed, w_ref, 2, v_ref)

time: 36.7 us -> 36.6 us (level)
  no operation moved by 1% of the time
where the time goes in v10:
time: 36.6 us; the launch traced here: 36.4 us
  starting transfers between devices  20.2 us (55%)
  Pallas kernels  9.15 us (25%)
  waiting for transfers between devices  4.9 us (13%)
  local copies, waits for them, and re-layouts  0.97 us (3%)
  between operations  0.82 us (2%)
    ppermute x6, starting transfers between devices, over_group(): lax.ppermute(x, 'seq', [(i, i ^ 2 * partner(m, groups)) for i in range(ow...  9.32 us
    pallas_call x7, Pallas kernels, call(): pl.pallas_call(kernel, out_shape=[jax.ShapeDtypeStruct(*o) for o in outs]...  9.15 us
    ppermute x9, starting transfers between devices, over_bin(): return lax.ppermute(x, 'bin', [(i, i ^ m) for i in range(4)])  5.8 us
    ppermute x4, starting transfers between devices, over_pair(): return lax.ppermute(x, 'seq', [(i, i ^ 1) for i in range(owners)])  5.07 us
    ppermute x6, waiting for transfers between devices, over_group(): lax.ppermute(x, 'seq', [(i, i ^ 2 * partner(m, groups)) for i in range(ow...  1.94 us
    ppermute x4, waiting for transfers between devices, over_pair(): return lax.ppermute(x, 'seq', [(i, i ^ 1) for i in range(owners)])  1.63 us
    ppermute x9, waiting for transfers between devices, over_bin(): return lax.ppermute(x, 'bin', [(i, i ^ m) for i in range(4)])  1.33 us
    unnamed x12, local copies, waits for them, and re-layouts  0.95 us
  transfers between devices with their start and end apart: 19, of which 7 were waited for; matrix products, arithmetic and copies ran while one was open for 1% of the time, Pallas kernels for 13%

profile of v10, /device:TPU:0, one launch (start us, length us, event | category | flops | bytes accessed | tf_op | source)
XLA Modules:
  0.0 36.4 jit_solution(12698840848648540161)
XLA Ops:
  0.0 0.9 %copy-done.4 = bf16[1,6,24,768]{3,2,1,0:T(8,128)(2,1)S(1)} copy-done((bf16[1,6,24,768]{3,2,1,0:T(8,128)(2,1)S(1)}, bf16[1,6,24,768]{3,2,1,0:T(8,128)(2,1)}, u32[]{:S(2)}) %copy-start.4) | copy-done | bytes 221208
  0.9 0.3 shard_map.73
  1.2 3.1 %collective-permute-start.1 = (bf16[40,768]{1,0:T(8,128)(2,1)S(1)}, bf16[40,768]{1,0:T(8,128)(2,1)S(1)}, u32[]{:S(2)}, u32[]{:S(2)}) collective-permute-start(bf16[40,768]{1,0:T(8,128)(2,1)S(1)} %get-tuple-element.33), channel_id=1, source_target_pairs={{0,8},{4,12},{8,0},{12,4},{16,24},{20,28},{24,16},{28,20},{1,9},{5... | collective-permute-start | bytes 184328 | tf_op jit(solution)/shard_map/ppermute | solution.py:294
  4.3 2.6 %collective-permute-start.3 = (bf16[40,768]{1,0:T(8,128)(2,1)S(1)}, bf16[40,768]{1,0:T(8,128)(2,1)S(1)}, u32[]{:S(2)}, u32[]{:S(2)}) collective-permute-start(bf16[40,768]{1,0:T(8,128)(2,1)S(1)} %get-tuple-element.35), channel_id=1, source_target_pairs={{0,16},{4,20},{8,24},{12,28},{16,0},{20,4},{24,8},{28,12},{1,17},{... | collective-permute-start | bytes 184328 | tf_op jit(solution)/shard_map/ppermute | solution.py:294
  6.9 1.7 %collective-permute-start = (bf16[40,768]{1,0:T(8,128)(2,1)S(1)}, bf16[40,768]{1,0:T(8,128)(2,1)S(1)}, u32[]{:S(2)}, u32[]{:S(2)}) collective-permute-start(bf16[40,768]{1,0:T(8,128)(2,1)S(1)} %get-tuple-element.32.refs_0_), channel_id=1, source_target_pairs={{0,4},{4,0},{8,12},{12,8},{16,20},{20,16},{24,28},{28,24},{1,5},{5... | collective-permute-start | bytes 184328 | tf_op jit(solution)/shard_map/ppermute | solution.py:297
  9.4 0.3 fusion
  9.7 0.4 %collective-permute-start.2 = (bf16[40,768]{1,0:T(8,128)(2,1)S(1)}, bf16[40,768]{1,0:T(8,128)(2,1)S(1)}, u32[]{:S(2)}, u32[]{:S(2)}) collective-permute-start(bf16[40,768]{1,0:T(8,128)(2,1)S(1)} %collective-permute-done.1.refs_1_), channel_id=1, source_target_pairs={{0,4},{4,0},{8,12},{12,8},{16,20},{20,16},{24,28},{28,24},{1,5},{5... | collective-permute-start | bytes 184328 | tf_op jit(solution)/shard_map/ppermute | solution.py:297
  10.1 0.6 %collective-permute-done.3.refs_2_ = bf16[40,768]{1,0:T(8,128)(2,1)S(1)} collective-permute-done((bf16[40,768]{1,0:T(8,128)(2,1)S(1)}, bf16[40,768]{1,0:T(8,128)(2,1)S(1)}, u32[]{:S(2)}, u32[]{:S(2)}) %collective-permute-start.3) | collective-permute-done | bytes 61472 | tf_op jit(solution)/shard_map/ppermute | solution.py:294
  10.7 1.5 %collective-permute-start.4 = (bf16[40,768]{1,0:T(8,128)(2,1)S(1)}, bf16[40,768]{1,0:T(8,128)(2,1)S(1)}, u32[]{:S(2)}, u32[]{:S(2)}) collective-permute-start(bf16[40,768]{1,0:T(8,128)(2,1)S(1)} %collective-permute-done.3.refs_2_), channel_id=1, source_target_pairs={{0,4},{4,0},{8,12},{12,8},{16,20},{20,16},{24,28},{28,24},{1,5},{5... | collective-permute-start | bytes 184328 | tf_op jit(solution)/shard_map/ppermute | solution.py:297
  12.1 0.8 %collective-permute-done.5.refs_3_ = bf16[40,768]{1,0:T(8,128)(2,1)S(1)} collective-permute-done((bf16[40,768]{1,0:T(8,128)(2,1)S(1)}, bf16[40,768]{1,0:T(8,128)(2,1)S(1)}, u32[]{:S(2)}, u32[]{:S(2)}) %collective-permute-start.5) | collective-permute-done | bytes 61472 | tf_op jit(solution)/shard_map/ppermute | solution.py:294
  12.9 1.5 %collective-permute-start.6 = (bf16[40,768]{1,0:T(8,128)(2,1)S(1)}, bf16[40,768]{1,0:T(8,128)(2,1)S(1)}, u32[]{:S(2)}, u32[]{:S(2)}) collective-permute-start(bf16[40,768]{1,0:T(8,128)(2,1)S(1)} %collective-permute-done.5.refs_3_), channel_id=1, source_target_pairs={{0,4},{4,0},{8,12},{12,8},{16,20},{20,16},{24,28},{28,24},{1,5},{5... | collective-permute-start | bytes 184328 | tf_op jit(solution)/shard_map/ppermute | solution.py:297
  14.4 1.1 %shard_map.74 = (bf16[144,768]{1,0:T(8,128)(2,1)S(1)}, bf16[144,768]{1,0:T(8,128)(2,1)S(1)}, bf16[144,768]{1,0:T(8,128)(2,1)S(1)}, bf16[144,768]{1,0:T(8,128)(2,1)S(1)}) custom-call(bf16[40,768]{1,0:T(8,128)(2,1)S(1)} %get-tuple-element.32.refs_0_, bf16[40,768]{1,0:T(8,128)(2,1)S(1)} %collective-permute-done.1.refs_1_, ...), custom_call_target="tpu_custom_call" | custom-call | flops 1000000 | bytes 1000 | tf_op jit(solution)/shard_map/pallas_call | solution.py:273
  15.5 1.6 %collective-permute-done.6.refs_3_ = bf16[40,768]{1,0:T(8,128)(2,1)S(1)} collective-permute-done((bf16[40,768]{1,0:T(8,128)(2,1)S(1)}, bf16[40,768]{1,0:T(8,128)(2,1)S(1)}, u32[]{:S(2)}, u32[]{:S(2)}) %collective-permute-start.6) | collective-permute-done | bytes 61472 | tf_op jit(solution)/shard_map/ppermute | solution.py:297
  17.1 2.0 %shard_map.75 = (bf16[40,768]{1,0:T(8,128)(2,1)S(1)}, bf16[40,768]{1,0:T(8,128)(2,1)S(1)}, bf16[40,768]{1,0:T(8,128)(2,1)S(1)}, bf16[40,768]{1,0:T(8,128)(2,1)S(1)}) custom-call(bf16[40,768]{1,0:T(8,128)(2,1)S(1)} %collective-permute-done.refs_0_, bf16[40,768]{1,0:T(8,128)(2,1)S(1)} %collective-permute-done.2.refs_1_, ...), custom_call_target="tpu_custom_call" | custom-call | flops 1000000 | bytes 1000 | tf_op jit(solution)/shard_map/pallas_call | solution.py:273
  19.1 0.3 collective-permute-start.10
  19.4 2.9 %collective-permute-start.12 = (bf16[40,768]{1,0:T(8,128)(2,1)S(1)}, bf16[40,768]{1,0:T(8,128)(2,1)S(1)}, u32[]{:S(2)}, u32[]{:S(2)}) collective-permute-start(bf16[40,768]{1,0:T(8,128)(2,1)S(1)} %get-tuple-element.45), channel_id=1, source_target_pairs={{0,24},{4,28},{8,16},{12,20},{16,8},{20,12},{24,0},{28,4},{1,25},{... | collective-permute-start | bytes 184328 | tf_op jit(solution)/shard_map/ppermute | solution.py:294
  22.3 0.5 %collective-permute-start.7 = (bf16[40,768]{1,0:T(8,128)(2,1)S(1)}, bf16[40,768]{1,0:T(8,128)(2,1)S(1)}, u32[]{:S(2)}, u32[]{:S(2)}) collective-permute-start(bf16[40,768]{1,0:T(8,128)(2,1)S(1)} %get-tuple-element.42), channel_id=1, source_target_pairs={{0,16},{4,20},{8,24},{12,28},{16,0},{20,4},{24,8},{28,12},{1,17},{... | collective-permute-start | bytes 184328 | tf_op jit(solution)/shard_map/ppermute | solution.py:294
  22.8 1.5 %collective-permute-start.9 = (bf16[40,768]{1,0:T(8,128)(2,1)S(1)}, bf16[40,768]{1,0:T(8,128)(2,1)S(1)}, u32[]{:S(2)}, u32[]{:S(2)}) collective-permute-start(bf16[40,768]{1,0:T(8,128)(2,1)S(1)} %get-tuple-element.43.refs_0_), channel_id=1, source_target_pairs={{0,2},{1,3},{2,0},{3,1},{4,6},{5,7},{6,4},{7,5},{8,10},{9,11},{10,... | collective-permute-start | bytes 184328 | tf_op jit(solution)/shard_map/ppermute | solution.py:300
  24.3 0.6 %collective-permute-start.11 = (bf16[40,768]{1,0:T(8,128)(2,1)S(1)}, bf16[40,768]{1,0:T(8,128)(2,1)S(1)}, u32[]{:S(2)}, u32[]{:S(2)}) collective-permute-start(bf16[40,768]{1,0:T(8,128)(2,1)S(1)} %collective-permute-done.10.refs_1_), channel_id=1, source_target_pairs={{0,2},{1,3},{2,0},{3,1},{4,6},{5,7},{6,4},{7,5},{8,10},{9,11},{10,... | collective-permute-start | bytes 184328 | tf_op jit(solution)/shard_map/ppermute | solution.py:300
  24.9 0.6 %collective-permute-done.12.refs_2_ = bf16[40,768]{1,0:T(8,128)(2,1)S(1)} collective-permute-done((bf16[40,768]{1,0:T(8,128)(2,1)S(1)}, bf16[40,768]{1,0:T(8,128)(2,1)S(1)}, u32[]{:S(2)}, u32[]{:S(2)}) %collective-permute-start.12) | collective-permute-done | bytes 61472 | tf_op jit(solution)/shard_map/ppermute | solution.py:294
  25.5 1.5 %collective-permute-start.13 = (bf16[40,768]{1,0:T(8,128)(2,1)S(1)}, bf16[40,768]{1,0:T(8,128)(2,1)S(1)}, u32[]{:S(2)}, u32[]{:S(2)}) collective-permute-start(bf16[40,768]{1,0:T(8,128)(2,1)S(1)} %collective-permute-done.12.refs_2_), channel_id=1, source_target_pairs={{0,2},{1,3},{2,0},{3,1},{4,6},{5,7},{6,4},{7,5},{8,10},{9,11},{10,... | collective-permute-start | bytes 184328 | tf_op jit(solution)/shard_map/ppermute | solution.py:300
  27.0 1.0 %shard_map.76 = (bf16[120,768]{1,0:T(8,128)(2,1)S(1)}, bf16[120,768]{1,0:T(8,128)(2,1)S(1)}, f32[120,128]{1,0:T(8,128)S(1)}, bf16[120,768]{1,0:T(8,128)(2,1)S(1)}) custom-call(bf16[40,768]{1,0:T(8,128)(2,1)S(1)} %get-tuple-element.43.refs_0_, bf16[40,768]{1,0:T(8,128)(2,1)S(1)} %collective-permute-done.10.refs_1_, ...), custom_call_target="tpu_custom_call" | custom-call | flops 1000000 | bytes 1000 | tf_op jit(solution)/shard_map/pallas_call | solution.py:273
  28.1 0.1 collective-permute-start.15
  28.2 1.4 %collective-permute-start.8 = (bf16[40,768]{1,0:T(8,128)(2,1)S(1)}, bf16[40,768]{1,0:T(8,128)(2,1)S(1)}, u32[]{:S(2)}, u32[]{:S(2)}) collective-permute-start(bf16[40,768]{1,0:T(8,128)(2,1)S(1)} %collective-permute-done.7.own_ref.refs_3_), channel_id=1, source_target_pairs={{0,2},{1,3},{2,0},{3,1},{4,6},{5,7},{6,4},{7,5},{8,10},{9,11},{10,... | collective-permute-start | bytes 184328 | tf_op jit(solution)/shard_map/ppermute | solution.py:300
  29.6 0.1 collective-permute-done.13.refs_2_
  29.7 1.2 %shard_map.77 = (bf16[40,768]{1,0:T(8,128)(2,1)S(1)}, bf16[160,768]{1,0:T(8,128)(2,1)S(1)}, f32[160,128]{1,0:T(8,128)S(1)}, bf16[80,768]{1,0:T(8,128)(2,1)S(1)}, bf16[40,768]{1,0:T(8,128)(2,1)S(1)}) custom-call(bf16[40,768]{1,0:T(8,128)(2,1)S(1)} %collective-permute-done.7.own_ref.refs_3_, bf16[40,768]{1,0:T(8,128)(2,1)S(1)} %collective-permute-done.9.refs_0_, ...), custom_call_target="tpu_custom_call" | custom-call | flops 1000000 | bytes 1000 | tf_op jit(solution)/shard_map/pallas_call | solution.py:273
  31.0 0.5 %collective-permute-start.16 = (bf16[40,768]{1,0:T(8,128)(2,1)S(1)}, bf16[40,768]{1,0:T(8,128)(2,1)S(1)}, u32[]{:S(2)}, u32[]{:S(2)}) collective-permute-start(bf16[40,768]{1,0:T(8,128)(2,1)S(1)} %collective-permute-done.7.own_ref.refs_3_), channel_id=1, source_target_pairs={{0,1},{1,0},{2,3},{3,2},{4,5},{5,4},{6,7},{7,6},{8,9},{9,8},{10,11... | collective-permute-start | bytes 184328 | tf_op jit(solution)/shard_map/ppermute | solution.py:300
  31.5 0.1 collective-permute-start.18
  31.6 1.0 %collective-permute-done.8.refs_4_ = bf16[40,768]{1,0:T(8,128)(2,1)S(1)} collective-permute-done((bf16[40,768]{1,0:T(8,128)(2,1)S(1)}, bf16[40,768]{1,0:T(8,128)(2,1)S(1)}, u32[]{:S(2)}, u32[]{:S(2)}) %collective-permute-start.8) | collective-permute-done | bytes 61472 | tf_op jit(solution)/shard_map/ppermute | solution.py:300
  32.6 0.2 collective-permute-done.18.refs_3_
  32.8 1.3 %shard_map.78 = (bf16[320,768]{1,0:T(8,128)(2,1)S(1)}, f32[320,128]{1,0:T(8,128)S(1)}) custom-call(bf16[120,768]{1,0:T(8,128)(2,1)S(1)} %collective-permute-done.15.refs_0_, bf16[40,768]{1,0:T(8,128)(2,1)S(1)} %collective-permute-done.16.refs_1_, bf16[80,768]{1,0:T(8,128)(2,1)S(1)} %collective-permute-done.17.refs_2_, ...), custom_call_target="tpu_custom_call" | custom-call | flops 1000000 | bytes 1000 | tf_op jit(solution)/shard_map/pallas_call | solution.py:273
  34.0 2.4 %shard_map.79 = bf16[144,768]{1,0:T(8,128)(2,1)} custom-call(s32[1]{0:T(128)} %bitcast.z_ref, bf16[40,768]{1,0:T(8,128)(2,1)S(1)} %collective-permute-done.14.last_ref, bf16[40,768]{1,0:T(8,128)(2,1)S(1)} %get-tuple-element.43.refs_0_, bf16[40,768]{1,0:T(8,128)(2,1)S(1)} %collective-permute-done.10.refs_1_, ...), custom_call_target="tpu_custom_call" | custom-call | flops 1000000 | bytes 1000 | tf_op jit(solution)/shard_map/pallas_call | solution.py:273
  (30 shorter events, 0.2 us)
Async XLA Ops:
  0.0 0.9 %copy-start.4 = (bf16[1,6,24,768]{3,2,1,0:T(8,128)(2,1)S(1)}, bf16[1,6,24,768]{3,2,1,0:T(8,128)(2,1)}, u32[]{:S(2)}) copy-start(bf16[1,6,24,768]{3,2,1,0:T(8,128)(2,1)} %param.7) | copy-start | bytes 663556
  0.9 8.4 %copy-start.5 = (bf16[256,3072]{1,0:T(8,128)(2,1)S(1)}, bf16[256,3072]{1,0:T(8,128)(2,1)}, u32[]{:S(2)}) copy-start(bf16[256,3072]{1,0:T(8,128)(2,1)} %param.9) | copy-start | bytes 4718596
  0.9 13.5 %copy-start.1 = (bf16[768,2304]{1,0:T(8,128)(2,1)S(1)}, bf16[768,2304]{1,0:T(8,128)(2,1)}, u32[]{:S(2)}) copy-start(bf16[768,2304]{1,0:T(8,128)(2,1)} %refs_5_.4) | copy-start | bytes 10616836
  1.2 8.5 %collective-permute-start.1 = (bf16[40,768]{1,0:T(8,128)(2,1)S(1)}, bf16[40,768]{1,0:T(8,128)(2,1)S(1)}, u32[]{:S(2)}, u32[]{:S(2)}) collective-permute-start(bf16[40,768]{1,0:T(8,128)(2,1)S(1)} %get-tuple-element.33), channel_id=1, source_target_pairs={{0,8},{4,12},{8,0},{12,4},{16,24},{20,28},{24,16},{28,20},{1,9},{5... | collective-permute-start | bytes 184328 | tf_op jit(solution)/shard_map/ppermute | solution.py:294
  4.3 6.4 %collective-permute-start.3 = (bf16[40,768]{1,0:T(8,128)(2,1)S(1)}, bf16[40,768]{1,0:T(8,128)(2,1)S(1)}, u32[]{:S(2)}, u32[]{:S(2)}) collective-permute-start(bf16[40,768]{1,0:T(8,128)(2,1)S(1)} %get-tuple-element.35), channel_id=1, source_target_pairs={{0,16},{4,20},{8,24},{12,28},{16,0},{20,4},{24,8},{28,12},{1,17},{... | collective-permute-start | bytes 184328 | tf_op jit(solution)/shard_map/ppermute | solution.py:294
  6.9 6.0 %collective-permute-start.5 = (bf16[40,768]{1,0:T(8,128)(2,1)S(1)}, bf16[40,768]{1,0:T(8,128)(2,1)S(1)}, u32[]{:S(2)}, u32[]{:S(2)}) collective-permute-start(bf16[40,768]{1,0:T(8,128)(2,1)S(1)} %get-tuple-element.36), channel_id=1, source_target_pairs={{0,24},{4,28},{8,16},{12,20},{16,8},{20,12},{24,0},{28,4},{1,25},{... | collective-permute-start | bytes 184328 | tf_op jit(solution)/shard_map/ppermute | solution.py:294
  6.9 8.6 %collective-permute-start = (bf16[40,768]{1,0:T(8,128)(2,1)S(1)}, bf16[40,768]{1,0:T(8,128)(2,1)S(1)}, u32[]{:S(2)}, u32[]{:S(2)}) collective-permute-start(bf16[40,768]{1,0:T(8,128)(2,1)S(1)} %get-tuple-element.32.refs_0_), channel_id=1, source_target_pairs={{0,4},{4,0},{8,12},{12,8},{16,20},{20,16},{24,28},{28,24},{1,5},{5... | collective-permute-start | bytes 184328 | tf_op jit(solution)/shard_map/ppermute | solution.py:297
  9.7 7.5 %copy-start.2 = (bf16[768,768]{1,0:T(8,128)(2,1)S(1)}, bf16[768,768]{1,0:T(8,128)(2,1)}, u32[]{:S(2)}) copy-start(bf16[768,768]{1,0:T(8,128)(2,1)} %refs_6_.2) | copy-start | bytes 3538948
  9.7 5.8 %collective-permute-start.2 = (bf16[40,768]{1,0:T(8,128)(2,1)S(1)}, bf16[40,768]{1,0:T(8,128)(2,1)S(1)}, u32[]{:S(2)}, u32[]{:S(2)}) collective-permute-start(bf16[40,768]{1,0:T(8,128)(2,1)S(1)} %collective-permute-done.1.refs_1_), channel_id=1, source_target_pairs={{0,4},{4,0},{8,12},{12,8},{16,20},{20,16},{24,28},{28,24},{1,5},{5... | collective-permute-start | bytes 184328 | tf_op jit(solution)/shard_map/ppermute | solution.py:297
  10.7 4.8 %collective-permute-start.4 = (bf16[40,768]{1,0:T(8,128)(2,1)S(1)}, bf16[40,768]{1,0:T(8,128)(2,1)S(1)}, u32[]{:S(2)}, u32[]{:S(2)}) collective-permute-start(bf16[40,768]{1,0:T(8,128)(2,1)S(1)} %collective-permute-done.3.refs_2_), channel_id=1, source_target_pairs={{0,4},{4,0},{8,12},{12,8},{16,20},{20,16},{24,28},{28,24},{1,5},{5... | collective-permute-start | bytes 184328 | tf_op jit(solution)/shard_map/ppermute | solution.py:297
  12.9 4.2 %collective-permute-start.6 = (bf16[40,768]{1,0:T(8,128)(2,1)S(1)}, bf16[40,768]{1,0:T(8,128)(2,1)S(1)}, u32[]{:S(2)}, u32[]{:S(2)}) collective-permute-start(bf16[40,768]{1,0:T(8,128)(2,1)S(1)} %collective-permute-done.5.refs_3_), channel_id=1, source_target_pairs={{0,4},{4,0},{8,12},{12,8},{16,20},{20,16},{24,28},{28,24},{1,5},{5... | collective-permute-start | bytes 184328 | tf_op jit(solution)/shard_map/ppermute | solution.py:297
  17.1 9.9 %copy-start = (bf16[768,2304]{1,0:T(8,128)(2,1)S(1)}, bf16[768,2304]{1,0:T(8,128)(2,1)}, u32[]{:S(2)}) copy-start(bf16[768,2304]{1,0:T(8,128)(2,1)} %refs_6_.3) | copy-start | bytes 10616836
  19.1 5.2 %collective-permute-start.10 = (bf16[40,768]{1,0:T(8,128)(2,1)S(1)}, bf16[40,768]{1,0:T(8,128)(2,1)S(1)}, u32[]{:S(2)}, u32[]{:S(2)}) collective-permute-start(bf16[40,768]{1,0:T(8,128)(2,1)S(1)} %get-tuple-element.44), channel_id=1, source_target_pairs={{0,8},{4,12},{8,0},{12,4},{16,24},{20,28},{24,16},{28,20},{1,9},{5... | collective-permute-start | bytes 184328 | tf_op jit(solution)/shard_map/ppermute | solution.py:294
  19.4 6.1 %collective-permute-start.12 = (bf16[40,768]{1,0:T(8,128)(2,1)S(1)}, bf16[40,768]{1,0:T(8,128)(2,1)S(1)}, u32[]{:S(2)}, u32[]{:S(2)}) collective-permute-start(bf16[40,768]{1,0:T(8,128)(2,1)S(1)} %get-tuple-element.45), channel_id=1, source_target_pairs={{0,24},{4,28},{8,16},{12,20},{16,8},{20,12},{24,0},{28,4},{1,25},{... | collective-permute-start | bytes 184328 | tf_op jit(solution)/shard_map/ppermute | solution.py:294
  22.3 5.9 %collective-permute-start.7 = (bf16[40,768]{1,0:T(8,128)(2,1)S(1)}, bf16[40,768]{1,0:T(8,128)(2,1)S(1)}, u32[]{:S(2)}, u32[]{:S(2)}) collective-permute-start(bf16[40,768]{1,0:T(8,128)(2,1)S(1)} %get-tuple-element.42), channel_id=1, source_target_pairs={{0,16},{4,20},{8,24},{12,28},{16,0},{20,4},{24,8},{28,12},{1,17},{... | collective-permute-start | bytes 184328 | tf_op jit(solution)/shard_map/ppermute | solution.py:294
  22.8 6.8 %collective-permute-start.9 = (bf16[40,768]{1,0:T(8,128)(2,1)S(1)}, bf16[40,768]{1,0:T(8,128)(2,1)S(1)}, u32[]{:S(2)}, u32[]{:S(2)}) collective-permute-start(bf16[40,768]{1,0:T(8,128)(2,1)S(1)} %get-tuple-element.43.refs_0_), channel_id=1, source_target_pairs={{0,2},{1,3},{2,0},{3,1},{4,6},{5,7},{6,4},{7,5},{8,10},{9,11},{10,... | collective-permute-start | bytes 184328 | tf_op jit(solution)/shard_map/ppermute | solution.py:300
  24.3 5.3 %collective-permute-start.11 = (bf16[40,768]{1,0:T(8,128)(2,1)S(1)}, bf16[40,768]{1,0:T(8,128)(2,1)S(1)}, u32[]{:S(2)}, u32[]{:S(2)}) collective-permute-start(bf16[40,768]{1,0:T(8,128)(2,1)S(1)} %collective-permute-done.10.refs_1_), channel_id=1, source_target_pairs={{0,2},{1,3},{2,0},{3,1},{4,6},{5,7},{6,4},{7,5},{8,10},{9,11},{10,... | collective-permute-start | bytes 184328 | tf_op jit(solution)/shard_map/ppermute | solution.py:300
  25.5 4.2 %collective-permute-start.13 = (bf16[40,768]{1,0:T(8,128)(2,1)S(1)}, bf16[40,768]{1,0:T(8,128)(2,1)S(1)}, u32[]{:S(2)}, u32[]{:S(2)}) collective-permute-start(bf16[40,768]{1,0:T(8,128)(2,1)S(1)} %collective-permute-done.12.refs_2_), channel_id=1, source_target_pairs={{0,2},{1,3},{2,0},{3,1},{4,6},{5,7},{6,4},{7,5},{8,10},{9,11},{10,... | collective-permute-start | bytes 184328 | tf_op jit(solution)/shard_map/ppermute | solution.py:300
  28.1 4.7 %collective-permute-start.15 = (bf16[120,768]{1,0:T(8,128)(2,1)S(1)}, bf16[120,768]{1,0:T(8,128)(2,1)S(1)}, u32[]{:S(2)}, u32[]{:S(2)}) collective-permute-start(bf16[120,768]{1,0:T(8,128)(2,1)S(1)} %get-tuple-element.54), channel_id=1, source_target_pairs={{0,1},{1,0},{2,3},{3,2},{4,5},{5,4},{6,7},{7,6},{8,9},{9,8},{10,11... | collective-permute-start | bytes 552968 | tf_op jit(solution)/shard_map/ppermute | solution.py:300
  28.2 4.4 %collective-permute-start.8 = (bf16[40,768]{1,0:T(8,128)(2,1)S(1)}, bf16[40,768]{1,0:T(8,128)(2,1)S(1)}, u32[]{:S(2)}, u32[]{:S(2)}) collective-permute-start(bf16[40,768]{1,0:T(8,128)(2,1)S(1)} %collective-permute-done.7.own_ref.refs_3_), channel_id=1, source_target_pairs={{0,2},{1,3},{2,0},{3,1},{4,6},{5,7},{6,4},{7,5},{8,10},{9,11},{10,... | collective-permute-start | bytes 184328 | tf_op jit(solution)/shard_map/ppermute | solution.py:300
  30.9 1.8 %collective-permute-start.17 = (bf16[80,768]{1,0:T(8,128)(2,1)S(1)}, bf16[80,768]{1,0:T(8,128)(2,1)S(1)}, u32[]{:S(2)}, u32[]{:S(2)}) collective-permute-start(bf16[80,768]{1,0:T(8,128)(2,1)S(1)} %get-tuple-element.55), channel_id=1, source_target_pairs={{0,1},{1,0},{2,3},{3,2},{4,5},{5,4},{6,7},{7,6},{8,9},{9,8},{10,11... | collective-permute-start | bytes 368648 | tf_op jit(solution)/shard_map/ppermute | solution.py:300
  31.0 1.6 %collective-permute-start.16 = (bf16[40,768]{1,0:T(8,128)(2,1)S(1)}, bf16[40,768]{1,0:T(8,128)(2,1)S(1)}, u32[]{:S(2)}, u32[]{:S(2)}) collective-permute-start(bf16[40,768]{1,0:T(8,128)(2,1)S(1)} %collective-permute-done.7.own_ref.refs_3_), channel_id=1, source_target_pairs={{0,1},{1,0},{2,3},{3,2},{4,5},{5,4},{6,7},{7,6},{8,9},{9,8},{10,11... | collective-permute-start | bytes 184328 | tf_op jit(solution)/shard_map/ppermute | solution.py:300
  31.5 1.2 %collective-permute-start.18 = (bf16[40,768]{1,0:T(8,128)(2,1)S(1)}, bf16[40,768]{1,0:T(8,128)(2,1)S(1)}, u32[]{:S(2)}, u32[]{:S(2)}) collective-permute-start(bf16[40,768]{1,0:T(8,128)(2,1)S(1)} %get-tuple-element.56), channel_id=1, source_target_pairs={{0,1},{1,0},{2,3},{3,2},{4,5},{5,4},{6,7},{7,6},{8,9},{9,8},{10,11... | collective-permute-start | bytes 184328 | tf_op jit(solution)/shard_map/ppermute | solution.py:300
  32.6 1.4 %collective-permute-start.14 = (bf16[40,768]{1,0:T(8,128)(2,1)S(1)}, bf16[40,768]{1,0:T(8,128)(2,1)S(1)}, u32[]{:S(2)}, u32[]{:S(2)}) collective-permute-start(bf16[40,768]{1,0:T(8,128)(2,1)S(1)} %collective-permute-done.8.refs_4_), channel_id=1, source_target_pairs={{0,1},{1,0},{2,3},{3,2},{4,5},{5,4},{6,7},{7,6},{8,9},{9,8},{10,11... | collective-permute-start | bytes 184328 | tf_op jit(solution)/shard_map/ppermute | solution.py:300
  32.8 1.3 %copy-start.3 = (bf16[768,768]{1,0:T(8,128)(2,1)S(1)}, bf16[768,768]{1,0:T(8,128)(2,1)}, u32[]{:S(2)}) copy-start(bf16[768,768]{1,0:T(8,128)(2,1)} %refs_7_.1) | copy-start | bytes 3538948

commit v11 on v10

--- a/solution.py
+++ b/solution.py
@@ -255,11 +255,11 @@
     exps = [jnp.exp(s - top) for s in scores]
     scale = 1.0 / functools.reduce(jnp.add, exps)
     spread = head_lanes((128, D), 1)
-    c = None
-    for e, v in zip(exps, values):
-        p = jnp.dot((e * scale).astype(BF), spread, preferred_element_type=F32)
-        part = p * v
-        c = part if c is None else c + part
+    weights = jnp.concatenate([e * scale for e in exps], axis=0).astype(BF)
+    weights = jnp.dot(weights, spread, preferred_element_type=F32)
+    rows = scale.shape[0]
+    parts = (weights[i * rows : (i + 1) * rows] * v for i, v in enumerate(values))
+    c = functools.reduce(jnp.add, parts)
     out = jnp.dot(c.astype(BF), wo_ref[...], preferred_element_type=F32)
     out = (stacked(own) + out).astype(BF)
     put = token_rows(dims, own[0].shape[0], (out_ref.shape[0], n), z_ref[0])

time: 36.6 us -> 36.5 us (level)
  no operation moved by 1% of the time
where the time goes in v11:
time: 36.5 us; the launch traced here: 36.3 us
  starting transfers between devices  20.2 us (55%)
  Pallas kernels  9.06 us (25%)
  waiting for transfers between devices  4.9 us (13%)
  local copies, waits for them, and re-layouts  0.97 us (3%)
  between operations  0.82 us (2%)
    ppermute x6, starting transfers between devices, over_group(): lax.ppermute(x, 'seq', [(i, i ^ 2 * partner(m, groups)) for i in range(ow...  9.32 us
    pallas_call x7, Pallas kernels, call(): pl.pallas_call(kernel, out_shape=[jax.ShapeDtypeStruct(*o) for o in outs]...  9.06 us
    ppermute x9, starting transfers between devices, over_bin(): return lax.ppermute(x, 'bin', [(i, i ^ m) for i in range(4)])  5.8 us
    ppermute x4, starting transfers between devices, over_pair(): return lax.ppermute(x, 'seq', [(i, i ^ 1) for i in range(owners)])  5.07 us
    ppermute x6, waiting for transfers between devices, over_group(): lax.ppermute(x, 'seq', [(i, i ^ 2 * partner(m, groups)) for i in range(ow...  1.94 us
    ppermute x4, waiting for transfers between devices, over_pair(): return lax.ppermute(x, 'seq', [(i, i ^ 1) for i in range(owners)])  1.63 us
    ppermute x9, waiting for transfers between devices, over_bin(): return lax.ppermute(x, 'bin', [(i, i ^ m) for i in range(4)])  1.33 us
    unnamed x12, local copies, waits for them, and re-layouts  0.95 us
  transfers between devices with their start and end apart: 19, of which 7 were waited for; matrix products, arithmetic and copies ran while one was open for 1% of the time, Pallas kernels for 13%

profile of v11, /device:TPU:0, one launch (start us, length us, event | category | flops | bytes accessed | tf_op | source)
XLA Modules:
  0.0 36.3 jit_solution(10511512219564112678)
XLA Ops:
  0.0 0.9 %copy-done.4 = bf16[1,6,24,768]{3,2,1,0:T(8,128)(2,1)S(1)} copy-done((bf16[1,6,24,768]{3,2,1,0:T(8,128)(2,1)S(1)}, bf16[1,6,24,768]{3,2,1,0:T(8,128)(2,1)}, u32[]{:S(2)}) %copy-start.4) | copy-done | bytes 221208
  0.9 0.3 shard_map.73
  1.2 3.1 %collective-permute-start.1 = (bf16[40,768]{1,0:T(8,128)(2,1)S(1)}, bf16[40,768]{1,0:T(8,128)(2,1)S(1)}, u32[]{:S(2)}, u32[]{:S(2)}) collective-permute-start(bf16[40,768]{1,0:T(8,128)(2,1)S(1)} %get-tuple-element.33), channel_id=1, source_target_pairs={{0,8},{4,12},{8,0},{12,4},{16,24},{20,28},{24,16},{28,20},{1,9},{5... | collective-permute-start | bytes 184328 | tf_op jit(solution)/shard_map/ppermute | solution.py:294
  4.3 2.6 %collective-permute-start.3 = (bf16[40,768]{1,0:T(8,128)(2,1)S(1)}, bf16[40,768]{1,0:T(8,128)(2,1)S(1)}, u32[]{:S(2)}, u32[]{:S(2)}) collective-permute-start(bf16[40,768]{1,0:T(8,128)(2,1)S(1)} %get-tuple-element.35), channel_id=1, source_target_pairs={{0,16},{4,20},{8,24},{12,28},{16,0},{20,4},{24,8},{28,12},{1,17},{... | collective-permute-start | bytes 184328 | tf_op jit(solution)/shard_map/ppermute | solution.py:294
  6.9 1.7 %collective-permute-start = (bf16[40,768]{1,0:T(8,128)(2,1)S(1)}, bf16[40,768]{1,0:T(8,128)(2,1)S(1)}, u32[]{:S(2)}, u32[]{:S(2)}) collective-permute-start(bf16[40,768]{1,0:T(8,128)(2,1)S(1)} %get-tuple-element.32.refs_0_), channel_id=1, source_target_pairs={{0,4},{4,0},{8,12},{12,8},{16,20},{20,16},{24,28},{28,24},{1,5},{5... | collective-permute-start | bytes 184328 | tf_op jit(solution)/shard_map/ppermute | solution.py:297
  9.4 0.3 fusion
  9.7 0.4 %collective-permute-start.2 = (bf16[40,768]{1,0:T(8,128)(2,1)S(1)}, bf16[40,768]{1,0:T(8,128)(2,1)S(1)}, u32[]{:S(2)}, u32[]{:S(2)}) collective-permute-start(bf16[40,768]{1,0:T(8,128)(2,1)S(1)} %collective-permute-done.1.refs_1_), channel_id=1, source_target_pairs={{0,4},{4,0},{8,12},{12,8},{16,20},{20,16},{24,28},{28,24},{1,5},{5... | collective-permute-start | bytes 184328 | tf_op jit(solution)/shard_map/ppermute | solution.py:297
  10.1 0.6 %collective-permute-done.3.refs_2_ = bf16[40,768]{1,0:T(8,128)(2,1)S(1)} collective-permute-done((bf16[40,768]{1,0:T(8,128)(2,1)S(1)}, bf16[40,768]{1,0:T(8,128)(2,1)S(1)}, u32[]{:S(2)}, u32[]{:S(2)}) %collective-permute-start.3) | collective-permute-done | bytes 61472 | tf_op jit(solution)/shard_map/ppermute | solution.py:294
  10.7 1.5 %collective-permute-start.4 = (bf16[40,768]{1,0:T(8,128)(2,1)S(1)}, bf16[40,768]{1,0:T(8,128)(2,1)S(1)}, u32[]{:S(2)}, u32[]{:S(2)}) collective-permute-start(bf16[40,768]{1,0:T(8,128)(2,1)S(1)} %collective-permute-done.3.refs_2_), channel_id=1, source_target_pairs={{0,4},{4,0},{8,12},{12,8},{16,20},{20,16},{24,28},{28,24},{1,5},{5... | collective-permute-start | bytes 184328 | tf_op jit(solution)/shard_map/ppermute | solution.py:297
  12.1 0.8 %collective-permute-done.5.refs_3_ = bf16[40,768]{1,0:T(8,128)(2,1)S(1)} collective-permute-done((bf16[40,768]{1,0:T(8,128)(2,1)S(1)}, bf16[40,768]{1,0:T(8,128)(2,1)S(1)}, u32[]{:S(2)}, u32[]{:S(2)}) %collective-permute-start.5) | collective-permute-done | bytes 61472 | tf_op jit(solution)/shard_map/ppermute | solution.py:294
  12.9 1.5 %collective-permute-start.6 = (bf16[40,768]{1,0:T(8,128)(2,1)S(1)}, bf16[40,768]{1,0:T(8,128)(2,1)S(1)}, u32[]{:S(2)}, u32[]{:S(2)}) collective-permute-start(bf16[40,768]{1,0:T(8,128)(2,1)S(1)} %collective-permute-done.5.refs_3_), channel_id=1, source_target_pairs={{0,4},{4,0},{8,12},{12,8},{16,20},{20,16},{24,28},{28,24},{1,5},{5... | collective-permute-start | bytes 184328 | tf_op jit(solution)/shard_map/ppermute | solution.py:297
  14.4 1.1 %shard_map.74 = (bf16[144,768]{1,0:T(8,128)(2,1)S(1)}, bf16[144,768]{1,0:T(8,128)(2,1)S(1)}, bf16[144,768]{1,0:T(8,128)(2,1)S(1)}, bf16[144,768]{1,0:T(8,128)(2,1)S(1)}) custom-call(bf16[40,768]{1,0:T(8,128)(2,1)S(1)} %get-tuple-element.32.refs_0_, bf16[40,768]{1,0:T(8,128)(2,1)S(1)} %collective-permute-done.1.refs_1_, ...), custom_call_target="tpu_custom_call" | custom-call | flops 1000000 | bytes 1000 | tf_op jit(solution)/shard_map/pallas_call | solution.py:273
  15.5 1.6 %collective-permute-done.6.refs_3_ = bf16[40,768]{1,0:T(8,128)(2,1)S(1)} collective-permute-done((bf16[40,768]{1,0:T(8,128)(2,1)S(1)}, bf16[40,768]{1,0:T(8,128)(2,1)S(1)}, u32[]{:S(2)}, u32[]{:S(2)}) %collective-permute-start.6) | collective-permute-done | bytes 61472 | tf_op jit(solution)/shard_map/ppermute | solution.py:297
  17.1 2.0 %shard_map.75 = (bf16[40,768]{1,0:T(8,128)(2,1)S(1)}, bf16[40,768]{1,0:T(8,128)(2,1)S(1)}, bf16[40,768]{1,0:T(8,128)(2,1)S(1)}, bf16[40,768]{1,0:T(8,128)(2,1)S(1)}) custom-call(bf16[40,768]{1,0:T(8,128)(2,1)S(1)} %collective-permute-done.refs_0_, bf16[40,768]{1,0:T(8,128)(2,1)S(1)} %collective-permute-done.2.refs_1_, ...), custom_call_target="tpu_custom_call" | custom-call | flops 1000000 | bytes 1000 | tf_op jit(solution)/shard_map/pallas_call | solution.py:273
  19.1 0.3 collective-permute-start.10
  19.4 2.9 %collective-permute-start.12 = (bf16[40,768]{1,0:T(8,128)(2,1)S(1)}, bf16[40,768]{1,0:T(8,128)(2,1)S(1)}, u32[]{:S(2)}, u32[]{:S(2)}) collective-permute-start(bf16[40,768]{1,0:T(8,128)(2,1)S(1)} %get-tuple-element.45), channel_id=1, source_target_pairs={{0,24},{4,28},{8,16},{12,20},{16,8},{20,12},{24,0},{28,4},{1,25},{... | collective-permute-start | bytes 184328 | tf_op jit(solution)/shard_map/ppermute | solution.py:294
  22.3 0.5 %collective-permute-start.7 = (bf16[40,768]{1,0:T(8,128)(2,1)S(1)}, bf16[40,768]{1,0:T(8,128)(2,1)S(1)}, u32[]{:S(2)}, u32[]{:S(2)}) collective-permute-start(bf16[40,768]{1,0:T(8,128)(2,1)S(1)} %get-tuple-element.42), channel_id=1, source_target_pairs={{0,16},{4,20},{8,24},{12,28},{16,0},{20,4},{24,8},{28,12},{1,17},{... | collective-permute-start | bytes 184328 | tf_op jit(solution)/shard_map/ppermute | solution.py:294
  22.8 1.5 %collective-permute-start.9 = (bf16[40,768]{1,0:T(8,128)(2,1)S(1)}, bf16[40,768]{1,0:T(8,128)(2,1)S(1)}, u32[]{:S(2)}, u32[]{:S(2)}) collective-permute-start(bf16[40,768]{1,0:T(8,128)(2,1)S(1)} %get-tuple-element.43.refs_0_), channel_id=1, source_target_pairs={{0,2},{1,3},{2,0},{3,1},{4,6},{5,7},{6,4},{7,5},{8,10},{9,11},{10,... | collective-permute-start | bytes 184328 | tf_op jit(solution)/shard_map/ppermute | solution.py:300
  24.3 0.6 %collective-permute-start.11 = (bf16[40,768]{1,0:T(8,128)(2,1)S(1)}, bf16[40,768]{1,0:T(8,128)(2,1)S(1)}, u32[]{:S(2)}, u32[]{:S(2)}) collective-permute-start(bf16[40,768]{1,0:T(8,128)(2,1)S(1)} %collective-permute-done.10.refs_1_), channel_id=1, source_target_pairs={{0,2},{1,3},{2,0},{3,1},{4,6},{5,7},{6,4},{7,5},{8,10},{9,11},{10,... | collective-permute-start | bytes 184328 | tf_op jit(solution)/shard_map/ppermute | solution.py:300
  24.9 0.6 %collective-permute-done.12.refs_2_ = bf16[40,768]{1,0:T(8,128)(2,1)S(1)} collective-permute-done((bf16[40,768]{1,0:T(8,128)(2,1)S(1)}, bf16[40,768]{1,0:T(8,128)(2,1)S(1)}, u32[]{:S(2)}, u32[]{:S(2)}) %collective-permute-start.12) | collective-permute-done | bytes 61472 | tf_op jit(solution)/shard_map/ppermute | solution.py:294
  25.5 1.5 %collective-permute-start.13 = (bf16[40,768]{1,0:T(8,128)(2,1)S(1)}, bf16[40,768]{1,0:T(8,128)(2,1)S(1)}, u32[]{:S(2)}, u32[]{:S(2)}) collective-permute-start(bf16[40,768]{1,0:T(8,128)(2,1)S(1)} %collective-permute-done.12.refs_2_), channel_id=1, source_target_pairs={{0,2},{1,3},{2,0},{3,1},{4,6},{5,7},{6,4},{7,5},{8,10},{9,11},{10,... | collective-permute-start | bytes 184328 | tf_op jit(solution)/shard_map/ppermute | solution.py:300
  27.0 1.0 %shard_map.76 = (bf16[120,768]{1,0:T(8,128)(2,1)S(1)}, bf16[120,768]{1,0:T(8,128)(2,1)S(1)}, f32[120,128]{1,0:T(8,128)S(1)}, bf16[120,768]{1,0:T(8,128)(2,1)S(1)}) custom-call(bf16[40,768]{1,0:T(8,128)(2,1)S(1)} %get-tuple-element.43.refs_0_, bf16[40,768]{1,0:T(8,128)(2,1)S(1)} %collective-permute-done.10.refs_1_, ...), custom_call_target="tpu_custom_call" | custom-call | flops 1000000 | bytes 1000 | tf_op jit(solution)/shard_map/pallas_call | solution.py:273
  28.1 0.1 collective-permute-start.15
  28.2 1.4 %collective-permute-start.8 = (bf16[40,768]{1,0:T(8,128)(2,1)S(1)}, bf16[40,768]{1,0:T(8,128)(2,1)S(1)}, u32[]{:S(2)}, u32[]{:S(2)}) collective-permute-start(bf16[40,768]{1,0:T(8,128)(2,1)S(1)} %collective-permute-done.7.own_ref.refs_3_), channel_id=1, source_target_pairs={{0,2},{1,3},{2,0},{3,1},{4,6},{5,7},{6,4},{7,5},{8,10},{9,11},{10,... | collective-permute-start | bytes 184328 | tf_op jit(solution)/shard_map/ppermute | solution.py:300
  29.6 0.1 collective-permute-done.13.refs_2_
  29.7 1.2 %shard_map.77 = (bf16[40,768]{1,0:T(8,128)(2,1)S(1)}, bf16[160,768]{1,0:T(8,128)(2,1)S(1)}, f32[160,128]{1,0:T(8,128)S(1)}, bf16[80,768]{1,0:T(8,128)(2,1)S(1)}, bf16[40,768]{1,0:T(8,128)(2,1)S(1)}) custom-call(bf16[40,768]{1,0:T(8,128)(2,1)S(1)} %collective-permute-done.7.own_ref.refs_3_, bf16[40,768]{1,0:T(8,128)(2,1)S(1)} %collective-permute-done.9.refs_0_, ...), custom_call_target="tpu_custom_call" | custom-call | flops 1000000 | bytes 1000 | tf_op jit(solution)/shard_map/pallas_call | solution.py:273
  31.0 0.5 %collective-permute-start.16 = (bf16[40,768]{1,0:T(8,128)(2,1)S(1)}, bf16[40,768]{1,0:T(8,128)(2,1)S(1)}, u32[]{:S(2)}, u32[]{:S(2)}) collective-permute-start(bf16[40,768]{1,0:T(8,128)(2,1)S(1)} %collective-permute-done.7.own_ref.refs_3_), channel_id=1, source_target_pairs={{0,1},{1,0},{2,3},{3,2},{4,5},{5,4},{6,7},{7,6},{8,9},{9,8},{10,11... | collective-permute-start | bytes 184328 | tf_op jit(solution)/shard_map/ppermute | solution.py:300
  31.5 0.1 collective-permute-start.18
  31.6 1.0 %collective-permute-done.8.refs_4_ = bf16[40,768]{1,0:T(8,128)(2,1)S(1)} collective-permute-done((bf16[40,768]{1,0:T(8,128)(2,1)S(1)}, bf16[40,768]{1,0:T(8,128)(2,1)S(1)}, u32[]{:S(2)}, u32[]{:S(2)}) %collective-permute-start.8) | collective-permute-done | bytes 61472 | tf_op jit(solution)/shard_map/ppermute | solution.py:300
  32.6 0.2 collective-permute-done.18.refs_3_
  32.8 1.3 %shard_map.78 = (bf16[320,768]{1,0:T(8,128)(2,1)S(1)}, f32[320,128]{1,0:T(8,128)S(1)}) custom-call(bf16[120,768]{1,0:T(8,128)(2,1)S(1)} %collective-permute-done.15.refs_0_, bf16[40,768]{1,0:T(8,128)(2,1)S(1)} %collective-permute-done.16.refs_1_, bf16[80,768]{1,0:T(8,128)(2,1)S(1)} %collective-permute-done.17.refs_2_, ...), custom_call_target="tpu_custom_call" | custom-call | flops 1000000 | bytes 1000 | tf_op jit(solution)/shard_map/pallas_call | solution.py:273
  34.0 2.3 %shard_map.79 = bf16[144,768]{1,0:T(8,128)(2,1)} custom-call(s32[1]{0:T(128)} %bitcast.z_ref, bf16[40,768]{1,0:T(8,128)(2,1)S(1)} %collective-permute-done.14.last_ref, bf16[40,768]{1,0:T(8,128)(2,1)S(1)} %get-tuple-element.43.refs_0_, bf16[40,768]{1,0:T(8,128)(2,1)S(1)} %collective-permute-done.10.refs_1_, ...), custom_call_target="tpu_custom_call" | custom-call | flops 1000000 | bytes 1000 | tf_op jit(solution)/shard_map/pallas_call | solution.py:273
  (30 shorter events, 0.2 us)
Async XLA Ops:
  0.0 0.9 %copy-start.4 = (bf16[1,6,24,768]{3,2,1,0:T(8,128)(2,1)S(1)}, bf16[1,6,24,768]{3,2,1,0:T(8,128)(2,1)}, u32[]{:S(2)}) copy-start(bf16[1,6,24,768]{3,2,1,0:T(8,128)(2,1)} %param.7) | copy-start | bytes 663556
  0.9 8.4 %copy-start.5 = (bf16[256,3072]{1,0:T(8,128)(2,1)S(1)}, bf16[256,3072]{1,0:T(8,128)(2,1)}, u32[]{:S(2)}) copy-start(bf16[256,3072]{1,0:T(8,128)(2,1)} %param.9) | copy-start | bytes 4718596
  0.9 13.5 %copy-start.1 = (bf16[768,2304]{1,0:T(8,128)(2,1)S(1)}, bf16[768,2304]{1,0:T(8,128)(2,1)}, u32[]{:S(2)}) copy-start(bf16[768,2304]{1,0:T(8,128)(2,1)} %refs_5_.4) | copy-start | bytes 10616836
  1.2 8.5 %collective-permute-start.1 = (bf16[40,768]{1,0:T(8,128)(2,1)S(1)}, bf16[40,768]{1,0:T(8,128)(2,1)S(1)}, u32[]{:S(2)}, u32[]{:S(2)}) collective-permute-start(bf16[40,768]{1,0:T(8,128)(2,1)S(1)} %get-tuple-element.33), channel_id=1, source_target_pairs={{0,8},{4,12},{8,0},{12,4},{16,24},{20,28},{24,16},{28,20},{1,9},{5... | collective-permute-start | bytes 184328 | tf_op jit(solution)/shard_map/ppermute | solution.py:294
  4.3 6.4 %collective-permute-start.3 = (bf16[40,768]{1,0:T(8,128)(2,1)S(1)}, bf16[40,768]{1,0:T(8,128)(2,1)S(1)}, u32[]{:S(2)}, u32[]{:S(2)}) collective-permute-start(bf16[40,768]{1,0:T(8,128)(2,1)S(1)} %get-tuple-element.35), channel_id=1, source_target_pairs={{0,16},{4,20},{8,24},{12,28},{16,0},{20,4},{24,8},{28,12},{1,17},{... | collective-permute-start | bytes 184328 | tf_op jit(solution)/shard_map/ppermute | solution.py:294
  6.9 6.0 %collective-permute-start.5 = (bf16[40,768]{1,0:T(8,128)(2,1)S(1)}, bf16[40,768]{1,0:T(8,128)(2,1)S(1)}, u32[]{:S(2)}, u32[]{:S(2)}) collective-permute-start(bf16[40,768]{1,0:T(8,128)(2,1)S(1)} %get-tuple-element.36), channel_id=1, source_target_pairs={{0,24},{4,28},{8,16},{12,20},{16,8},{20,12},{24,0},{28,4},{1,25},{... | collective-permute-start | bytes 184328 | tf_op jit(solution)/shard_map/ppermute | solution.py:294
  6.9 8.6 %collective-permute-start = (bf16[40,768]{1,0:T(8,128)(2,1)S(1)}, bf16[40,768]{1,0:T(8,128)(2,1)S(1)}, u32[]{:S(2)}, u32[]{:S(2)}) collective-permute-start(bf16[40,768]{1,0:T(8,128)(2,1)S(1)} %get-tuple-element.32.refs_0_), channel_id=1, source_target_pairs={{0,4},{4,0},{8,12},{12,8},{16,20},{20,16},{24,28},{28,24},{1,5},{5... | collective-permute-start | bytes 184328 | tf_op jit(solution)/shard_map/ppermute | solution.py:297
  9.7 7.5 %copy-start.2 = (bf16[768,768]{1,0:T(8,128)(2,1)S(1)}, bf16[768,768]{1,0:T(8,128)(2,1)}, u32[]{:S(2)}) copy-start(bf16[768,768]{1,0:T(8,128)(2,1)} %refs_6_.2) | copy-start | bytes 3538948
  9.7 5.8 %collective-permute-start.2 = (bf16[40,768]{1,0:T(8,128)(2,1)S(1)}, bf16[40,768]{1,0:T(8,128)(2,1)S(1)}, u32[]{:S(2)}, u32[]{:S(2)}) collective-permute-start(bf16[40,768]{1,0:T(8,128)(2,1)S(1)} %collective-permute-done.1.refs_1_), channel_id=1, source_target_pairs={{0,4},{4,0},{8,12},{12,8},{16,20},{20,16},{24,28},{28,24},{1,5},{5... | collective-permute-start | bytes 184328 | tf_op jit(solution)/shard_map/ppermute | solution.py:297
  10.7 4.8 %collective-permute-start.4 = (bf16[40,768]{1,0:T(8,128)(2,1)S(1)}, bf16[40,768]{1,0:T(8,128)(2,1)S(1)}, u32[]{:S(2)}, u32[]{:S(2)}) collective-permute-start(bf16[40,768]{1,0:T(8,128)(2,1)S(1)} %collective-permute-done.3.refs_2_), channel_id=1, source_target_pairs={{0,4},{4,0},{8,12},{12,8},{16,20},{20,16},{24,28},{28,24},{1,5},{5... | collective-permute-start | bytes 184328 | tf_op jit(solution)/shard_map/ppermute | solution.py:297
  12.9 4.2 %collective-permute-start.6 = (bf16[40,768]{1,0:T(8,128)(2,1)S(1)}, bf16[40,768]{1,0:T(8,128)(2,1)S(1)}, u32[]{:S(2)}, u32[]{:S(2)}) collective-permute-start(bf16[40,768]{1,0:T(8,128)(2,1)S(1)} %collective-permute-done.5.refs_3_), channel_id=1, source_target_pairs={{0,4},{4,0},{8,12},{12,8},{16,20},{20,16},{24,28},{28,24},{1,5},{5... | collective-permute-start | bytes 184328 | tf_op jit(solution)/shard_map/ppermute | solution.py:297
  17.1 9.9 %copy-start = (bf16[768,2304]{1,0:T(8,128)(2,1)S(1)}, bf16[768,2304]{1,0:T(8,128)(2,1)}, u32[]{:S(2)}) copy-start(bf16[768,2304]{1,0:T(8,128)(2,1)} %refs_6_.3) | copy-start | bytes 10616836
  19.1 5.2 %collective-permute-start.10 = (bf16[40,768]{1,0:T(8,128)(2,1)S(1)}, bf16[40,768]{1,0:T(8,128)(2,1)S(1)}, u32[]{:S(2)}, u32[]{:S(2)}) collective-permute-start(bf16[40,768]{1,0:T(8,128)(2,1)S(1)} %get-tuple-element.44), channel_id=1, source_target_pairs={{0,8},{4,12},{8,0},{12,4},{16,24},{20,28},{24,16},{28,20},{1,9},{5... | collective-permute-start | bytes 184328 | tf_op jit(solution)/shard_map/ppermute | solution.py:294
  19.4 6.1 %collective-permute-start.12 = (bf16[40,768]{1,0:T(8,128)(2,1)S(1)}, bf16[40,768]{1,0:T(8,128)(2,1)S(1)}, u32[]{:S(2)}, u32[]{:S(2)}) collective-permute-start(bf16[40,768]{1,0:T(8,128)(2,1)S(1)} %get-tuple-element.45), channel_id=1, source_target_pairs={{0,24},{4,28},{8,16},{12,20},{16,8},{20,12},{24,0},{28,4},{1,25},{... | collective-permute-start | bytes 184328 | tf_op jit(solution)/shard_map/ppermute | solution.py:294
  22.3 5.9 %collective-permute-start.7 = (bf16[40,768]{1,0:T(8,128)(2,1)S(1)}, bf16[40,768]{1,0:T(8,128)(2,1)S(1)}, u32[]{:S(2)}, u32[]{:S(2)}) collective-permute-start(bf16[40,768]{1,0:T(8,128)(2,1)S(1)} %get-tuple-element.42), channel_id=1, source_target_pairs={{0,16},{4,20},{8,24},{12,28},{16,0},{20,4},{24,8},{28,12},{1,17},{... | collective-permute-start | bytes 184328 | tf_op jit(solution)/shard_map/ppermute | solution.py:294
  22.8 6.8 %collective-permute-start.9 = (bf16[40,768]{1,0:T(8,128)(2,1)S(1)}, bf16[40,768]{1,0:T(8,128)(2,1)S(1)}, u32[]{:S(2)}, u32[]{:S(2)}) collective-permute-start(bf16[40,768]{1,0:T(8,128)(2,1)S(1)} %get-tuple-element.43.refs_0_), channel_id=1, source_target_pairs={{0,2},{1,3},{2,0},{3,1},{4,6},{5,7},{6,4},{7,5},{8,10},{9,11},{10,... | collective-permute-start | bytes 184328 | tf_op jit(solution)/shard_map/ppermute | solution.py:300
  24.3 5.3 %collective-permute-start.11 = (bf16[40,768]{1,0:T(8,128)(2,1)S(1)}, bf16[40,768]{1,0:T(8,128)(2,1)S(1)}, u32[]{:S(2)}, u32[]{:S(2)}) collective-permute-start(bf16[40,768]{1,0:T(8,128)(2,1)S(1)} %collective-permute-done.10.refs_1_), channel_id=1, source_target_pairs={{0,2},{1,3},{2,0},{3,1},{4,6},{5,7},{6,4},{7,5},{8,10},{9,11},{10,... | collective-permute-start | bytes 184328 | tf_op jit(solution)/shard_map/ppermute | solution.py:300
  25.5 4.2 %collective-permute-start.13 = (bf16[40,768]{1,0:T(8,128)(2,1)S(1)}, bf16[40,768]{1,0:T(8,128)(2,1)S(1)}, u32[]{:S(2)}, u32[]{:S(2)}) collective-permute-start(bf16[40,768]{1,0:T(8,128)(2,1)S(1)} %collective-permute-done.12.refs_2_), channel_id=1, source_target_pairs={{0,2},{1,3},{2,0},{3,1},{4,6},{5,7},{6,4},{7,5},{8,10},{9,11},{10,... | collective-permute-start | bytes 184328 | tf_op jit(solution)/shard_map/ppermute | solution.py:300
  28.1 4.7 %collective-permute-start.15 = (bf16[120,768]{1,0:T(8,128)(2,1)S(1)}, bf16[120,768]{1,0:T(8,128)(2,1)S(1)}, u32[]{:S(2)}, u32[]{:S(2)}) collective-permute-start(bf16[120,768]{1,0:T(8,128)(2,1)S(1)} %get-tuple-element.54), channel_id=1, source_target_pairs={{0,1},{1,0},{2,3},{3,2},{4,5},{5,4},{6,7},{7,6},{8,9},{9,8},{10,11... | collective-permute-start | bytes 552968 | tf_op jit(solution)/shard_map/ppermute | solution.py:300
  28.2 4.4 %collective-permute-start.8 = (bf16[40,768]{1,0:T(8,128)(2,1)S(1)}, bf16[40,768]{1,0:T(8,128)(2,1)S(1)}, u32[]{:S(2)}, u32[]{:S(2)}) collective-permute-start(bf16[40,768]{1,0:T(8,128)(2,1)S(1)} %collective-permute-done.7.own_ref.refs_3_), channel_id=1, source_target_pairs={{0,2},{1,3},{2,0},{3,1},{4,6},{5,7},{6,4},{7,5},{8,10},{9,11},{10,... | collective-permute-start | bytes 184328 | tf_op jit(solution)/shard_map/ppermute | solution.py:300
  30.9 1.8 %collective-permute-start.17 = (bf16[80,768]{1,0:T(8,128)(2,1)S(1)}, bf16[80,768]{1,0:T(8,128)(2,1)S(1)}, u32[]{:S(2)}, u32[]{:S(2)}) collective-permute-start(bf16[80,768]{1,0:T(8,128)(2,1)S(1)} %get-tuple-element.55), channel_id=1, source_target_pairs={{0,1},{1,0},{2,3},{3,2},{4,5},{5,4},{6,7},{7,6},{8,9},{9,8},{10,11... | collective-permute-start | bytes 368648 | tf_op jit(solution)/shard_map/ppermute | solution.py:300
  31.0 1.6 %collective-permute-start.16 = (bf16[40,768]{1,0:T(8,128)(2,1)S(1)}, bf16[40,768]{1,0:T(8,128)(2,1)S(1)}, u32[]{:S(2)}, u32[]{:S(2)}) collective-permute-start(bf16[40,768]{1,0:T(8,128)(2,1)S(1)} %collective-permute-done.7.own_ref.refs_3_), channel_id=1, source_target_pairs={{0,1},{1,0},{2,3},{3,2},{4,5},{5,4},{6,7},{7,6},{8,9},{9,8},{10,11... | collective-permute-start | bytes 184328 | tf_op jit(solution)/shard_map/ppermute | solution.py:300
  31.5 1.2 %collective-permute-start.18 = (bf16[40,768]{1,0:T(8,128)(2,1)S(1)}, bf16[40,768]{1,0:T(8,128)(2,1)S(1)}, u32[]{:S(2)}, u32[]{:S(2)}) collective-permute-start(bf16[40,768]{1,0:T(8,128)(2,1)S(1)} %get-tuple-element.56), channel_id=1, source_target_pairs={{0,1},{1,0},{2,3},{3,2},{4,5},{5,4},{6,7},{7,6},{8,9},{9,8},{10,11... | collective-permute-start | bytes 184328 | tf_op jit(solution)/shard_map/ppermute | solution.py:300
  32.6 1.4 %collective-permute-start.14 = (bf16[40,768]{1,0:T(8,128)(2,1)S(1)}, bf16[40,768]{1,0:T(8,128)(2,1)S(1)}, u32[]{:S(2)}, u32[]{:S(2)}) collective-permute-start(bf16[40,768]{1,0:T(8,128)(2,1)S(1)} %collective-permute-done.8.refs_4_), channel_id=1, source_target_pairs={{0,1},{1,0},{2,3},{3,2},{4,5},{5,4},{6,7},{7,6},{8,9},{9,8},{10,11... | collective-permute-start | bytes 184328 | tf_op jit(solution)/shard_map/ppermute | solution.py:300
  32.8 1.3 %copy-start.3 = (bf16[768,768]{1,0:T(8,128)(2,1)S(1)}, bf16[768,768]{1,0:T(8,128)(2,1)}, u32[]{:S(2)}) copy-start(bf16[768,768]{1,0:T(8,128)(2,1)} %refs_7_.1) | copy-start | bytes 3538948
